TPU v7x, 32 devices: a whole 2x2x4 slice. The times are simulated.
32 devices in a mesh: pa: 8 (over z, y), sa: 4 (over x, core).
Axes of the slice: x: 2, y: 2, z: 4, core: 2. Of those that a mesh axis runs over, the one named last changes fastest.
Arguments:
- raw_echo: bfloat16 [256, 2, 32768], P('pa', None, 'sa'), may hold values from -6 to 6
- chirp_replica: bfloat16 [2, 1024], replicated, may hold values from -0.125 to 0.125
- azimuth_refs: bfloat16 [64, 2, 512], P('pa'), may hold values from -0.1875 to 0.1875
- migration_index: int32 [4, 8], replicated, may hold values from 0 to 63
- window_start: int32 [1], replicated, may hold values from 0 to 2047
Outputs:
- image: float32 [4, 4096, 2, 256], P('sa', 'pa')
All inputs are finite; a program needn't handle non-finite values.
Results may differ from a plain program's by a relative error of at most 0.0029.
Values may be sent and summed in bfloat16 or wider, within the bound.
No kernel may reach another device: no remote copies, remote signals or barrier semaphores. Data moves between devices by JAX's collectives and lax.ppermute only.
A program may use at most 64 MiB of HBM per device.

v0:
```python
import jax
import jax.numpy as jnp
from jax import lax
from jax.sharding import PartitionSpec as P

R = 16384
L = 512
RB = 256


def passed_along(value, axis, steps):
    count = lax.axis_size(axis)
    initial, last = (max(0, -steps), min(count, count - steps))
    return lax.ppermute(value, axis, [(source, source + steps) for source in range(initial, last)])


def toeplitz(diagonal_taps, size):
    span_size = 2 * size - 1
    reversed_taps = diagonal_taps[..., ::-1]
    shifted = jnp.concatenate(
        [reversed_taps[..., size - 1 :], reversed_taps[..., : size - 1]], axis=-1
    )
    reps = (1,) * (shifted.ndim - 1) + (size,)
    tiled_flat = jnp.tile(shifted, reps)[..., : size * (span_size - 1)]
    return tiled_flat.reshape(shifted.shape[:-1] + (size, span_size - 1))[..., :size]


def tap_blocks(tap_values, size):
    block_total = tap_values.shape[1] // size + 1
    padded_taps = jnp.pad(tap_values, ((0, 0), (size, 2 * size)))
    matrices = []
    for offset_block in range(block_total):
        first_tap = offset_block * size + 1
        parts = toeplitz(padded_taps[:, first_tap : first_tap + 2 * size - 1], size)
        real_part = parts[0]
        imag_part = parts[1]
        matrices.append(
            jnp.stack([jnp.stack([real_part, -imag_part]), jnp.stack([imag_part, real_part])])
        )
    return jnp.stack(matrices)


def correlate(blocked, matrices, output_count):
    summed = jnp.zeros((blocked.shape[0], 2, output_count, blocked.shape[3]), jnp.float32)
    for offset_block in range(matrices.shape[0]):
        piece_rows = blocked[:, :, offset_block : offset_block + output_count, :]
        summed = summed + jnp.einsum(
            "rcib,cdbn->rdin",
            piece_rows,
            matrices[offset_block],
            preferred_element_type=jnp.float32,
        )
    return summed


def compress(samples, matrices, output_count):
    pulse_count = samples.shape[0]
    blocked = samples.reshape(pulse_count, 2, -1, RB)
    focused = correlate(blocked, matrices, output_count)
    return focused.astype(jnp.bfloat16).reshape(pulse_count, 2, output_count * RB)


def cut_slots(source_data, base_offset, stride, length, slot_count):
    padded = jnp.pad(source_data, ((0, 0), (0, 0), (length, length)))
    limit = source_data.shape[2] + length
    slot_list = []
    for target in range(slot_count):
        slot_offset = jnp.clip(base_offset + target * stride + length, 0, limit)
        slot_list.append(lax.dynamic_slice_in_dim(padded, slot_offset, length, 2))
    return jnp.stack(slot_list)


def on_device(raw_echo, chirp_replica, azimuth_refs, migration_index, window_start):
    segment = raw_echo.shape[2]
    segment_devices = lax.axis_size("sa")
    pulse_devices = lax.axis_size("pa")
    sub_index = lax.axis_index("sa")
    bin_owner = lax.axis_index("pa")
    tap_count = chirp_replica.shape[1]
    kept_width = R // segment_devices
    window_first = window_start[0]
    range_mats = tap_blocks(chirp_replica, RB)
    base_offset = window_first - sub_index * segment
    next_edge = passed_along(raw_echo[:, :, :tap_count], "sa", -1)
    extended = jnp.concatenate([raw_echo, next_edge], axis=2)
    compressed = compress(extended, range_mats, segment // RB)
    slot_stack = cut_slots(compressed, base_offset, kept_width, kept_width, segment_devices)
    incoming = lax.all_to_all(slot_stack, "sa", split_axis=0, concat_axis=0, tiled=True)
    kept_bins = jnp.sum(incoming.astype(jnp.float32), axis=0).astype(jnp.bfloat16)
    pulse_count = kept_bins.shape[0]
    bin_count = kept_width // pulse_devices
    outgoing = jnp.transpose(kept_bins, (2, 1, 0)).reshape(pulse_devices, bin_count, 2, pulse_count)
    turned = lax.all_to_all(outgoing, "pa", split_axis=0, concat_axis=3, tiled=True)
    range_lines = turned[0]
    row_index = migration_index[sub_index, bin_owner]
    shard_piece = lax.all_gather(azimuth_refs, "pa", axis=0, tiled=True)
    row_ids = jnp.arange(shard_piece.shape[0])
    selector = (row_ids == row_index).astype(jnp.float32)
    chosen = jnp.tensordot(selector, shard_piece.astype(jnp.float32), axes=1)
    reference_row = chosen.astype(jnp.bfloat16)
    block_size = L // 2
    az_mats = tap_blocks(reference_row, block_size)
    total_pulses = range_lines.shape[2]
    block_count = total_pulses // block_size
    blocked = range_lines.reshape(bin_count, 2, block_count, block_size)
    blocked = jnp.pad(blocked, ((0, 0), (0, 0), (1, 1), (0, 0)))
    focused = correlate(blocked, az_mats, block_count)
    return focused.reshape(1, bin_count, 2, total_pulses)


def solution(mesh):
    placed = (P("pa", None, "sa"), P(), P("pa", None, None), P(), P())
    return jax.shard_map(
        on_device, mesh=mesh, in_specs=placed, out_specs=P("sa", "pa", None, None), check_vma=False
    )
```

profile of v0, /device:TPU:2, one launch (start us, length us, event | category | flops | bytes accessed | tf_op | source)
XLA Modules:
  0.0 102.1 jit_solution(13091503396666390175)
XLA Ops:
  1.0 1.9 %collective-permute-start = (bf16[32,2,1024]{2,1,0:T(2,128)(2,1)S(1)}, bf16[32,2,1024]{2,1,0:T(2,128)(2,1)}, u32[]{:S(2)}, u32[]{:S(2)}) collective-permute-start(bf16[32,2,1024]{2,1,0:T(2,128)(2,1)S(1)} %slice.259), channel_id=1, source_target_pairs={{1,0},{2,1},{3,2},{5,4},{6,5},{7,6},{9,8},{10,9},{11,10},{13,12},{... | collective-permute-start | bytes 393224 | tf_op jit(solution)/shard_map/ppermute | solution.py:14
  5.1 1.5 %tile.39 = bf16[2,130816]{1,0:T(2,128)(2,1)S(1)} reshape(bf16[2,256,511]{2,1,0:T(8,128)(2,1)S(1)} %tile.38) | data formatting | bytes 1046528 | tf_op jit(solution)/shard_map/tile | solution.py:24
  8.6 1.5 %tile.37 = bf16[2,130816]{1,0:T(2,128)(2,1)S(1)} reshape(bf16[2,256,511]{2,1,0:T(8,128)(2,1)S(1)} %tile.36) | data formatting | bytes 1046528 | tf_op jit(solution)/shard_map/tile | solution.py:24
  10.5 1.0 %reshape.82 = bf16[2,256,510]{2,1,0:T(8,128)(2,1)S(1)} reshape(bf16[2,130560]{1,0:T(2,128)(2,1)S(1)} %slice.305) | data formatting | bytes 1044480 | tf_op jit(solution)/shard_map/reshape | solution.py:25
  12.1 1.5 %tile.81 = bf16[2,130816]{1,0:T(2,128)(2,1)S(1)} reshape(bf16[2,256,511]{2,1,0:T(8,128)(2,1)S(1)} %tile.80) | data formatting | bytes 1046528 | tf_op jit(solution)/shard_map/tile | solution.py:24
  14.0 1.0 %reshape.85 = bf16[2,256,510]{2,1,0:T(8,128)(2,1)S(1)} reshape(bf16[2,130560]{1,0:T(2,128)(2,1)S(1)} %slice.313) | data formatting | bytes 1044480 | tf_op jit(solution)/shard_map/reshape | solution.py:25
  15.6 1.5 %tile.83 = bf16[2,130816]{1,0:T(2,128)(2,1)S(1)} reshape(bf16[2,256,511]{2,1,0:T(8,128)(2,1)S(1)} %tile.82) | data formatting | bytes 1046528 | tf_op jit(solution)/shard_map/tile | solution.py:24
  17.5 1.0 %reshape.86 = bf16[2,256,510]{2,1,0:T(8,128)(2,1)S(1)} reshape(bf16[2,130560]{1,0:T(2,128)(2,1)S(1)} %slice.317) | data formatting | bytes 1044480 | tf_op jit(solution)/shard_map/reshape | solution.py:25
  19.0 1.5 %tile.85 = bf16[2,130816]{1,0:T(2,128)(2,1)S(1)} reshape(bf16[2,256,511]{2,1,0:T(8,128)(2,1)S(1)} %tile.84) | data formatting | bytes 1046528 | tf_op jit(solution)/shard_map/tile | solution.py:24
  20.9 1.0 %reshape.87 = bf16[2,256,510]{2,1,0:T(8,128)(2,1)S(1)} reshape(bf16[2,130560]{1,0:T(2,128)(2,1)S(1)} %slice.321) | data formatting | bytes 1044480 | tf_op jit(solution)/shard_map/reshape | solution.py:25
  26.9 2.0 %pad_maximum_fusion.1 = bf16[32,2,9216]{2,1,0:T(2,128)(2,1)S(1)} fusion(bf16[32,2,1024]{2,1,0:T(2,128)(2,1)} %collective-permute-done, bf16[32,2,8192]{2,1,0:T(2,128)(2,1)S(1)} %copy-done), kind=kLoop, calls=%fused_computation.17 | loop fusion | flops 2359296 | bytes 2359296 | tf_op jit(solution)/shard_map/concatenate | solution.py:85
  29.7 1.8 %fusion.7 = f32[2,256,32,32,1]{1,3,4,2,0:T(8,128)S(1)} fusion(bf16[32,2,36,256]{3,2,1,0:T(8,128)(2,1)S(1)} %reshape.115, bf16[1,2,256,256]{3,2,0,1:T(8,128)(2,1)} %get-tuple-element.39, bf16[1,2,256,256]{3,2,0,1:T(8,128)(2,1)} %get-tuple-element.38), kind=kOutput, calls=%fused_computation.24 | convolution fusion | flops 537919488 | bytes 3670016 | tf_op jit(solution)/shard_map/rcib,cdbn->rdin/dot_general | solution.py:47
  37.0 1.6 %pad_maximum_fusion = bf16[4,32,2,4096]{3,1,2,0:T(8,128)(2,1)} fusion(bf16[1,32,2,4096]{3,1,2,0:T(8,128)(2,1)S(1)} %get-tuple-element.8, bf16[1,32,2,4096]{3,1,2,0:T(8,128)(2,1)S(1)} %get-tuple-element.7, bf16[1,32,2,4096]{3,1,2,0:T(8,128)(2,1)S(1)} %get-tuple-element.6, bf16[1,32,2,4096]{3,1,2,0:T(8,128)(2,1)S(1)} %get-tuple-element.5), kind=kLoop, calls=%fused_computation.4 | loop fusion | flops 3145728 | bytes 4194304 | tf_op jit(solution)/shard_map/stack | solution.py:70
  38.6 4.2 %all-to-all-start = ((bf16[4,32,2,4096]{3,1,2,0:T(8,128)(2,1)}), bf16[4,32,2,4096]{3,1,2,0:T(8,128)(2,1)S(1)}, u32[]{:S(2)}, u32[]{:S(2)}) async-start(bf16[4,32,2,4096]{3,1,2,0:T(8,128)(2,1)} %pad_maximum_fusion), calls=%async_computation | async-start | bytes 4194304 | tf_op jit(solution)/shard_map/all_to_all | solution.py:88
  42.8 1.3 %dynamic_slice.15 = s32[1,1]{1,0:T(1,128)} dynamic-slice(s32[4,8]{1,0:T(4,128)} %param.8, s32[]{:T(128)S(6)} %select_n.4, s32[]{:T(128)S(6)} %select_n.5), dynamic_slice_sizes={1,1} | dynamic-slice | bytes 12 | tf_op jit(solution)/shard_map/dynamic_slice | solution.py:95
  44.0 30.8 %all_gather.3 = bf16[64,2,512]{2,1,0:T(2,128)(2,1)S(1)} all-gather(bf16[8,2,512]{2,1,0:T(2,128)(2,1)S(1)} %copy-done.9), channel_id=1, replica_groups=mesh['pa'=8,'sa'=4] {'pa'}, dimensions={0}, use_global_device_ids=true | all-gather | bytes 147456 | tf_op jit(solution)/shard_map/all_gather | solution.py:96
  76.5 1.5 %tile.35 = bf16[2,130816]{1,0:T(2,128)(2,1)S(1)} reshape(bf16[2,256,511]{2,1,0:T(8,128)(2,1)S(1)} %tile.34) | data formatting | bytes 1046528 | tf_op jit(solution)/shard_map/tile | solution.py:24
  78.4 1.0 %reshape.81 = bf16[2,256,510]{2,1,0:T(8,128)(2,1)S(1)} reshape(bf16[2,130560]{1,0:T(2,128)(2,1)S(1)} %slice.302) | data formatting | bytes 1044480 | tf_op jit(solution)/shard_map/reshape | solution.py:25
  80.0 1.5 %tile.87 = bf16[2,130816]{1,0:T(2,128)(2,1)S(1)} reshape(bf16[2,256,511]{2,1,0:T(8,128)(2,1)S(1)} %tile.86) | data formatting | bytes 1046528 | tf_op jit(solution)/shard_map/tile | solution.py:24
  84.1 5.5 %all-to-all-start.1 = ((bf16[8,512,2,32]{1,3,2,0:T(8,128)(2,1)}), bf16[8,512,2,32]{1,3,2,0:T(8,128)(2,1)S(1)}, u32[]{:S(2)}, u32[]{:S(2)}) async-start(bf16[8,512,2,32]{1,3,2,0:T(8,128)(2,1)} %bitcast.181), calls=%async_computation.1 | async-start | bytes 1048576 | tf_op jit(solution)/shard_map/all_to_all | solution.py:93
  90.5 1.5 %tile.33 = bf16[2,130816]{1,0:T(2,128)(2,1)S(1)} reshape(bf16[2,256,511]{2,1,0:T(8,128)(2,1)S(1)} %tile.32) | data formatting | bytes 1046528 | tf_op jit(solution)/shard_map/tile | solution.py:24
  92.4 1.0 %reshape.80 = bf16[2,256,510]{2,1,0:T(8,128)(2,1)S(1)} reshape(bf16[2,130560]{1,0:T(2,128)(2,1)S(1)} %slice.297) | data formatting | bytes 1044480 | tf_op jit(solution)/shard_map/reshape | solution.py:25
  94.2 5.7 %all-to-all-done.1 = bf16[8,512,2,32]{1,3,2,0:T(8,128)(2,1)S(1)} async-done(((bf16[8,512,2,32]{1,3,2,0:T(8,128)(2,1)}), bf16[8,512,2,32]{1,3,2,0:T(8,128)(2,1)S(1)}, u32[]{:S(2)}, u32[]{:S(2)}) %all-to-all-start.1) | async-done | bytes 524320 | tf_op jit(solution)/shard_map/all_to_all | solution.py:93
  100.8 1.3 %copy.61 = f32[1,512,2,256]{3,2,1,0:T(2,128)} copy(f32[1,512,2,256]{1,3,2,0:T(8,128)S(1)} %fusion.4) | data formatting | bytes 2097152 | tf_op jit(solution)/shard_map/reshape | solution.py:108
  (113 shorter events, 26.3 us)
Async XLA Ops:
  1.0 25.9 %collective-permute-start = (bf16[32,2,1024]{2,1,0:T(2,128)(2,1)S(1)}, bf16[32,2,1024]{2,1,0:T(2,128)(2,1)}, u32[]{:S(2)}, u32[]{:S(2)}) collective-permute-start(bf16[32,2,1024]{2,1,0:T(2,128)(2,1)S(1)} %slice.259), channel_id=1, source_target_pairs={{1,0},{2,1},{3,2},{5,4},{6,5},{7,6},{9,8},{10,9},{11,10},{13,12},{... | collective-permute-start | bytes 393224 | tf_op jit(solution)/shard_map/ppermute | solution.py:14
  22.0 4.9 %copy-start = (bf16[32,2,8192]{2,1,0:T(2,128)(2,1)S(1)}, bf16[32,2,8192]{2,1,0:T(2,128)(2,1)}, u32[]{:S(2)}) copy-start(bf16[32,2,8192]{2,1,0:T(2,128)(2,1)} %param.5) | copy-start | bytes 3145732
  29.7 1.8 %copy-start.3 = (bf16[1,2,256,256]{3,2,0,1:T(8,128)(2,1)S(1)}, bf16[1,2,256,256]{3,2,0,1:T(8,128)(2,1)}, u32[]{:S(2)}) copy-start(bf16[1,2,256,256]{3,2,0,1:T(8,128)(2,1)} %get-tuple-element.36) | copy-start | bytes 786436
  29.7 1.8 %copy-start.4 = (bf16[1,2,256,256]{3,2,0,1:T(8,128)(2,1)S(1)}, bf16[1,2,256,256]{3,2,0,1:T(8,128)(2,1)}, u32[]{:S(2)}) copy-start(bf16[1,2,256,256]{3,2,0,1:T(8,128)(2,1)} %get-tuple-element.37) | copy-start | bytes 786436
  31.5 1.0 copy-start.5
  31.6 1.0 %copy-start.6 = (bf16[1,2,256,256]{3,2,0,1:T(8,128)(2,1)S(1)}, bf16[1,2,256,256]{3,2,0,1:T(8,128)(2,1)}, u32[]{:S(2)}) copy-start(bf16[1,2,256,256]{3,2,0,1:T(8,128)(2,1)} %get-tuple-element.41) | copy-start | bytes 786436
  32.6 0.9 copy-start.7
  32.6 1.0 %copy-start.8 = (bf16[1,2,256,256]{3,2,0,1:T(8,128)(2,1)S(1)}, bf16[1,2,256,256]{3,2,0,1:T(8,128)(2,1)}, u32[]{:S(2)}) copy-start(bf16[1,2,256,256]{3,2,0,1:T(8,128)(2,1)} %get-tuple-element.43) | copy-start | bytes 786436
  33.6 0.9 copy-start.1
  33.6 1.0 %copy-start.2 = (bf16[1,2,256,256]{3,2,0,1:T(8,128)(2,1)S(1)}, bf16[1,2,256,256]{3,2,0,1:T(8,128)(2,1)}, u32[]{:S(2)}) copy-start(bf16[1,2,256,256]{3,2,0,1:T(8,128)(2,1)} %get-tuple-element.35) | copy-start | bytes 786436
  38.6 5.4 %copy-start.9 = (bf16[8,2,512]{2,1,0:T(2,128)(2,1)S(1)}, bf16[8,2,512]{2,1,0:T(2,128)(2,1)}, u32[]{:S(2)}) copy-start(bf16[8,2,512]{2,1,0:T(2,128)(2,1)} %param.7) | copy-start | bytes 49156
  38.6 44.3 %all-to-all-start = ((bf16[4,32,2,4096]{3,1,2,0:T(8,128)(2,1)}), bf16[4,32,2,4096]{3,1,2,0:T(8,128)(2,1)S(1)}, u32[]{:S(2)}, u32[]{:S(2)}) async-start(bf16[4,32,2,4096]{3,1,2,0:T(8,128)(2,1)} %pad_maximum_fusion), calls=%async_computation | async-start | bytes 4194304 | tf_op jit(solution)/shard_map/all_to_all | solution.py:88
  84.1 15.8 %all-to-all-start.1 = ((bf16[8,512,2,32]{1,3,2,0:T(8,128)(2,1)}), bf16[8,512,2,32]{1,3,2,0:T(8,128)(2,1)S(1)}, u32[]{:S(2)}, u32[]{:S(2)}) async-start(bf16[8,512,2,32]{1,3,2,0:T(8,128)(2,1)} %bitcast.181), calls=%async_computation.1 | async-start | bytes 1048576 | tf_op jit(solution)/shard_map/all_to_all | solution.py:93
where the time goes:
time: 104 us; the launch traced here: 102 us
  local copies, waits for them, and re-layouts  37.3 us (36%)
  blocking collectives  30.8 us (30%)
  starting transfers between devices  11.6 us (11%)
  other arithmetic  8.59 us (8%)
  matrix products  6.83 us (7%)
  waiting for transfers between devices  5.73 us (6%)
  between operations  1.21 us (1%)
    all_gather x1, blocking collectives, on_device(): shard_piece = lax.all_gather(azimuth_refs, 'pa', axis=0, tiled=True)  30.8 us
    another operation x16, local copies, waits for them, and re-layouts, toeplitz(): tiled_flat = jnp.tile(shifted, reps)[..., :size * (span_size - 1)]  12.7 us
    reshape x8, local copies, waits for them, and re-layouts, toeplitz(): tiled_flat.reshape(shifted.shape[:-1] + (size, span_size - 1))[..., :size]  8.2 us
    dot_general x8, matrix products, correlate(): jnp.einsum('rcib,cdbn->rdin', piece_rows, matrices[offset_block], preferr...  6.05 us
    all_to_all x1, waiting for transfers between devices, on_device(): lax.all_to_all(outgoing, 'pa', split_axis=0, concat_axis=3, tiled=True)  5.72 us
    all_to_all x1, starting transfers between devices, on_device(): lax.all_to_all(outgoing, 'pa', split_axis=0, concat_axis=3, tiled=True)  5.53 us
    another operation x8, other arithmetic, tap_blocks(): jnp.stack([jnp.stack([real_part, -imag_part]), jnp.stack([imag_part, real...  4.35 us
    all_to_all x1, starting transfers between devices, on_device(): lax.all_to_all(slot_stack, 'sa', split_axis=0, concat_axis=0, tiled=True)  4.17 us
  transfers between devices with their start and end apart: 3, of which 1 were waited for; matrix products, arithmetic and copies ran while one was open for 36% of the time, Pallas kernels for 0%

commit v1 on v0

v1 whole, which is shorter than its diff:
```python
import jax
import jax.numpy as jnp
from jax import lax
from jax.experimental import pallas as pl
from jax.experimental.pallas import tpu as pltpu
from jax.sharding import PartitionSpec as P

R = 16384
L = 512
LANES = 128
BF = jnp.bfloat16
F32 = jnp.float32


def reversed_lanes(row):
    row_id = lax.broadcasted_iota(jnp.int32, (LANES, LANES), 0)
    col_id = lax.broadcasted_iota(jnp.int32, (LANES, LANES), 1)
    flip = (row_id + col_id == LANES - 1).astype(BF)
    tiles = row.shape[1] // LANES
    pieces = [row[:, t * LANES : (t + 1) * LANES] for t in reversed(range(tiles))]
    return jnp.concatenate([jnp.dot(piece, flip, preferred_element_type=F32) for piece in pieces], axis=1)


def prep_kernel(window_ref, index_ref, chirp_ref, refs_ref, taps_ref, rows_ref):
    taps = chirp_ref.shape[1]
    blocks = taps_ref.shape[0] // LANES
    width = blocks * LANES
    shift = lax.rem(window_ref[0], LANES)
    chirp = jnp.concatenate([chirp_ref[...], jnp.zeros((14, taps), BF)], axis=0)
    flipped = reversed_lanes(chirp)
    padded = jnp.concatenate([jnp.zeros((16, 2 * LANES), F32), flipped], axis=1)
    padded = jnp.concatenate([padded, jnp.zeros((16, width + LANES - padded.shape[1]), F32)], axis=1)
    moved = pltpu.roll(padded, width + LANES - 127 - shift, 1)[:, :width]
    for part in range(2):
        spread = jnp.broadcast_to(moved[part : part + 1], (LANES, width))
        skewed = pltpu.roll(spread, 0, 1, stride=1, stride_axis=0)
        for t in range(blocks):
            first = LANES * (blocks - 1 - t)
            taps_ref[t * LANES : (t + 1) * LANES, part * LANES : (part + 1) * LANES] = skewed[
                :, first : first + LANES
            ].astype(BF)
    own = refs_ref.shape[0]
    sub_index = lax.axis_index("sa")
    first_row = lax.axis_index("pa") * own

    def fill(target, carry):
        local = index_ref[sub_index, target] - first_row
        held = jnp.logical_and(local >= 0, local < own)
        row = refs_ref[jnp.clip(local, 0, own - 1)]
        rows_ref[target] = jnp.where(held, row, jnp.zeros_like(row))
        return carry

    lax.fori_loop(0, rows_ref.shape[0], fill, 0)


def compress_kernel(window_ref, own_ref, near_ref, far_ref, taps_ref, out_ref, held, sems):
    half = far_ref.shape[0]
    span = near_ref.shape[0]
    segment = own_ref.shape[0]
    tail = held.shape[0] - span
    offset = window_ref[0] // LANES
    sub_index = lax.axis_index("sa")

    @pl.when(sub_index == 0)
    def _():
        copy = pltpu.make_async_copy(own_ref.at[pl.ds(offset, span)], held.at[pl.ds(0, span)], sems.at[0])
        copy.start()
        copy.wait()

    @pl.when(sub_index == 1)
    def _():
        first = pltpu.make_async_copy(near_ref, held.at[pl.ds(0, span)], sems.at[0])
        second = pltpu.make_async_copy(own_ref.at[pl.ds(0, tail)], held.at[pl.ds(span, tail)], sems.at[1])
        first.start()
        second.start()
        first.wait()
        second.wait()

    @pl.when(sub_index == 2)
    def _():
        copy = pltpu.make_async_copy(near_ref, held.at[pl.ds(0, span)], sems.at[0])
        copy.start()
        copy.wait()

    @pl.when(sub_index == 3)
    def _():
        first = pltpu.make_async_copy(far_ref, held.at[pl.ds(0, half)], sems.at[0])
        second = pltpu.make_async_copy(near_ref.at[pl.ds(0, tail)], held.at[pl.ds(half, tail)], sems.at[1])
        first.start()
        second.start()
        first.wait()
        second.wait()

    base = jnp.where(sub_index == 1, span - (segment - half) + offset, jnp.where(sub_index == 3, offset, 0))
    rows = held.shape[1]
    tap_blocks = taps_ref.shape[0] // LANES
    even = lax.rem(lax.broadcasted_iota(jnp.int32, (1, 8, LANES), 1), 2) == 0
    group = 8
    for step in range(out_ref.shape[0] // group):
        blocks = [
            held[pl.ds(base + group * step + t, group)].reshape(group * rows, LANES) for t in range(tap_blocks)
        ]
        product = jnp.dot(jnp.concatenate(blocks, axis=1), taps_ref[...], preferred_element_type=F32)
        straight = product[:, :LANES].reshape(-1, 8, LANES)
        crossed = product[:, LANES:].reshape(-1, 8, LANES)
        total = straight + jnp.where(even, pltpu.roll(crossed, 7, 1), -pltpu.roll(crossed, 1, 1))
        out_ref[group * step : group * (step + 1)] = total.astype(BF).reshape(group, rows, LANES)


def azimuth_taps_kernel(rows_ref, out_ref, scratch):
    size = out_ref.shape[0] // 2
    row = jnp.sum(rows_ref[...].astype(F32), axis=0).astype(BF)
    row = jnp.concatenate([row, jnp.zeros((14, row.shape[1]), BF)], axis=0)
    flipped = reversed_lanes(row)
    moved = pltpu.roll(flipped, row.shape[1] - (size - 1), 1)
    parts = []
    for part in range(2):
        spread = jnp.broadcast_to(moved[part : part + 1], (size, row.shape[1]))
        parts.append(pltpu.roll(spread, 0, 1, stride=1, stride_axis=0)[:, :size])
    columns = size // LANES
    for part, pair in enumerate(((parts[0], -parts[1]), (parts[1], parts[0]))):
        for target in range(2):
            for column in range(columns):
                scratch[target * columns + column, pl.ds(part, size, stride=2), :] = pair[target][
                    :, column * LANES : (column + 1) * LANES
                ]
    for column in range(2 * columns):
        out_ref[:, column * LANES : (column + 1) * LANES] = scratch[column].astype(BF)


def azimuth_kernel(lines_ref, taps_ref, out_ref):
    sources, tiles, rows, _ = lines_ref.shape
    pulses = out_ref.shape[2]
    for tile in range(tiles):
        lines = lines_ref[:, tile].reshape(sources * rows, LANES)
        focused = lax.dot_general(
            lines, taps_ref[...], (((0,), (0,)), ((), ())), preferred_element_type=F32
        )
        out_ref[tile * LANES : (tile + 1) * LANES, 0, :] = focused[:, :pulses]
        out_ref[tile * LANES : (tile + 1) * LANES, 1, :] = focused[:, pulses:]


def toeplitz(diagonal_taps, size):
    span_size = 2 * size - 1
    reversed_taps = diagonal_taps[..., ::-1]
    shifted = jnp.concatenate(
        [reversed_taps[..., size - 1 :], reversed_taps[..., : size - 1]], axis=-1
    )
    reps = (1,) * (shifted.ndim - 1) + (size,)
    tiled_flat = jnp.tile(shifted, reps)[..., : size * (span_size - 1)]
    return tiled_flat.reshape(shifted.shape[:-1] + (size, span_size - 1))[..., :size]


def tap_blocks(tap_values, size):
    block_total = tap_values.shape[1] // size + 1
    padded_taps = jnp.pad(tap_values, ((0, 0), (size, 2 * size)))
    matrices = []
    for offset_block in range(block_total):
        first_tap = offset_block * size + 1
        parts = toeplitz(padded_taps[:, first_tap : first_tap + 2 * size - 1], size)
        real_part = parts[0]
        imag_part = parts[1]
        matrices.append(
            jnp.stack([jnp.stack([real_part, -imag_part]), jnp.stack([imag_part, real_part])])
        )
    return jnp.stack(matrices)


def correlate(blocked, matrices, output_count):
    summed = jnp.zeros((blocked.shape[0], 2, output_count, blocked.shape[3]), F32)
    for offset_block in range(matrices.shape[0]):
        piece_rows = blocked[:, :, offset_block : offset_block + output_count, :]
        summed = summed + jnp.einsum(
            "rcib,cdbn->rdin", piece_rows, matrices[offset_block], preferred_element_type=F32
        )
    return summed


def focus_long(range_lines, reference_row):
    block_size = L // 2
    bin_count, _, total_pulses = range_lines.shape
    block_count = total_pulses // block_size
    blocked = range_lines.reshape(bin_count, 2, block_count, block_size)
    blocked = jnp.pad(blocked, ((0, 0), (0, 0), (1, 1), (0, 0)))
    focused = correlate(blocked, tap_blocks(reference_row, block_size), block_count)
    return focused.reshape(1, bin_count, 2, total_pulses)


def call(kernel, outs, specs, flops, moved, scratch=(), vmem=48 * 2**20):
    space = {"s": pltpu.SMEM, "v": pltpu.VMEM, "a": pl.ANY}
    return pl.pallas_call(
        kernel,
        out_shape=outs,
        in_specs=[pl.BlockSpec(memory_space=space[kind]) for kind in specs],
        out_specs=jax.tree.map(lambda _: pl.BlockSpec(memory_space=pltpu.VMEM), outs),
        scratch_shapes=list(scratch),
        compiler_params=pltpu.CompilerParams(vmem_limit_bytes=vmem),
        cost_estimate=pl.CostEstimate(flops=flops, bytes_accessed=moved, transcendentals=0),
    )


def on_device(raw_echo, chirp_replica, azimuth_refs, migration_index, window_start):
    pulses, _, segment = raw_echo.shape
    segment_devices = lax.axis_size("sa")
    pulse_devices = lax.axis_size("pa")
    sub_index = lax.axis_index("sa")
    tap_count = chirp_replica.shape[1]
    kept_width = R // segment_devices
    bin_count = kept_width // pulse_devices
    total_pulses = pulses * pulse_devices
    rows = 2 * pulses
    tiles = segment // LANES
    half = kept_width // LANES
    tap_tiles = tap_count // LANES + 2
    span = half + tap_tiles - 1
    offset = window_start[0] // LANES

    tiled = raw_echo.reshape(pulses, 2, tiles, LANES).transpose(2, 0, 1, 3).reshape(tiles, rows, LANES)
    near_first = jnp.where(sub_index == 0, tiles - span, jnp.where(sub_index == 1, offset, 0))
    near = lax.dynamic_slice_in_dim(tiled, near_first, span, 0)
    far = tiled[tiles - half :]
    near = lax.ppermute(near, "sa", [(0, 1), (1, 2), (2, 3)])
    far = lax.ppermute(far, "sa", [(1, 3)])

    taps, own_rows = call(
        prep_kernel,
        (
            jax.ShapeDtypeStruct((tap_tiles * LANES, 2 * LANES), BF),
            jax.ShapeDtypeStruct((pulse_devices, 2, L), BF),
        ),
        "ssvv",
        10**7,
        10**6,
    )(window_start, migration_index, chirp_replica, azimuth_refs)
    rows_in = lax.all_to_all(own_rows, "pa", split_axis=0, concat_axis=0, tiled=True)

    tail = 16 + tap_tiles - 1
    compressed = call(
        compress_kernel,
        jax.ShapeDtypeStruct((half, rows, LANES), BF),
        "saaav",
        2 * half * rows * tap_tiles * LANES * 2 * LANES,
        4 * 10**6,
        [pltpu.VMEM((span + tail, rows, LANES), BF), pltpu.SemaphoreType.DMA((2,))],
    )(window_start, tiled, near, far, taps)

    if bin_count % LANES or total_pulses != L // 2:
        kept = compressed.reshape(half, pulses, 2, LANES).transpose(0, 3, 2, 1)
        outgoing = kept.reshape(pulse_devices, bin_count, 2, pulses)
        turned = lax.all_to_all(outgoing, "pa", split_axis=0, concat_axis=3, tiled=True)
        reference_row = jnp.sum(rows_in.astype(F32), axis=0).astype(BF)
        return focus_long(turned[0], reference_row)

    azimuth_taps = call(
        azimuth_taps_kernel,
        jax.ShapeDtypeStruct((2 * total_pulses, 2 * total_pulses), BF),
        "v",
        10**6,
        10**6,
        [pltpu.VMEM((2 * total_pulses // LANES, 2 * total_pulses, LANES), F32)],
    )(rows_in)
    outgoing = compressed.reshape(pulse_devices, bin_count // LANES, rows, LANES)
    lines = lax.all_to_all(outgoing, "pa", split_axis=0, concat_axis=0, tiled=True)
    focused = call(
        azimuth_kernel,
        jax.ShapeDtypeStruct((bin_count, 2, total_pulses), F32),
        "vv",
        8 * bin_count * total_pulses * total_pulses,
        2 * 10**6,
    )(lines, azimuth_taps)
    return focused[None]


def solution(mesh):
    placed = (P("pa", None, "sa"), P(), P("pa", None, None), P(), P())
    return jax.shard_map(
        on_device, mesh=mesh, in_specs=placed, out_specs=P("sa", "pa", None, None), check_vma=False
    )
```

time: 104 us -> 46.1 us (0.44)
  the two profiles are of different devices: /device:TPU:2 before, /device:TPU:1 now
where the time goes in v1:
time: 46.1 us; the launch traced here: 45.7 us
  starting transfers between devices  16.9 us (37%)
  waiting for transfers between devices  13.7 us (30%)
  local copies, waits for them, and re-layouts  7.64 us (17%)
  Pallas kernels  6.6 us (14%)
  between operations  0.84 us (2%)
    all_to_all x1, waiting for transfers between devices, on_device(): lax.all_to_all(outgoing, 'pa', split_axis=0, concat_axis=0, tiled=True)  10.9 us
    all_to_all x1, starting transfers between devices, on_device(): lax.all_to_all(outgoing, 'pa', split_axis=0, concat_axis=0, tiled=True)  5.56 us
    all_to_all x1, starting transfers between devices, on_device(): lax.all_to_all(own_rows, 'pa', split_axis=0, concat_axis=0, tiled=True)  5.55 us
    ppermute x1, starting transfers between devices, on_device(): near = lax.ppermute(near, 'sa', [(0, 1), (1, 2), (2, 3)])  4.5 us
    transpose x1, local copies, waits for them, and re-layouts, on_device(): raw_echo.reshape(pulses, 2, tiles, LANES).transpose(2, 0, 1, 3)  3.08 us
    ppermute x1, waiting for transfers between devices, on_device(): far = lax.ppermute(far, 'sa', [(1, 3)])  2.83 us
    pallas_call x1, Pallas kernels, on_device(): call(compress_kernel, jax.ShapeDtypeStruct((half, rows, LANES), BF), 'saa...  2.77 us
    unnamed x14, local copies, waits for them, and re-layouts  2.45 us
  transfers between devices with their start and end apart: 4, of which 2 were waited for; matrix products, arithmetic and copies ran while one was open for 3% of the time, Pallas kernels for 11%

profile of v1, /device:TPU:1, one launch (start us, length us, event | category | flops | bytes accessed | tf_op | source)
XLA Modules:
  0.0 45.7 jit_solution(16506652091961784016)
XLA Ops:
  0.0 0.0 copy-start
  0.7 0.5 %copy-done = bf16[32,2,8192]{2,1,0:T(2,128)(2,1)S(1)} copy-done((bf16[32,2,8192]{2,1,0:T(2,128)(2,1)S(1)}, bf16[32,2,8192]{2,1,0:T(2,128)(2,1)}, u32[]{:S(2)}) %copy-start) | copy-done | bytes 1048600
  1.2 3.1 %fusion = (bf16[64,32,2,128]{3,2,1,0:T(2,128)(2,1)}, bf16[32,2,64,128]{3,1,0,2:T(2,128)(2,1)S(1)}) fusion(bf16[32,2,8192]{2,1,0:T(2,128)(2,1)S(1)} %copy-done), kind=kLoop, calls=%fused_computation.2 | loop fusion | bytes 3145728 | tf_op jit(solution)/shard_map/transpose | solution.py:218
  4.3 0.9 %constant_dynamic-slice_fusion = bf16[41,64,128]{2,1,0:T(8,128)(2,1)} fusion(bf16[64,64,128]{2,1,0:T(8,128)(2,1)S(1)} %bitcast.19, s32[]{:T(128)S(6)} %select_n.19), kind=kLoop, calls=%fused_computation.1 | loop fusion | bytes 1343492 | tf_op jit(solution)/shard_map/dynamic_slice | solution.py:220
  5.2 4.5 %collective-permute-start = (bf16[41,64,128]{2,1,0:T(8,128)(2,1)}, bf16[41,64,128]{2,1,0:T(8,128)(2,1)S(1)}, u32[]{:S(2)}, u32[]{:S(2)}) collective-permute-start(bf16[41,64,128]{2,1,0:T(8,128)(2,1)} %constant_dynamic-slice_fusion), channel_id=1, source_target_pairs={{0,1},{1,2},{2,3},{4,5},{5,6},{6,7},{8,9},{9,10},{10,11},{12,13},{... | collective-permute-start | bytes 2015240 | tf_op jit(solution)/shard_map/ppermute | solution.py:222
  9.7 0.0 copy-done.6
  9.7 0.0 copy-start.1
  9.7 0.0 copy-start.2
  9.7 0.0 copy-start.3
  9.8 1.2 %slice.8 = bf16[32,32,2,128]{3,2,1,0:T(2,128)(2,1)} slice(bf16[64,32,2,128]{3,2,1,0:T(2,128)(2,1)S(1)} %copy-done.6), slice={[32:64], [0:32], [0:2], [0:128]} | slice | bytes 1048576 | tf_op jit(solution)/shard_map/slice | solution.py:221
  11.0 1.3 %collective-permute-start.1 = (bf16[32,64,128]{2,1,0:T(8,128)(2,1)}, bf16[32,64,128]{2,1,0:T(8,128)(2,1)S(1)}, u32[]{:S(2)}, u32[]{:S(2)}) collective-permute-start(bf16[32,64,128]{2,1,0:T(8,128)(2,1)} %bitcast.4), channel_id=1, source_target_pairs={{1,3},{5,7},{9,11},{13,15},{17,19},{21,23},{25,27},{29,31}} | collective-permute-start | bytes 1572872 | tf_op jit(solution)/shard_map/ppermute | solution.py:223
  12.3 0.0 copy-done.1
  12.3 1.8 %shard_map.55 = (bf16[1280,256]{1,0:T(8,128)(2,1)S(1)}, bf16[8,2,512]{2,1,0:T(2,128)(2,1)}) custom-call(s32[1]{0:T(128)} %copy.11.window_ref, s32[4,8]{1,0:T(4,128)S(1)} %copy-done.3, bf16[2,1024]{1,0:T(2,128)(2,1)S(1)} %copy-done.2, bf16[8,2,512]{2,1,0:T(2,128)(2,1)S(1)} %copy-done.1), custom_call_target="tpu_custom_call" | custom-call | flops 10000000 | bytes 1000000 | tf_op jit(solution)/shard_map/pallas_call | solution.py:225
  14.1 0.8 %copy-done.4 = bf16[1280,256]{1,0:T(8,128)(2,1)} copy-done((bf16[1280,256]{1,0:T(8,128)(2,1)}, bf16[1280,256]{1,0:T(8,128)(2,1)S(1)}, u32[]{:S(2)}) %copy-start.4) | copy-done | bytes 655384
  14.9 5.6 %all-to-all-start.1 = ((bf16[8,2,512]{2,1,0:T(2,128)(2,1)}), bf16[8,2,512]{2,1,0:T(2,128)(2,1)S(1)}, u32[]{:S(2)}, u32[]{:S(2)}) async-start(bf16[8,2,512]{2,1,0:T(2,128)(2,1)} %get-tuple-element.8), calls=%async_computation.1 | async-start | bytes 32768 | tf_op jit(solution)/shard_map/all_to_all | solution.py:235
  20.5 2.8 %collective-permute-done.1.far_ref = bf16[32,64,128]{2,1,0:T(8,128)(2,1)S(1)} collective-permute-done((bf16[32,64,128]{2,1,0:T(8,128)(2,1)}, bf16[32,64,128]{2,1,0:T(8,128)(2,1)S(1)}, u32[]{:S(2)}, u32[]{:S(2)}) %collective-permute-start.1) | collective-permute-done | bytes 524320 | tf_op jit(solution)/shard_map/ppermute | solution.py:223
  23.3 0.0 collective-permute-done.near_ref
  23.3 1.1 %copy-done.5 = bf16[1280,256]{1,0:T(8,128)(2,1)S(1)} copy-done((bf16[1280,256]{1,0:T(8,128)(2,1)S(1)}, bf16[1280,256]{1,0:T(8,128)(2,1)}, u32[]{:S(2)}) %copy-start.5) | copy-done | bytes 655384
  24.4 2.8 %shard_map.56 = bf16[32,64,128]{2,1,0:T(8,128)(2,1)} custom-call(s32[1]{0:T(128)} %copy.11.window_ref, bf16[64,64,128]{2,1,0:T(8,128)(2,1)S(1)} %bitcast.20, bf16[41,64,128]{2,1,0:T(8,128)(2,1)S(1)} %collective-permute-done.near_ref, bf16[32,64,128]{2,1,0:T(8,128)(2,1)S(1)} %collective-permute-done.1.far_ref, bf16[1280,256]{1,0:T(8,128)(2,1)S(1)} %copy-done.5), custom_call_target="tpu_custom_call" | custom-call | flops 1342177280 | bytes 4000000 | tf_op jit(solution)/shard_map/pallas_call | solution.py:238
  27.2 0.0 all-to-all-done.1.rows_ref
  27.2 5.6 %all-to-all-start = ((bf16[8,4,64,128]{3,2,1,0:T(8,128)(2,1)}), bf16[8,4,64,128]{3,2,1,0:T(8,128)(2,1)S(1)}, u32[]{:S(2)}, u32[]{:S(2)}) async-start(bf16[8,4,64,128]{3,2,1,0:T(8,128)(2,1)} %bitcast.5), calls=%async_computation | async-start | bytes 1048576 | tf_op jit(solution)/shard_map/all_to_all | solution.py:263
  32.8 0.5 %shard_map.57.taps_ref = bf16[512,512]{1,0:T(8,128)(2,1)S(1)} custom-call(bf16[8,2,512]{2,1,0:T(2,128)(2,1)S(1)} %all-to-all-done.1.rows_ref), custom_call_target="tpu_custom_call" | custom-call | flops 1000000 | bytes 1000000 | tf_op jit(solution)/shard_map/pallas_call | solution.py:254
  33.3 10.9 %all-to-all-done.lines_ref = bf16[8,4,64,128]{3,2,1,0:T(8,128)(2,1)S(1)} async-done(((bf16[8,4,64,128]{3,2,1,0:T(8,128)(2,1)}), bf16[8,4,64,128]{3,2,1,0:T(8,128)(2,1)S(1)}, u32[]{:S(2)}, u32[]{:S(2)}) %all-to-all-start) | async-done | bytes 524320 | tf_op jit(solution)/shard_map/all_to_all | solution.py:263
  44.2 1.6 %shard_map.58 = f32[512,2,256]{2,1,0:T(2,128)} custom-call(bf16[8,4,64,128]{3,2,1,0:T(8,128)(2,1)S(1)} %all-to-all-done.lines_ref, bf16[512,512]{1,0:T(8,128)(2,1)S(1)} %shard_map.57.taps_ref), custom_call_target="tpu_custom_call" | custom-call | flops 268435456 | bytes 2000000 | tf_op jit(solution)/shard_map/pallas_call | solution.py:264
  (5 shorter events, 0.0 us)
Async XLA Ops:
  0.0 1.2 %copy-start = (bf16[32,2,8192]{2,1,0:T(2,128)(2,1)S(1)}, bf16[32,2,8192]{2,1,0:T(2,128)(2,1)}, u32[]{:S(2)}) copy-start(bf16[32,2,8192]{2,1,0:T(2,128)(2,1)} %param.5) | copy-start | bytes 3145732
  4.3 5.4 %copy-start.6 = (bf16[64,32,2,128]{3,2,1,0:T(2,128)(2,1)S(1)}, bf16[64,32,2,128]{3,2,1,0:T(2,128)(2,1)}, u32[]{:S(2)}) copy-start(bf16[64,32,2,128]{3,2,1,0:T(2,128)(2,1)} %get-tuple-element.9) | copy-start | bytes 3145732
  5.2 18.1 %collective-permute-start = (bf16[41,64,128]{2,1,0:T(8,128)(2,1)}, bf16[41,64,128]{2,1,0:T(8,128)(2,1)S(1)}, u32[]{:S(2)}, u32[]{:S(2)}) collective-permute-start(bf16[41,64,128]{2,1,0:T(8,128)(2,1)} %constant_dynamic-slice_fusion), channel_id=1, source_target_pairs={{0,1},{1,2},{2,3},{4,5},{5,6},{6,7},{8,9},{9,10},{10,11},{12,13},{... | collective-permute-start | bytes 2015240 | tf_op jit(solution)/shard_map/ppermute | solution.py:222
  9.7 2.6 %copy-start.1 = (bf16[8,2,512]{2,1,0:T(2,128)(2,1)S(1)}, bf16[8,2,512]{2,1,0:T(2,128)(2,1)}, u32[]{:S(2)}) copy-start(bf16[8,2,512]{2,1,0:T(2,128)(2,1)} %refs_ref.1) | copy-start | bytes 49156
  9.7 2.6 %copy-start.2 = (bf16[2,1024]{1,0:T(2,128)(2,1)S(1)}, bf16[2,1024]{1,0:T(2,128)(2,1)}, u32[]{:S(2)}) copy-start(bf16[2,1024]{1,0:T(2,128)(2,1)} %chirp_ref.1) | copy-start | bytes 12292
  9.7 2.6 %copy-start.3 = (s32[4,8]{1,0:T(4,128)S(1)}, s32[4,8]{1,0:T(4,128)}, u32[]{:S(2)}) copy-start(s32[4,8]{1,0:T(4,128)} %index_ref.1) | copy-start | bytes 388
  11.0 12.3 %collective-permute-start.1 = (bf16[32,64,128]{2,1,0:T(8,128)(2,1)}, bf16[32,64,128]{2,1,0:T(8,128)(2,1)S(1)}, u32[]{:S(2)}, u32[]{:S(2)}) collective-permute-start(bf16[32,64,128]{2,1,0:T(8,128)(2,1)} %bitcast.4), channel_id=1, source_target_pairs={{1,3},{5,7},{9,11},{13,15},{17,19},{21,23},{25,27},{29,31}} | collective-permute-start | bytes 1572872 | tf_op jit(solution)/shard_map/ppermute | solution.py:223
  14.1 0.8 %copy-start.4 = (bf16[1280,256]{1,0:T(8,128)(2,1)}, bf16[1280,256]{1,0:T(8,128)(2,1)S(1)}, u32[]{:S(2)}) copy-start(bf16[1280,256]{1,0:T(8,128)(2,1)S(1)} %get-tuple-element.7.taps_ref) | copy-start | bytes 1966084
  14.9 12.3 %all-to-all-start.1 = ((bf16[8,2,512]{2,1,0:T(2,128)(2,1)}), bf16[8,2,512]{2,1,0:T(2,128)(2,1)S(1)}, u32[]{:S(2)}, u32[]{:S(2)}) async-start(bf16[8,2,512]{2,1,0:T(2,128)(2,1)} %get-tuple-element.8), calls=%async_computation.1 | async-start | bytes 32768 | tf_op jit(solution)/shard_map/all_to_all | solution.py:235
  23.3 1.1 %copy-start.5 = (bf16[1280,256]{1,0:T(8,128)(2,1)S(1)}, bf16[1280,256]{1,0:T(8,128)(2,1)}, u32[]{:S(2)}) copy-start(bf16[1280,256]{1,0:T(8,128)(2,1)} %copy-done.4) | copy-start | bytes 1966084
  27.2 17.0 %all-to-all-start = ((bf16[8,4,64,128]{3,2,1,0:T(8,128)(2,1)}), bf16[8,4,64,128]{3,2,1,0:T(8,128)(2,1)S(1)}, u32[]{:S(2)}, u32[]{:S(2)}) async-start(bf16[8,4,64,128]{3,2,1,0:T(8,128)(2,1)} %bitcast.5), calls=%async_computation | async-start | bytes 1048576 | tf_op jit(solution)/shard_map/all_to_all | solution.py:263

commit v2 on v1

v2 whole, which is shorter than its diff:
```python
import functools

import jax
import jax.numpy as jnp
from jax import lax
from jax.experimental import pallas as pl
from jax.experimental.pallas import tpu as pltpu
from jax.sharding import PartitionSpec as P

R = 16384
L = 512
LANES = 128
BF = jnp.bfloat16
F32 = jnp.float32


def reversed_lanes(row):
    row_id = lax.broadcasted_iota(jnp.int32, (LANES, LANES), 0)
    col_id = lax.broadcasted_iota(jnp.int32, (LANES, LANES), 1)
    flip = (row_id + col_id == LANES - 1).astype(BF)
    tiles = row.shape[1] // LANES
    pieces = [row[:, t * LANES : (t + 1) * LANES] for t in reversed(range(tiles))]
    return jnp.concatenate([jnp.dot(piece, flip, preferred_element_type=F32) for piece in pieces], axis=1)


def retile(source, target, tiles):
    for t in range(tiles):
        target[t] = source[:, :, t * LANES : (t + 1) * LANES]


def send_kernel(part, window_ref, raw_ref, near_ref, far_ref, near_raw, far_raw, sems):
    span, pulses = near_ref.shape[:2]
    half = far_ref.shape[0]
    tiles = raw_ref.shape[2] // LANES
    sub_index = lax.axis_index("sa")
    offset = window_ref[0] // LANES
    first = jnp.where(sub_index == 0, tiles - span, jnp.where(sub_index == 1, offset, 0))
    own = pl.ds(part * pulses, pulses)
    near_from = raw_ref.at[own, :, pl.ds(pl.multiple_of(first * LANES, LANES), span * LANES)]
    far_from = raw_ref.at[own, :, pl.ds((tiles - half) * LANES, half * LANES)]
    near_copy = pltpu.make_async_copy(near_from, near_raw, sems.at[0])
    far_copy = pltpu.make_async_copy(far_from, far_raw, sems.at[1])

    @pl.when(sub_index < 3)
    def _():
        near_copy.start()

    @pl.when(sub_index == 1)
    def _():
        far_copy.start()

    @pl.when(sub_index < 3)
    def _():
        near_copy.wait()
        retile(near_raw, near_ref, span)

    @pl.when(sub_index == 1)
    def _():
        far_copy.wait()
        retile(far_raw, far_ref, half)


def prep_kernel(window_ref, index_ref, chirp_ref, refs_ref, raw_ref, taps_ref, rows_ref, own_ref, own_raw, sem):
    sub_index = lax.axis_index("sa")
    halves, span, pulses = own_ref.shape[:3]
    first_tile = jnp.where(sub_index == 0, window_ref[0] // LANES, 0)
    own_copy = pltpu.make_async_copy(
        raw_ref.at[:, :, pl.ds(pl.multiple_of(first_tile * LANES, LANES), span * LANES)], own_raw, sem
    )

    @pl.when(sub_index < 2)
    def _():
        own_copy.start()

    taps = chirp_ref.shape[1]
    blocks = taps_ref.shape[0] // LANES
    width = blocks * LANES
    shift = lax.rem(window_ref[0], LANES)
    chirp = jnp.concatenate([chirp_ref[...], jnp.zeros((14, taps), BF)], axis=0)
    flipped = reversed_lanes(chirp)
    padded = jnp.concatenate([jnp.zeros((16, 2 * LANES), F32), flipped], axis=1)
    padded = jnp.concatenate([padded, jnp.zeros((16, width + LANES - padded.shape[1]), F32)], axis=1)
    moved = pltpu.roll(padded, width + LANES - 127 - shift, 1)[:, :width]
    for part in range(2):
        spread = jnp.broadcast_to(moved[part : part + 1], (LANES, width))
        skewed = pltpu.roll(spread, 0, 1, stride=1, stride_axis=0)
        for t in range(blocks):
            first = LANES * (blocks - 1 - t)
            taps_ref[t * LANES : (t + 1) * LANES, part * LANES : (part + 1) * LANES] = skewed[
                :, first : first + LANES
            ].astype(BF)
    own = refs_ref.shape[0]
    first_row = lax.axis_index("pa") * own

    def fill(target, carry):
        local = index_ref[sub_index, target] - first_row
        held = jnp.logical_and(local >= 0, local < own)
        row = refs_ref[jnp.clip(local, 0, own - 1)].astype(F32)
        row = jnp.where(held, row, jnp.zeros_like(row))
        pieces = [row[part : part + 1, t * LANES : (t + 1) * LANES] for part in range(2) for t in range(L // LANES)]
        rows_ref[target] = jnp.concatenate(pieces + [jnp.zeros((8, LANES), F32)], axis=0).astype(BF)
        return carry

    lax.fori_loop(0, rows_ref.shape[0], fill, 0)

    @pl.when(sub_index < 2)
    def _():
        own_copy.wait()
        for part in range(halves):
            retile(own_raw.at[pl.ds(part * pulses, pulses)], own_ref.at[part], span)


def compress_kernel(part, window_ref, own_ref, near_ref, far_ref, taps_ref, rows_ref, out_ref, held, taps, sems):
    half = far_ref.shape[0]
    span = near_ref.shape[0]
    tail = held.shape[0] - span
    offset = window_ref[0] // LANES
    sub_index = lax.axis_index("sa")
    taps_copy = pltpu.make_async_copy(taps_ref, taps, sems.at[2])
    taps_copy.start()

    def fetch(*pairs):
        copies = [pltpu.make_async_copy(*pair, sems.at[at]) for at, pair in enumerate(pairs)]
        for copy in copies:
            copy.start()
        for copy in copies:
            copy.wait()

    @pl.when(sub_index == 0)
    def _():
        fetch((own_ref.at[part], held.at[pl.ds(0, span)]))

    @pl.when(sub_index == 1)
    def _():
        fetch((near_ref, held.at[pl.ds(0, span)]), (own_ref.at[part, pl.ds(0, tail)], held.at[pl.ds(span, tail)]))

    @pl.when(sub_index == 2)
    def _():
        fetch((near_ref, held.at[pl.ds(0, span)]))

    @pl.when(sub_index == 3)
    def _():
        fetch((far_ref, held.at[pl.ds(0, half)]), (near_ref.at[pl.ds(0, tail)], held.at[pl.ds(half, tail)]))

    taps_copy.wait()
    base = jnp.where(sub_index == 1, span - half + offset, jnp.where(sub_index == 3, offset, 0))
    rows = held.shape[1]
    tap_tiles = taps.shape[0] // LANES
    even = lax.rem(lax.broadcasted_iota(jnp.int32, (1, 8, LANES), 1), 2) == 0
    targets = out_ref.shape[0]
    per_target = half // targets
    group = 16
    for step in range(half // group):
        blocks = [
            held[pl.ds(base + group * step + t, group)].reshape(group * rows, LANES) for t in range(tap_tiles)
        ]
        product = jnp.dot(jnp.concatenate(blocks, axis=1), taps[...], preferred_element_type=F32)
        straight = product[:, :LANES].reshape(-1, 8, LANES)
        crossed = product[:, LANES:].reshape(-1, 8, LANES)
        total = straight + jnp.where(even, pltpu.roll(crossed, 7, 1), -pltpu.roll(crossed, 1, 1))
        total = total.astype(BF).reshape(group // per_target, per_target * rows, LANES)
        for at in range(group // per_target):
            out_ref[step * (group // per_target) + at, : per_target * rows] = total[at]
    if out_ref.shape[1] > per_target * rows:
        out_ref[:, per_target * rows :] = rows_ref[...]


def azimuth_taps(row, scratch, size):
    row = jnp.concatenate([row, jnp.zeros((14, row.shape[1]), BF)], axis=0)
    flipped = reversed_lanes(row)
    moved = pltpu.roll(flipped, row.shape[1] - (size - 1), 1)
    parts = []
    for part in range(2):
        spread = jnp.broadcast_to(moved[part : part + 1], (size, row.shape[1]))
        parts.append(pltpu.roll(spread, 0, 1, stride=1, stride_axis=0)[:, :size])
    columns = size // LANES
    for part, pair in enumerate(((parts[0], -parts[1]), (parts[1], parts[0]))):
        for target in range(2):
            for column in range(columns):
                scratch[target * columns + column, pl.ds(part, size, stride=2), :] = pair[target][
                    :, column * LANES : (column + 1) * LANES
                ]


def azimuth_product(lines_ref, tile, rows, taps):
    sources = lines_ref.shape[0]
    lines = lines_ref[:, tile * rows : (tile + 1) * rows].reshape(sources * rows, LANES)
    return lax.dot_general(lines, taps, (((0,), (0,)), ((), ())), preferred_element_type=F32)


def azimuth_first_kernel(lines_ref, later_ref, sum_ref, scratch, taps):
    size = scratch.shape[1] // 2
    sources = lines_ref.shape[0]
    tiles = sum_ref.shape[0] // LANES
    rows = (lines_ref.shape[1] - 16) // tiles
    picked = jnp.sum(lines_ref[:, tiles * rows :].astype(F32), axis=0)
    columns = L // LANES
    row = jnp.concatenate(
        [
            jnp.concatenate([picked[part * columns + t : part * columns + t + 1] for t in range(columns)], axis=1)
            for part in range(2)
        ],
        axis=0,
    ).astype(BF)
    azimuth_taps(row, scratch, size)
    for column in range(scratch.shape[0]):
        lanes = slice(column * LANES, (column + 1) * LANES)
        for source in range(sources):
            into = slice(source * rows, (source + 1) * rows)
            start = source * 2 * rows
            taps[into, lanes] = scratch[column, start : start + rows].astype(BF)
            later_ref[into, lanes] = scratch[column, start + rows : start + 2 * rows].astype(BF)
    for tile in range(tiles):
        sum_ref[tile * LANES : (tile + 1) * LANES] = azimuth_product(lines_ref, tile, rows, taps[...])


def azimuth_last_kernel(lines_ref, taps_ref, sum_ref, out_ref):
    pulses = out_ref.shape[2]
    tiles = out_ref.shape[0] // LANES
    rows = lines_ref.shape[1] // tiles
    for tile in range(tiles):
        bins = slice(tile * LANES, (tile + 1) * LANES)
        focused = sum_ref[bins] + azimuth_product(lines_ref, tile, rows, taps_ref[...])
        out_ref[bins, 0, :] = focused[:, :pulses]
        out_ref[bins, 1, :] = focused[:, pulses:]


def toeplitz(diagonal_taps, size):
    span_size = 2 * size - 1
    reversed_taps = diagonal_taps[..., ::-1]
    shifted = jnp.concatenate(
        [reversed_taps[..., size - 1 :], reversed_taps[..., : size - 1]], axis=-1
    )
    reps = (1,) * (shifted.ndim - 1) + (size,)
    tiled_flat = jnp.tile(shifted, reps)[..., : size * (span_size - 1)]
    return tiled_flat.reshape(shifted.shape[:-1] + (size, span_size - 1))[..., :size]


def tap_blocks(tap_values, size):
    block_total = tap_values.shape[1] // size + 1
    padded_taps = jnp.pad(tap_values, ((0, 0), (size, 2 * size)))
    matrices = []
    for offset_block in range(block_total):
        first_tap = offset_block * size + 1
        parts = toeplitz(padded_taps[:, first_tap : first_tap + 2 * size - 1], size)
        real_part = parts[0]
        imag_part = parts[1]
        matrices.append(
            jnp.stack([jnp.stack([real_part, -imag_part]), jnp.stack([imag_part, real_part])])
        )
    return jnp.stack(matrices)


def correlate(blocked, matrices, output_count):
    summed = jnp.zeros((blocked.shape[0], 2, output_count, blocked.shape[3]), F32)
    for offset_block in range(matrices.shape[0]):
        piece_rows = blocked[:, :, offset_block : offset_block + output_count, :]
        summed = summed + jnp.einsum(
            "rcib,cdbn->rdin", piece_rows, matrices[offset_block], preferred_element_type=F32
        )
    return summed


def focus_long(range_lines, reference_row):
    block_size = L // 2
    bin_count, _, total_pulses = range_lines.shape
    block_count = total_pulses // block_size
    blocked = range_lines.reshape(bin_count, 2, block_count, block_size)
    blocked = jnp.pad(blocked, ((0, 0), (0, 0), (1, 1), (0, 0)))
    focused = correlate(blocked, tap_blocks(reference_row, block_size), block_count)
    return focused.reshape(1, bin_count, 2, total_pulses)


def call(kernel, outs, specs, flops, moved, scratch=(), vmem=40 * 2**20):
    space = {"s": pltpu.SMEM, "v": pltpu.VMEM, "a": pl.ANY}
    return pl.pallas_call(
        kernel,
        out_shape=outs,
        in_specs=[pl.BlockSpec(memory_space=space[kind]) for kind in specs],
        out_specs=jax.tree.map(lambda _: pl.BlockSpec(memory_space=pltpu.VMEM), outs),
        scratch_shapes=list(scratch),
        compiler_params=pltpu.CompilerParams(vmem_limit_bytes=vmem),
        cost_estimate=pl.CostEstimate(flops=flops, bytes_accessed=moved, transcendentals=0),
    )


def on_device(raw_echo, chirp_replica, azimuth_refs, migration_index, window_start):
    pulses = raw_echo.shape[0]
    segment_devices = lax.axis_size("sa")
    pulse_devices = lax.axis_size("pa")
    tap_count = chirp_replica.shape[1]
    kept_width = R // segment_devices
    bin_count = kept_width // pulse_devices
    total_pulses = pulses * pulse_devices
    half = kept_width // LANES
    tap_tiles = tap_count // LANES + 2
    span = half + tap_tiles - 1

    parts = 2
    pulses_each = pulses // parts
    rows_each = 2 * pulses_each
    short = bin_count % LANES == 0 and total_pulses == L // 2

    nears, fars = [], []
    turn = window_start
    for part in range(parts):
        near, far = call(
            functools.partial(send_kernel, part),
            (
                jax.ShapeDtypeStruct((span, pulses_each, 2, LANES), BF),
                jax.ShapeDtypeStruct((half, pulses_each, 2, LANES), BF),
            ),
            "sa",
            10**5,
            2 * 10**6,
            [
                pltpu.VMEM((pulses_each, 2, span * LANES), BF),
                pltpu.VMEM((pulses_each, 2, half * LANES), BF),
                pltpu.SemaphoreType.DMA((2,)),
            ],
            60 * 2**20,
        )(turn, raw_echo)
        turn = lax.optimization_barrier((window_start, near))[0]
        near = near.reshape(span, rows_each, LANES)
        far = far.reshape(half, rows_each, LANES)
        nears.append(lax.ppermute(near, "sa", [(0, 1), (1, 2), (2, 3)]))
        fars.append(lax.ppermute(far, "sa", [(1, 3)]))

    taps, own_rows, own = call(
        prep_kernel,
        (
            jax.ShapeDtypeStruct((tap_tiles * LANES, 2 * LANES), BF),
            jax.ShapeDtypeStruct((pulse_devices, 16, LANES), BF),
            jax.ShapeDtypeStruct((parts, span, pulses_each, 2, LANES), BF),
        ),
        "ssvva",
        10**7,
        10**6,
        [pltpu.VMEM((pulses, 2, span * LANES), BF), pltpu.SemaphoreType.DMA],
    )(turn, migration_index, chirp_replica, azimuth_refs, raw_echo)
    own = own.reshape(parts, span, rows_each, LANES)

    tail = 16 + tap_tiles - 1
    targets = pulse_devices if short else 2
    squeezed = []
    turn = window_start
    for part in range(parts):
        extra = 16 if short and part == 0 else 0
        squeezed.append(
            call(
                functools.partial(compress_kernel, part),
                jax.ShapeDtypeStruct((targets, half // targets * rows_each + extra, LANES), BF),
                "saaaav" if extra else "saaaaa",
                2 * half * rows_each * tap_tiles * LANES * 2 * LANES,
                4 * 10**6,
                [
                    pltpu.VMEM((span + tail, rows_each, LANES), BF),
                    pltpu.VMEM((tap_tiles * LANES, 2 * LANES), BF),
                    pltpu.SemaphoreType.DMA((3,)),
                ],
            )(turn, own, nears[part], fars[part], taps, own_rows)
        )
        turn = lax.optimization_barrier((window_start, squeezed[-1]))[0]

    if not short:
        kept = jnp.stack(squeezed).reshape(parts, half, pulses_each, 2, LANES).transpose(1, 4, 3, 0, 2)
        outgoing = kept.reshape(pulse_devices, bin_count, 2, pulses)
        turned = lax.all_to_all(outgoing, "pa", split_axis=0, concat_axis=3, tiled=True)
        rows_in = lax.all_to_all(own_rows, "pa", split_axis=0, concat_axis=0, tiled=True)
        reference_row = jnp.sum(rows_in[:, :8].astype(F32), axis=0).astype(BF).reshape(2, L)
        return focus_long(turned[0], reference_row)

    lines = [lax.all_to_all(part, "pa", split_axis=0, concat_axis=0, tiled=True) for part in squeezed]
    width = 2 * total_pulses
    later_taps, first_sum = call(
        azimuth_first_kernel,
        (jax.ShapeDtypeStruct((width // 2, width), BF), jax.ShapeDtypeStruct((bin_count, width), F32)),
        "v",
        4 * bin_count * total_pulses * total_pulses,
        2 * 10**6,
        [pltpu.VMEM((width // LANES, width, LANES), F32), pltpu.VMEM((width // 2, width), BF)],
    )(lines[0])
    focused = call(
        azimuth_last_kernel,
        jax.ShapeDtypeStruct((bin_count, 2, total_pulses), F32),
        "vvv",
        4 * bin_count * total_pulses * total_pulses,
        2 * 10**6,
    )(lines[1], later_taps, first_sum)
    return focused[None]


def solution(mesh):
    placed = (P("pa", None, "sa"), P(), P("pa", None, None), P(), P())
    return jax.shard_map(
        on_device, mesh=mesh, in_specs=placed, out_specs=P("sa", "pa", None, None), check_vma=False
    )
```

time: 46.1 us -> 50.6 us (1.098)
  the two profiles are of different devices: /device:TPU:1 before, /device:TPU:3 now
where the time goes in v2:
time: 50.6 us; the launch traced here: 50.1 us
  waiting for transfers between devices  23 us (45%)
  starting transfers between devices  16.2 us (32%)
  Pallas kernels  9.32 us (18%)
  between operations  0.88 us (2%)
  local copies, waits for them, and re-layouts  0.73 us (1%)
    ppermute x2, waiting for transfers between devices, on_device(): fars.append(lax.ppermute(far, 'sa', [(1, 3)]))  16.1 us
    all_to_all x2, starting transfers between devices, on_device(): lax.all_to_all(part, 'pa', split_axis=0, concat_axis=0, tiled=True)  11 us
    all_to_all x2, waiting for transfers between devices, on_device(): lax.all_to_all(part, 'pa', split_axis=0, concat_axis=0, tiled=True)  6.93 us
    pallas_call x2, Pallas kernels, on_device(): call(functools.partial(compress_kernel, part), jax.ShapeDtypeStruct((targ...  4.17 us
    ppermute x2, starting transfers between devices, on_device(): nears.append(lax.ppermute(near, 'sa', [(0, 1), (1, 2), (2, 3)]))  2.58 us
    ppermute x2, starting transfers between devices, on_device(): fars.append(lax.ppermute(far, 'sa', [(1, 3)]))  2.58 us
    pallas_call x2, Pallas kernels, on_device(): call(functools.partial(send_kernel, part), (jax.ShapeDtypeStruct((span, p...  1.68 us
    pallas_call x1, Pallas kernels, on_device(): call(azimuth_last_kernel, jax.ShapeDtypeStruct((bin_count, 2, total_pulse...  1.54 us
  transfers between devices with their start and end apart: 6, of which 3 were waited for; matrix products, arithmetic and copies ran while one was open for 0% of the time, Pallas kernels for 10%

profile of v2, /device:TPU:3, one launch (start us, length us, event | category | flops | bytes accessed | tf_op | source)
XLA Modules:
  0.0 50.1 jit_solution(12499629607454511731)
XLA Ops:
  0.7 0.8 %shard_map.55 = (bf16[41,16,2,128]{3,2,1,0:T(2,128)(2,1)}, bf16[32,16,2,128]{3,2,1,0:T(2,128)(2,1)}) custom-call(s32[1]{0:T(128)S(6)} %copy.6.window_ref, bf16[32,2,8192]{2,1,0:T(2,128)(2,1)} %raw_ref.5), custom_call_target="tpu_custom_call" | custom-call | flops 100000 | bytes 2000000 | tf_op jit(solution)/shard_map/pallas_call | solution.py:307
  1.6 0.0 copy-start.2
  1.6 0.0 copy-start.3
  1.6 1.3 %collective-permute-start = (bf16[41,32,128]{2,1,0:T(8,128)(2,1)}, bf16[41,32,128]{2,1,0:T(8,128)(2,1)S(1)}, u32[]{:S(2)}, u32[]{:S(2)}) collective-permute-start(bf16[41,32,128]{2,1,0:T(8,128)(2,1)} %bitcast.8), channel_id=1, source_target_pairs={{0,1},{1,2},{2,3},{4,5},{5,6},{6,7},{8,9},{9,10},{10,11},{12,13},{... | collective-permute-start | bytes 1007624 | tf_op jit(solution)/shard_map/ppermute | solution.py:326
  2.9 1.3 %collective-permute-start.1 = (bf16[32,32,128]{2,1,0:T(8,128)(2,1)}, bf16[32,32,128]{2,1,0:T(8,128)(2,1)S(1)}, u32[]{:S(2)}, u32[]{:S(2)}) collective-permute-start(bf16[32,32,128]{2,1,0:T(8,128)(2,1)} %bitcast.10), channel_id=1, source_target_pairs={{1,3},{5,7},{9,11},{13,15},{17,19},{21,23},{25,27},{29,31}} | collective-permute-start | bytes 786440 | tf_op jit(solution)/shard_map/ppermute | solution.py:327
  4.2 0.0 copy-done
  4.3 0.0 copy-start.1
  4.3 0.7 %copy-done.1 = bf16[8,2,512]{2,1,0:T(2,128)(2,1)S(1)} copy-done((bf16[8,2,512]{2,1,0:T(2,128)(2,1)S(1)}, bf16[8,2,512]{2,1,0:T(2,128)(2,1)}, u32[]{:S(2)}) %copy-start.1) | copy-done | bytes 16408
  5.0 1.2 %shard_map.57 = (bf16[1280,256]{1,0:T(8,128)(2,1)S(1)}, bf16[8,16,128]{2,1,0:T(8,128)(2,1)S(1)}, bf16[2,41,16,2,128]{4,3,2,1,0:T(2,128)(2,1)S(1)}) custom-call(s32[1]{0:T(128)S(6)} %copy.6.window_ref, s32[4,8]{1,0:T(4,128)S(1)} %copy-done.3, bf16[2,1024]{1,0:T(2,128)(2,1)S(1)} %copy-done.2, bf16[8,2,512]{2,1,0:T(2,128)(2,1)S(1)} %copy-done.1, ...), custom_call_target="tpu_custom_call" | custom-call | flops 10000000 | bytes 1000000 | tf_op jit(solution)/shard_map/pallas_call | solution.py:329
  6.2 8.1 %collective-permute-done.1.far_ref = bf16[32,32,128]{2,1,0:T(8,128)(2,1)S(1)} collective-permute-done((bf16[32,32,128]{2,1,0:T(8,128)(2,1)}, bf16[32,32,128]{2,1,0:T(8,128)(2,1)S(1)}, u32[]{:S(2)}, u32[]{:S(2)}) %collective-permute-start.1) | collective-permute-done | bytes 262176 | tf_op jit(solution)/shard_map/ppermute | solution.py:327
  14.3 0.0 collective-permute-done.near_ref
  14.3 2.1 %shard_map.58 = bf16[8,144,128]{2,1,0:T(8,128)(2,1)} custom-call(s32[1]{0:T(128)S(6)} %copy.6.window_ref, bf16[2,41,32,128]{3,2,1,0:T(8,128)(2,1)S(1)} %bitcast.6, bf16[41,32,128]{2,1,0:T(8,128)(2,1)S(1)} %collective-permute-done.near_ref, bf16[32,32,128]{2,1,0:T(8,128)(2,1)S(1)} %collective-permute-done.1.far_ref, ...), custom_call_target="tpu_custom_call" | custom-call | flops 671088640 | bytes 4000000 | tf_op jit(solution)/shard_map/pallas_call | solution.py:350
  16.4 5.6 %all-to-all-start.1 = ((bf16[8,144,128]{2,1,0:T(8,128)(2,1)}), bf16[8,144,128]{2,1,0:T(8,128)(2,1)S(1)}, u32[]{:S(2)}, u32[]{:S(2)}) async-start(bf16[8,144,128]{2,1,0:T(8,128)(2,1)} %shard_map.58), calls=%async_computation.1 | async-start | bytes 589824 | tf_op jit(solution)/shard_map/all_to_all | solution.py:373
  22.0 0.8 %shard_map.56 = (bf16[41,16,2,128]{3,2,1,0:T(2,128)(2,1)}, bf16[32,16,2,128]{3,2,1,0:T(2,128)(2,1)}) custom-call(s32[1]{0:T(128)S(6)} %copy.6.window_ref, bf16[32,2,8192]{2,1,0:T(2,128)(2,1)} %raw_ref.5), custom_call_target="tpu_custom_call" | custom-call | flops 100000 | bytes 2000000 | tf_op jit(solution)/shard_map/pallas_call | solution.py:307
  22.8 1.3 %collective-permute-start.2 = (bf16[41,32,128]{2,1,0:T(8,128)(2,1)}, bf16[41,32,128]{2,1,0:T(8,128)(2,1)S(1)}, u32[]{:S(2)}, u32[]{:S(2)}) collective-permute-start(bf16[41,32,128]{2,1,0:T(8,128)(2,1)} %bitcast.9), channel_id=1, source_target_pairs={{0,1},{1,2},{2,3},{4,5},{5,6},{6,7},{8,9},{9,10},{10,11},{12,13},{... | collective-permute-start | bytes 1007624 | tf_op jit(solution)/shard_map/ppermute | solution.py:326
  24.1 1.3 %collective-permute-start.3 = (bf16[32,32,128]{2,1,0:T(8,128)(2,1)}, bf16[32,32,128]{2,1,0:T(8,128)(2,1)S(1)}, u32[]{:S(2)}, u32[]{:S(2)}) collective-permute-start(bf16[32,32,128]{2,1,0:T(8,128)(2,1)} %bitcast.11), channel_id=1, source_target_pairs={{1,3},{5,7},{9,11},{13,15},{17,19},{21,23},{25,27},{29,31}} | collective-permute-start | bytes 786440 | tf_op jit(solution)/shard_map/ppermute | solution.py:327
  25.4 8.0 %collective-permute-done.3.far_ref = bf16[32,32,128]{2,1,0:T(8,128)(2,1)S(1)} collective-permute-done((bf16[32,32,128]{2,1,0:T(8,128)(2,1)}, bf16[32,32,128]{2,1,0:T(8,128)(2,1)S(1)}, u32[]{:S(2)}, u32[]{:S(2)}) %collective-permute-start.3) | collective-permute-done | bytes 262176 | tf_op jit(solution)/shard_map/ppermute | solution.py:327
  33.4 0.0 collective-permute-done.2.near_ref
  33.4 2.1 %shard_map.59 = bf16[8,128,128]{2,1,0:T(8,128)(2,1)} custom-call(s32[1]{0:T(128)S(6)} %copy.6.window_ref, bf16[2,41,32,128]{3,2,1,0:T(8,128)(2,1)S(1)} %bitcast.7, bf16[41,32,128]{2,1,0:T(8,128)(2,1)S(1)} %collective-permute-done.2.near_ref, bf16[32,32,128]{2,1,0:T(8,128)(2,1)S(1)} %collective-permute-done.3.far_ref, ...), custom_call_target="tpu_custom_call" | custom-call | flops 671088640 | bytes 4000000 | tf_op jit(solution)/shard_map/pallas_call | solution.py:350
  35.5 0.0 all-to-all-done.1.lines_ref
  35.5 5.4 %all-to-all-start = ((bf16[8,128,128]{2,1,0:T(8,128)(2,1)}), bf16[8,128,128]{2,1,0:T(8,128)(2,1)S(1)}, u32[]{:S(2)}, u32[]{:S(2)}) async-start(bf16[8,128,128]{2,1,0:T(8,128)(2,1)} %shard_map.59), calls=%async_computation | async-start | bytes 524288 | tf_op jit(solution)/shard_map/all_to_all | solution.py:373
  41.0 0.7 %shard_map.60 = (bf16[256,512]{1,0:T(8,128)(2,1)S(1)}, f32[512,512]{1,0:T(8,128)S(1)}) custom-call(bf16[8,144,128]{2,1,0:T(8,128)(2,1)S(1)} %all-to-all-done.1.lines_ref), custom_call_target="tpu_custom_call" | custom-call | flops 134217728 | bytes 2000000 | tf_op jit(solution)/shard_map/pallas_call | solution.py:375
  41.6 6.9 %all-to-all-done.lines_ref = bf16[8,128,128]{2,1,0:T(8,128)(2,1)S(1)} async-done(((bf16[8,128,128]{2,1,0:T(8,128)(2,1)}), bf16[8,128,128]{2,1,0:T(8,128)(2,1)S(1)}, u32[]{:S(2)}, u32[]{:S(2)}) %all-to-all-start) | async-done | bytes 262176 | tf_op jit(solution)/shard_map/all_to_all | solution.py:373
  48.6 1.5 %shard_map.61 = f32[512,2,256]{2,1,0:T(2,128)} custom-call(bf16[8,128,128]{2,1,0:T(8,128)(2,1)S(1)} %all-to-all-done.lines_ref, bf16[256,512]{1,0:T(8,128)(2,1)S(1)} %get-tuple-element.27.taps_ref, f32[512,512]{1,0:T(8,128)S(1)} %get-tuple-element.28.sum_ref), custom_call_target="tpu_custom_call" | custom-call | flops 134217728 | bytes 2000000 | tf_op jit(solution)/shard_map/pallas_call | solution.py:383
  (3 shorter events, 0.0 us)
Async XLA Ops:
  0.0 4.2 %copy-start = (bf16[32,2,8192]{2,1,0:T(2,128)(2,1)S(1)}, bf16[32,2,8192]{2,1,0:T(2,128)(2,1)}, u32[]{:S(2)}) copy-start(bf16[32,2,8192]{2,1,0:T(2,128)(2,1)} %raw_ref.5) | copy-start | bytes 3145732
  1.6 2.6 %copy-start.2 = (bf16[2,1024]{1,0:T(2,128)(2,1)S(1)}, bf16[2,1024]{1,0:T(2,128)(2,1)}, u32[]{:S(2)}) copy-start(bf16[2,1024]{1,0:T(2,128)(2,1)} %chirp_ref.1) | copy-start | bytes 12292
  1.6 2.6 %copy-start.3 = (s32[4,8]{1,0:T(4,128)S(1)}, s32[4,8]{1,0:T(4,128)}, u32[]{:S(2)}) copy-start(s32[4,8]{1,0:T(4,128)} %index_ref.1) | copy-start | bytes 388
  1.6 12.7 %collective-permute-start = (bf16[41,32,128]{2,1,0:T(8,128)(2,1)}, bf16[41,32,128]{2,1,0:T(8,128)(2,1)S(1)}, u32[]{:S(2)}, u32[]{:S(2)}) collective-permute-start(bf16[41,32,128]{2,1,0:T(8,128)(2,1)} %bitcast.8), channel_id=1, source_target_pairs={{0,1},{1,2},{2,3},{4,5},{5,6},{6,7},{8,9},{9,10},{10,11},{12,13},{... | collective-permute-start | bytes 1007624 | tf_op jit(solution)/shard_map/ppermute | solution.py:326
  2.9 11.4 %collective-permute-start.1 = (bf16[32,32,128]{2,1,0:T(8,128)(2,1)}, bf16[32,32,128]{2,1,0:T(8,128)(2,1)S(1)}, u32[]{:S(2)}, u32[]{:S(2)}) collective-permute-start(bf16[32,32,128]{2,1,0:T(8,128)(2,1)} %bitcast.10), channel_id=1, source_target_pairs={{1,3},{5,7},{9,11},{13,15},{17,19},{21,23},{25,27},{29,31}} | collective-permute-start | bytes 786440 | tf_op jit(solution)/shard_map/ppermute | solution.py:327
  4.3 0.7 %copy-start.1 = (bf16[8,2,512]{2,1,0:T(2,128)(2,1)S(1)}, bf16[8,2,512]{2,1,0:T(2,128)(2,1)}, u32[]{:S(2)}) copy-start(bf16[8,2,512]{2,1,0:T(2,128)(2,1)} %refs_ref.1) | copy-start | bytes 49156
  16.4 19.1 %all-to-all-start.1 = ((bf16[8,144,128]{2,1,0:T(8,128)(2,1)}), bf16[8,144,128]{2,1,0:T(8,128)(2,1)S(1)}, u32[]{:S(2)}, u32[]{:S(2)}) async-start(bf16[8,144,128]{2,1,0:T(8,128)(2,1)} %shard_map.58), calls=%async_computation.1 | async-start | bytes 589824 | tf_op jit(solution)/shard_map/all_to_all | solution.py:373
  22.8 10.6 %collective-permute-start.2 = (bf16[41,32,128]{2,1,0:T(8,128)(2,1)}, bf16[41,32,128]{2,1,0:T(8,128)(2,1)S(1)}, u32[]{:S(2)}, u32[]{:S(2)}) collective-permute-start(bf16[41,32,128]{2,1,0:T(8,128)(2,1)} %bitcast.9), channel_id=1, source_target_pairs={{0,1},{1,2},{2,3},{4,5},{5,6},{6,7},{8,9},{9,10},{10,11},{12,13},{... | collective-permute-start | bytes 1007624 | tf_op jit(solution)/shard_map/ppermute | solution.py:326
  24.1 9.3 %collective-permute-start.3 = (bf16[32,32,128]{2,1,0:T(8,128)(2,1)}, bf16[32,32,128]{2,1,0:T(8,128)(2,1)S(1)}, u32[]{:S(2)}, u32[]{:S(2)}) collective-permute-start(bf16[32,32,128]{2,1,0:T(8,128)(2,1)} %bitcast.11), channel_id=1, source_target_pairs={{1,3},{5,7},{9,11},{13,15},{17,19},{21,23},{25,27},{29,31}} | collective-permute-start | bytes 786440 | tf_op jit(solution)/shard_map/ppermute | solution.py:327
  35.5 13.1 %all-to-all-start = ((bf16[8,128,128]{2,1,0:T(8,128)(2,1)}), bf16[8,128,128]{2,1,0:T(8,128)(2,1)S(1)}, u32[]{:S(2)}, u32[]{:S(2)}) async-start(bf16[8,128,128]{2,1,0:T(8,128)(2,1)} %shard_map.59), calls=%async_computation | async-start | bytes 524288 | tf_op jit(solution)/shard_map/all_to_all | solution.py:373

commit v3 on v2

--- a/solution.py
+++ b/solution.py
@@ -272,7 +272,7 @@
 
 
 def call(kernel, outs, specs, flops, moved, scratch=(), vmem=40 * 2**20):
-    space = {"s": pltpu.SMEM, "v": pltpu.VMEM, "a": pl.ANY}
+    space = {"s": pltpu.SMEM, "v": pltpu.VMEM, "a": pl.ANY, "h": pltpu.HBM}
     return pl.pallas_call(
         kernel,
         out_shape=outs,
@@ -310,9 +310,9 @@
                 jax.ShapeDtypeStruct((span, pulses_each, 2, LANES), BF),
                 jax.ShapeDtypeStruct((half, pulses_each, 2, LANES), BF),
             ),
-            "sa",
-            10**5,
-            2 * 10**6,
+            "sh",
+            1000,
+            1000,
             [
                 pltpu.VMEM((pulses_each, 2, span * LANES), BF),
                 pltpu.VMEM((pulses_each, 2, half * LANES), BF),
@@ -333,17 +333,17 @@
             jax.ShapeDtypeStruct((pulse_devices, 16, LANES), BF),
             jax.ShapeDtypeStruct((parts, span, pulses_each, 2, LANES), BF),
         ),
-        "ssvva",
-        10**7,
-        10**6,
+        "ssvvh",
+        1000,
+        1000,
         [pltpu.VMEM((pulses, 2, span * LANES), BF), pltpu.SemaphoreType.DMA],
+        60 * 2**20,
     )(turn, migration_index, chirp_replica, azimuth_refs, raw_echo)
     own = own.reshape(parts, span, rows_each, LANES)
 
     tail = 16 + tap_tiles - 1
     targets = pulse_devices if short else 2
     squeezed = []
-    turn = window_start
     for part in range(parts):
         extra = 16 if short and part == 0 else 0
         squeezed.append(
@@ -351,8 +351,8 @@
                 functools.partial(compress_kernel, part),
                 jax.ShapeDtypeStruct((targets, half // targets * rows_each + extra, LANES), BF),
                 "saaaav" if extra else "saaaaa",
-                2 * half * rows_each * tap_tiles * LANES * 2 * LANES,
-                4 * 10**6,
+                1000,
+                1000,
                 [
                     pltpu.VMEM((span + tail, rows_each, LANES), BF),
                     pltpu.VMEM((tap_tiles * LANES, 2 * LANES), BF),

time: 50.6 us -> 54 us (1.067)
  local copies, waits for them, and re-layouts: 0.73 us -> 2.95 us
  Pallas kernels: 9.32 us -> 10.6 us
    unnamed x8 -> x12, local copies, waits for them, and re-layouts: 0.73 us -> 2.95 us
    pallas_call x1, Pallas kernels: 1.24 us -> 2.48 us  [on_device(): call(prep_kernel, (jax.ShapeDtypeStruct((tap_tiles * LANES, 2 * LANES), B...]
  transfers between devices with their start and end apart: 6 -> 6, of which waited for: 3 -> 3; matrix products, arithmetic and copies ran while one was open for 0% -> 0% of each run, Pallas kernels for 10% -> 11%
where the time goes in v3:
time: 54 us; the launch traced here: 53.3 us
  waiting for transfers between devices  22.6 us (42%)
  starting transfers between devices  16.3 us (30%)
  Pallas kernels  10.6 us (20%)
  local copies, waits for them, and re-layouts  2.95 us (5%)
  between operations  0.78 us (1%)
    ppermute x2, waiting for transfers between devices, on_device(): fars.append(lax.ppermute(far, 'sa', [(1, 3)]))  15.7 us
    all_to_all x2, starting transfers between devices, on_device(): lax.all_to_all(part, 'pa', split_axis=0, concat_axis=0, tiled=True)  11.1 us
    all_to_all x2, waiting for transfers between devices, on_device(): lax.all_to_all(part, 'pa', split_axis=0, concat_axis=0, tiled=True)  6.92 us
    pallas_call x2, Pallas kernels, on_device(): call(functools.partial(compress_kernel, part), jax.ShapeDtypeStruct((targ...  4.22 us
    unnamed x12, local copies, waits for them, and re-layouts  2.95 us
    ppermute x2, starting transfers between devices, on_device(): nears.append(lax.ppermute(near, 'sa', [(0, 1), (1, 2), (2, 3)]))  2.58 us
    ppermute x2, starting transfers between devices, on_device(): fars.append(lax.ppermute(far, 'sa', [(1, 3)]))  2.58 us
    pallas_call x1, Pallas kernels, on_device(): call(prep_kernel, (jax.ShapeDtypeStruct((tap_tiles * LANES, 2 * LANES), B...  2.48 us
  transfers between devices with their start and end apart: 6, of which 3 were waited for; matrix products, arithmetic and copies ran while one was open for 0% of the time, Pallas kernels for 11%

profile of v3, /device:TPU:3, one launch (start us, length us, event | category | flops | bytes accessed | tf_op | source)
XLA Modules:
  0.0 53.3 jit_solution(1479610351380003087)
XLA Ops:
  0.7 0.9 %shard_map.55 = (bf16[41,16,2,128]{3,2,1,0:T(2,128)(2,1)}, bf16[32,16,2,128]{3,2,1,0:T(2,128)(2,1)}) custom-call(s32[1]{0:T(128)S(6)} %copy.6.window_ref, bf16[32,2,8192]{2,1,0:T(2,128)(2,1)} %raw_ref.5), custom_call_target="tpu_custom_call" | custom-call | flops 1000 | bytes 1000 | tf_op jit(solution)/shard_map/pallas_call | solution.py:307
  1.5 1.3 %collective-permute-start = (bf16[41,32,128]{2,1,0:T(8,128)(2,1)}, bf16[41,32,128]{2,1,0:T(8,128)(2,1)S(1)}, u32[]{:S(2)}, u32[]{:S(2)}) collective-permute-start(bf16[41,32,128]{2,1,0:T(8,128)(2,1)} %bitcast.8), channel_id=1, source_target_pairs={{0,1},{1,2},{2,3},{4,5},{5,6},{6,7},{8,9},{9,10},{10,11},{12,13},{... | collective-permute-start | bytes 1007624 | tf_op jit(solution)/shard_map/ppermute | solution.py:326
  2.8 1.3 %collective-permute-start.1 = (bf16[32,32,128]{2,1,0:T(8,128)(2,1)}, bf16[32,32,128]{2,1,0:T(8,128)(2,1)S(1)}, u32[]{:S(2)}, u32[]{:S(2)}) collective-permute-start(bf16[32,32,128]{2,1,0:T(8,128)(2,1)} %bitcast.10), channel_id=1, source_target_pairs={{1,3},{5,7},{9,11},{13,15},{17,19},{21,23},{25,27},{29,31}} | collective-permute-start | bytes 786440 | tf_op jit(solution)/shard_map/ppermute | solution.py:327
  4.1 2.5 %shard_map.57 = (bf16[1280,256]{1,0:T(8,128)(2,1)}, bf16[8,16,128]{2,1,0:T(8,128)(2,1)}, bf16[2,41,16,2,128]{4,3,2,1,0:T(2,128)(2,1)}) custom-call(s32[1]{0:T(128)S(6)} %copy.6.window_ref, s32[4,8]{1,0:T(4,128)} %index_ref.1, bf16[2,1024]{1,0:T(2,128)(2,1)} %chirp_ref.1, bf16[8,2,512]{2,1,0:T(2,128)(2,1)} %refs_ref.1, bf16[32,2,8192]{2,1,0:T(2,128)(2,1)} %raw_ref.5), custom_call_target="tpu_custom_call" | custom-call | flops 1000 | bytes 1000 | tf_op jit(solution)/shard_map/pallas_call | solution.py:329
  6.6 7.6 %collective-permute-done.1.far_ref = bf16[32,32,128]{2,1,0:T(8,128)(2,1)S(1)} collective-permute-done((bf16[32,32,128]{2,1,0:T(8,128)(2,1)}, bf16[32,32,128]{2,1,0:T(8,128)(2,1)S(1)}, u32[]{:S(2)}, u32[]{:S(2)}) %collective-permute-start.1) | collective-permute-done | bytes 262176 | tf_op jit(solution)/shard_map/ppermute | solution.py:327
  14.2 0.0 collective-permute-done.near_ref
  14.2 1.1 %copy-done = bf16[2,41,16,2,128]{4,3,2,1,0:T(2,128)(2,1)S(1)} copy-done((bf16[2,41,16,2,128]{4,3,2,1,0:T(2,128)(2,1)S(1)}, bf16[2,41,16,2,128]{4,3,2,1,0:T(2,128)(2,1)}, u32[]{:S(2)}) %copy-start) | copy-done | bytes 671768
  15.3 1.1 %copy-done.2 = bf16[1280,256]{1,0:T(8,128)(2,1)S(1)} copy-done((bf16[1280,256]{1,0:T(8,128)(2,1)S(1)}, bf16[1280,256]{1,0:T(8,128)(2,1)}, u32[]{:S(2)}) %copy-start.2) | copy-done | bytes 655384
  16.4 0.8 %copy-done.4 = bf16[8,16,128]{2,1,0:T(8,128)(2,1)S(1)} copy-done((bf16[8,16,128]{2,1,0:T(8,128)(2,1)S(1)}, bf16[8,16,128]{2,1,0:T(8,128)(2,1)}, u32[]{:S(2)}) %copy-start.4) | copy-done | bytes 32792
  17.1 2.1 %shard_map.58 = bf16[8,144,128]{2,1,0:T(8,128)(2,1)} custom-call(s32[1]{0:T(128)S(6)} %copy.6.window_ref, bf16[2,41,32,128]{3,2,1,0:T(8,128)(2,1)S(1)} %bitcast.6, bf16[41,32,128]{2,1,0:T(8,128)(2,1)S(1)} %collective-permute-done.near_ref, bf16[32,32,128]{2,1,0:T(8,128)(2,1)S(1)} %collective-permute-done.1.far_ref, bf16[1280,256]{1,0:T(8,128)(2,1)S(1)} %copy-done.2, ...), custom_call_target="tpu_custom_call" | custom-call | flops 1000 | bytes 1000 | tf_op jit(solution)/shard_map/pallas_call | solution.py:350
  19.3 0.0 copy-start.3
  19.3 5.7 %all-to-all-start.1 = ((bf16[8,144,128]{2,1,0:T(8,128)(2,1)}), bf16[8,144,128]{2,1,0:T(8,128)(2,1)S(1)}, u32[]{:S(2)}, u32[]{:S(2)}) async-start(bf16[8,144,128]{2,1,0:T(8,128)(2,1)} %shard_map.58), calls=%async_computation.1 | async-start | bytes 589824 | tf_op jit(solution)/shard_map/all_to_all | solution.py:373
  25.0 0.0 copy-start.5
  25.0 0.9 %shard_map.56 = (bf16[41,16,2,128]{3,2,1,0:T(2,128)(2,1)}, bf16[32,16,2,128]{3,2,1,0:T(2,128)(2,1)}) custom-call(s32[1]{0:T(128)S(6)} %copy.6.window_ref, bf16[32,2,8192]{2,1,0:T(2,128)(2,1)} %raw_ref.5), custom_call_target="tpu_custom_call" | custom-call | flops 1000 | bytes 1000 | tf_op jit(solution)/shard_map/pallas_call | solution.py:307
  25.9 1.3 %collective-permute-start.2 = (bf16[41,32,128]{2,1,0:T(8,128)(2,1)}, bf16[41,32,128]{2,1,0:T(8,128)(2,1)S(1)}, u32[]{:S(2)}, u32[]{:S(2)}) collective-permute-start(bf16[41,32,128]{2,1,0:T(8,128)(2,1)} %bitcast.9), channel_id=1, source_target_pairs={{0,1},{1,2},{2,3},{4,5},{5,6},{6,7},{8,9},{9,10},{10,11},{12,13},{... | collective-permute-start | bytes 1007624 | tf_op jit(solution)/shard_map/ppermute | solution.py:326
  27.2 1.3 %collective-permute-start.3 = (bf16[32,32,128]{2,1,0:T(8,128)(2,1)}, bf16[32,32,128]{2,1,0:T(8,128)(2,1)S(1)}, u32[]{:S(2)}, u32[]{:S(2)}) collective-permute-start(bf16[32,32,128]{2,1,0:T(8,128)(2,1)} %bitcast.11), channel_id=1, source_target_pairs={{1,3},{5,7},{9,11},{13,15},{17,19},{21,23},{25,27},{29,31}} | collective-permute-start | bytes 786440 | tf_op jit(solution)/shard_map/ppermute | solution.py:327
  28.5 8.1 %collective-permute-done.3.far_ref = bf16[32,32,128]{2,1,0:T(8,128)(2,1)S(1)} collective-permute-done((bf16[32,32,128]{2,1,0:T(8,128)(2,1)}, bf16[32,32,128]{2,1,0:T(8,128)(2,1)S(1)}, u32[]{:S(2)}, u32[]{:S(2)}) %collective-permute-start.3) | collective-permute-done | bytes 262176 | tf_op jit(solution)/shard_map/ppermute | solution.py:327
  36.5 0.0 collective-permute-done.2.near_ref
  36.5 2.1 %shard_map.59 = bf16[8,128,128]{2,1,0:T(8,128)(2,1)} custom-call(s32[1]{0:T(128)S(6)} %copy.6.window_ref, bf16[2,41,32,128]{3,2,1,0:T(8,128)(2,1)S(1)} %bitcast.7, bf16[41,32,128]{2,1,0:T(8,128)(2,1)S(1)} %collective-permute-done.2.near_ref, bf16[32,32,128]{2,1,0:T(8,128)(2,1)S(1)} %collective-permute-done.3.far_ref, bf16[1280,256]{1,0:T(8,128)(2,1)S(1)} %copy-done.3, ...), custom_call_target="tpu_custom_call" | custom-call | flops 1000 | bytes 1000 | tf_op jit(solution)/shard_map/pallas_call | solution.py:350
  38.7 0.0 all-to-all-done.1.lines_ref
  38.7 5.4 %all-to-all-start = ((bf16[8,128,128]{2,1,0:T(8,128)(2,1)}), bf16[8,128,128]{2,1,0:T(8,128)(2,1)S(1)}, u32[]{:S(2)}, u32[]{:S(2)}) async-start(bf16[8,128,128]{2,1,0:T(8,128)(2,1)} %shard_map.59), calls=%async_computation | async-start | bytes 524288 | tf_op jit(solution)/shard_map/all_to_all | solution.py:373
  44.1 0.7 %shard_map.60 = (bf16[256,512]{1,0:T(8,128)(2,1)S(1)}, f32[512,512]{1,0:T(8,128)S(1)}) custom-call(bf16[8,144,128]{2,1,0:T(8,128)(2,1)S(1)} %all-to-all-done.1.lines_ref), custom_call_target="tpu_custom_call" | custom-call | flops 134217728 | bytes 2000000 | tf_op jit(solution)/shard_map/pallas_call | solution.py:375
  44.8 6.9 %all-to-all-done.lines_ref = bf16[8,128,128]{2,1,0:T(8,128)(2,1)S(1)} async-done(((bf16[8,128,128]{2,1,0:T(8,128)(2,1)}), bf16[8,128,128]{2,1,0:T(8,128)(2,1)S(1)}, u32[]{:S(2)}, u32[]{:S(2)}) %all-to-all-start) | async-done | bytes 262176 | tf_op jit(solution)/shard_map/all_to_all | solution.py:373
  51.7 1.5 %shard_map.61 = f32[512,2,256]{2,1,0:T(2,128)} custom-call(bf16[8,128,128]{2,1,0:T(8,128)(2,1)S(1)} %all-to-all-done.lines_ref, bf16[256,512]{1,0:T(8,128)(2,1)S(1)} %get-tuple-element.27.taps_ref, f32[512,512]{1,0:T(8,128)S(1)} %get-tuple-element.28.sum_ref), custom_call_target="tpu_custom_call" | custom-call | flops 134217728 | bytes 2000000 | tf_op jit(solution)/shard_map/pallas_call | solution.py:383
  (7 shorter events, 0.0 us)
Async XLA Ops:
  1.5 12.7 %collective-permute-start = (bf16[41,32,128]{2,1,0:T(8,128)(2,1)}, bf16[41,32,128]{2,1,0:T(8,128)(2,1)S(1)}, u32[]{:S(2)}, u32[]{:S(2)}) collective-permute-start(bf16[41,32,128]{2,1,0:T(8,128)(2,1)} %bitcast.8), channel_id=1, source_target_pairs={{0,1},{1,2},{2,3},{4,5},{5,6},{6,7},{8,9},{9,10},{10,11},{12,13},{... | collective-permute-start | bytes 1007624 | tf_op jit(solution)/shard_map/ppermute | solution.py:326
  2.8 11.4 %collective-permute-start.1 = (bf16[32,32,128]{2,1,0:T(8,128)(2,1)}, bf16[32,32,128]{2,1,0:T(8,128)(2,1)S(1)}, u32[]{:S(2)}, u32[]{:S(2)}) collective-permute-start(bf16[32,32,128]{2,1,0:T(8,128)(2,1)} %bitcast.10), channel_id=1, source_target_pairs={{1,3},{5,7},{9,11},{13,15},{17,19},{21,23},{25,27},{29,31}} | collective-permute-start | bytes 786440 | tf_op jit(solution)/shard_map/ppermute | solution.py:327
  14.2 1.1 %copy-start = (bf16[2,41,16,2,128]{4,3,2,1,0:T(2,128)(2,1)S(1)}, bf16[2,41,16,2,128]{4,3,2,1,0:T(2,128)(2,1)}, u32[]{:S(2)}) copy-start(bf16[2,41,16,2,128]{4,3,2,1,0:T(2,128)(2,1)} %get-tuple-element.21) | copy-start | bytes 2015236
  15.3 1.1 %copy-start.2 = (bf16[1280,256]{1,0:T(8,128)(2,1)S(1)}, bf16[1280,256]{1,0:T(8,128)(2,1)}, u32[]{:S(2)}) copy-start(bf16[1280,256]{1,0:T(8,128)(2,1)} %get-tuple-element.23.taps_ref) | copy-start | bytes 1966084
  16.4 0.8 %copy-start.4 = (bf16[8,16,128]{2,1,0:T(8,128)(2,1)S(1)}, bf16[8,16,128]{2,1,0:T(8,128)(2,1)}, u32[]{:S(2)}) copy-start(bf16[8,16,128]{2,1,0:T(8,128)(2,1)} %get-tuple-element.24.rows_ref) | copy-start | bytes 98308
  19.3 17.3 %copy-start.3 = (bf16[1280,256]{1,0:T(8,128)(2,1)S(1)}, bf16[1280,256]{1,0:T(8,128)(2,1)}, u32[]{:S(2)}) copy-start(bf16[1280,256]{1,0:T(8,128)(2,1)} %get-tuple-element.23.taps_ref) | copy-start | bytes 1966084
  19.3 19.4 %all-to-all-start.1 = ((bf16[8,144,128]{2,1,0:T(8,128)(2,1)}), bf16[8,144,128]{2,1,0:T(8,128)(2,1)S(1)}, u32[]{:S(2)}, u32[]{:S(2)}) async-start(bf16[8,144,128]{2,1,0:T(8,128)(2,1)} %shard_map.58), calls=%async_computation.1 | async-start | bytes 589824 | tf_op jit(solution)/shard_map/all_to_all | solution.py:373
  25.0 11.5 %copy-start.1 = (bf16[2,41,16,2,128]{4,3,2,1,0:T(2,128)(2,1)S(1)}, bf16[2,41,16,2,128]{4,3,2,1,0:T(2,128)(2,1)}, u32[]{:S(2)}) copy-start(bf16[2,41,16,2,128]{4,3,2,1,0:T(2,128)(2,1)} %get-tuple-element.21) | copy-start | bytes 2015236
  25.0 11.5 %copy-start.5 = (bf16[8,16,128]{2,1,0:T(8,128)(2,1)S(1)}, bf16[8,16,128]{2,1,0:T(8,128)(2,1)}, u32[]{:S(2)}) copy-start(bf16[8,16,128]{2,1,0:T(8,128)(2,1)} %get-tuple-element.24.rows_ref) | copy-start | bytes 98308
  25.9 10.7 %collective-permute-start.2 = (bf16[41,32,128]{2,1,0:T(8,128)(2,1)}, bf16[41,32,128]{2,1,0:T(8,128)(2,1)S(1)}, u32[]{:S(2)}, u32[]{:S(2)}) collective-permute-start(bf16[41,32,128]{2,1,0:T(8,128)(2,1)} %bitcast.9), channel_id=1, source_target_pairs={{0,1},{1,2},{2,3},{4,5},{5,6},{6,7},{8,9},{9,10},{10,11},{12,13},{... | collective-permute-start | bytes 1007624 | tf_op jit(solution)/shard_map/ppermute | solution.py:326
  27.2 9.4 %collective-permute-start.3 = (bf16[32,32,128]{2,1,0:T(8,128)(2,1)}, bf16[32,32,128]{2,1,0:T(8,128)(2,1)S(1)}, u32[]{:S(2)}, u32[]{:S(2)}) collective-permute-start(bf16[32,32,128]{2,1,0:T(8,128)(2,1)} %bitcast.11), channel_id=1, source_target_pairs={{1,3},{5,7},{9,11},{13,15},{17,19},{21,23},{25,27},{29,31}} | collective-permute-start | bytes 786440 | tf_op jit(solution)/shard_map/ppermute | solution.py:327
  38.7 13.1 %all-to-all-start = ((bf16[8,128,128]{2,1,0:T(8,128)(2,1)}), bf16[8,128,128]{2,1,0:T(8,128)(2,1)S(1)}, u32[]{:S(2)}, u32[]{:S(2)}) async-start(bf16[8,128,128]{2,1,0:T(8,128)(2,1)} %shard_map.59), calls=%async_computation | async-start | bytes 524288 | tf_op jit(solution)/shard_map/all_to_all | solution.py:373

commit v4 on v3

--- a/solution.py
+++ b/solution.py
@@ -28,7 +28,8 @@
         target[t] = source[:, :, t * LANES : (t + 1) * LANES]
 
 
-def send_kernel(part, window_ref, raw_ref, near_ref, far_ref, near_raw, far_raw, sems):
+def send_kernel(part, window_ref, raw_ref, near_ref, far_ref, turn_ref, near_raw, far_raw, sems):
+    turn_ref[0] = window_ref[0]
     span, pulses = near_ref.shape[:2]
     half = far_ref.shape[0]
     tiles = raw_ref.shape[2] // LANES
@@ -277,7 +278,9 @@
         kernel,
         out_shape=outs,
         in_specs=[pl.BlockSpec(memory_space=space[kind]) for kind in specs],
-        out_specs=jax.tree.map(lambda _: pl.BlockSpec(memory_space=pltpu.VMEM), outs),
+        out_specs=jax.tree.map(
+            lambda out: pl.BlockSpec(memory_space=pltpu.SMEM if out.dtype == jnp.int32 else pltpu.VMEM), outs
+        ),
         scratch_shapes=list(scratch),
         compiler_params=pltpu.CompilerParams(vmem_limit_bytes=vmem),
         cost_estimate=pl.CostEstimate(flops=flops, bytes_accessed=moved, transcendentals=0),
@@ -304,11 +307,12 @@
     nears, fars = [], []
     turn = window_start
     for part in range(parts):
-        near, far = call(
+        near, far, turn = call(
             functools.partial(send_kernel, part),
             (
                 jax.ShapeDtypeStruct((span, pulses_each, 2, LANES), BF),
                 jax.ShapeDtypeStruct((half, pulses_each, 2, LANES), BF),
+                jax.ShapeDtypeStruct((1,), jnp.int32),
             ),
             "sh",
             1000,
@@ -320,7 +324,6 @@
             ],
             60 * 2**20,
         )(turn, raw_echo)
-        turn = lax.optimization_barrier((window_start, near))[0]
         near = near.reshape(span, rows_each, LANES)
         far = far.reshape(half, rows_each, LANES)
         nears.append(lax.ppermute(near, "sa", [(0, 1), (1, 2), (2, 3)]))
@@ -337,7 +340,6 @@
         1000,
         1000,
         [pltpu.VMEM((pulses, 2, span * LANES), BF), pltpu.SemaphoreType.DMA],
-        60 * 2**20,
     )(turn, migration_index, chirp_replica, azimuth_refs, raw_echo)
     own = own.reshape(parts, span, rows_each, LANES)
 
@@ -360,7 +362,6 @@
                 ],
             )(turn, own, nears[part], fars[part], taps, own_rows)
         )
-        turn = lax.optimization_barrier((window_start, squeezed[-1]))[0]
 
     if not short:
         kept = jnp.stack(squeezed).reshape(parts, half, pulses_each, 2, LANES).transpose(1, 4, 3, 0, 2)

time: 54 us -> 49.7 us (0.920)
  local copies, waits for them, and re-layouts: 2.95 us -> 0.03 us
  waiting for transfers between devices: 22.6 us -> 20.1 us
  Pallas kernels: 10.6 us -> 11.9 us
    unnamed x12, local copies, waits for them, and re-layouts: 2.95 us -> 0.03 us
    ppermute x2, waiting for transfers between devices: 15.7 us -> 13.1 us  [on_device(): fars.append(lax.ppermute(far, 'sa', [(1, 3)]))]
    pallas_call x2, Pallas kernels: 4.22 us -> 5.49 us  [on_device(): call(functools.partial(compress_kernel, part), jax.ShapeDtypeStruct((targ...]
    pallas_call x2, Pallas kernels: 1.71 us -> 2.35 us  [on_device(): call(functools.partial(send_kernel, part), (jax.ShapeDtypeStruct((span, p...]
    pallas_call x1, Pallas kernels: 2.48 us -> 1.87 us  [on_device(): call(prep_kernel, (jax.ShapeDtypeStruct((tap_tiles * LANES, 2 * LANES), B...]
  transfers between devices with their start and end apart: 6 -> 6, of which waited for: 3 -> 3; matrix products, arithmetic and copies ran while one was open for 0% -> 0% of each run, Pallas kernels for 11% -> 14%
where the time goes in v4:
time: 49.7 us; the launch traced here: 49.2 us
  waiting for transfers between devices  20.1 us (40%)
  starting transfers between devices  16.3 us (33%)
  Pallas kernels  11.9 us (24%)
  between operations  0.83 us (2%)
    ppermute x2, waiting for transfers between devices, on_device(): fars.append(lax.ppermute(far, 'sa', [(1, 3)]))  13.1 us
    all_to_all x2, starting transfers between devices, on_device(): lax.all_to_all(part, 'pa', split_axis=0, concat_axis=0, tiled=True)  11.1 us
    all_to_all x2, waiting for transfers between devices, on_device(): lax.all_to_all(part, 'pa', split_axis=0, concat_axis=0, tiled=True)  6.94 us
    pallas_call x2, Pallas kernels, on_device(): call(functools.partial(compress_kernel, part), jax.ShapeDtypeStruct((targ...  5.49 us
    ppermute x2, starting transfers between devices, on_device(): nears.append(lax.ppermute(near, 'sa', [(0, 1), (1, 2), (2, 3)]))  2.58 us
    ppermute x2, starting transfers between devices, on_device(): fars.append(lax.ppermute(far, 'sa', [(1, 3)]))  2.58 us
    pallas_call x2, Pallas kernels, on_device(): call(functools.partial(send_kernel, part), (jax.ShapeDtypeStruct((span, p...  2.35 us
    pallas_call x1, Pallas kernels, on_device(): call(prep_kernel, (jax.ShapeDtypeStruct((tap_tiles * LANES, 2 * LANES), B...  1.87 us
  transfers between devices with their start and end apart: 6, of which 3 were waited for; matrix products, arithmetic and copies ran while one was open for 0% of the time, Pallas kernels for 14%

profile of v4, /device:TPU:3, one launch (start us, length us, event | category | flops | bytes accessed | tf_op | source)
XLA Modules:
  0.0 49.2 jit_solution(2810044673621251136)
XLA Ops:
  0.7 0.0 copy-start
  0.7 0.9 %shard_map.55 = (bf16[41,16,2,128]{3,2,1,0:T(2,128)(2,1)}, bf16[32,16,2,128]{3,2,1,0:T(2,128)(2,1)}, s32[1]{0:T(128)}) custom-call(s32[1]{0:T(128)S(6)} %copy.6.window_ref, bf16[32,2,8192]{2,1,0:T(2,128)(2,1)} %raw_ref.5), custom_call_target="tpu_custom_call" | custom-call | flops 1000 | bytes 1000 | tf_op jit(solution)/shard_map/pallas_call | solution.py:310
  1.5 1.3 %collective-permute-start.2 = (bf16[41,32,128]{2,1,0:T(8,128)(2,1)}, bf16[41,32,128]{2,1,0:T(8,128)(2,1)S(1)}, u32[]{:S(2)}, u32[]{:S(2)}) collective-permute-start(bf16[41,32,128]{2,1,0:T(8,128)(2,1)} %bitcast.9), channel_id=1, source_target_pairs={{0,1},{1,2},{2,3},{4,5},{5,6},{6,7},{8,9},{9,10},{10,11},{12,13},{... | collective-permute-start | bytes 1007624 | tf_op jit(solution)/shard_map/ppermute | solution.py:329
  2.8 1.3 %collective-permute-start.3 = (bf16[32,32,128]{2,1,0:T(8,128)(2,1)}, bf16[32,32,128]{2,1,0:T(8,128)(2,1)S(1)}, u32[]{:S(2)}, u32[]{:S(2)}) collective-permute-start(bf16[32,32,128]{2,1,0:T(8,128)(2,1)} %bitcast.11), channel_id=1, source_target_pairs={{1,3},{5,7},{9,11},{13,15},{17,19},{21,23},{25,27},{29,31}} | collective-permute-start | bytes 786440 | tf_op jit(solution)/shard_map/ppermute | solution.py:330
  4.1 0.0 copy-start.1
  4.1 0.0 copy-start.2
  4.2 0.0 copy-start.3
  4.2 1.5 %shard_map.56 = (bf16[41,16,2,128]{3,2,1,0:T(2,128)(2,1)}, bf16[32,16,2,128]{3,2,1,0:T(2,128)(2,1)}, s32[1]{0:T(128)}) custom-call(s32[1]{0:T(128)} %get-tuple-element.16.window_ref, bf16[32,2,8192]{2,1,0:T(2,128)(2,1)} %raw_ref.5), custom_call_target="tpu_custom_call" | custom-call | flops 1000 | bytes 1000 | tf_op jit(solution)/shard_map/pallas_call | solution.py:310
  5.7 0.0 copy-done
  5.7 1.9 %shard_map.57 = (bf16[1280,256]{1,0:T(8,128)(2,1)S(1)}, bf16[8,16,128]{2,1,0:T(8,128)(2,1)S(1)}, bf16[2,41,16,2,128]{4,3,2,1,0:T(2,128)(2,1)S(1)}) custom-call(s32[1]{0:T(128)} %get-tuple-element.17.window_ref, s32[4,8]{1,0:T(4,128)S(1)} %copy-done.3, bf16[2,1024]{1,0:T(2,128)(2,1)S(1)} %copy-done.2, bf16[8,2,512]{2,1,0:T(2,128)(2,1)S(1)} %copy-done.1, ...), custom_call_target="tpu_custom_call" | custom-call | flops 1000 | bytes 1000 | tf_op jit(solution)/shard_map/pallas_call | solution.py:332
  7.6 6.7 %collective-permute-done.3.far_ref = bf16[32,32,128]{2,1,0:T(8,128)(2,1)S(1)} collective-permute-done((bf16[32,32,128]{2,1,0:T(8,128)(2,1)}, bf16[32,32,128]{2,1,0:T(8,128)(2,1)S(1)}, u32[]{:S(2)}, u32[]{:S(2)}) %collective-permute-start.3) | collective-permute-done | bytes 262176 | tf_op jit(solution)/shard_map/ppermute | solution.py:330
  14.3 0.0 collective-permute-done.2.near_ref
  14.3 2.8 %shard_map.59 = bf16[8,144,128]{2,1,0:T(8,128)(2,1)} custom-call(s32[1]{0:T(128)} %get-tuple-element.17.window_ref, bf16[2,41,32,128]{3,2,1,0:T(8,128)(2,1)S(1)} %bitcast.6, bf16[41,32,128]{2,1,0:T(8,128)(2,1)S(1)} %collective-permute-done.2.near_ref, bf16[32,32,128]{2,1,0:T(8,128)(2,1)S(1)} %collective-permute-done.3.far_ref, ...), custom_call_target="tpu_custom_call" | custom-call | flops 1000 | bytes 1000 | tf_op jit(solution)/shard_map/pallas_call | solution.py:352
  17.1 5.7 %all-to-all-start.1 = ((bf16[8,144,128]{2,1,0:T(8,128)(2,1)}), bf16[8,144,128]{2,1,0:T(8,128)(2,1)S(1)}, u32[]{:S(2)}, u32[]{:S(2)}) async-start(bf16[8,144,128]{2,1,0:T(8,128)(2,1)} %shard_map.59), calls=%async_computation.1 | async-start | bytes 589824 | tf_op jit(solution)/shard_map/all_to_all | solution.py:374
  22.8 1.3 %collective-permute-start = (bf16[41,32,128]{2,1,0:T(8,128)(2,1)S(1)}, bf16[41,32,128]{2,1,0:T(8,128)(2,1)S(1)}, u32[]{:S(2)}, u32[]{:S(2)}) collective-permute-start(bf16[41,32,128]{2,1,0:T(8,128)(2,1)S(1)} %bitcast.8), channel_id=1, source_target_pairs={{0,1},{1,2},{2,3},{4,5},{5,6},{6,7},{8,9},{9,10},{10,11},{12,13},{... | collective-permute-start | bytes 1007624 | tf_op jit(solution)/shard_map/ppermute | solution.py:329
  24.1 1.3 %collective-permute-start.1 = (bf16[32,32,128]{2,1,0:T(8,128)(2,1)S(1)}, bf16[32,32,128]{2,1,0:T(8,128)(2,1)S(1)}, u32[]{:S(2)}, u32[]{:S(2)}) collective-permute-start(bf16[32,32,128]{2,1,0:T(8,128)(2,1)S(1)} %bitcast.10), channel_id=1, source_target_pairs={{1,3},{5,7},{9,11},{13,15},{17,19},{21,23},{25,27},{29,31}} | collective-permute-start | bytes 786440 | tf_op jit(solution)/shard_map/ppermute | solution.py:330
  25.4 6.4 %collective-permute-done.1.far_ref = bf16[32,32,128]{2,1,0:T(8,128)(2,1)S(1)} collective-permute-done((bf16[32,32,128]{2,1,0:T(8,128)(2,1)S(1)}, bf16[32,32,128]{2,1,0:T(8,128)(2,1)S(1)}, u32[]{:S(2)}, u32[]{:S(2)}) %collective-permute-start.1) | collective-permute-done | bytes 262176 | tf_op jit(solution)/shard_map/ppermute | solution.py:330
  31.8 0.0 collective-permute-done.near_ref
  31.8 2.7 %shard_map.58 = bf16[8,128,128]{2,1,0:T(8,128)(2,1)} custom-call(s32[1]{0:T(128)} %get-tuple-element.17.window_ref, bf16[2,41,32,128]{3,2,1,0:T(8,128)(2,1)S(1)} %bitcast.7, bf16[41,32,128]{2,1,0:T(8,128)(2,1)S(1)} %collective-permute-done.near_ref, bf16[32,32,128]{2,1,0:T(8,128)(2,1)S(1)} %collective-permute-done.1.far_ref, ...), custom_call_target="tpu_custom_call" | custom-call | flops 1000 | bytes 1000 | tf_op jit(solution)/shard_map/pallas_call | solution.py:352
  34.6 0.0 all-to-all-done.1.lines_ref
  34.6 5.4 %all-to-all-start = ((bf16[8,128,128]{2,1,0:T(8,128)(2,1)}), bf16[8,128,128]{2,1,0:T(8,128)(2,1)S(1)}, u32[]{:S(2)}, u32[]{:S(2)}) async-start(bf16[8,128,128]{2,1,0:T(8,128)(2,1)} %shard_map.58), calls=%async_computation | async-start | bytes 524288 | tf_op jit(solution)/shard_map/all_to_all | solution.py:374
  40.0 0.7 %shard_map.60 = (bf16[256,512]{1,0:T(8,128)(2,1)S(1)}, f32[512,512]{1,0:T(8,128)S(1)}) custom-call(bf16[8,144,128]{2,1,0:T(8,128)(2,1)S(1)} %all-to-all-done.1.lines_ref), custom_call_target="tpu_custom_call" | custom-call | flops 134217728 | bytes 2000000 | tf_op jit(solution)/shard_map/pallas_call | solution.py:376
  40.7 6.9 %all-to-all-done.lines_ref = bf16[8,128,128]{2,1,0:T(8,128)(2,1)S(1)} async-done(((bf16[8,128,128]{2,1,0:T(8,128)(2,1)}), bf16[8,128,128]{2,1,0:T(8,128)(2,1)S(1)}, u32[]{:S(2)}, u32[]{:S(2)}) %all-to-all-start) | async-done | bytes 262176 | tf_op jit(solution)/shard_map/all_to_all | solution.py:374
  47.6 1.5 %shard_map.61 = f32[512,2,256]{2,1,0:T(2,128)} custom-call(bf16[8,128,128]{2,1,0:T(8,128)(2,1)S(1)} %all-to-all-done.lines_ref, bf16[256,512]{1,0:T(8,128)(2,1)S(1)} %get-tuple-element.25.taps_ref, f32[512,512]{1,0:T(8,128)S(1)} %get-tuple-element.26.sum_ref), custom_call_target="tpu_custom_call" | custom-call | flops 134217728 | bytes 2000000 | tf_op jit(solution)/shard_map/pallas_call | solution.py:384
  (7 shorter events, 0.0 us)
Async XLA Ops:
  0.7 5.0 %copy-start = (bf16[32,2,8192]{2,1,0:T(2,128)(2,1)S(1)}, bf16[32,2,8192]{2,1,0:T(2,128)(2,1)}, u32[]{:S(2)}) copy-start(bf16[32,2,8192]{2,1,0:T(2,128)(2,1)} %raw_ref.5) | copy-start | bytes 3145732
  1.5 12.8 %collective-permute-start.2 = (bf16[41,32,128]{2,1,0:T(8,128)(2,1)}, bf16[41,32,128]{2,1,0:T(8,128)(2,1)S(1)}, u32[]{:S(2)}, u32[]{:S(2)}) collective-permute-start(bf16[41,32,128]{2,1,0:T(8,128)(2,1)} %bitcast.9), channel_id=1, source_target_pairs={{0,1},{1,2},{2,3},{4,5},{5,6},{6,7},{8,9},{9,10},{10,11},{12,13},{... | collective-permute-start | bytes 1007624 | tf_op jit(solution)/shard_map/ppermute | solution.py:329
  2.8 11.5 %collective-permute-start.3 = (bf16[32,32,128]{2,1,0:T(8,128)(2,1)}, bf16[32,32,128]{2,1,0:T(8,128)(2,1)S(1)}, u32[]{:S(2)}, u32[]{:S(2)}) collective-permute-start(bf16[32,32,128]{2,1,0:T(8,128)(2,1)} %bitcast.11), channel_id=1, source_target_pairs={{1,3},{5,7},{9,11},{13,15},{17,19},{21,23},{25,27},{29,31}} | collective-permute-start | bytes 786440 | tf_op jit(solution)/shard_map/ppermute | solution.py:330
  4.1 1.5 %copy-start.1 = (bf16[8,2,512]{2,1,0:T(2,128)(2,1)S(1)}, bf16[8,2,512]{2,1,0:T(2,128)(2,1)}, u32[]{:S(2)}) copy-start(bf16[8,2,512]{2,1,0:T(2,128)(2,1)} %refs_ref.1) | copy-start | bytes 49156
  4.1 1.5 %copy-start.2 = (bf16[2,1024]{1,0:T(2,128)(2,1)S(1)}, bf16[2,1024]{1,0:T(2,128)(2,1)}, u32[]{:S(2)}) copy-start(bf16[2,1024]{1,0:T(2,128)(2,1)} %chirp_ref.1) | copy-start | bytes 12292
  4.2 1.5 %copy-start.3 = (s32[4,8]{1,0:T(4,128)S(1)}, s32[4,8]{1,0:T(4,128)}, u32[]{:S(2)}) copy-start(s32[4,8]{1,0:T(4,128)} %index_ref.1) | copy-start | bytes 388
  14.3 9.8 %copy-start.5 = (bf16[32,16,2,128]{3,2,1,0:T(2,128)(2,1)S(1)}, bf16[32,16,2,128]{3,2,1,0:T(2,128)(2,1)}, u32[]{:S(2)}) copy-start(bf16[32,16,2,128]{3,2,1,0:T(2,128)(2,1)} %get-tuple-element.20) | copy-start | bytes 786436
  17.1 5.7 %copy-start.4 = (bf16[41,16,2,128]{3,2,1,0:T(2,128)(2,1)S(1)}, bf16[41,16,2,128]{3,2,1,0:T(2,128)(2,1)}, u32[]{:S(2)}) copy-start(bf16[41,16,2,128]{3,2,1,0:T(2,128)(2,1)} %get-tuple-element.19) | copy-start | bytes 1007620
  17.1 17.5 %all-to-all-start.1 = ((bf16[8,144,128]{2,1,0:T(8,128)(2,1)}), bf16[8,144,128]{2,1,0:T(8,128)(2,1)S(1)}, u32[]{:S(2)}, u32[]{:S(2)}) async-start(bf16[8,144,128]{2,1,0:T(8,128)(2,1)} %shard_map.59), calls=%async_computation.1 | async-start | bytes 589824 | tf_op jit(solution)/shard_map/all_to_all | solution.py:374
  22.8 9.0 %collective-permute-start = (bf16[41,32,128]{2,1,0:T(8,128)(2,1)S(1)}, bf16[41,32,128]{2,1,0:T(8,128)(2,1)S(1)}, u32[]{:S(2)}, u32[]{:S(2)}) collective-permute-start(bf16[41,32,128]{2,1,0:T(8,128)(2,1)S(1)} %bitcast.8), channel_id=1, source_target_pairs={{0,1},{1,2},{2,3},{4,5},{5,6},{6,7},{8,9},{9,10},{10,11},{12,13},{... | collective-permute-start | bytes 1007624 | tf_op jit(solution)/shard_map/ppermute | solution.py:329
  24.1 7.7 %collective-permute-start.1 = (bf16[32,32,128]{2,1,0:T(8,128)(2,1)S(1)}, bf16[32,32,128]{2,1,0:T(8,128)(2,1)S(1)}, u32[]{:S(2)}, u32[]{:S(2)}) collective-permute-start(bf16[32,32,128]{2,1,0:T(8,128)(2,1)S(1)} %bitcast.10), channel_id=1, source_target_pairs={{1,3},{5,7},{9,11},{13,15},{17,19},{21,23},{25,27},{29,31}} | collective-permute-start | bytes 786440 | tf_op jit(solution)/shard_map/ppermute | solution.py:330
  34.6 13.1 %all-to-all-start = ((bf16[8,128,128]{2,1,0:T(8,128)(2,1)}), bf16[8,128,128]{2,1,0:T(8,128)(2,1)S(1)}, u32[]{:S(2)}, u32[]{:S(2)}) async-start(bf16[8,128,128]{2,1,0:T(8,128)(2,1)} %shard_map.58), calls=%async_computation | async-start | bytes 524288 | tf_op jit(solution)/shard_map/all_to_all | solution.py:374

commit v5 on v1

v5 whole, which is shorter than its diff:
```python
import jax
import jax.numpy as jnp
from jax import lax
from jax.experimental import pallas as pl
from jax.experimental.pallas import tpu as pltpu
from jax.sharding import PartitionSpec as P

R = 16384
L = 512
LANES = 128
BF = jnp.bfloat16
F32 = jnp.float32


def reversed_lanes(row):
    row_id = lax.broadcasted_iota(jnp.int32, (LANES, LANES), 0)
    col_id = lax.broadcasted_iota(jnp.int32, (LANES, LANES), 1)
    flip = (row_id + col_id == LANES - 1).astype(BF)
    tiles = row.shape[1] // LANES
    pieces = [row[:, t * LANES : (t + 1) * LANES] for t in reversed(range(tiles))]
    return jnp.concatenate([jnp.dot(piece, flip, preferred_element_type=F32) for piece in pieces], axis=1)


def retile(source, target, first, tiles):
    shape = target.shape[1:]
    for t in range(tiles):
        target[first + t] = source[:, :, t * LANES : (t + 1) * LANES].reshape(shape)


def copy_all(sems, *pairs):
    copies = [pltpu.make_async_copy(*pair, sems.at[at]) for at, pair in enumerate(pairs)]
    for copy in copies:
        copy.start()
    for copy in copies:
        copy.wait()


def far_kernel(raw_ref, far_ref, turn_ref, sems):
    turn_ref[0] = 0
    width = far_ref.shape[2]

    @pl.when(lax.axis_index("sa") == 1)
    def _():
        copy_all(sems, (raw_ref.at[:, :, pl.ds(raw_ref.shape[2] - width, width)], far_ref))


def near_kernel(turn_in_ref, window_ref, raw_ref, near_ref, turn_ref, natural, held, sems):
    turn_ref[0] = turn_in_ref[0]
    span = near_ref.shape[0]
    tiles = raw_ref.shape[2] // LANES
    sub_index = lax.axis_index("sa")
    offset = window_ref[0] // LANES
    first = jnp.where(sub_index == 0, tiles - span, jnp.where(sub_index == 1, offset, 0))

    @pl.when(sub_index < 3)
    def _():
        copy_all(sems, (raw_ref.at[:, :, pl.ds(pl.multiple_of(first * LANES, LANES), span * LANES)], natural))
        retile(natural, held, 0, span)
        copy_all(sems, (held, near_ref))


def rows_kernel(turn_in_ref, index_ref, refs_ref, rows_ref, turn_ref):
    turn_ref[0] = turn_in_ref[0]
    own = refs_ref.shape[0]
    sub_index = lax.axis_index("sa")
    first_row = lax.axis_index("pa") * own

    def fill(target, carry):
        local = index_ref[sub_index, target] - first_row
        held = jnp.logical_and(local >= 0, local < own)
        row = refs_ref[jnp.clip(local, 0, own - 1)]
        rows_ref[target] = jnp.where(held, row, jnp.zeros_like(row))
        return carry

    lax.fori_loop(0, rows_ref.shape[0], fill, 0)


def range_taps_kernel(turn_in_ref, window_ref, chirp_ref, taps_ref):
    taps = chirp_ref.shape[1]
    blocks = taps_ref.shape[0] // LANES
    width = blocks * LANES
    shift = lax.rem(window_ref[0], LANES)
    chirp = jnp.concatenate([chirp_ref[...], jnp.zeros((14, taps), BF)], axis=0)
    flipped = reversed_lanes(chirp)
    padded = jnp.concatenate([jnp.zeros((16, 2 * LANES), F32), flipped], axis=1)
    padded = jnp.concatenate([padded, jnp.zeros((16, width + LANES - padded.shape[1]), F32)], axis=1)
    moved = pltpu.roll(padded, width + LANES - 127 - shift, 1)[:, :width]
    for part in range(2):
        spread = jnp.broadcast_to(moved[part : part + 1], (LANES, width))
        skewed = pltpu.roll(spread, 0, 1, stride=1, stride_axis=0)
        for t in range(blocks):
            first = LANES * (blocks - 1 - t)
            taps_ref[t * LANES : (t + 1) * LANES, part * LANES : (part + 1) * LANES] = skewed[
                :, first : first + LANES
            ].astype(BF)


def compress_kernel(window_ref, raw_ref, near_ref, far_ref, taps_ref, out_ref, natural, held, made, sems):
    half = out_ref.shape[0]
    span, rows, _ = near_ref.shape
    tail = held.shape[0] - span
    offset = window_ref[0] // LANES
    sub_index = lax.axis_index("sa")

    @pl.when(sub_index == 0)
    def _():
        copy_all(sems, (raw_ref.at[:, :, pl.ds(pl.multiple_of(offset * LANES, LANES), span * LANES)], natural))
        retile(natural, held, 0, span)

    @pl.when(sub_index == 1)
    def _():
        part = natural.at[:, :, pl.ds(0, tail * LANES)]
        copy_all(sems, (raw_ref.at[:, :, pl.ds(0, tail * LANES)], part), (near_ref, held.at[pl.ds(0, span)]))
        retile(natural, held, span, tail)

    @pl.when(sub_index == 2)
    def _():
        copy_all(sems, (near_ref, held.at[pl.ds(0, span)]))

    @pl.when(sub_index == 3)
    def _():
        part = natural.at[:, :, pl.ds(0, half * LANES)]
        copy_all(sems, (far_ref, part), (near_ref.at[pl.ds(0, tail)], held.at[pl.ds(half, tail)]))
        retile(natural, held, 0, half)

    base = jnp.where(sub_index == 1, span - half + offset, jnp.where(sub_index == 3, offset, 0))
    tap_tiles = taps_ref.shape[0] // LANES
    even = lax.rem(lax.broadcasted_iota(jnp.int32, (1, 8, LANES), 1), 2) == 0
    group = 8
    copies = []
    for step in range(half // group):
        into = pl.ds(group * step, group)
        blocks = [
            held[pl.ds(base + group * step + t, group)].reshape(group * rows, LANES) for t in range(tap_tiles)
        ]
        product = jnp.dot(jnp.concatenate(blocks, axis=1), taps_ref[...], preferred_element_type=F32)
        straight = product[:, :LANES].reshape(-1, 8, LANES)
        crossed = product[:, LANES:].reshape(-1, 8, LANES)
        total = straight + jnp.where(even, pltpu.roll(crossed, 7, 1), -pltpu.roll(crossed, 1, 1))
        made[into] = total.astype(BF).reshape(group, rows, LANES)
        copies.append(pltpu.make_async_copy(made.at[into], out_ref.at[into], sems.at[step]))
        copies[-1].start()
    for copy in copies:
        copy.wait()


def azimuth_taps_kernel(rows_ref, out_ref, scratch):
    size = out_ref.shape[0] // 2
    row = jnp.sum(rows_ref[...].astype(F32), axis=0).astype(BF)
    row = jnp.concatenate([row, jnp.zeros((14, row.shape[1]), BF)], axis=0)
    flipped = reversed_lanes(row)
    moved = pltpu.roll(flipped, row.shape[1] - (size - 1), 1)
    parts = []
    for part in range(2):
        spread = jnp.broadcast_to(moved[part : part + 1], (size, row.shape[1]))
        parts.append(pltpu.roll(spread, 0, 1, stride=1, stride_axis=0)[:, :size])
    columns = size // LANES
    for part, pair in enumerate(((parts[0], -parts[1]), (parts[1], parts[0]))):
        for target in range(2):
            for column in range(columns):
                scratch[target * columns + column, pl.ds(part, size, stride=2), :] = pair[target][
                    :, column * LANES : (column + 1) * LANES
                ]
    for column in range(2 * columns):
        out_ref[:, column * LANES : (column + 1) * LANES] = scratch[column].astype(BF)


def azimuth_kernel(lines_ref, taps_ref, out_ref, made, sems):
    sources, tiles, rows, _ = lines_ref.shape
    pulses = out_ref.shape[2]
    copies = []
    for tile in range(tiles):
        lines = lines_ref[:, tile].reshape(sources * rows, LANES)
        focused = lax.dot_general(
            lines, taps_ref[...], (((0,), (0,)), ((), ())), preferred_element_type=F32
        )
        into = pl.ds(tile * LANES, LANES)
        made[into, 0, :] = focused[:, :pulses]
        made[into, 1, :] = focused[:, pulses:]
        copies.append(pltpu.make_async_copy(made.at[into], out_ref.at[into], sems.at[tile]))
        copies[-1].start()
    for copy in copies:
        copy.wait()


def toeplitz(diagonal_taps, size):
    span_size = 2 * size - 1
    reversed_taps = diagonal_taps[..., ::-1]
    shifted = jnp.concatenate(
        [reversed_taps[..., size - 1 :], reversed_taps[..., : size - 1]], axis=-1
    )
    reps = (1,) * (shifted.ndim - 1) + (size,)
    tiled_flat = jnp.tile(shifted, reps)[..., : size * (span_size - 1)]
    return tiled_flat.reshape(shifted.shape[:-1] + (size, span_size - 1))[..., :size]


def tap_blocks(tap_values, size):
    block_total = tap_values.shape[1] // size + 1
    padded_taps = jnp.pad(tap_values, ((0, 0), (size, 2 * size)))
    matrices = []
    for offset_block in range(block_total):
        first_tap = offset_block * size + 1
        parts = toeplitz(padded_taps[:, first_tap : first_tap + 2 * size - 1], size)
        real_part = parts[0]
        imag_part = parts[1]
        matrices.append(
            jnp.stack([jnp.stack([real_part, -imag_part]), jnp.stack([imag_part, real_part])])
        )
    return jnp.stack(matrices)


def correlate(blocked, matrices, output_count):
    summed = jnp.zeros((blocked.shape[0], 2, output_count, blocked.shape[3]), F32)
    for offset_block in range(matrices.shape[0]):
        piece_rows = blocked[:, :, offset_block : offset_block + output_count, :]
        summed = summed + jnp.einsum(
            "rcib,cdbn->rdin", piece_rows, matrices[offset_block], preferred_element_type=F32
        )
    return summed


def focus_long(range_lines, reference_row):
    block_size = L // 2
    bin_count, _, total_pulses = range_lines.shape
    block_count = total_pulses // block_size
    blocked = range_lines.reshape(bin_count, 2, block_count, block_size)
    blocked = jnp.pad(blocked, ((0, 0), (0, 0), (1, 1), (0, 0)))
    focused = correlate(blocked, tap_blocks(reference_row, block_size), block_count)
    return focused.reshape(1, bin_count, 2, total_pulses)


def call(kernel, outs, specs, scratch=(), vmem=40):
    space = {"s": pltpu.SMEM, "v": pltpu.VMEM, "a": pl.ANY}
    blocks = [pl.BlockSpec(memory_space=space[kind]) for kind in specs]
    return pl.pallas_call(
        kernel,
        out_shape=outs,
        in_specs=blocks[: -len(outs)],
        out_specs=tuple(blocks[-len(outs) :]),
        scratch_shapes=list(scratch),
        compiler_params=pltpu.CompilerParams(vmem_limit_bytes=vmem * 2**20),
        cost_estimate=pl.CostEstimate(flops=1000, bytes_accessed=1000, transcendentals=0),
    )


def on_device(raw_echo, chirp_replica, azimuth_refs, migration_index, window_start):
    pulses = raw_echo.shape[0]
    segment_devices = lax.axis_size("sa")
    pulse_devices = lax.axis_size("pa")
    tap_count = chirp_replica.shape[1]
    kept_width = R // segment_devices
    bin_count = kept_width // pulse_devices
    total_pulses = pulses * pulse_devices
    half = kept_width // LANES
    tap_tiles = tap_count // LANES + 2
    span = half + tap_tiles - 1

    rows = 2 * pulses
    tail = 16 + tap_tiles - 1
    token = jax.ShapeDtypeStruct((1,), jnp.int32)
    shape = jax.ShapeDtypeStruct
    dma = pltpu.SemaphoreType.DMA

    far, turn = call(far_kernel, (shape((pulses, 2, half * LANES), BF), token), "aas", [dma((1,))], 60)(raw_echo)
    far = lax.ppermute(far, "sa", [(1, 3)])
    near, turn = call(
        near_kernel,
        (shape((span, rows, LANES), BF), token),
        "ssaas",
        [pltpu.VMEM((pulses, 2, span * LANES), BF), pltpu.VMEM((span, rows, LANES), BF), dma((1,))],
        60,
    )(turn, window_start, raw_echo)
    near = lax.ppermute(near, "sa", [(0, 1), (1, 2), (2, 3)])
    own_rows, turn = call(rows_kernel, (shape((pulse_devices, 2, L), BF), token), "ssvvs")(
        turn, migration_index, azimuth_refs
    )
    rows_in = lax.all_to_all(own_rows, "pa", split_axis=0, concat_axis=0, tiled=True)
    (taps,) = call(range_taps_kernel, (shape((tap_tiles * LANES, 2 * LANES), BF),), "ssvv")(
        turn, window_start, chirp_replica
    )
    (compressed,) = call(
        compress_kernel,
        (shape((half, rows, LANES), BF),),
        "saaava",
        [
            pltpu.VMEM((pulses, 2, span * LANES), BF),
            pltpu.VMEM((span + tail, rows, LANES), BF),
            pltpu.VMEM((half, rows, LANES), BF),
            dma((half // 8,)),
        ],
        60,
    )(window_start, raw_echo, near, far, taps)

    if bin_count % LANES or total_pulses != L // 2:
        kept = compressed.reshape(half, pulses, 2, LANES).transpose(0, 3, 2, 1)
        outgoing = kept.reshape(pulse_devices, bin_count, 2, pulses)
        turned = lax.all_to_all(outgoing, "pa", split_axis=0, concat_axis=3, tiled=True)
        reference_row = jnp.sum(rows_in.astype(F32), axis=0).astype(BF)
        return focus_long(turned[0], reference_row)

    width = 2 * total_pulses
    (azimuth_taps,) = call(
        azimuth_taps_kernel, (shape((width, width), BF),), "vv", [pltpu.VMEM((width // LANES, width, LANES), F32)]
    )(rows_in)
    outgoing = compressed.reshape(pulse_devices, bin_count // LANES, rows, LANES)
    lines = lax.all_to_all(outgoing, "pa", split_axis=0, concat_axis=0, tiled=True)
    (focused,) = call(
        azimuth_kernel,
        (shape((bin_count, 2, total_pulses), F32),),
        "vva",
        [pltpu.VMEM((bin_count, 2, total_pulses), F32), dma((bin_count // LANES,))],
    )(lines, azimuth_taps)
    return focused[None]


def solution(mesh):
    placed = (P("pa", None, "sa"), P(), P("pa", None, None), P(), P())
    return jax.shard_map(
        on_device, mesh=mesh, in_specs=placed, out_specs=P("sa", "pa", None, None), check_vma=False
    )
```

time: 46.1 us -> 64.9 us (1.41)
  Pallas kernels: 6.6 us -> 30.6 us
  local copies, waits for them, and re-layouts: 7.64 us -> 2.5 us
  starting transfers between devices: 16.9 us -> 16 us
  waiting for transfers between devices: 13.7 us -> 14.5 us
    pallas_call x4 -> x7, Pallas kernels: 6.6 us -> 30.6 us  [the longest x1 17.5 us: on_device(): call(far_kernel, (shape((pulses, 2, half * LANES), BF), token), 'aas', [d...]
    transpose x1 -> x0, local copies, waits for them, and re-layouts: 3.08 us -> none  [on_device(): raw_echo.reshape(pulses, 2, tiles, LANES).transpose(2, 0, 1, 3)]
    ppermute x1, starting transfers between devices: 4.5 us -> 1.92 us  [on_device(): near = lax.ppermute(near, 'sa', [(0, 1), (1, 2), (2, 3)])]
    all_to_all x1, waiting for transfers between devices: 10.9 us -> 12.7 us  [on_device(): lax.all_to_all(outgoing, 'pa', split_axis=0, concat_axis=0, tiled=True)]
    slice x1 -> x0, local copies, waits for them, and re-layouts: 1.23 us -> none  [on_device(): far = tiled[tiles - half:]]
    ppermute x1, waiting for transfers between devices: 2.83 us -> 1.84 us  [on_device(): far = lax.ppermute(far, 'sa', [(1, 3)])]
    dynamic_slice x1 -> x0, local copies, waits for them, and re-layouts: 0.89 us -> none  [on_device(): near = lax.dynamic_slice_in_dim(tiled, near_first, span, 0)]
    all_to_all x1, starting transfers between devices: 5.55 us -> 6.4 us  [on_device(): lax.all_to_all(own_rows, 'pa', split_axis=0, concat_axis=0, tiled=True)]
  transfers between devices with their start and end apart: 4 -> 4, of which waited for: 2 -> 2; matrix products, arithmetic and copies ran while one was open for 3% -> 0% of each run, Pallas kernels for 11% -> 13%
where the time goes in v5:
time: 64.9 us; the launch traced here: 64.5 us
  Pallas kernels  30.6 us (47%)
  starting transfers between devices  16 us (25%)
  waiting for transfers between devices  14.5 us (22%)
  local copies, waits for them, and re-layouts  2.5 us (4%)
  between operations  0.8 us (1%)
    pallas_call x1, Pallas kernels, on_device(): call(far_kernel, (shape((pulses, 2, half * LANES), BF), token), 'aas', [d...  17.5 us
    all_to_all x1, waiting for transfers between devices, on_device(): lax.all_to_all(outgoing, 'pa', split_axis=0, concat_axis=0, tiled=True)  12.7 us
    all_to_all x1, starting transfers between devices, on_device(): lax.all_to_all(own_rows, 'pa', split_axis=0, concat_axis=0, tiled=True)  6.4 us
    all_to_all x1, starting transfers between devices, on_device(): lax.all_to_all(outgoing, 'pa', split_axis=0, concat_axis=0, tiled=True)  6.4 us
    pallas_call x1, Pallas kernels, on_device(): call(compress_kernel, (shape((half, rows, LANES), BF),), 'saaava', [pltpu...  4.78 us
    pallas_call x1, Pallas kernels, on_device(): call(near_kernel, (shape((span, rows, LANES), BF), token), 'ssaas', [pltp...  3.42 us
    unnamed x14, local copies, waits for them, and re-layouts  2.5 us
    ppermute x1, starting transfers between devices, on_device(): near = lax.ppermute(near, 'sa', [(0, 1), (1, 2), (2, 3)])  1.92 us
  transfers between devices with their start and end apart: 4, of which 2 were waited for; matrix products, arithmetic and copies ran while one was open for 0% of the time, Pallas kernels for 13%

profile of v5, /device:TPU:1, one launch (start us, length us, event | category | flops | bytes accessed | tf_op | source)
XLA Modules:
  0.0 64.5 jit_solution(12127485721046249505)
XLA Ops:
  0.7 17.5 %shard_map.55 = (bf16[32,2,4096]{2,1,0:T(2,128)(2,1)}, s32[1]{0:T(128)}) custom-call(bf16[32,2,8192]{2,1,0:T(2,128)(2,1)} %raw_ref.5), custom_call_target="tpu_custom_call" | custom-call | flops 1000 | bytes 1000 | tf_op jit(solution)/shard_map/pallas_call | solution.py:264
  18.2 0.0 copy-start.1
  18.2 3.4 %shard_map.56 = (bf16[41,64,128]{2,1,0:T(8,128)(2,1)}, s32[1]{0:T(128)}) custom-call(s32[1]{0:T(128)} %get-tuple-element.11.turn_in_ref, s32[1]{0:T(128)S(6)} %copy.6.window_ref, bf16[32,2,8192]{2,1,0:T(2,128)(2,1)} %raw_ref.5), custom_call_target="tpu_custom_call" | custom-call | flops 1000 | bytes 1000 | tf_op jit(solution)/shard_map/pallas_call | solution.py:266
  21.6 0.0 copy-start.3
  21.6 1.9 %collective-permute-start = (bf16[41,64,128]{2,1,0:T(8,128)(2,1)}, bf16[41,64,128]{2,1,0:T(8,128)(2,1)S(1)}, u32[]{:S(2)}, u32[]{:S(2)}) collective-permute-start(bf16[41,64,128]{2,1,0:T(8,128)(2,1)} %get-tuple-element.12), channel_id=1, source_target_pairs={{0,1},{1,2},{2,3},{4,5},{5,6},{6,7},{8,9},{9,10},{10,11},{12,13},{... | collective-permute-start | bytes 2015240 | tf_op jit(solution)/shard_map/ppermute | solution.py:273
  23.6 1.3 %collective-permute-start.1 = (bf16[32,2,4096]{2,1,0:T(2,128)(2,1)S(1)}, bf16[32,2,4096]{2,1,0:T(2,128)(2,1)S(1)}, u32[]{:S(2)}, u32[]{:S(2)}) collective-permute-start(bf16[32,2,4096]{2,1,0:T(2,128)(2,1)S(1)} %copy-done.6), channel_id=1, source_target_pairs={{1,3},{5,7},{9,11},{13,15},{17,19},{21,23},{25,27},{29,31}} | collective-permute-start | bytes 1572872 | tf_op jit(solution)/shard_map/ppermute | solution.py:265
  24.9 0.0 copy-done.1
  24.9 0.0 copy-done.3
  24.9 1.9 %shard_map.57 = (bf16[8,2,512]{2,1,0:T(2,128)(2,1)}, s32[1]{0:T(128)}) custom-call(s32[1]{0:T(128)} %get-tuple-element.14.turn_in_ref, s32[4,8]{1,0:T(4,128)S(1)} %copy-done.3, bf16[8,2,512]{2,1,0:T(2,128)(2,1)S(1)} %copy-done.1), custom_call_target="tpu_custom_call" | custom-call | flops 1000 | bytes 1000 | tf_op jit(solution)/shard_map/pallas_call | solution.py:274
  26.8 0.0 copy-start.2
  26.9 6.4 %all-to-all-start.1 = ((bf16[8,2,512]{2,1,0:T(2,128)(2,1)}), bf16[8,2,512]{2,1,0:T(2,128)(2,1)S(1)}, u32[]{:S(2)}, u32[]{:S(2)}) async-start(bf16[8,2,512]{2,1,0:T(2,128)(2,1)} %get-tuple-element.16), calls=%async_computation.1 | async-start | bytes 32768 | tf_op jit(solution)/shard_map/all_to_all | solution.py:277
  33.3 0.0 copy-done.2
  33.3 1.1 %shard_map.58.taps_ref = bf16[1280,256]{1,0:T(8,128)(2,1)S(1)} custom-call(s32[1]{0:T(128)} %get-tuple-element.15.turn_in_ref, s32[1]{0:T(128)S(6)} %copy.6.window_ref, bf16[2,1024]{1,0:T(2,128)(2,1)S(1)} %copy-done.2), custom_call_target="tpu_custom_call" | custom-call | flops 1000 | bytes 1000 | tf_op jit(solution)/shard_map/pallas_call | solution.py:278
  34.4 0.8 %copy-done = bf16[1280,256]{1,0:T(8,128)(2,1)} copy-done((bf16[1280,256]{1,0:T(8,128)(2,1)}, bf16[1280,256]{1,0:T(8,128)(2,1)S(1)}, u32[]{:S(2)}) %copy-start) | copy-done | bytes 655384
  35.2 1.8 %collective-permute-done.1.far_ref = bf16[32,2,4096]{2,1,0:T(2,128)(2,1)S(1)} collective-permute-done((bf16[32,2,4096]{2,1,0:T(2,128)(2,1)S(1)}, bf16[32,2,4096]{2,1,0:T(2,128)(2,1)S(1)}, u32[]{:S(2)}, u32[]{:S(2)}) %collective-permute-start.1) | collective-permute-done | bytes 524320 | tf_op jit(solution)/shard_map/ppermute | solution.py:265
  37.1 0.0 collective-permute-done.near_ref
  37.1 0.8 %copy-done.5 = bf16[32,2,4096]{2,1,0:T(2,128)(2,1)} copy-done((bf16[32,2,4096]{2,1,0:T(2,128)(2,1)}, bf16[32,2,4096]{2,1,0:T(2,128)(2,1)S(1)}, u32[]{:S(2)}) %copy-start.5) | copy-done | bytes 524312
  37.9 0.8 %copy-done.4 = bf16[41,64,128]{2,1,0:T(8,128)(2,1)} copy-done((bf16[41,64,128]{2,1,0:T(8,128)(2,1)}, bf16[41,64,128]{2,1,0:T(8,128)(2,1)S(1)}, u32[]{:S(2)}) %copy-start.4) | copy-done | bytes 671768
  38.7 4.8 %shard_map.59 = bf16[32,64,128]{2,1,0:T(8,128)(2,1)} custom-call(s32[1]{0:T(128)S(6)} %copy.6.window_ref, bf16[32,2,8192]{2,1,0:T(2,128)(2,1)} %raw_ref.5, bf16[41,64,128]{2,1,0:T(8,128)(2,1)} %copy-done.4, bf16[32,2,4096]{2,1,0:T(2,128)(2,1)} %copy-done.5, bf16[1280,256]{1,0:T(8,128)(2,1)} %copy-done), custom_call_target="tpu_custom_call" | custom-call | flops 1000 | bytes 1000 | tf_op jit(solution)/shard_map/pallas_call | solution.py:281
  43.5 0.0 all-to-all-done.1.rows_ref
  43.5 6.4 %all-to-all-start = ((bf16[8,4,64,128]{3,2,1,0:T(8,128)(2,1)}), bf16[8,4,64,128]{3,2,1,0:T(8,128)(2,1)S(1)}, u32[]{:S(2)}, u32[]{:S(2)}) async-start(bf16[8,4,64,128]{3,2,1,0:T(8,128)(2,1)} %bitcast.2), calls=%async_computation | async-start | bytes 1048576 | tf_op jit(solution)/shard_map/all_to_all | solution.py:306
  49.9 0.5 shard_map.60.taps_ref
  50.4 12.7 %all-to-all-done.lines_ref = bf16[8,4,64,128]{3,2,1,0:T(8,128)(2,1)S(1)} async-done(((bf16[8,4,64,128]{3,2,1,0:T(8,128)(2,1)}), bf16[8,4,64,128]{3,2,1,0:T(8,128)(2,1)S(1)}, u32[]{:S(2)}, u32[]{:S(2)}) %all-to-all-start) | async-done | bytes 524320 | tf_op jit(solution)/shard_map/all_to_all | solution.py:306
  63.1 1.3 %shard_map.61 = f32[512,2,256]{2,1,0:T(2,128)} custom-call(bf16[8,4,64,128]{3,2,1,0:T(8,128)(2,1)S(1)} %all-to-all-done.lines_ref, bf16[512,512]{1,0:T(8,128)(2,1)S(1)} %shard_map.60.taps_ref), custom_call_target="tpu_custom_call" | custom-call | flops 1000 | bytes 1000 | tf_op jit(solution)/shard_map/pallas_call | solution.py:307
  (5 shorter events, 0.0 us)
Async XLA Ops:
  18.2 5.4 %copy-start.6 = (bf16[32,2,4096]{2,1,0:T(2,128)(2,1)S(1)}, bf16[32,2,4096]{2,1,0:T(2,128)(2,1)}, u32[]{:S(2)}) copy-start(bf16[32,2,4096]{2,1,0:T(2,128)(2,1)} %get-tuple-element.13) | copy-start | bytes 1572868
  18.2 6.7 %copy-start.1 = (bf16[8,2,512]{2,1,0:T(2,128)(2,1)S(1)}, bf16[8,2,512]{2,1,0:T(2,128)(2,1)}, u32[]{:S(2)}) copy-start(bf16[8,2,512]{2,1,0:T(2,128)(2,1)} %refs_ref.1) | copy-start | bytes 49156
  21.6 3.3 %copy-start.3 = (s32[4,8]{1,0:T(4,128)S(1)}, s32[4,8]{1,0:T(4,128)}, u32[]{:S(2)}) copy-start(s32[4,8]{1,0:T(4,128)} %index_ref.1) | copy-start | bytes 388
  21.6 15.4 %collective-permute-start = (bf16[41,64,128]{2,1,0:T(8,128)(2,1)}, bf16[41,64,128]{2,1,0:T(8,128)(2,1)S(1)}, u32[]{:S(2)}, u32[]{:S(2)}) collective-permute-start(bf16[41,64,128]{2,1,0:T(8,128)(2,1)} %get-tuple-element.12), channel_id=1, source_target_pairs={{0,1},{1,2},{2,3},{4,5},{5,6},{6,7},{8,9},{9,10},{10,11},{12,13},{... | collective-permute-start | bytes 2015240 | tf_op jit(solution)/shard_map/ppermute | solution.py:273
  23.6 13.5 %collective-permute-start.1 = (bf16[32,2,4096]{2,1,0:T(2,128)(2,1)S(1)}, bf16[32,2,4096]{2,1,0:T(2,128)(2,1)S(1)}, u32[]{:S(2)}, u32[]{:S(2)}) collective-permute-start(bf16[32,2,4096]{2,1,0:T(2,128)(2,1)S(1)} %copy-done.6), channel_id=1, source_target_pairs={{1,3},{5,7},{9,11},{13,15},{17,19},{21,23},{25,27},{29,31}} | collective-permute-start | bytes 1572872 | tf_op jit(solution)/shard_map/ppermute | solution.py:265
  26.8 6.4 %copy-start.2 = (bf16[2,1024]{1,0:T(2,128)(2,1)S(1)}, bf16[2,1024]{1,0:T(2,128)(2,1)}, u32[]{:S(2)}) copy-start(bf16[2,1024]{1,0:T(2,128)(2,1)} %chirp_ref.1) | copy-start | bytes 12292
  26.9 16.7 %all-to-all-start.1 = ((bf16[8,2,512]{2,1,0:T(2,128)(2,1)}), bf16[8,2,512]{2,1,0:T(2,128)(2,1)S(1)}, u32[]{:S(2)}, u32[]{:S(2)}) async-start(bf16[8,2,512]{2,1,0:T(2,128)(2,1)} %get-tuple-element.16), calls=%async_computation.1 | async-start | bytes 32768 | tf_op jit(solution)/shard_map/all_to_all | solution.py:277
  34.4 0.8 %copy-start = (bf16[1280,256]{1,0:T(8,128)(2,1)}, bf16[1280,256]{1,0:T(8,128)(2,1)S(1)}, u32[]{:S(2)}) copy-start(bf16[1280,256]{1,0:T(8,128)(2,1)S(1)} %shard_map.58.taps_ref) | copy-start | bytes 1966084
  37.1 0.8 %copy-start.5 = (bf16[32,2,4096]{2,1,0:T(2,128)(2,1)}, bf16[32,2,4096]{2,1,0:T(2,128)(2,1)S(1)}, u32[]{:S(2)}) copy-start(bf16[32,2,4096]{2,1,0:T(2,128)(2,1)S(1)} %collective-permute-done.1.far_ref) | copy-start | bytes 1572868
  37.9 0.8 %copy-start.4 = (bf16[41,64,128]{2,1,0:T(8,128)(2,1)}, bf16[41,64,128]{2,1,0:T(8,128)(2,1)S(1)}, u32[]{:S(2)}) copy-start(bf16[41,64,128]{2,1,0:T(8,128)(2,1)S(1)} %collective-permute-done.near_ref) | copy-start | bytes 2015236
  43.5 19.6 %all-to-all-start = ((bf16[8,4,64,128]{3,2,1,0:T(8,128)(2,1)}), bf16[8,4,64,128]{3,2,1,0:T(8,128)(2,1)S(1)}, u32[]{:S(2)}, u32[]{:S(2)}) async-start(bf16[8,4,64,128]{3,2,1,0:T(8,128)(2,1)} %bitcast.2), calls=%async_computation | async-start | bytes 1048576 | tf_op jit(solution)/shard_map/all_to_all | solution.py:306

commit v6 on v5

v6 whole, which is shorter than its diff:
```python
import jax
import jax.numpy as jnp
from jax import lax
from jax.experimental import pallas as pl
from jax.experimental.pallas import tpu as pltpu
from jax.sharding import PartitionSpec as P

R = 16384
L = 512
LANES = 128
BF = jnp.bfloat16
F32 = jnp.float32


def reversed_lanes(row):
    row_id = lax.broadcasted_iota(jnp.int32, (LANES, LANES), 0)
    col_id = lax.broadcasted_iota(jnp.int32, (LANES, LANES), 1)
    flip = (row_id + col_id == LANES - 1).astype(BF)
    tiles = row.shape[1] // LANES
    pieces = [row[:, t * LANES : (t + 1) * LANES] for t in reversed(range(tiles))]
    return jnp.concatenate([jnp.dot(piece, flip, preferred_element_type=F32) for piece in pieces], axis=1)


def retile(source, target, first, tiles):
    shape = target.shape[1:]
    for t in range(tiles):
        target[first + t] = source[:, :, t * LANES : (t + 1) * LANES].reshape(shape)


def copy_all(sems, *pairs):
    copies = [pltpu.make_async_copy(*pair, sems.at[at]) for at, pair in enumerate(pairs)]
    for copy in copies:
        copy.start()
    for copy in copies:
        copy.wait()


def far_kernel(raw_ref, far_ref, turn_ref, held, in_sems, out_sems):
    turn_ref[0] = 0
    pulses, _, width = far_ref.shape
    pieces = in_sems.shape[0]
    each = pulses // pieces

    @pl.when(lax.axis_index("sa") == 1)
    def _():
        moves = []
        for at in range(pieces):
            own = pl.ds(at * each, each)
            source = raw_ref.at[own, :, pl.ds(raw_ref.shape[2] - width, width)]
            moves.append(
                (
                    pltpu.make_async_copy(source, held.at[own], in_sems.at[at]),
                    pltpu.make_async_copy(held.at[own], far_ref.at[own], out_sems.at[at]),
                )
            )
        for inward, _ in moves:
            inward.start()
        for inward, outward in moves:
            inward.wait()
            outward.start()
        for _, outward in moves:
            outward.wait()


def near_kernel(turn_in_ref, window_ref, raw_ref, near_ref, turn_ref, natural, held, in_sems, out_sems):
    turn_ref[0] = turn_in_ref[0]
    span = near_ref.shape[0]
    tiles = raw_ref.shape[2] // LANES
    sub_index = lax.axis_index("sa")
    offset = window_ref[0] // LANES
    first = jnp.where(sub_index == 0, tiles - span, jnp.where(sub_index == 1, offset, 0))
    pieces = in_sems.shape[0]
    cuts = [span * at // pieces for at in range(pieces + 1)]

    @pl.when(sub_index < 3)
    def _():
        moves = []
        for at in range(pieces):
            count = cuts[at + 1] - cuts[at]
            start = pl.multiple_of((first + cuts[at]) * LANES, LANES)
            part = natural.at[:, :, pl.ds(cuts[at] * LANES, count * LANES)]
            own = pl.ds(cuts[at], count)
            moves.append(
                (
                    pltpu.make_async_copy(raw_ref.at[:, :, pl.ds(start, count * LANES)], part, in_sems.at[at]),
                    pltpu.make_async_copy(held.at[own], near_ref.at[own], out_sems.at[at]),
                    (part, held, cuts[at], count),
                )
            )
        for inward, _, _ in moves:
            inward.start()
        for inward, outward, order in moves:
            inward.wait()
            retile(*order)
            outward.start()
        for _, outward, _ in moves:
            outward.wait()


def prep_kernel(turn_in_ref, window_ref, index_ref, chirp_ref, refs_ref, taps_ref, rows_ref, turn_ref):
    turn_ref[0] = turn_in_ref[0]
    taps = chirp_ref.shape[1]
    blocks = taps_ref.shape[0] // LANES
    width = blocks * LANES
    shift = lax.rem(window_ref[0], LANES)
    chirp = jnp.concatenate([chirp_ref[...], jnp.zeros((14, taps), BF)], axis=0)
    flipped = reversed_lanes(chirp)
    padded = jnp.concatenate([jnp.zeros((16, 2 * LANES), F32), flipped], axis=1)
    padded = jnp.concatenate([padded, jnp.zeros((16, width + LANES - padded.shape[1]), F32)], axis=1)
    moved = pltpu.roll(padded, width + LANES - 127 - shift, 1)[:, :width]
    for part in range(2):
        spread = jnp.broadcast_to(moved[part : part + 1], (LANES, width))
        skewed = pltpu.roll(spread, 0, 1, stride=1, stride_axis=0)
        for t in range(blocks):
            first = LANES * (blocks - 1 - t)
            taps_ref[t * LANES : (t + 1) * LANES, part * LANES : (part + 1) * LANES] = skewed[
                :, first : first + LANES
            ].astype(BF)
    own = refs_ref.shape[0]
    sub_index = lax.axis_index("sa")
    first_row = lax.axis_index("pa") * own

    def fill(target, carry):
        local = index_ref[sub_index, target] - first_row
        held = jnp.logical_and(local >= 0, local < own)
        row = refs_ref[jnp.clip(local, 0, own - 1)].astype(F32)
        row = jnp.where(held, row, jnp.zeros_like(row))
        pieces = [row[part : part + 1, t * LANES : (t + 1) * LANES] for part in range(2) for t in range(L // LANES)]
        rows_ref[target] = jnp.concatenate(pieces + [jnp.zeros((8, LANES), F32)], axis=0).astype(BF)
        return carry

    lax.fori_loop(0, rows_ref.shape[0], fill, 0)


def arrange_kernel(turn_in_ref, window_ref, raw_ref, far_ref, out_ref, natural, sems):
    span = natural.shape[2] // LANES
    tail = out_ref.shape[0] - span
    half = far_ref.shape[2] // LANES
    offset = window_ref[0] // LANES + turn_in_ref[0]
    sub_index = lax.axis_index("sa")

    @pl.when(sub_index == 0)
    def _():
        copy_all(sems, (raw_ref.at[:, :, pl.ds(pl.multiple_of(offset * LANES, LANES), span * LANES)], natural))
        retile(natural, out_ref, 0, span)

    @pl.when(sub_index == 1)
    def _():
        part = natural.at[:, :, pl.ds(0, tail * LANES)]
        copy_all(sems, (raw_ref.at[:, :, pl.ds(0, tail * LANES)], part))
        retile(natural, out_ref, span, tail)

    @pl.when(sub_index == 3)
    def _():
        part = natural.at[:, :, pl.ds(0, half * LANES)]
        copy_all(sems, (far_ref, part))
        retile(natural, out_ref, 0, half)


def compress_kernel(window_ref, arranged_ref, near_ref, taps_ref, rows_ref, out_ref, held, made, sems):
    span, rows, _ = near_ref.shape
    targets, _, _ = out_ref.shape
    tail = held.shape[0] - span
    group = 8
    tap_tiles = taps_ref.shape[0] // LANES
    half = span - tap_tiles + 1
    per_target = half // targets
    offset = window_ref[0] // LANES
    sub_index = lax.axis_index("sa")

    def both(at, count):
        return arranged_ref.at[pl.ds(at, count)], held.at[pl.ds(at, count)]

    @pl.when(sub_index == 0)
    def _():
        copy_all(sems, both(0, span))

    @pl.when(sub_index == 1)
    def _():
        copy_all(sems, both(span, tail), (near_ref, held.at[pl.ds(0, span)]))

    @pl.when(sub_index == 2)
    def _():
        copy_all(sems, (near_ref, held.at[pl.ds(0, span)]))

    @pl.when(sub_index == 3)
    def _():
        copy_all(sems, both(0, half), (near_ref.at[pl.ds(0, tail)], held.at[pl.ds(half, tail)]))

    base = jnp.where(sub_index == 1, span - half + offset, jnp.where(sub_index == 3, offset, 0))
    even = lax.rem(lax.broadcasted_iota(jnp.int32, (1, 8, LANES), 1), 2) == 0
    if out_ref.shape[1] > per_target * rows:
        made[:, per_target * rows :] = rows_ref[...]
    copies = []
    for step in range(half // group):
        blocks = [
            held[pl.ds(base + group * step + t, group)].reshape(group * rows, LANES) for t in range(tap_tiles)
        ]
        product = jnp.dot(jnp.concatenate(blocks, axis=1), taps_ref[...], preferred_element_type=F32)
        straight = product[:, :LANES].reshape(-1, 8, LANES)
        crossed = product[:, LANES:].reshape(-1, 8, LANES)
        total = straight + jnp.where(even, pltpu.roll(crossed, 7, 1), -pltpu.roll(crossed, 1, 1))
        count = group // per_target
        into = pl.ds(step * count, count)
        made[into, : per_target * rows] = total.astype(BF).reshape(count, per_target * rows, LANES)
        copies.append(pltpu.make_async_copy(made.at[into], out_ref.at[into], sems.at[step]))
        copies[-1].start()
    for copy in copies:
        copy.wait()


def azimuth_kernel(lines_ref, out_ref, columns_held, taps, made, sems):
    bins, _, pulses = out_ref.shape
    tiles = bins // LANES
    sources = lines_ref.shape[0]
    rows = (lines_ref.shape[1] - 16) // tiles
    picked = jnp.sum(lines_ref[:, tiles * rows :].astype(F32), axis=0)
    pieces = L // LANES
    row = [
        jnp.concatenate([picked[part * pieces + t : part * pieces + t + 1] for t in range(pieces)], axis=1)
        for part in range(2)
    ]
    row = jnp.concatenate(row + [jnp.zeros((14, L), F32)], axis=0).astype(BF)
    moved = pltpu.roll(reversed_lanes(row), L - (pulses - 1), 1)
    parts = []
    for part in range(2):
        spread = jnp.broadcast_to(moved[part : part + 1], (pulses, L))
        parts.append(pltpu.roll(spread, 0, 1, stride=1, stride_axis=0)[:, :pulses])
    columns = pulses // LANES
    for part, pair in enumerate(((parts[0], -parts[1]), (parts[1], parts[0]))):
        for target in range(2):
            for column in range(columns):
                columns_held[target * columns + column, pl.ds(part, pulses, stride=2), :] = pair[target][
                    :, column * LANES : (column + 1) * LANES
                ]
    for column in range(2 * columns):
        taps[:, column * LANES : (column + 1) * LANES] = columns_held[column].astype(BF)
    copies = []
    for tile in range(tiles):
        lines = lines_ref[:, tile * rows : (tile + 1) * rows].reshape(sources * rows, LANES)
        focused = lax.dot_general(lines, taps[...], (((0,), (0,)), ((), ())), preferred_element_type=F32)
        into = pl.ds(tile * LANES, LANES)
        made[into, 0, :] = focused[:, :pulses]
        made[into, 1, :] = focused[:, pulses:]
        copies.append(pltpu.make_async_copy(made.at[into], out_ref.at[into], sems.at[tile]))
        copies[-1].start()
    for copy in copies:
        copy.wait()


def toeplitz(diagonal_taps, size):
    span_size = 2 * size - 1
    reversed_taps = diagonal_taps[..., ::-1]
    shifted = jnp.concatenate(
        [reversed_taps[..., size - 1 :], reversed_taps[..., : size - 1]], axis=-1
    )
    reps = (1,) * (shifted.ndim - 1) + (size,)
    tiled_flat = jnp.tile(shifted, reps)[..., : size * (span_size - 1)]
    return tiled_flat.reshape(shifted.shape[:-1] + (size, span_size - 1))[..., :size]


def tap_blocks(tap_values, size):
    block_total = tap_values.shape[1] // size + 1
    padded_taps = jnp.pad(tap_values, ((0, 0), (size, 2 * size)))
    matrices = []
    for offset_block in range(block_total):
        first_tap = offset_block * size + 1
        parts = toeplitz(padded_taps[:, first_tap : first_tap + 2 * size - 1], size)
        real_part = parts[0]
        imag_part = parts[1]
        matrices.append(
            jnp.stack([jnp.stack([real_part, -imag_part]), jnp.stack([imag_part, real_part])])
        )
    return jnp.stack(matrices)


def correlate(blocked, matrices, output_count):
    summed = jnp.zeros((blocked.shape[0], 2, output_count, blocked.shape[3]), F32)
    for offset_block in range(matrices.shape[0]):
        piece_rows = blocked[:, :, offset_block : offset_block + output_count, :]
        summed = summed + jnp.einsum(
            "rcib,cdbn->rdin", piece_rows, matrices[offset_block], preferred_element_type=F32
        )
    return summed


def focus_long(range_lines, reference_row):
    block_size = L // 2
    bin_count, _, total_pulses = range_lines.shape
    block_count = total_pulses // block_size
    blocked = range_lines.reshape(bin_count, 2, block_count, block_size)
    blocked = jnp.pad(blocked, ((0, 0), (0, 0), (1, 1), (0, 0)))
    focused = correlate(blocked, tap_blocks(reference_row, block_size), block_count)
    return focused.reshape(1, bin_count, 2, total_pulses)


def call(kernel, outs, specs, scratch=(), vmem=24, flops=1000):
    space = {"s": pltpu.SMEM, "v": pltpu.VMEM, "a": pl.ANY}
    blocks = [pl.BlockSpec(memory_space=space[kind]) for kind in specs]
    return pl.pallas_call(
        kernel,
        out_shape=outs,
        in_specs=blocks[: -len(outs)],
        out_specs=tuple(blocks[-len(outs) :]),
        scratch_shapes=list(scratch),
        compiler_params=pltpu.CompilerParams(vmem_limit_bytes=vmem * 2**20),
        cost_estimate=pl.CostEstimate(flops=flops, bytes_accessed=1000, transcendentals=0),
    )


def on_device(raw_echo, chirp_replica, azimuth_refs, migration_index, window_start):
    pulses = raw_echo.shape[0]
    segment_devices = lax.axis_size("sa")
    pulse_devices = lax.axis_size("pa")
    tap_count = chirp_replica.shape[1]
    kept_width = R // segment_devices
    bin_count = kept_width // pulse_devices
    total_pulses = pulses * pulse_devices
    half = kept_width // LANES
    tap_tiles = tap_count // LANES + 2
    span = half + tap_tiles - 1

    rows = 2 * pulses
    tail = 16 + tap_tiles - 1
    token = jax.ShapeDtypeStruct((1,), jnp.int32)
    shape = jax.ShapeDtypeStruct
    dma = pltpu.SemaphoreType.DMA

    short = bin_count % LANES == 0 and total_pulses == L // 2
    natural = pltpu.VMEM((pulses, 2, span * LANES), BF)
    far, turn = call(
        far_kernel,
        (shape((pulses, 2, half * LANES), BF), token),
        "aas",
        [pltpu.VMEM((pulses, 2, half * LANES), BF), dma((8,)), dma((8,))],
        60,
    )(raw_echo)
    far = lax.ppermute(far, "sa", [(1, 3)])
    near, turn = call(
        near_kernel,
        (shape((span, rows, LANES), BF), token),
        "ssaas",
        [natural, pltpu.VMEM((span, rows, LANES), BF), dma((4,)), dma((4,))],
        60,
    )(turn, window_start, raw_echo)
    near = lax.ppermute(near, "sa", [(0, 1), (1, 2), (2, 3)])
    taps, own_rows, turn = call(
        prep_kernel,
        (shape((tap_tiles * LANES, 2 * LANES), BF), shape((pulse_devices, 16, LANES), BF), token),
        "sssvvvvs",
    )(turn, window_start, migration_index, chirp_replica, azimuth_refs)
    (arranged,) = call(
        arrange_kernel, (shape((span + tail, rows, LANES), BF),), "ssaav", [natural, dma((1,))], flops=10**10
    )(turn, window_start, raw_echo, far)

    targets, extra = (pulse_devices, 16) if short else (half // 8, 0)
    made = (targets, half // targets * rows + extra, LANES)
    (compressed,) = call(
        compress_kernel,
        (shape(made, BF),),
        "saavva",
        [pltpu.VMEM((span + tail, rows, LANES), BF), pltpu.VMEM(made, BF), dma((half // 8,))],
    )(window_start, arranged, near, taps, own_rows)

    if not short:
        kept = compressed.reshape(half, pulses, 2, LANES).transpose(0, 3, 2, 1)
        outgoing = kept.reshape(pulse_devices, bin_count, 2, pulses)
        turned = lax.all_to_all(outgoing, "pa", split_axis=0, concat_axis=3, tiled=True)
        rows_in = lax.all_to_all(own_rows, "pa", split_axis=0, concat_axis=0, tiled=True)
        reference_row = jnp.sum(rows_in[:, :8].astype(F32), axis=0).astype(BF).reshape(2, L)
        return focus_long(turned[0], reference_row)

    lines = lax.all_to_all(compressed, "pa", split_axis=0, concat_axis=0, tiled=True)
    width = 2 * total_pulses
    (focused,) = call(
        azimuth_kernel,
        (shape((bin_count, 2, total_pulses), F32),),
        "va",
        [
            pltpu.VMEM((width // LANES, width, LANES), F32),
            pltpu.VMEM((width, width), BF),
            pltpu.VMEM((bin_count, 2, total_pulses), F32),
            dma((bin_count // LANES,)),
        ],
    )(lines)
    return focused[None]


def solution(mesh):
    placed = (P("pa", None, "sa"), P(), P("pa", None, None), P(), P())
    return jax.shard_map(
        on_device, mesh=mesh, in_specs=placed, out_specs=P("sa", "pa", None, None), check_vma=False
    )
```

time: 64.9 us -> 43.1 us (0.66)
  blocking collectives: 0 us -> 18.2 us
  Pallas kernels: 30.6 us -> 15.1 us
  starting transfers between devices: 16 us -> 4.15 us
  waiting for transfers between devices: 14.5 us -> 4.68 us
  local copies, waits for them, and re-layouts: 2.5 us -> 0.02 us
    all_to_all x0 -> x1, blocking collectives: none -> 18.2 us  [on_device(): lax.all_to_all(compressed, 'pa', split_axis=0, concat_axis=0, tiled=True)]
    pallas_call x7 -> x6, Pallas kernels: 30.6 us -> 15.1 us  [the longest x1 4.5 us: on_device(): call(compress_kernel, (shape(made, BF),), 'saavva', [pltpu.VMEM((span + t...]
    all_to_all x2 -> x0, starting transfers between devices: 12.8 us -> none  [the longest x1 6.4 us: on_device(): lax.all_to_all(own_rows, 'pa', split_axis=0, concat_axis=0, tiled=True)]
    all_to_all x2 -> x0, waiting for transfers between devices: 12.7 us -> none  [the longest x1 12.7 us: on_device(): lax.all_to_all(outgoing, 'pa', split_axis=0, concat_axis=0, tiled=True)]
    ppermute x1, waiting for transfers between devices: 0.01 us -> 4.68 us  [on_device(): near = lax.ppermute(near, 'sa', [(0, 1), (1, 2), (2, 3)])]
    unnamed x14 -> x8, local copies, waits for them, and re-layouts: 2.5 us -> 0.02 us
    ppermute x1, waiting for transfers between devices: 1.84 us -> 0.01 us  [on_device(): far = lax.ppermute(far, 'sa', [(1, 3)])]
    ppermute x1, starting transfers between devices: 1.32 us -> 2.23 us  [on_device(): far = lax.ppermute(far, 'sa', [(1, 3)])]
  transfers between devices with their start and end apart: 4 -> 2, of which waited for: 2 -> 1; matrix products, arithmetic and copies ran while one was open for 0% -> 0% of each run, Pallas kernels for 13% -> 15%
where the time goes in v6:
time: 43.1 us; the launch traced here: 42.9 us
  blocking collectives  18.2 us (42%)
  Pallas kernels  15.1 us (35%)
  waiting for transfers between devices  4.68 us (11%)
  starting transfers between devices  4.15 us (10%)
  between operations  0.76 us (2%)
    all_to_all x1, blocking collectives, on_device(): lax.all_to_all(compressed, 'pa', split_axis=0, concat_axis=0, tiled=True)  18.2 us
    ppermute x1, waiting for transfers between devices, on_device(): near = lax.ppermute(near, 'sa', [(0, 1), (1, 2), (2, 3)])  4.68 us
    pallas_call x1, Pallas kernels, on_device(): call(compress_kernel, (shape(made, BF),), 'saavva', [pltpu.VMEM((span + t...  4.5 us
    pallas_call x1, Pallas kernels, on_device(): call(near_kernel, (shape((span, rows, LANES), BF), token), 'ssaas', [natu...  3.16 us
    pallas_call x1, Pallas kernels, on_device(): call(far_kernel, (shape((pulses, 2, half * LANES), BF), token), 'aas', [p...  2.44 us
    pallas_call x1, Pallas kernels, on_device(): call(prep_kernel, (shape((tap_tiles * LANES, 2 * LANES), BF), shape((puls...  2.35 us
    ppermute x1, starting transfers between devices, on_device(): far = lax.ppermute(far, 'sa', [(1, 3)])  2.23 us
    ppermute x1, starting transfers between devices, on_device(): near = lax.ppermute(near, 'sa', [(0, 1), (1, 2), (2, 3)])  1.92 us
  transfers between devices with their start and end apart: 2, of which 1 were waited for; matrix products, arithmetic and copies ran while one was open for 0% of the time, Pallas kernels for 15%

profile of v6, /device:TPU:1, one launch (start us, length us, event | category | flops | bytes accessed | tf_op | source)
XLA Modules:
  0.0 42.9 jit_solution(485960095355259661)
XLA Ops:
  0.0 0.0 copy-start
  0.0 0.0 copy-start.3
  0.0 0.0 copy-start.1
  0.0 0.0 copy-start.2
  0.0 2.4 %shard_map.55 = (bf16[32,2,4096]{2,1,0:T(2,128)(2,1)}, s32[1]{0:T(128)}) custom-call(bf16[32,2,8192]{2,1,0:T(2,128)(2,1)} %raw_ref.5), custom_call_target="tpu_custom_call" | custom-call | flops 1000 | bytes 1000 | tf_op jit(solution)/shard_map/pallas_call | solution.py:331
  2.5 2.2 %collective-permute-start = (bf16[32,2,4096]{2,1,0:T(2,128)(2,1)}, bf16[32,2,4096]{2,1,0:T(2,128)(2,1)S(1)}, u32[]{:S(2)}, u32[]{:S(2)}) collective-permute-start(bf16[32,2,4096]{2,1,0:T(2,128)(2,1)} %get-tuple-element.15), channel_id=1, source_target_pairs={{1,3},{5,7},{9,11},{13,15},{17,19},{21,23},{25,27},{29,31}} | collective-permute-start | bytes 1572872 | tf_op jit(solution)/shard_map/ppermute | solution.py:338
  5.4 3.2 %shard_map.56 = (bf16[41,64,128]{2,1,0:T(8,128)(2,1)}, s32[1]{0:T(128)}) custom-call(s32[1]{0:T(128)} %get-tuple-element.12.turn_in_ref, s32[1]{0:T(128)S(6)} %copy.6.window_ref, bf16[32,2,8192]{2,1,0:T(2,128)(2,1)} %raw_ref.5), custom_call_target="tpu_custom_call" | custom-call | flops 1000 | bytes 1000 | tf_op jit(solution)/shard_map/pallas_call | solution.py:339
  8.5 1.9 %collective-permute-start.1 = (bf16[41,64,128]{2,1,0:T(8,128)(2,1)}, bf16[41,64,128]{2,1,0:T(8,128)(2,1)S(1)}, u32[]{:S(2)}, u32[]{:S(2)}) collective-permute-start(bf16[41,64,128]{2,1,0:T(8,128)(2,1)} %get-tuple-element.16), channel_id=1, source_target_pairs={{0,1},{1,2},{2,3},{4,5},{5,6},{6,7},{8,9},{9,10},{10,11},{12,13},{... | collective-permute-start | bytes 2015240 | tf_op jit(solution)/shard_map/ppermute | solution.py:346
  10.4 0.0 copy-done.3
  10.5 0.0 copy-done.1
  10.5 0.0 copy-done.2
  10.5 2.3 %shard_map.57 = (bf16[1280,256]{1,0:T(8,128)(2,1)S(1)}, bf16[8,16,128]{2,1,0:T(8,128)(2,1)S(1)}, s32[1]{0:T(128)}) custom-call(s32[1]{0:T(128)} %get-tuple-element.13.turn_in_ref, s32[1]{0:T(128)S(6)} %copy.6.window_ref, s32[4,8]{1,0:T(4,128)S(1)} %copy-done.3, bf16[2,1024]{1,0:T(2,128)(2,1)S(1)} %copy-done.2, bf16[8,2,512]{2,1,0:T(2,128)(2,1)S(1)} %copy-done.1), custom_call_target="tpu_custom_call" | custom-call | flops 1000 | bytes 1000 | tf_op jit(solution)/shard_map/pallas_call | solution.py:347
  12.8 0.0 collective-permute-done.far_ref
  12.8 0.0 copy-done
  12.9 0.9 %shard_map.58.arranged_ref = bf16[66,64,128]{2,1,0:T(8,128)(2,1)S(1)} custom-call(s32[1]{0:T(128)} %get-tuple-element.14.turn_in_ref, s32[1]{0:T(128)S(6)} %copy.6.window_ref, bf16[32,2,8192]{2,1,0:T(2,128)(2,1)S(1)} %copy-done, bf16[32,2,4096]{2,1,0:T(2,128)(2,1)S(1)} %collective-permute-done.far_ref), custom_call_target="tpu_custom_call" | custom-call | flops 10000000000 | bytes 1000 | tf_op jit(solution)/shard_map/pallas_call | solution.py:352
  13.8 4.7 %collective-permute-done.1.near_ref = bf16[41,64,128]{2,1,0:T(8,128)(2,1)S(1)} collective-permute-done((bf16[41,64,128]{2,1,0:T(8,128)(2,1)}, bf16[41,64,128]{2,1,0:T(8,128)(2,1)S(1)}, u32[]{:S(2)}, u32[]{:S(2)}) %collective-permute-start.1) | collective-permute-done | bytes 671776 | tf_op jit(solution)/shard_map/ppermute | solution.py:346
  18.4 4.5 %shard_map.59 = bf16[8,272,128]{2,1,0:T(8,128)(2,1)S(1)} custom-call(s32[1]{0:T(128)S(6)} %copy.6.window_ref, bf16[66,64,128]{2,1,0:T(8,128)(2,1)S(1)} %shard_map.58.arranged_ref, bf16[41,64,128]{2,1,0:T(8,128)(2,1)S(1)} %collective-permute-done.1.near_ref, bf16[1280,256]{1,0:T(8,128)(2,1)S(1)} %get-tuple-element.17.taps_ref, ...), custom_call_target="tpu_custom_call" | custom-call | flops 1000 | bytes 1000 | tf_op jit(solution)/shard_map/pallas_call | solution.py:358
  23.0 18.2 %all_to_all.5.lines_ref = bf16[8,272,128]{2,1,0:T(8,128)(2,1)S(1)} all-to-all(bf16[8,272,128]{2,1,0:T(8,128)(2,1)S(1)} %shard_map.59), channel_id=1, replica_groups=mesh['pa'=8,'sa'=4] {'pa'}, dimensions={0} | all-to-all | bytes 1114112 | tf_op jit(solution)/shard_map/all_to_all | solution.py:373
  41.1 1.8 %shard_map.60 = f32[512,2,256]{2,1,0:T(2,128)} custom-call(bf16[8,272,128]{2,1,0:T(8,128)(2,1)S(1)} %all_to_all.5.lines_ref), custom_call_target="tpu_custom_call" | custom-call | flops 1000 | bytes 1000 | tf_op jit(solution)/shard_map/pallas_call | solution.py:375
Async XLA Ops:
  0.0 12.8 %copy-start = (bf16[32,2,8192]{2,1,0:T(2,128)(2,1)S(1)}, bf16[32,2,8192]{2,1,0:T(2,128)(2,1)}, u32[]{:S(2)}) copy-start(bf16[32,2,8192]{2,1,0:T(2,128)(2,1)} %raw_ref.5) | copy-start | bytes 3145732
  0.0 10.4 %copy-start.3 = (s32[4,8]{1,0:T(4,128)S(1)}, s32[4,8]{1,0:T(4,128)}, u32[]{:S(2)}) copy-start(s32[4,8]{1,0:T(4,128)} %index_ref.1) | copy-start | bytes 388
  0.0 10.5 %copy-start.1 = (bf16[8,2,512]{2,1,0:T(2,128)(2,1)S(1)}, bf16[8,2,512]{2,1,0:T(2,128)(2,1)}, u32[]{:S(2)}) copy-start(bf16[8,2,512]{2,1,0:T(2,128)(2,1)} %refs_ref.1) | copy-start | bytes 49156
  0.0 10.5 %copy-start.2 = (bf16[2,1024]{1,0:T(2,128)(2,1)S(1)}, bf16[2,1024]{1,0:T(2,128)(2,1)}, u32[]{:S(2)}) copy-start(bf16[2,1024]{1,0:T(2,128)(2,1)} %chirp_ref.1) | copy-start | bytes 12292
  2.5 10.4 %collective-permute-start = (bf16[32,2,4096]{2,1,0:T(2,128)(2,1)}, bf16[32,2,4096]{2,1,0:T(2,128)(2,1)S(1)}, u32[]{:S(2)}, u32[]{:S(2)}) collective-permute-start(bf16[32,2,4096]{2,1,0:T(2,128)(2,1)} %get-tuple-element.15), channel_id=1, source_target_pairs={{1,3},{5,7},{9,11},{13,15},{17,19},{21,23},{25,27},{29,31}} | collective-permute-start | bytes 1572872 | tf_op jit(solution)/shard_map/ppermute | solution.py:338
  8.5 9.9 %collective-permute-start.1 = (bf16[41,64,128]{2,1,0:T(8,128)(2,1)}, bf16[41,64,128]{2,1,0:T(8,128)(2,1)S(1)}, u32[]{:S(2)}, u32[]{:S(2)}) collective-permute-start(bf16[41,64,128]{2,1,0:T(8,128)(2,1)} %get-tuple-element.16), channel_id=1, source_target_pairs={{0,1},{1,2},{2,3},{4,5},{5,6},{6,7},{8,9},{9,10},{10,11},{12,13},{... | collective-permute-start | bytes 2015240 | tf_op jit(solution)/shard_map/ppermute | solution.py:346

commit v7 on v6

--- a/solution.py
+++ b/solution.py
@@ -25,14 +25,6 @@
     shape = target.shape[1:]
     for t in range(tiles):
         target[first + t] = source[:, :, t * LANES : (t + 1) * LANES].reshape(shape)
-
-
-def copy_all(sems, *pairs):
-    copies = [pltpu.make_async_copy(*pair, sems.at[at]) for at, pair in enumerate(pairs)]
-    for copy in copies:
-        copy.start()
-    for copy in copies:
-        copy.wait()
 
 
 def far_kernel(raw_ref, far_ref, turn_ref, held, in_sems, out_sems):
@@ -132,66 +124,63 @@
     lax.fori_loop(0, rows_ref.shape[0], fill, 0)
 
 
-def arrange_kernel(turn_in_ref, window_ref, raw_ref, far_ref, out_ref, natural, sems):
-    span = natural.shape[2] // LANES
-    tail = out_ref.shape[0] - span
+def arrange_kernel(turn_in_ref, window_ref, raw_ref, far_ref, out_ref, ahead_ref):
+    span = out_ref.shape[0]
+    ahead = ahead_ref.shape[0]
+    tail = 16 + ahead
     half = far_ref.shape[2] // LANES
     offset = window_ref[0] // LANES + turn_in_ref[0]
     sub_index = lax.axis_index("sa")
 
+    start = pl.multiple_of(offset * LANES, LANES)
+
     @pl.when(sub_index == 0)
     def _():
-        copy_all(sems, (raw_ref.at[:, :, pl.ds(pl.multiple_of(offset * LANES, LANES), span * LANES)], natural))
-        retile(natural, out_ref, 0, span)
+        retile(raw_ref.at[:, :, pl.ds(start, span * LANES)], out_ref, 0, span)
 
     @pl.when(sub_index == 1)
     def _():
-        part = natural.at[:, :, pl.ds(0, tail * LANES)]
-        copy_all(sems, (raw_ref.at[:, :, pl.ds(0, tail * LANES)], part))
-        retile(natural, out_ref, span, tail)
+        retile(raw_ref, out_ref, 0, tail)
 
     @pl.when(sub_index == 3)
     def _():
-        part = natural.at[:, :, pl.ds(0, half * LANES)]
-        copy_all(sems, (far_ref, part))
-        retile(natural, out_ref, 0, half)
-
-
-def compress_kernel(window_ref, arranged_ref, near_ref, taps_ref, rows_ref, out_ref, held, made, sems):
-    span, rows, _ = near_ref.shape
+        retile(far_ref.at[:, :, pl.ds(start, ahead * LANES)], ahead_ref, 0, ahead)
+        retile(far_ref, out_ref, 0, half)
+
+
+def compress_kernel(window_ref, arranged_ref, near_ref, ahead_ref, taps_ref, rows_ref, out_ref, held):
+    half, rows, _ = near_ref.shape
     targets, _, _ = out_ref.shape
-    tail = held.shape[0] - span
+    span = arranged_ref.shape[0]
+    tail = held.shape[0] - half
     group = 8
     tap_tiles = taps_ref.shape[0] // LANES
-    half = span - tap_tiles + 1
     per_target = half // targets
-    offset = window_ref[0] // LANES
     sub_index = lax.axis_index("sa")
 
-    def both(at, count):
-        return arranged_ref.at[pl.ds(at, count)], held.at[pl.ds(at, count)]
-
     @pl.when(sub_index == 0)
     def _():
-        copy_all(sems, both(0, span))
+        held[:span] = arranged_ref[...]
 
     @pl.when(sub_index == 1)
     def _():
-        copy_all(sems, both(span, tail), (near_ref, held.at[pl.ds(0, span)]))
+        held[:half] = near_ref[...]
+        held[half:] = arranged_ref[:tail]
 
     @pl.when(sub_index == 2)
     def _():
-        copy_all(sems, (near_ref, held.at[pl.ds(0, span)]))
+        held[:half] = near_ref[...]
+        held[half:span] = ahead_ref[...]
 
     @pl.when(sub_index == 3)
     def _():
-        copy_all(sems, both(0, half), (near_ref.at[pl.ds(0, tail)], held.at[pl.ds(half, tail)]))
-
-    base = jnp.where(sub_index == 1, span - half + offset, jnp.where(sub_index == 3, offset, 0))
+        held[:half] = arranged_ref[:half]
+        held[half:] = near_ref[:tail]
+
+    base = jnp.where(lax.rem(sub_index, 2) == 1, window_ref[0] // LANES, 0)
     even = lax.rem(lax.broadcasted_iota(jnp.int32, (1, 8, LANES), 1), 2) == 0
     if out_ref.shape[1] > per_target * rows:
-        made[:, per_target * rows :] = rows_ref[...]
-    copies = []
+        out_ref[:, per_target * rows :] = rows_ref[...]
     for step in range(half // group):
         blocks = [
             held[pl.ds(base + group * step + t, group)].reshape(group * rows, LANES) for t in range(tap_tiles)
@@ -201,12 +190,9 @@
         crossed = product[:, LANES:].reshape(-1, 8, LANES)
         total = straight + jnp.where(even, pltpu.roll(crossed, 7, 1), -pltpu.roll(crossed, 1, 1))
         count = group // per_target
-        into = pl.ds(step * count, count)
-        made[into, : per_target * rows] = total.astype(BF).reshape(count, per_target * rows, LANES)
-        copies.append(pltpu.make_async_copy(made.at[into], out_ref.at[into], sems.at[step]))
-        copies[-1].start()
-    for copy in copies:
-        copy.wait()
+        out_ref[pl.ds(step * count, count), : per_target * rows] = total.astype(BF).reshape(
+            count, per_target * rows, LANES
+        )
 
 
 def azimuth_kernel(lines_ref, out_ref, columns_held, taps, made, sems):
@@ -321,13 +307,11 @@
     span = half + tap_tiles - 1
 
     rows = 2 * pulses
-    tail = 16 + tap_tiles - 1
     token = jax.ShapeDtypeStruct((1,), jnp.int32)
     shape = jax.ShapeDtypeStruct
     dma = pltpu.SemaphoreType.DMA
 
     short = bin_count % LANES == 0 and total_pulses == L // 2
-    natural = pltpu.VMEM((pulses, 2, span * LANES), BF)
     far, turn = call(
         far_kernel,
         (shape((pulses, 2, half * LANES), BF), token),
@@ -338,9 +322,9 @@
     far = lax.ppermute(far, "sa", [(1, 3)])
     near, turn = call(
         near_kernel,
-        (shape((span, rows, LANES), BF), token),
+        (shape((half, rows, LANES), BF), token),
         "ssaas",
-        [natural, pltpu.VMEM((span, rows, LANES), BF), dma((4,)), dma((4,))],
+        [pltpu.VMEM((pulses, 2, half * LANES), BF), pltpu.VMEM((half, rows, LANES), BF), dma((4,)), dma((4,))],
         60,
     )(turn, window_start, raw_echo)
     near = lax.ppermute(near, "sa", [(0, 1), (1, 2), (2, 3)])
@@ -349,18 +333,22 @@
         (shape((tap_tiles * LANES, 2 * LANES), BF), shape((pulse_devices, 16, LANES), BF), token),
         "sssvvvvs",
     )(turn, window_start, migration_index, chirp_replica, azimuth_refs)
-    (arranged,) = call(
-        arrange_kernel, (shape((span + tail, rows, LANES), BF),), "ssaav", [natural, dma((1,))], flops=10**10
+    arranged, ahead = call(
+        arrange_kernel,
+        (shape((span, rows, LANES), BF), shape((span - half, rows, LANES), BF)),
+        "ssvvvv",
+        flops=10**10,
     )(turn, window_start, raw_echo, far)
+    ahead = lax.ppermute(ahead, "sa", [(3, 2)])
 
     targets, extra = (pulse_devices, 16) if short else (half // 8, 0)
     made = (targets, half // targets * rows + extra, LANES)
     (compressed,) = call(
         compress_kernel,
         (shape(made, BF),),
-        "saavva",
-        [pltpu.VMEM((span + tail, rows, LANES), BF), pltpu.VMEM(made, BF), dma((half // 8,))],
-    )(window_start, arranged, near, taps, own_rows)
+        "svvvvvv",
+        [pltpu.VMEM((span + 16, rows, LANES), BF)],
+    )(window_start, arranged, near, ahead, taps, own_rows)
 
     if not short:
         kept = compressed.reshape(half, pulses, 2, LANES).transpose(0, 3, 2, 1)

time: 43.1 us -> 40.9 us (0.949)
  Pallas kernels: 15.1 us -> 12 us
  blocking collectives: 18.2 us -> 20.5 us
  waiting for transfers between devices: 4.68 us -> 2.52 us
  starting transfers between devices: 4.15 us -> 4.8 us
    pallas_call x3, Pallas kernels: 8.57 us -> 5.56 us  [the longest x1 3.1 us: on_device(): call(near_kernel, (shape((half, rows, LANES), BF), token), 'ssaas', [pltp...]
    all_to_all x1, blocking collectives: 18.2 us -> 20.5 us  [on_device(): lax.all_to_all(compressed, 'pa', split_axis=0, concat_axis=0, tiled=True)]
    ppermute x1, waiting for transfers between devices: 4.68 us -> 2.52 us  [on_device(): near = lax.ppermute(near, 'sa', [(0, 1), (1, 2), (2, 3)])]
    ppermute x0 -> x1, starting transfers between devices: none -> 0.67 us  [on_device(): ahead = lax.ppermute(ahead, 'sa', [(3, 2)])]
  transfers between devices with their start and end apart: 2 -> 3, of which waited for: 1 -> 1; matrix products, arithmetic and copies ran while one was open for 0% -> 0% of each run, Pallas kernels for 15% -> 15%
where the time goes in v7:
time: 40.9 us; the launch traced here: 40.6 us
  blocking collectives  20.5 us (50%)
  Pallas kernels  12 us (29%)
  starting transfers between devices  4.8 us (12%)
  waiting for transfers between devices  2.52 us (6%)
  between operations  0.78 us (2%)
    all_to_all x1, blocking collectives, on_device(): lax.all_to_all(compressed, 'pa', split_axis=0, concat_axis=0, tiled=True)  20.5 us
    pallas_call x1, Pallas kernels, on_device(): call(near_kernel, (shape((half, rows, LANES), BF), token), 'ssaas', [pltp...  3.1 us
    ppermute x1, waiting for transfers between devices, on_device(): near = lax.ppermute(near, 'sa', [(0, 1), (1, 2), (2, 3)])  2.52 us
    pallas_call x1, Pallas kernels, on_device(): call(far_kernel, (shape((pulses, 2, half * LANES), BF), token), 'aas', [p...  2.43 us
    pallas_call x1, Pallas kernels, on_device(): call(prep_kernel, (shape((tap_tiles * LANES, 2 * LANES), BF), shape((puls...  2.29 us
    ppermute x1, starting transfers between devices, on_device(): far = lax.ppermute(far, 'sa', [(1, 3)])  2.21 us
    ppermute x1, starting transfers between devices, on_device(): near = lax.ppermute(near, 'sa', [(0, 1), (1, 2), (2, 3)])  1.92 us
    pallas_call x1, Pallas kernels, on_device(): call(azimuth_kernel, (shape((bin_count, 2, total_pulses), F32),), 'va', [...  1.76 us
  transfers between devices with their start and end apart: 3, of which 1 were waited for; matrix products, arithmetic and copies ran while one was open for 0% of the time, Pallas kernels for 15%

profile of v7, /device:TPU:1, one launch (start us, length us, event | category | flops | bytes accessed | tf_op | source)
XLA Modules:
  0.0 40.6 jit_solution(13643298212238525175)
XLA Ops:
  0.0 0.0 copy-start
  0.0 2.4 %shard_map.55 = (bf16[32,2,4096]{2,1,0:T(2,128)(2,1)}, s32[1]{0:T(128)}) custom-call(bf16[32,2,8192]{2,1,0:T(2,128)(2,1)} %raw_ref.5), custom_call_target="tpu_custom_call" | custom-call | flops 1000 | bytes 1000 | tf_op jit(solution)/shard_map/pallas_call | solution.py:315
  2.4 2.2 %collective-permute-start = (bf16[32,2,4096]{2,1,0:T(2,128)(2,1)}, bf16[32,2,4096]{2,1,0:T(2,128)(2,1)S(1)}, u32[]{:S(2)}, u32[]{:S(2)}) collective-permute-start(bf16[32,2,4096]{2,1,0:T(2,128)(2,1)} %get-tuple-element.17), channel_id=1, source_target_pairs={{1,3},{5,7},{9,11},{13,15},{17,19},{21,23},{25,27},{29,31}} | collective-permute-start | bytes 1572872 | tf_op jit(solution)/shard_map/ppermute | solution.py:322
  5.3 0.0 copy-start.1
  5.3 0.0 copy-start.2
  5.3 3.1 %shard_map.56 = (bf16[32,64,128]{2,1,0:T(8,128)(2,1)}, s32[1]{0:T(128)}) custom-call(s32[1]{0:T(128)} %get-tuple-element.14.turn_in_ref, s32[1]{0:T(128)S(6)} %copy.6.window_ref, bf16[32,2,8192]{2,1,0:T(2,128)(2,1)} %raw_ref.5), custom_call_target="tpu_custom_call" | custom-call | flops 1000 | bytes 1000 | tf_op jit(solution)/shard_map/pallas_call | solution.py:323
  8.4 0.0 copy-start.3
  8.5 1.9 %collective-permute-start.1 = (bf16[32,64,128]{2,1,0:T(8,128)(2,1)}, bf16[32,64,128]{2,1,0:T(8,128)(2,1)S(1)}, u32[]{:S(2)}, u32[]{:S(2)}) collective-permute-start(bf16[32,64,128]{2,1,0:T(8,128)(2,1)} %get-tuple-element.19), channel_id=1, source_target_pairs={{0,1},{1,2},{2,3},{4,5},{5,6},{6,7},{8,9},{9,10},{10,11},{12,13},{... | collective-permute-start | bytes 1572872 | tf_op jit(solution)/shard_map/ppermute | solution.py:330
  10.4 0.0 copy-done.1
  10.4 0.0 copy-done.2
  10.4 0.0 copy-done.3
  10.4 2.3 %shard_map.57 = (bf16[1280,256]{1,0:T(8,128)(2,1)S(1)}, bf16[8,16,128]{2,1,0:T(8,128)(2,1)S(1)}, s32[1]{0:T(128)}) custom-call(s32[1]{0:T(128)} %get-tuple-element.15.turn_in_ref, s32[1]{0:T(128)S(6)} %copy.6.window_ref, s32[4,8]{1,0:T(4,128)S(1)} %copy-done.3, bf16[2,1024]{1,0:T(2,128)(2,1)S(1)} %copy-done.2, bf16[8,2,512]{2,1,0:T(2,128)(2,1)S(1)} %copy-done.1), custom_call_target="tpu_custom_call" | custom-call | flops 1000 | bytes 1000 | tf_op jit(solution)/shard_map/pallas_call | solution.py:331
  12.7 0.0 collective-permute-done.far_ref
  12.7 0.0 copy-done
  12.7 0.9 %shard_map.58 = (bf16[41,64,128]{2,1,0:T(8,128)(2,1)S(1)}, bf16[9,64,128]{2,1,0:T(8,128)(2,1)S(1)}) custom-call(s32[1]{0:T(128)} %get-tuple-element.16.turn_in_ref, s32[1]{0:T(128)S(6)} %copy.6.window_ref, bf16[32,2,8192]{2,1,0:T(2,128)(2,1)S(1)} %copy-done, bf16[32,2,4096]{2,1,0:T(2,128)(2,1)S(1)} %collective-permute-done.far_ref), custom_call_target="tpu_custom_call" | custom-call | flops 10000000000 | bytes 1000 | tf_op jit(solution)/shard_map/pallas_call | solution.py:336
  13.6 0.7 %collective-permute-start.2 = (bf16[9,64,128]{2,1,0:T(8,128)(2,1)S(1)}, bf16[9,64,128]{2,1,0:T(8,128)(2,1)S(1)}, u32[]{:S(2)}, u32[]{:S(2)}) collective-permute-start(bf16[9,64,128]{2,1,0:T(8,128)(2,1)S(1)} %get-tuple-element.20), channel_id=1, source_target_pairs={{3,2},{7,6},{11,10},{15,14},{19,18},{23,22},{27,26},{31,30}} | collective-permute-start | bytes 442376 | tf_op jit(solution)/shard_map/ppermute | solution.py:342
  14.3 2.5 %collective-permute-done.1.near_ref = bf16[32,64,128]{2,1,0:T(8,128)(2,1)S(1)} collective-permute-done((bf16[32,64,128]{2,1,0:T(8,128)(2,1)}, bf16[32,64,128]{2,1,0:T(8,128)(2,1)S(1)}, u32[]{:S(2)}, u32[]{:S(2)}) %collective-permute-start.1) | collective-permute-done | bytes 524320 | tf_op jit(solution)/shard_map/ppermute | solution.py:330
  16.8 0.0 collective-permute-done.2.ahead_ref
  16.8 1.6 %shard_map.59 = bf16[8,272,128]{2,1,0:T(8,128)(2,1)S(1)} custom-call(s32[1]{0:T(128)S(6)} %copy.6.window_ref, bf16[41,64,128]{2,1,0:T(8,128)(2,1)S(1)} %get-tuple-element.18.arranged_ref, bf16[32,64,128]{2,1,0:T(8,128)(2,1)S(1)} %collective-permute-done.1.near_ref, bf16[9,64,128]{2,1,0:T(8,128)(2,1)S(1)} %collective-permute-done.2.ahead_ref, ...), custom_call_target="tpu_custom_call" | custom-call | flops 1000 | bytes 1000 | tf_op jit(solution)/shard_map/pallas_call | solution.py:346
  18.4 20.5 %all_to_all.5.lines_ref = bf16[8,272,128]{2,1,0:T(8,128)(2,1)S(1)} all-to-all(bf16[8,272,128]{2,1,0:T(8,128)(2,1)S(1)} %shard_map.59), channel_id=1, replica_groups=mesh['pa'=8,'sa'=4] {'pa'}, dimensions={0} | all-to-all | bytes 1114112 | tf_op jit(solution)/shard_map/all_to_all | solution.py:361
  38.9 1.8 %shard_map.60 = f32[512,2,256]{2,1,0:T(2,128)} custom-call(bf16[8,272,128]{2,1,0:T(8,128)(2,1)S(1)} %all_to_all.5.lines_ref), custom_call_target="tpu_custom_call" | custom-call | flops 1000 | bytes 1000 | tf_op jit(solution)/shard_map/pallas_call | solution.py:363
Async XLA Ops:
  0.0 12.7 %copy-start = (bf16[32,2,8192]{2,1,0:T(2,128)(2,1)S(1)}, bf16[32,2,8192]{2,1,0:T(2,128)(2,1)}, u32[]{:S(2)}) copy-start(bf16[32,2,8192]{2,1,0:T(2,128)(2,1)} %raw_ref.5) | copy-start | bytes 3145732
  2.4 10.3 %collective-permute-start = (bf16[32,2,4096]{2,1,0:T(2,128)(2,1)}, bf16[32,2,4096]{2,1,0:T(2,128)(2,1)S(1)}, u32[]{:S(2)}, u32[]{:S(2)}) collective-permute-start(bf16[32,2,4096]{2,1,0:T(2,128)(2,1)} %get-tuple-element.17), channel_id=1, source_target_pairs={{1,3},{5,7},{9,11},{13,15},{17,19},{21,23},{25,27},{29,31}} | collective-permute-start | bytes 1572872 | tf_op jit(solution)/shard_map/ppermute | solution.py:322
  5.3 5.1 %copy-start.1 = (bf16[8,2,512]{2,1,0:T(2,128)(2,1)S(1)}, bf16[8,2,512]{2,1,0:T(2,128)(2,1)}, u32[]{:S(2)}) copy-start(bf16[8,2,512]{2,1,0:T(2,128)(2,1)} %refs_ref.1) | copy-start | bytes 49156
  5.3 5.1 %copy-start.2 = (bf16[2,1024]{1,0:T(2,128)(2,1)S(1)}, bf16[2,1024]{1,0:T(2,128)(2,1)}, u32[]{:S(2)}) copy-start(bf16[2,1024]{1,0:T(2,128)(2,1)} %chirp_ref.1) | copy-start | bytes 12292
  8.4 2.0 %copy-start.3 = (s32[4,8]{1,0:T(4,128)S(1)}, s32[4,8]{1,0:T(4,128)}, u32[]{:S(2)}) copy-start(s32[4,8]{1,0:T(4,128)} %index_ref.1) | copy-start | bytes 388
  8.5 8.3 %collective-permute-start.1 = (bf16[32,64,128]{2,1,0:T(8,128)(2,1)}, bf16[32,64,128]{2,1,0:T(8,128)(2,1)S(1)}, u32[]{:S(2)}, u32[]{:S(2)}) collective-permute-start(bf16[32,64,128]{2,1,0:T(8,128)(2,1)} %get-tuple-element.19), channel_id=1, source_target_pairs={{0,1},{1,2},{2,3},{4,5},{5,6},{6,7},{8,9},{9,10},{10,11},{12,13},{... | collective-permute-start | bytes 1572872 | tf_op jit(solution)/shard_map/ppermute | solution.py:330
  13.6 3.2 %collective-permute-start.2 = (bf16[9,64,128]{2,1,0:T(8,128)(2,1)S(1)}, bf16[9,64,128]{2,1,0:T(8,128)(2,1)S(1)}, u32[]{:S(2)}, u32[]{:S(2)}) collective-permute-start(bf16[9,64,128]{2,1,0:T(8,128)(2,1)S(1)} %get-tuple-element.20), channel_id=1, source_target_pairs={{3,2},{7,6},{11,10},{15,14},{19,18},{23,22},{27,26},{31,30}} | collective-permute-start | bytes 442376 | tf_op jit(solution)/shard_map/ppermute | solution.py:342

commit v8 on v7

--- a/solution.py
+++ b/solution.py
@@ -27,70 +27,46 @@
         target[first + t] = source[:, :, t * LANES : (t + 1) * LANES].reshape(shape)
 
 
-def far_kernel(raw_ref, far_ref, turn_ref, held, in_sems, out_sems):
-    turn_ref[0] = 0
-    pulses, _, width = far_ref.shape
-    pieces = in_sems.shape[0]
-    each = pulses // pieces
+def far_kernel(raw_ref, far_ref, turn_ref):
+    turn_ref[...] = jnp.zeros_like(turn_ref)
+    width = far_ref.shape[2]
 
     @pl.when(lax.axis_index("sa") == 1)
     def _():
-        moves = []
-        for at in range(pieces):
-            own = pl.ds(at * each, each)
-            source = raw_ref.at[own, :, pl.ds(raw_ref.shape[2] - width, width)]
-            moves.append(
-                (
-                    pltpu.make_async_copy(source, held.at[own], in_sems.at[at]),
-                    pltpu.make_async_copy(held.at[own], far_ref.at[own], out_sems.at[at]),
-                )
-            )
-        for inward, _ in moves:
-            inward.start()
-        for inward, outward in moves:
-            inward.wait()
-            outward.start()
-        for _, outward in moves:
-            outward.wait()
-
-
-def near_kernel(turn_in_ref, window_ref, raw_ref, near_ref, turn_ref, natural, held, in_sems, out_sems):
-    turn_ref[0] = turn_in_ref[0]
+        far_ref[...] = raw_ref[:, :, raw_ref.shape[2] - width :]
+
+
+def near_kernel(turn_in_ref, window_ref, raw_ref, near_ref, turn_ref):
+    turn_ref[...] = turn_in_ref[...]
     span = near_ref.shape[0]
     tiles = raw_ref.shape[2] // LANES
     sub_index = lax.axis_index("sa")
     offset = window_ref[0] // LANES
     first = jnp.where(sub_index == 0, tiles - span, jnp.where(sub_index == 1, offset, 0))
-    pieces = in_sems.shape[0]
-    cuts = [span * at // pieces for at in range(pieces + 1)]
 
     @pl.when(sub_index < 3)
     def _():
-        moves = []
-        for at in range(pieces):
-            count = cuts[at + 1] - cuts[at]
-            start = pl.multiple_of((first + cuts[at]) * LANES, LANES)
-            part = natural.at[:, :, pl.ds(cuts[at] * LANES, count * LANES)]
-            own = pl.ds(cuts[at], count)
-            moves.append(
-                (
-                    pltpu.make_async_copy(raw_ref.at[:, :, pl.ds(start, count * LANES)], part, in_sems.at[at]),
-                    pltpu.make_async_copy(held.at[own], near_ref.at[own], out_sems.at[at]),
-                    (part, held, cuts[at], count),
-                )
-            )
-        for inward, _, _ in moves:
-            inward.start()
-        for inward, outward, order in moves:
-            inward.wait()
-            retile(*order)
-            outward.start()
-        for _, outward, _ in moves:
-            outward.wait()
-
-
-def prep_kernel(turn_in_ref, window_ref, index_ref, chirp_ref, refs_ref, taps_ref, rows_ref, turn_ref):
-    turn_ref[0] = turn_in_ref[0]
+        start = pl.multiple_of(first * LANES, LANES)
+        retile(raw_ref.at[:, :, pl.ds(start, span * LANES)], near_ref, 0, span)
+
+
+def rows_kernel(turn_in_ref, index_ref, refs_ref, rows_ref, turn_ref):
+    turn_ref[...] = turn_in_ref[...]
+    own = refs_ref.shape[0]
+    groups, targets = index_ref.shape
+    first_row = lax.axis_index("pa") * own
+    mine = lax.broadcasted_iota(jnp.int32, (groups, targets), 0) == lax.axis_index("sa")
+    wanted = jnp.sum(jnp.where(mine, index_ref[...], 0), axis=0, keepdims=True)
+    row_id = lax.broadcasted_iota(jnp.int32, (own, targets), 0) + first_row
+    picks = (row_id == jnp.broadcast_to(wanted, (own, targets))).astype(F32)
+    for part in range(2):
+        rows_ref[:, part, :] = lax.dot_general(
+            picks, refs_ref[:, part, :].astype(F32), (((0,), (0,)), ((), ())), preferred_element_type=F32
+        ).astype(BF)
+
+
+def range_taps_kernel(turn_in_ref, window_ref, chirp_ref, taps_ref, turn_ref):
+    turn_ref[...] = turn_in_ref[...]
     taps = chirp_ref.shape[1]
     blocks = taps_ref.shape[0] // LANES
     width = blocks * LANES
@@ -108,20 +84,6 @@
             taps_ref[t * LANES : (t + 1) * LANES, part * LANES : (part + 1) * LANES] = skewed[
                 :, first : first + LANES
             ].astype(BF)
-    own = refs_ref.shape[0]
-    sub_index = lax.axis_index("sa")
-    first_row = lax.axis_index("pa") * own
-
-    def fill(target, carry):
-        local = index_ref[sub_index, target] - first_row
-        held = jnp.logical_and(local >= 0, local < own)
-        row = refs_ref[jnp.clip(local, 0, own - 1)].astype(F32)
-        row = jnp.where(held, row, jnp.zeros_like(row))
-        pieces = [row[part : part + 1, t * LANES : (t + 1) * LANES] for part in range(2) for t in range(L // LANES)]
-        rows_ref[target] = jnp.concatenate(pieces + [jnp.zeros((8, LANES), F32)], axis=0).astype(BF)
-        return carry
-
-    lax.fori_loop(0, rows_ref.shape[0], fill, 0)
 
 
 def arrange_kernel(turn_in_ref, window_ref, raw_ref, far_ref, out_ref, ahead_ref):
@@ -129,7 +91,7 @@
     ahead = ahead_ref.shape[0]
     tail = 16 + ahead
     half = far_ref.shape[2] // LANES
-    offset = window_ref[0] // LANES + turn_in_ref[0]
+    offset = window_ref[0] // LANES
     sub_index = lax.axis_index("sa")
 
     start = pl.multiple_of(offset * LANES, LANES)
@@ -148,7 +110,7 @@
         retile(far_ref, out_ref, 0, half)
 
 
-def compress_kernel(window_ref, arranged_ref, near_ref, ahead_ref, taps_ref, rows_ref, out_ref, held):
+def compress_kernel(window_ref, arranged_ref, near_ref, ahead_ref, taps_ref, out_ref, held):
     half, rows, _ = near_ref.shape
     targets, _, _ = out_ref.shape
     span = arranged_ref.shape[0]
@@ -179,8 +141,6 @@
 
     base = jnp.where(lax.rem(sub_index, 2) == 1, window_ref[0] // LANES, 0)
     even = lax.rem(lax.broadcasted_iota(jnp.int32, (1, 8, LANES), 1), 2) == 0
-    if out_ref.shape[1] > per_target * rows:
-        out_ref[:, per_target * rows :] = rows_ref[...]
     for step in range(half // group):
         blocks = [
             held[pl.ds(base + group * step + t, group)].reshape(group * rows, LANES) for t in range(tap_tiles)
@@ -190,23 +150,13 @@
         crossed = product[:, LANES:].reshape(-1, 8, LANES)
         total = straight + jnp.where(even, pltpu.roll(crossed, 7, 1), -pltpu.roll(crossed, 1, 1))
         count = group // per_target
-        out_ref[pl.ds(step * count, count), : per_target * rows] = total.astype(BF).reshape(
-            count, per_target * rows, LANES
-        )
-
-
-def azimuth_kernel(lines_ref, out_ref, columns_held, taps, made, sems):
-    bins, _, pulses = out_ref.shape
-    tiles = bins // LANES
-    sources = lines_ref.shape[0]
-    rows = (lines_ref.shape[1] - 16) // tiles
-    picked = jnp.sum(lines_ref[:, tiles * rows :].astype(F32), axis=0)
-    pieces = L // LANES
-    row = [
-        jnp.concatenate([picked[part * pieces + t : part * pieces + t + 1] for t in range(pieces)], axis=1)
-        for part in range(2)
-    ]
-    row = jnp.concatenate(row + [jnp.zeros((14, L), F32)], axis=0).astype(BF)
+        out_ref[pl.ds(step * count, count)] = total.astype(BF).reshape(count, per_target * rows, LANES)
+
+
+def azimuth_taps_kernel(rows_ref, taps_ref, columns_held):
+    pulses = taps_ref.shape[0] // 2
+    row = jnp.sum(rows_ref[...].astype(F32), axis=0)
+    row = jnp.concatenate([row, jnp.zeros((14, L), F32)], axis=0).astype(BF)
     moved = pltpu.roll(reversed_lanes(row), L - (pulses - 1), 1)
     parts = []
     for part in range(2):
@@ -220,11 +170,18 @@
                     :, column * LANES : (column + 1) * LANES
                 ]
     for column in range(2 * columns):
-        taps[:, column * LANES : (column + 1) * LANES] = columns_held[column].astype(BF)
+        taps_ref[:, column * LANES : (column + 1) * LANES] = columns_held[column].astype(BF)
+
+
+def azimuth_kernel(lines_ref, taps_ref, out_ref, made, sems):
+    bins, _, pulses = out_ref.shape
+    tiles = bins // LANES
+    sources = lines_ref.shape[0]
+    rows = lines_ref.shape[1] // tiles
     copies = []
     for tile in range(tiles):
         lines = lines_ref[:, tile * rows : (tile + 1) * rows].reshape(sources * rows, LANES)
-        focused = lax.dot_general(lines, taps[...], (((0,), (0,)), ((), ())), preferred_element_type=F32)
+        focused = lax.dot_general(lines, taps_ref[...], (((0,), (0,)), ((), ())), preferred_element_type=F32)
         into = pl.ds(tile * LANES, LANES)
         made[into, 0, :] = focused[:, :pulses]
         made[into, 1, :] = focused[:, pulses:]
@@ -307,70 +264,55 @@
     span = half + tap_tiles - 1
 
     rows = 2 * pulses
-    token = jax.ShapeDtypeStruct((1,), jnp.int32)
     shape = jax.ShapeDtypeStruct
-    dma = pltpu.SemaphoreType.DMA
-
+    token = shape((8, LANES), F32)
     short = bin_count % LANES == 0 and total_pulses == L // 2
-    far, turn = call(
-        far_kernel,
-        (shape((pulses, 2, half * LANES), BF), token),
-        "aas",
-        [pltpu.VMEM((pulses, 2, half * LANES), BF), dma((8,)), dma((8,))],
-        60,
-    )(raw_echo)
+
+    far, turn = call(far_kernel, (shape((pulses, 2, half * LANES), BF), token), "vvv")(raw_echo)
     far = lax.ppermute(far, "sa", [(1, 3)])
-    near, turn = call(
-        near_kernel,
-        (shape((half, rows, LANES), BF), token),
-        "ssaas",
-        [pltpu.VMEM((pulses, 2, half * LANES), BF), pltpu.VMEM((half, rows, LANES), BF), dma((4,)), dma((4,))],
-        60,
-    )(turn, window_start, raw_echo)
+    near, turn = call(near_kernel, (shape((half, rows, LANES), BF), token), "vsvvv")(turn, window_start, raw_echo)
     near = lax.ppermute(near, "sa", [(0, 1), (1, 2), (2, 3)])
-    taps, own_rows, turn = call(
-        prep_kernel,
-        (shape((tap_tiles * LANES, 2 * LANES), BF), shape((pulse_devices, 16, LANES), BF), token),
-        "sssvvvvs",
-    )(turn, window_start, migration_index, chirp_replica, azimuth_refs)
+    own_rows, turn = call(rows_kernel, (shape((pulse_devices, 2, L), BF), token), "vvvvv")(
+        turn, migration_index, azimuth_refs
+    )
+    rows_in = lax.all_to_all(own_rows, "pa", split_axis=0, concat_axis=0, tiled=True)
+    taps, turn = call(range_taps_kernel, (shape((tap_tiles * LANES, 2 * LANES), BF), token), "vsvvv")(
+        turn, window_start, chirp_replica
+    )
     arranged, ahead = call(
         arrange_kernel,
         (shape((span, rows, LANES), BF), shape((span - half, rows, LANES), BF)),
-        "ssvvvv",
+        "vsvvvv",
         flops=10**10,
     )(turn, window_start, raw_echo, far)
     ahead = lax.ppermute(ahead, "sa", [(3, 2)])
 
-    targets, extra = (pulse_devices, 16) if short else (half // 8, 0)
-    made = (targets, half // targets * rows + extra, LANES)
+    targets = pulse_devices if short else half // 8
     (compressed,) = call(
         compress_kernel,
-        (shape(made, BF),),
-        "svvvvvv",
+        (shape((targets, half // targets * rows, LANES), BF),),
+        "svvvvv",
         [pltpu.VMEM((span + 16, rows, LANES), BF)],
-    )(window_start, arranged, near, ahead, taps, own_rows)
+    )(window_start, arranged, near, ahead, taps)
 
     if not short:
         kept = compressed.reshape(half, pulses, 2, LANES).transpose(0, 3, 2, 1)
         outgoing = kept.reshape(pulse_devices, bin_count, 2, pulses)
         turned = lax.all_to_all(outgoing, "pa", split_axis=0, concat_axis=3, tiled=True)
-        rows_in = lax.all_to_all(own_rows, "pa", split_axis=0, concat_axis=0, tiled=True)
-        reference_row = jnp.sum(rows_in[:, :8].astype(F32), axis=0).astype(BF).reshape(2, L)
+        reference_row = jnp.sum(rows_in.astype(F32), axis=0).astype(BF)
         return focus_long(turned[0], reference_row)
 
     lines = lax.all_to_all(compressed, "pa", split_axis=0, concat_axis=0, tiled=True)
     width = 2 * total_pulses
+    (azimuth_taps,) = call(
+        azimuth_taps_kernel, (shape((width, width), BF),), "vv", [pltpu.VMEM((width // LANES, width, LANES), F32)]
+    )(rows_in)
     (focused,) = call(
         azimuth_kernel,
         (shape((bin_count, 2, total_pulses), F32),),
-        "va",
-        [
-            pltpu.VMEM((width // LANES, width, LANES), F32),
-            pltpu.VMEM((width, width), BF),
-            pltpu.VMEM((bin_count, 2, total_pulses), F32),
-            dma((bin_count // LANES,)),
-        ],
-    )(lines)
+        "vva",
+        [pltpu.VMEM((bin_count, 2, total_pulses), F32), pltpu.SemaphoreType.DMA((bin_count // LANES,))],
+    )(lines, azimuth_taps)
     return focused[None]
 
 

time: 40.9 us -> 43.8 us (1.071)
  the two profiles are of different devices: /device:TPU:1 before, /device:TPU:0 now
where the time goes in v8:
time: 43.8 us; the launch traced here: 43.5 us
  waiting for transfers between devices  18.7 us (43%)
  starting transfers between devices  16.5 us (38%)
  Pallas kernels  6.22 us (14%)
  local copies, waits for them, and re-layouts  1.25 us (3%)
  between operations  0.78 us (2%)
    all_to_all x1, waiting for transfers between devices, on_device(): lax.all_to_all(compressed, 'pa', split_axis=0, concat_axis=0, tiled=True)  14.5 us
    all_to_all x1, starting transfers between devices, on_device(): lax.all_to_all(own_rows, 'pa', split_axis=0, concat_axis=0, tiled=True)  5.85 us
    ppermute x1, starting transfers between devices, on_device(): near = lax.ppermute(near, 'sa', [(0, 1), (1, 2), (2, 3)])  5.67 us
    all_to_all x1, waiting for transfers between devices, on_device(): lax.all_to_all(own_rows, 'pa', split_axis=0, concat_axis=0, tiled=True)  4.17 us
    all_to_all x1, starting transfers between devices, on_device(): lax.all_to_all(compressed, 'pa', split_axis=0, concat_axis=0, tiled=True)  3.49 us
    pallas_call x1, Pallas kernels, on_device(): call(compress_kernel, (shape((targets, half // targets * rows, LANES), BF...  2.39 us
    pallas_call x1, Pallas kernels, on_device(): call(azimuth_kernel, (shape((bin_count, 2, total_pulses), F32),), 'vva',...  1.34 us
    unnamed x10, local copies, waits for them, and re-layouts  1.25 us
  transfers between devices with their start and end apart: 5, of which 2 were waited for; matrix products, arithmetic and copies ran while one was open for 0% of the time, Pallas kernels for 11%

profile of v8, /device:TPU:0, one launch (start us, length us, event | category | flops | bytes accessed | tf_op | source)
XLA Modules:
  0.0 43.5 jit_solution(7232748200844127166)
XLA Ops:
  0.0 1.2 %copy-done = bf16[32,2,8192]{2,1,0:T(2,128)(2,1)S(1)} copy-done((bf16[32,2,8192]{2,1,0:T(2,128)(2,1)S(1)}, bf16[32,2,8192]{2,1,0:T(2,128)(2,1)}, u32[]{:S(2)}) %copy-start) | copy-done | bytes 1048600
  1.2 0.8 %collective-permute-start = (bf16[32,2,4096]{2,1,0:T(2,128)(2,1)S(1)}, bf16[32,2,4096]{2,1,0:T(2,128)(2,1)S(1)}, u32[]{:S(2)}, u32[]{:S(2)}) collective-permute-start(bf16[32,2,4096]{2,1,0:T(2,128)(2,1)S(1)} %get-tuple-element.19), channel_id=1, source_target_pairs={{1,3},{5,7},{9,11},{13,15},{17,19},{21,23},{25,27},{29,31}} | collective-permute-start | bytes 1572872 | tf_op jit(solution)/shard_map/ppermute | solution.py:272
  2.7 0.0 copy-start.2
  2.7 0.3 shard_map.56
  3.0 0.0 copy-start.4
  3.0 5.7 %collective-permute-start.1 = (bf16[32,64,128]{2,1,0:T(8,128)(2,1)S(1)}, bf16[32,64,128]{2,1,0:T(8,128)(2,1)S(1)}, u32[]{:S(2)}, u32[]{:S(2)}) collective-permute-start(bf16[32,64,128]{2,1,0:T(8,128)(2,1)S(1)} %get-tuple-element.21), channel_id=1, source_target_pairs={{0,1},{1,2},{2,3},{4,5},{5,6},{6,7},{8,9},{9,10},{10,11},{12,13},{... | collective-permute-start | bytes 1572872 | tf_op jit(solution)/shard_map/ppermute | solution.py:274
  8.7 0.0 copy-done.2
  8.7 0.0 copy-done.4
  8.7 0.0 copy-start.3
  8.7 0.8 %shard_map.57 = (bf16[8,2,512]{2,1,0:T(2,128)(2,1)}, f32[8,128]{1,0:T(8,128)S(1)}) custom-call(f32[8,128]{1,0:T(8,128)S(1)} %get-tuple-element.16.turn_in_ref, s32[4,8]{1,0:T(4,128)S(1)} %copy-done.4, bf16[8,2,512]{2,1,0:T(2,128)(2,1)S(1)} %copy-done.2), custom_call_target="tpu_custom_call" | custom-call | flops 1000 | bytes 1000 | tf_op jit(solution)/shard_map/pallas_call | solution.py:275
  9.5 0.0 copy-done.3
  9.5 0.5 %shard_map.58 = (bf16[1280,256]{1,0:T(8,128)(2,1)S(1)}, f32[8,128]{1,0:T(8,128)S(1)}) custom-call(f32[8,128]{1,0:T(8,128)S(1)} %get-tuple-element.17.turn_in_ref, s32[1]{0:T(128)S(6)} %copy.6.window_ref, bf16[2,1024]{1,0:T(2,128)(2,1)S(1)} %copy-done.3), custom_call_target="tpu_custom_call" | custom-call | flops 1000 | bytes 1000 | tf_op jit(solution)/shard_map/pallas_call | solution.py:279
  10.1 0.0 collective-permute-done.far_ref
  10.1 0.4 shard_map.59
  10.5 0.7 %collective-permute-start.2 = (bf16[9,64,128]{2,1,0:T(8,128)(2,1)S(1)}, bf16[9,64,128]{2,1,0:T(8,128)(2,1)S(1)}, u32[]{:S(2)}, u32[]{:S(2)}) collective-permute-start(bf16[9,64,128]{2,1,0:T(8,128)(2,1)S(1)} %get-tuple-element.22), channel_id=1, source_target_pairs={{3,2},{7,6},{11,10},{15,14},{19,18},{23,22},{27,26},{31,30}} | collective-permute-start | bytes 442376 | tf_op jit(solution)/shard_map/ppermute | solution.py:288
  11.1 5.8 %all-to-all-start.1 = ((bf16[8,2,512]{2,1,0:T(2,128)(2,1)}), bf16[8,2,512]{2,1,0:T(2,128)(2,1)S(1)}, u32[]{:S(2)}, u32[]{:S(2)}) async-start(bf16[8,2,512]{2,1,0:T(2,128)(2,1)} %get-tuple-element.24), calls=%async_computation.1 | async-start | bytes 32768 | tf_op jit(solution)/shard_map/all_to_all | solution.py:278
  17.0 0.0 collective-permute-done.1.near_ref
  17.0 0.0 collective-permute-done.2.ahead_ref
  17.0 2.4 %shard_map.60 = bf16[8,256,128]{2,1,0:T(8,128)(2,1)} custom-call(s32[1]{0:T(128)S(6)} %copy.6.window_ref, bf16[41,64,128]{2,1,0:T(8,128)(2,1)S(1)} %get-tuple-element.20.arranged_ref, bf16[32,64,128]{2,1,0:T(8,128)(2,1)S(1)} %collective-permute-done.1.near_ref, bf16[9,64,128]{2,1,0:T(8,128)(2,1)S(1)} %collective-permute-done.2.ahead_ref, ...), custom_call_target="tpu_custom_call" | custom-call | flops 1000 | bytes 1000 | tf_op jit(solution)/shard_map/pallas_call | solution.py:291
  19.4 4.2 %all-to-all-done.1.rows_ref = bf16[8,2,512]{2,1,0:T(2,128)(2,1)S(1)} async-done(((bf16[8,2,512]{2,1,0:T(2,128)(2,1)}), bf16[8,2,512]{2,1,0:T(2,128)(2,1)S(1)}, u32[]{:S(2)}, u32[]{:S(2)}) %all-to-all-start.1) | async-done | bytes 16416 | tf_op jit(solution)/shard_map/all_to_all | solution.py:278
  23.6 3.5 %all-to-all-start = ((bf16[8,256,128]{2,1,0:T(8,128)(2,1)}), bf16[8,256,128]{2,1,0:T(8,128)(2,1)S(1)}, u32[]{:S(2)}, u32[]{:S(2)}) async-start(bf16[8,256,128]{2,1,0:T(8,128)(2,1)} %shard_map.60), calls=%async_computation | async-start | bytes 1048576 | tf_op jit(solution)/shard_map/all_to_all | solution.py:305
  27.1 0.5 %shard_map.61.taps_ref = bf16[512,512]{1,0:T(8,128)(2,1)S(1)} custom-call(bf16[8,2,512]{2,1,0:T(2,128)(2,1)S(1)} %all-to-all-done.1.rows_ref), custom_call_target="tpu_custom_call" | custom-call | flops 1000 | bytes 1000 | tf_op jit(solution)/shard_map/pallas_call | solution.py:307
  27.6 14.5 %all-to-all-done.lines_ref = bf16[8,256,128]{2,1,0:T(8,128)(2,1)S(1)} async-done(((bf16[8,256,128]{2,1,0:T(8,128)(2,1)}), bf16[8,256,128]{2,1,0:T(8,128)(2,1)S(1)}, u32[]{:S(2)}, u32[]{:S(2)}) %all-to-all-start) | async-done | bytes 524320 | tf_op jit(solution)/shard_map/all_to_all | solution.py:305
  42.1 1.3 %shard_map.62 = f32[512,2,256]{2,1,0:T(2,128)} custom-call(bf16[8,256,128]{2,1,0:T(8,128)(2,1)S(1)} %all-to-all-done.lines_ref, bf16[512,512]{1,0:T(8,128)(2,1)S(1)} %shard_map.61.taps_ref), custom_call_target="tpu_custom_call" | custom-call | flops 1000 | bytes 1000 | tf_op jit(solution)/shard_map/pallas_call | solution.py:310
  (4 shorter events, 0.0 us)
Async XLA Ops:
  0.0 1.2 %copy-start = (bf16[32,2,8192]{2,1,0:T(2,128)(2,1)S(1)}, bf16[32,2,8192]{2,1,0:T(2,128)(2,1)}, u32[]{:S(2)}) copy-start(bf16[32,2,8192]{2,1,0:T(2,128)(2,1)} %raw_ref.5) | copy-start | bytes 3145732
  1.2 8.8 %copy-start.1 = (bf16[32,2,8192]{2,1,0:T(2,128)(2,1)S(1)}, bf16[32,2,8192]{2,1,0:T(2,128)(2,1)}, u32[]{:S(2)}) copy-start(bf16[32,2,8192]{2,1,0:T(2,128)(2,1)} %raw_ref.5) | copy-start | bytes 3145732
  1.2 8.8 %collective-permute-start = (bf16[32,2,4096]{2,1,0:T(2,128)(2,1)S(1)}, bf16[32,2,4096]{2,1,0:T(2,128)(2,1)S(1)}, u32[]{:S(2)}, u32[]{:S(2)}) collective-permute-start(bf16[32,2,4096]{2,1,0:T(2,128)(2,1)S(1)} %get-tuple-element.19), channel_id=1, source_target_pairs={{1,3},{5,7},{9,11},{13,15},{17,19},{21,23},{25,27},{29,31}} | collective-permute-start | bytes 1572872 | tf_op jit(solution)/shard_map/ppermute | solution.py:272
  2.7 6.0 %copy-start.2 = (bf16[8,2,512]{2,1,0:T(2,128)(2,1)S(1)}, bf16[8,2,512]{2,1,0:T(2,128)(2,1)}, u32[]{:S(2)}) copy-start(bf16[8,2,512]{2,1,0:T(2,128)(2,1)} %refs_ref.1) | copy-start | bytes 49156
  3.0 5.7 %copy-start.4 = (s32[4,8]{1,0:T(4,128)S(1)}, s32[4,8]{1,0:T(4,128)}, u32[]{:S(2)}) copy-start(s32[4,8]{1,0:T(4,128)} %index_ref.1) | copy-start | bytes 388
  3.0 14.0 %collective-permute-start.1 = (bf16[32,64,128]{2,1,0:T(8,128)(2,1)S(1)}, bf16[32,64,128]{2,1,0:T(8,128)(2,1)S(1)}, u32[]{:S(2)}, u32[]{:S(2)}) collective-permute-start(bf16[32,64,128]{2,1,0:T(8,128)(2,1)S(1)} %get-tuple-element.21), channel_id=1, source_target_pairs={{0,1},{1,2},{2,3},{4,5},{5,6},{6,7},{8,9},{9,10},{10,11},{12,13},{... | collective-permute-start | bytes 1572872 | tf_op jit(solution)/shard_map/ppermute | solution.py:274
  8.7 0.8 %copy-start.3 = (bf16[2,1024]{1,0:T(2,128)(2,1)S(1)}, bf16[2,1024]{1,0:T(2,128)(2,1)}, u32[]{:S(2)}) copy-start(bf16[2,1024]{1,0:T(2,128)(2,1)} %chirp_ref.1) | copy-start | bytes 12292
  10.5 6.5 %collective-permute-start.2 = (bf16[9,64,128]{2,1,0:T(8,128)(2,1)S(1)}, bf16[9,64,128]{2,1,0:T(8,128)(2,1)S(1)}, u32[]{:S(2)}, u32[]{:S(2)}) collective-permute-start(bf16[9,64,128]{2,1,0:T(8,128)(2,1)S(1)} %get-tuple-element.22), channel_id=1, source_target_pairs={{3,2},{7,6},{11,10},{15,14},{19,18},{23,22},{27,26},{31,30}} | collective-permute-start | bytes 442376 | tf_op jit(solution)/shard_map/ppermute | solution.py:288
  11.1 12.4 %all-to-all-start.1 = ((bf16[8,2,512]{2,1,0:T(2,128)(2,1)}), bf16[8,2,512]{2,1,0:T(2,128)(2,1)S(1)}, u32[]{:S(2)}, u32[]{:S(2)}) async-start(bf16[8,2,512]{2,1,0:T(2,128)(2,1)} %get-tuple-element.24), calls=%async_computation.1 | async-start | bytes 32768 | tf_op jit(solution)/shard_map/all_to_all | solution.py:278
  23.6 18.6 %all-to-all-start = ((bf16[8,256,128]{2,1,0:T(8,128)(2,1)}), bf16[8,256,128]{2,1,0:T(8,128)(2,1)S(1)}, u32[]{:S(2)}, u32[]{:S(2)}) async-start(bf16[8,256,128]{2,1,0:T(8,128)(2,1)} %shard_map.60), calls=%async_computation | async-start | bytes 1048576 | tf_op jit(solution)/shard_map/all_to_all | solution.py:305

commit v9 on v8

--- a/solution.py
+++ b/solution.py
@@ -50,22 +50,7 @@
         retile(raw_ref.at[:, :, pl.ds(start, span * LANES)], near_ref, 0, span)
 
 
-def rows_kernel(turn_in_ref, index_ref, refs_ref, rows_ref, turn_ref):
-    turn_ref[...] = turn_in_ref[...]
-    own = refs_ref.shape[0]
-    groups, targets = index_ref.shape
-    first_row = lax.axis_index("pa") * own
-    mine = lax.broadcasted_iota(jnp.int32, (groups, targets), 0) == lax.axis_index("sa")
-    wanted = jnp.sum(jnp.where(mine, index_ref[...], 0), axis=0, keepdims=True)
-    row_id = lax.broadcasted_iota(jnp.int32, (own, targets), 0) + first_row
-    picks = (row_id == jnp.broadcast_to(wanted, (own, targets))).astype(F32)
-    for part in range(2):
-        rows_ref[:, part, :] = lax.dot_general(
-            picks, refs_ref[:, part, :].astype(F32), (((0,), (0,)), ((), ())), preferred_element_type=F32
-        ).astype(BF)
-
-
-def range_taps_kernel(turn_in_ref, window_ref, chirp_ref, taps_ref, turn_ref):
+def prep_kernel(turn_in_ref, window_ref, index_ref, chirp_ref, refs_ref, taps_ref, rows_ref, turn_ref):
     turn_ref[...] = turn_in_ref[...]
     taps = chirp_ref.shape[1]
     blocks = taps_ref.shape[0] // LANES
@@ -84,6 +69,21 @@
             taps_ref[t * LANES : (t + 1) * LANES, part * LANES : (part + 1) * LANES] = skewed[
                 :, first : first + LANES
             ].astype(BF)
+    own = refs_ref.shape[0]
+    groups, targets = index_ref.shape
+    first_row = lax.axis_index("pa") * own
+    mine = lax.broadcasted_iota(jnp.int32, (groups, targets), 0) == lax.axis_index("sa")
+    wanted = jnp.sum(jnp.where(mine, index_ref[...], 0), axis=0, keepdims=True)
+    row_id = lax.broadcasted_iota(jnp.int32, (own, targets), 0) + first_row
+    picks = (row_id == jnp.broadcast_to(wanted, (own, targets))).astype(F32)
+    pieces = []
+    for part in range(2):
+        picked = lax.dot_general(
+            picks, refs_ref[:, part, :].astype(F32), (((0,), (0,)), ((), ())), preferred_element_type=F32
+        )
+        pieces += [picked[:, t * LANES : (t + 1) * LANES] for t in range(L // LANES)]
+    pieces += [jnp.zeros((targets, LANES), F32)] * (rows_ref.shape[1] - len(pieces))
+    rows_ref[...] = jnp.stack(pieces, axis=1).astype(BF)
 
 
 def arrange_kernel(turn_in_ref, window_ref, raw_ref, far_ref, out_ref, ahead_ref):
@@ -110,7 +110,7 @@
         retile(far_ref, out_ref, 0, half)
 
 
-def compress_kernel(window_ref, arranged_ref, near_ref, ahead_ref, taps_ref, out_ref, held):
+def compress_kernel(window_ref, arranged_ref, near_ref, ahead_ref, taps_ref, rows_ref, out_ref, held):
     half, rows, _ = near_ref.shape
     targets, _, _ = out_ref.shape
     span = arranged_ref.shape[0]
@@ -141,6 +141,8 @@
 
     base = jnp.where(lax.rem(sub_index, 2) == 1, window_ref[0] // LANES, 0)
     even = lax.rem(lax.broadcasted_iota(jnp.int32, (1, 8, LANES), 1), 2) == 0
+    if out_ref.shape[1] > per_target * rows:
+        out_ref[:, per_target * rows :] = rows_ref[...]
     for step in range(half // group):
         blocks = [
             held[pl.ds(base + group * step + t, group)].reshape(group * rows, LANES) for t in range(tap_tiles)
@@ -150,13 +152,23 @@
         crossed = product[:, LANES:].reshape(-1, 8, LANES)
         total = straight + jnp.where(even, pltpu.roll(crossed, 7, 1), -pltpu.roll(crossed, 1, 1))
         count = group // per_target
-        out_ref[pl.ds(step * count, count)] = total.astype(BF).reshape(count, per_target * rows, LANES)
-
-
-def azimuth_taps_kernel(rows_ref, taps_ref, columns_held):
-    pulses = taps_ref.shape[0] // 2
-    row = jnp.sum(rows_ref[...].astype(F32), axis=0)
-    row = jnp.concatenate([row, jnp.zeros((14, L), F32)], axis=0).astype(BF)
+        out_ref[pl.ds(step * count, count), : per_target * rows] = total.astype(BF).reshape(
+            count, per_target * rows, LANES
+        )
+
+
+def azimuth_kernel(lines_ref, out_ref, columns_held, taps, made, sems):
+    bins, _, pulses = out_ref.shape
+    tiles = bins // LANES
+    sources = lines_ref.shape[0]
+    rows = (lines_ref.shape[1] - 16) // tiles
+    picked = jnp.sum(lines_ref[:, tiles * rows :].astype(F32), axis=0)
+    pieces = L // LANES
+    row = [
+        jnp.concatenate([picked[part * pieces + t : part * pieces + t + 1] for t in range(pieces)], axis=1)
+        for part in range(2)
+    ]
+    row = jnp.concatenate(row + [jnp.zeros((14, L), F32)], axis=0).astype(BF)
     moved = pltpu.roll(reversed_lanes(row), L - (pulses - 1), 1)
     parts = []
     for part in range(2):
@@ -170,18 +182,11 @@
                     :, column * LANES : (column + 1) * LANES
                 ]
     for column in range(2 * columns):
-        taps_ref[:, column * LANES : (column + 1) * LANES] = columns_held[column].astype(BF)
-
-
-def azimuth_kernel(lines_ref, taps_ref, out_ref, made, sems):
-    bins, _, pulses = out_ref.shape
-    tiles = bins // LANES
-    sources = lines_ref.shape[0]
-    rows = lines_ref.shape[1] // tiles
+        taps[:, column * LANES : (column + 1) * LANES] = columns_held[column].astype(BF)
     copies = []
     for tile in range(tiles):
         lines = lines_ref[:, tile * rows : (tile + 1) * rows].reshape(sources * rows, LANES)
-        focused = lax.dot_general(lines, taps_ref[...], (((0,), (0,)), ((), ())), preferred_element_type=F32)
+        focused = lax.dot_general(lines, taps[...], (((0,), (0,)), ((), ())), preferred_element_type=F32)
         into = pl.ds(tile * LANES, LANES)
         made[into, 0, :] = focused[:, :pulses]
         made[into, 1, :] = focused[:, pulses:]
@@ -272,13 +277,11 @@
     far = lax.ppermute(far, "sa", [(1, 3)])
     near, turn = call(near_kernel, (shape((half, rows, LANES), BF), token), "vsvvv")(turn, window_start, raw_echo)
     near = lax.ppermute(near, "sa", [(0, 1), (1, 2), (2, 3)])
-    own_rows, turn = call(rows_kernel, (shape((pulse_devices, 2, L), BF), token), "vvvvv")(
-        turn, migration_index, azimuth_refs
-    )
-    rows_in = lax.all_to_all(own_rows, "pa", split_axis=0, concat_axis=0, tiled=True)
-    taps, turn = call(range_taps_kernel, (shape((tap_tiles * LANES, 2 * LANES), BF), token), "vsvvv")(
-        turn, window_start, chirp_replica
-    )
+    taps, own_rows, turn = call(
+        prep_kernel,
+        (shape((tap_tiles * LANES, 2 * LANES), BF), shape((pulse_devices, 16, LANES), BF), token),
+        "vsvvvvvv",
+    )(turn, window_start, migration_index, chirp_replica, azimuth_refs)
     arranged, ahead = call(
         arrange_kernel,
         (shape((span, rows, LANES), BF), shape((span - half, rows, LANES), BF)),
@@ -287,32 +290,35 @@
     )(turn, window_start, raw_echo, far)
     ahead = lax.ppermute(ahead, "sa", [(3, 2)])
 
-    targets = pulse_devices if short else half // 8
+    targets, extra = (pulse_devices, 16) if short else (half // 8, 0)
     (compressed,) = call(
         compress_kernel,
-        (shape((targets, half // targets * rows, LANES), BF),),
-        "svvvvv",
+        (shape((targets, half // targets * rows + extra, LANES), BF),),
+        "svvvvvv",
         [pltpu.VMEM((span + 16, rows, LANES), BF)],
-    )(window_start, arranged, near, ahead, taps)
+    )(window_start, arranged, near, ahead, taps, own_rows)
 
     if not short:
         kept = compressed.reshape(half, pulses, 2, LANES).transpose(0, 3, 2, 1)
         outgoing = kept.reshape(pulse_devices, bin_count, 2, pulses)
         turned = lax.all_to_all(outgoing, "pa", split_axis=0, concat_axis=3, tiled=True)
-        reference_row = jnp.sum(rows_in.astype(F32), axis=0).astype(BF)
+        rows_in = lax.all_to_all(own_rows, "pa", split_axis=0, concat_axis=0, tiled=True)
+        reference_row = jnp.sum(rows_in[:, :8].astype(F32), axis=0).astype(BF).reshape(2, L)
         return focus_long(turned[0], reference_row)
 
     lines = lax.all_to_all(compressed, "pa", split_axis=0, concat_axis=0, tiled=True)
     width = 2 * total_pulses
-    (azimuth_taps,) = call(
-        azimuth_taps_kernel, (shape((width, width), BF),), "vv", [pltpu.VMEM((width // LANES, width, LANES), F32)]
-    )(rows_in)
     (focused,) = call(
         azimuth_kernel,
         (shape((bin_count, 2, total_pulses), F32),),
-        "vva",
-        [pltpu.VMEM((bin_count, 2, total_pulses), F32), pltpu.SemaphoreType.DMA((bin_count // LANES,))],
-    )(lines, azimuth_taps)
+        "va",
+        [
+            pltpu.VMEM((width // LANES, width, LANES), F32),
+            pltpu.VMEM((width, width), BF),
+            pltpu.VMEM((bin_count, 2, total_pulses), F32),
+            pltpu.SemaphoreType.DMA((bin_count // LANES,)),
+        ],
+    )(lines)
     return focused[None]
 
 

time: 43.8 us -> 39.1 us (0.89)
  the two profiles are of different devices: /device:TPU:0 before, /device:TPU:2 now
where the time goes in v9:
time: 39.1 us; the launch traced here: 38.9 us
  blocking collectives  18.6 us (48%)
  waiting for transfers between devices  9.89 us (25%)
  Pallas kernels  4.18 us (11%)
  starting transfers between devices  4.17 us (11%)
  local copies, waits for them, and re-layouts  1.25 us (3%)
  between operations  0.77 us (2%)
    all_to_all x1, blocking collectives, on_device(): lax.all_to_all(compressed, 'pa', split_axis=0, concat_axis=0, tiled=True)  18.6 us
    ppermute x1, waiting for transfers between devices, on_device(): near = lax.ppermute(near, 'sa', [(0, 1), (1, 2), (2, 3)])  9.88 us
    ppermute x1, starting transfers between devices, on_device(): near = lax.ppermute(near, 'sa', [(0, 1), (1, 2), (2, 3)])  2.06 us
    pallas_call x1, Pallas kernels, on_device(): call(azimuth_kernel, (shape((bin_count, 2, total_pulses), F32),), 'va', [...  1.76 us
    pallas_call x1, Pallas kernels, on_device(): call(compress_kernel, (shape((targets, half // targets * rows + extra, LA...  1.57 us
    ppermute x1, starting transfers between devices, on_device(): ahead = lax.ppermute(ahead, 'sa', [(3, 2)])  1.29 us
    unnamed x10, local copies, waits for them, and re-layouts  1.25 us
    ppermute x1, starting transfers between devices, on_device(): far = lax.ppermute(far, 'sa', [(1, 3)])  0.81 us
  transfers between devices with their start and end apart: 3, of which 1 were waited for; matrix products, arithmetic and copies ran while one was open for 0% of the time, Pallas kernels for 2%

profile of v9, /device:TPU:2, one launch (start us, length us, event | category | flops | bytes accessed | tf_op | source)
XLA Modules:
  0.0 38.9 jit_solution(10335544362791617737)
XLA Ops:
  0.0 0.0 copy-start
  0.0 1.2 %copy-done = bf16[32,2,8192]{2,1,0:T(2,128)(2,1)S(1)} copy-done((bf16[32,2,8192]{2,1,0:T(2,128)(2,1)S(1)}, bf16[32,2,8192]{2,1,0:T(2,128)(2,1)}, u32[]{:S(2)}) %copy-start) | copy-done | bytes 1048600
  1.2 0.0 copy-start.1
  1.2 0.8 %collective-permute-start = (bf16[32,2,4096]{2,1,0:T(2,128)(2,1)S(1)}, bf16[32,2,4096]{2,1,0:T(2,128)(2,1)S(1)}, u32[]{:S(2)}, u32[]{:S(2)}) collective-permute-start(bf16[32,2,4096]{2,1,0:T(2,128)(2,1)S(1)} %get-tuple-element.17), channel_id=1, source_target_pairs={{1,3},{5,7},{9,11},{13,15},{17,19},{21,23},{25,27},{29,31}} | collective-permute-start | bytes 1572872 | tf_op jit(solution)/shard_map/ppermute | solution.py:277
  2.7 0.0 copy-start.2
  2.7 0.0 copy-start.3
  2.7 0.3 shard_map.56
  3.0 0.0 copy-start.4
  3.0 2.1 %collective-permute-start.1 = (bf16[32,64,128]{2,1,0:T(8,128)(2,1)S(1)}, bf16[32,64,128]{2,1,0:T(8,128)(2,1)S(1)}, u32[]{:S(2)}, u32[]{:S(2)}) collective-permute-start(bf16[32,64,128]{2,1,0:T(8,128)(2,1)S(1)} %get-tuple-element.19), channel_id=1, source_target_pairs={{0,1},{1,2},{2,3},{4,5},{5,6},{6,7},{8,9},{9,10},{10,11},{12,13},{... | collective-permute-start | bytes 1572872 | tf_op jit(solution)/shard_map/ppermute | solution.py:279
  5.1 0.0 copy-done.2
  5.1 0.0 copy-done.3
  5.1 0.0 copy-done.4
  5.1 0.5 %shard_map.57 = (bf16[1280,256]{1,0:T(8,128)(2,1)S(1)}, bf16[8,16,128]{2,1,0:T(8,128)(2,1)S(1)}, f32[8,128]{1,0:T(8,128)S(1)}) custom-call(f32[8,128]{1,0:T(8,128)S(1)} %get-tuple-element.15.turn_in_ref, s32[1]{0:T(128)S(6)} %copy.6.window_ref, s32[4,8]{1,0:T(4,128)S(1)} %copy-done.4, bf16[2,1024]{1,0:T(2,128)(2,1)S(1)} %copy-done.3, ...), custom_call_target="tpu_custom_call" | custom-call | flops 1000 | bytes 1000 | tf_op jit(solution)/shard_map/pallas_call | solution.py:280
  5.7 0.0 collective-permute-done.far_ref
  5.7 0.0 copy-done.1
  5.7 1.3 %collective-permute-start.2 = (bf16[9,64,128]{2,1,0:T(8,128)(2,1)S(1)}, bf16[9,64,128]{2,1,0:T(8,128)(2,1)S(1)}, u32[]{:S(2)}, u32[]{:S(2)}) collective-permute-start(bf16[9,64,128]{2,1,0:T(8,128)(2,1)S(1)} %get-tuple-element.20), channel_id=1, source_target_pairs={{3,2},{7,6},{11,10},{15,14},{19,18},{23,22},{27,26},{31,30}} | collective-permute-start | bytes 442376 | tf_op jit(solution)/shard_map/ppermute | solution.py:291
  7.0 9.9 %collective-permute-done.1.near_ref = bf16[32,64,128]{2,1,0:T(8,128)(2,1)S(1)} collective-permute-done((bf16[32,64,128]{2,1,0:T(8,128)(2,1)S(1)}, bf16[32,64,128]{2,1,0:T(8,128)(2,1)S(1)}, u32[]{:S(2)}, u32[]{:S(2)}) %collective-permute-start.1) | collective-permute-done | bytes 524320 | tf_op jit(solution)/shard_map/ppermute | solution.py:279
  16.9 0.0 collective-permute-done.2.ahead_ref
  16.9 1.6 %shard_map.59 = bf16[8,272,128]{2,1,0:T(8,128)(2,1)S(1)} custom-call(s32[1]{0:T(128)S(6)} %copy.6.window_ref, bf16[41,64,128]{2,1,0:T(8,128)(2,1)S(1)} %get-tuple-element.18.arranged_ref, bf16[32,64,128]{2,1,0:T(8,128)(2,1)S(1)} %collective-permute-done.1.near_ref, bf16[9,64,128]{2,1,0:T(8,128)(2,1)S(1)} %collective-permute-done.2.ahead_ref, ...), custom_call_target="tpu_custom_call" | custom-call | flops 1000 | bytes 1000 | tf_op jit(solution)/shard_map/pallas_call | solution.py:294
  18.5 18.6 %all_to_all.5.lines_ref = bf16[8,272,128]{2,1,0:T(8,128)(2,1)S(1)} all-to-all(bf16[8,272,128]{2,1,0:T(8,128)(2,1)S(1)} %shard_map.59), channel_id=1, replica_groups=mesh['pa'=8,'sa'=4] {'pa'}, dimensions={0} | all-to-all | bytes 1114112 | tf_op jit(solution)/shard_map/all_to_all | solution.py:309
  37.1 1.8 %shard_map.60 = f32[512,2,256]{2,1,0:T(2,128)} custom-call(bf16[8,272,128]{2,1,0:T(8,128)(2,1)S(1)} %all_to_all.5.lines_ref), custom_call_target="tpu_custom_call" | custom-call | flops 1000 | bytes 1000 | tf_op jit(solution)/shard_map/pallas_call | solution.py:311
  (2 shorter events, 0.0 us)
Async XLA Ops:
  0.0 1.2 %copy-start = (bf16[32,2,8192]{2,1,0:T(2,128)(2,1)S(1)}, bf16[32,2,8192]{2,1,0:T(2,128)(2,1)}, u32[]{:S(2)}) copy-start(bf16[32,2,8192]{2,1,0:T(2,128)(2,1)} %raw_ref.5) | copy-start | bytes 3145732
  1.2 4.5 %copy-start.1 = (bf16[32,2,8192]{2,1,0:T(2,128)(2,1)S(1)}, bf16[32,2,8192]{2,1,0:T(2,128)(2,1)}, u32[]{:S(2)}) copy-start(bf16[32,2,8192]{2,1,0:T(2,128)(2,1)} %raw_ref.5) | copy-start | bytes 3145732
  1.2 4.4 %collective-permute-start = (bf16[32,2,4096]{2,1,0:T(2,128)(2,1)S(1)}, bf16[32,2,4096]{2,1,0:T(2,128)(2,1)S(1)}, u32[]{:S(2)}, u32[]{:S(2)}) collective-permute-start(bf16[32,2,4096]{2,1,0:T(2,128)(2,1)S(1)} %get-tuple-element.17), channel_id=1, source_target_pairs={{1,3},{5,7},{9,11},{13,15},{17,19},{21,23},{25,27},{29,31}} | collective-permute-start | bytes 1572872 | tf_op jit(solution)/shard_map/ppermute | solution.py:277
  2.7 2.4 %copy-start.2 = (bf16[8,2,512]{2,1,0:T(2,128)(2,1)S(1)}, bf16[8,2,512]{2,1,0:T(2,128)(2,1)}, u32[]{:S(2)}) copy-start(bf16[8,2,512]{2,1,0:T(2,128)(2,1)} %refs_ref.1) | copy-start | bytes 49156
  2.7 2.4 %copy-start.3 = (bf16[2,1024]{1,0:T(2,128)(2,1)S(1)}, bf16[2,1024]{1,0:T(2,128)(2,1)}, u32[]{:S(2)}) copy-start(bf16[2,1024]{1,0:T(2,128)(2,1)} %chirp_ref.1) | copy-start | bytes 12292
  3.0 2.1 %copy-start.4 = (s32[4,8]{1,0:T(4,128)S(1)}, s32[4,8]{1,0:T(4,128)}, u32[]{:S(2)}) copy-start(s32[4,8]{1,0:T(4,128)} %index_ref.1) | copy-start | bytes 388
  3.0 13.9 %collective-permute-start.1 = (bf16[32,64,128]{2,1,0:T(8,128)(2,1)S(1)}, bf16[32,64,128]{2,1,0:T(8,128)(2,1)S(1)}, u32[]{:S(2)}, u32[]{:S(2)}) collective-permute-start(bf16[32,64,128]{2,1,0:T(8,128)(2,1)S(1)} %get-tuple-element.19), channel_id=1, source_target_pairs={{0,1},{1,2},{2,3},{4,5},{5,6},{6,7},{8,9},{9,10},{10,11},{12,13},{... | collective-permute-start | bytes 1572872 | tf_op jit(solution)/shard_map/ppermute | solution.py:279
  5.7 11.2 %collective-permute-start.2 = (bf16[9,64,128]{2,1,0:T(8,128)(2,1)S(1)}, bf16[9,64,128]{2,1,0:T(8,128)(2,1)S(1)}, u32[]{:S(2)}, u32[]{:S(2)}) collective-permute-start(bf16[9,64,128]{2,1,0:T(8,128)(2,1)S(1)} %get-tuple-element.20), channel_id=1, source_target_pairs={{3,2},{7,6},{11,10},{15,14},{19,18},{23,22},{27,26},{31,30}} | collective-permute-start | bytes 442376 | tf_op jit(solution)/shard_map/ppermute | solution.py:291

commit v10 on v9

--- a/solution.py
+++ b/solution.py
@@ -1,3 +1,5 @@
+import functools
+
 import jax
 import jax.numpy as jnp
 from jax import lax
@@ -27,18 +29,20 @@
         target[first + t] = source[:, :, t * LANES : (t + 1) * LANES].reshape(shape)
 
 
-def far_kernel(raw_ref, far_ref, turn_ref):
-    turn_ref[...] = jnp.zeros_like(turn_ref)
-    width = far_ref.shape[2]
+def far_kernel(part, turn_in_ref, raw_ref, far_ref, turn_ref):
+    turn_ref[...] = turn_in_ref[...]
+    pulses, _, width = far_ref.shape
 
     @pl.when(lax.axis_index("sa") == 1)
     def _():
-        far_ref[...] = raw_ref[:, :, raw_ref.shape[2] - width :]
-
-
-def near_kernel(turn_in_ref, window_ref, raw_ref, near_ref, turn_ref):
+        far_ref[...] = raw_ref[part * pulses : (part + 1) * pulses, :, raw_ref.shape[2] - width :]
+
+
+def near_kernel(part, turn_in_ref, window_ref, raw_ref, near_ref, turn_ref):
     turn_ref[...] = turn_in_ref[...]
     span = near_ref.shape[0]
+    pulses = near_ref.shape[1] // 2
+    own = pl.ds(part * pulses, pulses)
     tiles = raw_ref.shape[2] // LANES
     sub_index = lax.axis_index("sa")
     offset = window_ref[0] // LANES
@@ -47,7 +51,7 @@
     @pl.when(sub_index < 3)
     def _():
         start = pl.multiple_of(first * LANES, LANES)
-        retile(raw_ref.at[:, :, pl.ds(start, span * LANES)], near_ref, 0, span)
+        retile(raw_ref.at[own, :, pl.ds(start, span * LANES)], near_ref, 0, span)
 
 
 def prep_kernel(turn_in_ref, window_ref, index_ref, chirp_ref, refs_ref, taps_ref, rows_ref, turn_ref):
@@ -86,39 +90,39 @@
     rows_ref[...] = jnp.stack(pieces, axis=1).astype(BF)
 
 
-def arrange_kernel(turn_in_ref, window_ref, raw_ref, far_ref, out_ref, ahead_ref):
+def arrange_kernel(part, turn_in_ref, window_ref, raw_ref, far_ref, out_ref, turn_ref):
+    turn_ref[...] = turn_in_ref[...]
     span = out_ref.shape[0]
-    ahead = ahead_ref.shape[0]
-    tail = 16 + ahead
     half = far_ref.shape[2] // LANES
-    offset = window_ref[0] // LANES
+    pulses = far_ref.shape[0]
+    own = pl.ds(part * pulses, pulses)
     sub_index = lax.axis_index("sa")
 
-    start = pl.multiple_of(offset * LANES, LANES)
-
     @pl.when(sub_index == 0)
     def _():
-        retile(raw_ref.at[:, :, pl.ds(start, span * LANES)], out_ref, 0, span)
+        start = pl.multiple_of(window_ref[0] // LANES * LANES, LANES)
+        retile(raw_ref.at[own, :, pl.ds(start, span * LANES)], out_ref, 0, span)
 
     @pl.when(sub_index == 1)
     def _():
-        retile(raw_ref, out_ref, 0, tail)
+        retile(raw_ref.at[own], out_ref, 0, span - half + 16)
 
     @pl.when(sub_index == 3)
     def _():
-        retile(far_ref.at[:, :, pl.ds(start, ahead * LANES)], ahead_ref, 0, ahead)
         retile(far_ref, out_ref, 0, half)
 
 
-def compress_kernel(window_ref, arranged_ref, near_ref, ahead_ref, taps_ref, rows_ref, out_ref, held):
-    half, rows, _ = near_ref.shape
+def compress_kernel(turn_in_ref, window_ref, arranged_ref, near_ref, taps_ref, rows_ref, out_ref, turn_ref, held):
+    turn_ref[...] = turn_in_ref[...]
+    span, rows, _ = near_ref.shape
     targets, _, _ = out_ref.shape
-    span = arranged_ref.shape[0]
-    tail = held.shape[0] - half
-    group = 8
+    tail = held.shape[0] - span
     tap_tiles = taps_ref.shape[0] // LANES
+    half = span - tap_tiles + 1
+    group = 16
     per_target = half // targets
     sub_index = lax.axis_index("sa")
+    offset = window_ref[0] // LANES
 
     @pl.when(sub_index == 0)
     def _():
@@ -126,20 +130,19 @@
 
     @pl.when(sub_index == 1)
     def _():
-        held[:half] = near_ref[...]
-        held[half:] = arranged_ref[:tail]
+        held[:span] = near_ref[...]
+        held[span:] = arranged_ref[:tail]
 
     @pl.when(sub_index == 2)
     def _():
-        held[:half] = near_ref[...]
-        held[half:span] = ahead_ref[...]
+        held[:span] = near_ref[...]
 
     @pl.when(sub_index == 3)
     def _():
         held[:half] = arranged_ref[:half]
-        held[half:] = near_ref[:tail]
-
-    base = jnp.where(lax.rem(sub_index, 2) == 1, window_ref[0] // LANES, 0)
+        held[half : half + tail] = near_ref[:tail]
+
+    base = jnp.where(sub_index == 1, span - half + offset, jnp.where(sub_index == 3, offset, 0))
     even = lax.rem(lax.broadcasted_iota(jnp.int32, (1, 8, LANES), 1), 2) == 0
     if out_ref.shape[1] > per_target * rows:
         out_ref[:, per_target * rows :] = rows_ref[...]
@@ -157,37 +160,63 @@
         )
 
 
-def azimuth_kernel(lines_ref, out_ref, columns_held, taps, made, sems):
-    bins, _, pulses = out_ref.shape
-    tiles = bins // LANES
-    sources = lines_ref.shape[0]
-    rows = (lines_ref.shape[1] - 16) // tiles
-    picked = jnp.sum(lines_ref[:, tiles * rows :].astype(F32), axis=0)
-    pieces = L // LANES
-    row = [
-        jnp.concatenate([picked[part * pieces + t : part * pieces + t + 1] for t in range(pieces)], axis=1)
-        for part in range(2)
-    ]
-    row = jnp.concatenate(row + [jnp.zeros((14, L), F32)], axis=0).astype(BF)
-    moved = pltpu.roll(reversed_lanes(row), L - (pulses - 1), 1)
+def azimuth_taps(row, scratch, size):
+    row = jnp.concatenate([row, jnp.zeros((14, row.shape[1]), BF)], axis=0)
+    flipped = reversed_lanes(row)
+    moved = pltpu.roll(flipped, row.shape[1] - (size - 1), 1)
     parts = []
     for part in range(2):
-        spread = jnp.broadcast_to(moved[part : part + 1], (pulses, L))
-        parts.append(pltpu.roll(spread, 0, 1, stride=1, stride_axis=0)[:, :pulses])
-    columns = pulses // LANES
+        spread = jnp.broadcast_to(moved[part : part + 1], (size, row.shape[1]))
+        parts.append(pltpu.roll(spread, 0, 1, stride=1, stride_axis=0)[:, :size])
+    columns = size // LANES
     for part, pair in enumerate(((parts[0], -parts[1]), (parts[1], parts[0]))):
         for target in range(2):
             for column in range(columns):
-                columns_held[target * columns + column, pl.ds(part, pulses, stride=2), :] = pair[target][
+                scratch[target * columns + column, pl.ds(part, size, stride=2), :] = pair[target][
                     :, column * LANES : (column + 1) * LANES
                 ]
-    for column in range(2 * columns):
-        taps[:, column * LANES : (column + 1) * LANES] = columns_held[column].astype(BF)
+
+
+def azimuth_product(lines_ref, tile, rows, taps):
+    sources = lines_ref.shape[0]
+    lines = lines_ref[:, tile * rows : (tile + 1) * rows].reshape(sources * rows, LANES)
+    return lax.dot_general(lines, taps, (((0,), (0,)), ((), ())), preferred_element_type=F32)
+
+
+def azimuth_first_kernel(lines_ref, later_ref, sum_ref, scratch, taps):
+    size = scratch.shape[1] // 2
+    sources = lines_ref.shape[0]
+    tiles = sum_ref.shape[0] // LANES
+    rows = (lines_ref.shape[1] - 16) // tiles
+    picked = jnp.sum(lines_ref[:, tiles * rows :].astype(F32), axis=0)
+    columns = L // LANES
+    row = jnp.concatenate(
+        [
+            jnp.concatenate([picked[part * columns + t : part * columns + t + 1] for t in range(columns)], axis=1)
+            for part in range(2)
+        ],
+        axis=0,
+    ).astype(BF)
+    azimuth_taps(row, scratch, size)
+    for column in range(scratch.shape[0]):
+        lanes = slice(column * LANES, (column + 1) * LANES)
+        for source in range(sources):
+            into = slice(source * rows, (source + 1) * rows)
+            start = source * 2 * rows
+            taps[into, lanes] = scratch[column, start : start + rows].astype(BF)
+            later_ref[into, lanes] = scratch[column, start + rows : start + 2 * rows].astype(BF)
+    for tile in range(tiles):
+        sum_ref[tile * LANES : (tile + 1) * LANES] = azimuth_product(lines_ref, tile, rows, taps[...])
+
+
+def azimuth_last_kernel(lines_ref, taps_ref, sum_ref, out_ref, made, sems):
+    bins, _, pulses = out_ref.shape
+    tiles = bins // LANES
+    rows = lines_ref.shape[1] // tiles
     copies = []
     for tile in range(tiles):
-        lines = lines_ref[:, tile * rows : (tile + 1) * rows].reshape(sources * rows, LANES)
-        focused = lax.dot_general(lines, taps[...], (((0,), (0,)), ((), ())), preferred_element_type=F32)
         into = pl.ds(tile * LANES, LANES)
+        focused = sum_ref[into] + azimuth_product(lines_ref, tile, rows, taps_ref[...])
         made[into, 0, :] = focused[:, :pulses]
         made[into, 1, :] = focused[:, pulses:]
         copies.append(pltpu.make_async_copy(made.at[into], out_ref.at[into], sems.at[tile]))
@@ -273,52 +302,76 @@
     token = shape((8, LANES), F32)
     short = bin_count % LANES == 0 and total_pulses == L // 2
 
-    far, turn = call(far_kernel, (shape((pulses, 2, half * LANES), BF), token), "vvv")(raw_echo)
-    far = lax.ppermute(far, "sa", [(1, 3)])
-    near, turn = call(near_kernel, (shape((half, rows, LANES), BF), token), "vsvvv")(turn, window_start, raw_echo)
-    near = lax.ppermute(near, "sa", [(0, 1), (1, 2), (2, 3)])
+    parts = 2
+    pulses_each = pulses // parts
+    rows_each = 2 * pulses_each
+    turn = jnp.zeros(token.shape, token.dtype)
+
+    def send(part, turn):
+        far, turn = call(
+            functools.partial(far_kernel, part), (shape((pulses_each, 2, half * LANES), BF), token), "vvvv"
+        )(turn, raw_echo)
+        far = lax.ppermute(far, "sa", [(1, 3)])
+        near, turn = call(
+            functools.partial(near_kernel, part), (shape((span, rows_each, LANES), BF), token), "vsvvv"
+        )(turn, window_start, raw_echo)
+        return far, lax.ppermute(near, "sa", [(0, 1), (1, 2), (2, 3)]), turn
+
+    def arrange(part, turn, far):
+        return call(
+            functools.partial(arrange_kernel, part),
+            (shape((span, rows_each, LANES), BF), token),
+            "vsvvvv",
+            flops=1000 if part else 10**10,
+        )(turn, window_start, raw_echo, far)
+
+    targets = pulse_devices if short else half // 16
+
+    def compress(part, turn, arranged, near):
+        extra = 16 if short and part == 0 else 0
+        return call(
+            compress_kernel,
+            (shape((targets, half // targets * rows_each + extra, LANES), BF), token),
+            "vsvvvvvv" if extra else "vsvvvavv",
+            [pltpu.VMEM((span + 16 + tap_tiles - 1, rows_each, LANES), BF)],
+            flops=10**12 if part else 1000,
+        )(turn, window_start, arranged, near, taps, own_rows)
+
+    far, near, turn = send(0, turn)
     taps, own_rows, turn = call(
         prep_kernel,
         (shape((tap_tiles * LANES, 2 * LANES), BF), shape((pulse_devices, 16, LANES), BF), token),
         "vsvvvvvv",
     )(turn, window_start, migration_index, chirp_replica, azimuth_refs)
-    arranged, ahead = call(
-        arrange_kernel,
-        (shape((span, rows, LANES), BF), shape((span - half, rows, LANES), BF)),
-        "vsvvvv",
-        flops=10**10,
-    )(turn, window_start, raw_echo, far)
-    ahead = lax.ppermute(ahead, "sa", [(3, 2)])
-
-    targets, extra = (pulse_devices, 16) if short else (half // 8, 0)
-    (compressed,) = call(
-        compress_kernel,
-        (shape((targets, half // targets * rows + extra, LANES), BF),),
-        "svvvvvv",
-        [pltpu.VMEM((span + 16, rows, LANES), BF)],
-    )(window_start, arranged, near, ahead, taps, own_rows)
+    arranged, turn = arrange(0, turn, far)
+    far, near_later, turn = send(1, turn)
+    first, turn = compress(0, turn, arranged, near)
+    arranged, turn = arrange(1, turn, far)
+    second, turn = compress(1, turn, arranged, near_later)
+    squeezed = [first, second]
 
     if not short:
-        kept = compressed.reshape(half, pulses, 2, LANES).transpose(0, 3, 2, 1)
+        kept = jnp.stack(squeezed).reshape(parts, half, pulses_each, 2, LANES).transpose(1, 4, 3, 0, 2)
         outgoing = kept.reshape(pulse_devices, bin_count, 2, pulses)
         turned = lax.all_to_all(outgoing, "pa", split_axis=0, concat_axis=3, tiled=True)
         rows_in = lax.all_to_all(own_rows, "pa", split_axis=0, concat_axis=0, tiled=True)
         reference_row = jnp.sum(rows_in[:, :8].astype(F32), axis=0).astype(BF).reshape(2, L)
         return focus_long(turned[0], reference_row)
 
-    lines = lax.all_to_all(compressed, "pa", split_axis=0, concat_axis=0, tiled=True)
+    lines = [lax.all_to_all(part, "pa", split_axis=0, concat_axis=0, tiled=True) for part in squeezed]
     width = 2 * total_pulses
+    later_taps, first_sum = call(
+        azimuth_first_kernel,
+        (shape((width // 2, width), BF), shape((bin_count, width), F32)),
+        "vvv",
+        [pltpu.VMEM((width // LANES, width, LANES), F32), pltpu.VMEM((width // 2, width), BF)],
+    )(lines[0])
     (focused,) = call(
-        azimuth_kernel,
+        azimuth_last_kernel,
         (shape((bin_count, 2, total_pulses), F32),),
-        "va",
-        [
-            pltpu.VMEM((width // LANES, width, LANES), F32),
-            pltpu.VMEM((width, width), BF),
-            pltpu.VMEM((bin_count, 2, total_pulses), F32),
-            pltpu.SemaphoreType.DMA((bin_count // LANES,)),
-        ],
-    )(lines)
+        "vvva",
+        [pltpu.VMEM((bin_count, 2, total_pulses), F32), pltpu.SemaphoreType.DMA((bin_count // LANES,))],
+    )(lines[1], later_taps, first_sum)
     return focused[None]
 
 

time: 39.1 us -> 45.1 us (1.15)
  the two profiles are of different devices: /device:TPU:2 before, /device:TPU:0 now
where the time goes in v10:
time: 45.1 us; the launch traced here: 44.6 us
  starting transfers between devices  19.8 us (44%)
  waiting for transfers between devices  15.3 us (34%)
  Pallas kernels  7.51 us (17%)
  local copies, waits for them, and re-layouts  1.25 us (3%)
  between operations  0.82 us (2%)
    all_to_all x2, waiting for transfers between devices, on_device(): lax.all_to_all(part, 'pa', split_axis=0, concat_axis=0, tiled=True)  15.2 us
    all_to_all x2, starting transfers between devices, on_device(): lax.all_to_all(part, 'pa', split_axis=0, concat_axis=0, tiled=True)  10.8 us
    ppermute x2, starting transfers between devices, send(): return (far, lax.ppermute(near, 'sa', [(0, 1), (1, 2), (2, 3)]), turn)  7.52 us
    pallas_call x2, Pallas kernels, compress(): call(compress_kernel, (shape((targets, half // targets * rows_each + extr...  3.21 us
    pallas_call x1, Pallas kernels, on_device(): call(azimuth_first_kernel, (shape((width // 2, width), BF), shape((bin_co...  1.65 us
    ppermute x2, starting transfers between devices, send(): far = lax.ppermute(far, 'sa', [(1, 3)])  1.47 us
    pallas_call x1, Pallas kernels, on_device(): call(azimuth_last_kernel, (shape((bin_count, 2, total_pulses), F32),), 'v...  1.31 us
    unnamed x10, local copies, waits for them, and re-layouts  1.25 us
  transfers between devices with their start and end apart: 6, of which 2 were waited for; matrix products, arithmetic and copies ran while one was open for 0% of the time, Pallas kernels for 14%

profile of v10, /device:TPU:0, one launch (start us, length us, event | category | flops | bytes accessed | tf_op | source)
XLA Modules:
  0.0 44.6 jit_solution(18146546748403476061)
XLA Ops:
  0.0 1.2 %copy-done = bf16[32,2,8192]{2,1,0:T(2,128)(2,1)S(1)} copy-done((bf16[32,2,8192]{2,1,0:T(2,128)(2,1)S(1)}, bf16[32,2,8192]{2,1,0:T(2,128)(2,1)}, u32[]{:S(2)}) %copy-start) | copy-done | bytes 1048600
  1.2 0.8 %collective-permute-start = (bf16[16,2,4096]{2,1,0:T(2,128)(2,1)S(1)}, bf16[16,2,4096]{2,1,0:T(2,128)(2,1)S(1)}, u32[]{:S(2)}, u32[]{:S(2)}) collective-permute-start(bf16[16,2,4096]{2,1,0:T(2,128)(2,1)S(1)} %get-tuple-element.28), channel_id=1, source_target_pairs={{1,3},{5,7},{9,11},{13,15},{17,19},{21,23},{25,27},{29,31}} | collective-permute-start | bytes 786440 | tf_op jit(solution)/shard_map/ppermute | solution.py:314
  2.7 0.0 copy-start.2
  2.7 0.0 copy-start.3
  2.7 0.2 shard_map.56
  2.9 0.0 copy-start.4
  2.9 5.7 %collective-permute-start.1 = (bf16[41,32,128]{2,1,0:T(8,128)(2,1)S(1)}, bf16[41,32,128]{2,1,0:T(8,128)(2,1)S(1)}, u32[]{:S(2)}, u32[]{:S(2)}) collective-permute-start(bf16[41,32,128]{2,1,0:T(8,128)(2,1)S(1)} %get-tuple-element.33), channel_id=1, source_target_pairs={{0,1},{1,2},{2,3},{4,5},{5,6},{6,7},{8,9},{9,10},{10,11},{12,13},{... | collective-permute-start | bytes 1007624 | tf_op jit(solution)/shard_map/ppermute | solution.py:318
  8.6 0.5 %shard_map.57 = (bf16[1280,256]{1,0:T(8,128)(2,1)S(1)}, bf16[8,16,128]{2,1,0:T(8,128)(2,1)S(1)}, f32[8,128]{1,0:T(8,128)S(1)}) custom-call(f32[8,128]{1,0:T(8,128)S(1)} %get-tuple-element.26.turn_in_ref, s32[1]{0:T(128)S(6)} %copy.6.window_ref, s32[4,8]{1,0:T(4,128)S(1)} %copy-done.4, bf16[2,1024]{1,0:T(2,128)(2,1)S(1)} %copy-done.3, ...), custom_call_target="tpu_custom_call" | custom-call | flops 1000 | bytes 1000 | tf_op jit(solution)/shard_map/pallas_call | solution.py:341
  9.2 0.2 shard_map.58
  9.4 0.2 shard_map.60
  9.6 1.9 %collective-permute-start.3 = (bf16[41,32,128]{2,1,0:T(8,128)(2,1)S(1)}, bf16[41,32,128]{2,1,0:T(8,128)(2,1)S(1)}, u32[]{:S(2)}, u32[]{:S(2)}) collective-permute-start(bf16[41,32,128]{2,1,0:T(8,128)(2,1)S(1)} %get-tuple-element.40), channel_id=1, source_target_pairs={{0,1},{1,2},{2,3},{4,5},{5,6},{6,7},{8,9},{9,10},{10,11},{12,13},{... | collective-permute-start | bytes 1007624 | tf_op jit(solution)/shard_map/ppermute | solution.py:318
  11.5 0.7 %collective-permute-start.2 = (bf16[16,2,4096]{2,1,0:T(2,128)(2,1)S(1)}, bf16[16,2,4096]{2,1,0:T(2,128)(2,1)S(1)}, u32[]{:S(2)}, u32[]{:S(2)}) collective-permute-start(bf16[16,2,4096]{2,1,0:T(2,128)(2,1)S(1)} %get-tuple-element.37), channel_id=1, source_target_pairs={{1,3},{5,7},{9,11},{13,15},{17,19},{21,23},{25,27},{29,31}} | collective-permute-start | bytes 786440 | tf_op jit(solution)/shard_map/ppermute | solution.py:314
  12.2 0.0 collective-permute-done.1.near_ref
  12.2 1.6 %shard_map.61 = (bf16[8,144,128]{2,1,0:T(8,128)(2,1)}, f32[8,128]{1,0:T(8,128)S(1)}) custom-call(f32[8,128]{1,0:T(8,128)S(1)} %get-tuple-element.31.turn_in_ref, s32[1]{0:T(128)S(6)} %copy.6.window_ref, bf16[41,32,128]{2,1,0:T(8,128)(2,1)S(1)} %get-tuple-element.32.arranged_ref, bf16[41,32,128]{2,1,0:T(8,128)(2,1)S(1)} %collective-permute-done.1.near_ref, ...), custom_call_target="tpu_custom_call" | custom-call | flops 1000 | bytes 1000 | tf_op jit(solution)/shard_map/pallas_call | solution.py:332
  13.8 5.8 %all-to-all-start.1 = ((bf16[8,144,128]{2,1,0:T(8,128)(2,1)}), bf16[8,144,128]{2,1,0:T(8,128)(2,1)}, u32[]{:S(2)}, u32[]{:S(2)}) async-start(bf16[8,144,128]{2,1,0:T(8,128)(2,1)} %get-tuple-element.42), calls=%async_computation.1 | async-start | bytes 589824 | tf_op jit(solution)/shard_map/all_to_all | solution.py:361
  19.6 0.0 collective-permute-done.2.far_ref
  19.6 0.2 shard_map.62
  19.8 0.0 collective-permute-done.3.near_ref
  19.8 1.6 %shard_map.63 = (bf16[8,128,128]{2,1,0:T(8,128)(2,1)}, f32[8,128]{1,0:T(8,128)}) custom-call(f32[8,128]{1,0:T(8,128)S(1)} %get-tuple-element.38.turn_in_ref, s32[1]{0:T(128)S(6)} %copy.6.window_ref, bf16[41,32,128]{2,1,0:T(8,128)(2,1)S(1)} %get-tuple-element.39.arranged_ref, bf16[41,32,128]{2,1,0:T(8,128)(2,1)S(1)} %collective-permute-done.3.near_ref, ...), custom_call_target="tpu_custom_call" | custom-call | flops 999999995904 | bytes 1000 | tf_op jit(solution)/shard_map/pallas_call | solution.py:332
  21.4 7.7 %all-to-all-done.1.lines_ref = bf16[8,144,128]{2,1,0:T(8,128)(2,1)} async-done(((bf16[8,144,128]{2,1,0:T(8,128)(2,1)}), bf16[8,144,128]{2,1,0:T(8,128)(2,1)}, u32[]{:S(2)}, u32[]{:S(2)}) %all-to-all-start.1) | async-done | bytes 294944 | tf_op jit(solution)/shard_map/all_to_all | solution.py:361
  29.1 5.0 %all-to-all-start = ((bf16[8,128,128]{2,1,0:T(8,128)(2,1)}), bf16[8,128,128]{2,1,0:T(8,128)(2,1)S(1)}, u32[]{:S(2)}, u32[]{:S(2)}) async-start(bf16[8,128,128]{2,1,0:T(8,128)(2,1)} %get-tuple-element.41), calls=%async_computation | async-start | bytes 524288 | tf_op jit(solution)/shard_map/all_to_all | solution.py:361
  34.1 1.6 %shard_map.64 = (bf16[256,512]{1,0:T(8,128)(2,1)S(1)}, f32[512,512]{1,0:T(8,128)S(1)}) custom-call(bf16[8,144,128]{2,1,0:T(8,128)(2,1)} %all-to-all-done.1.lines_ref), custom_call_target="tpu_custom_call" | custom-call | flops 1000 | bytes 1000 | tf_op jit(solution)/shard_map/pallas_call | solution.py:363
  35.8 7.5 %all-to-all-done.lines_ref = bf16[8,128,128]{2,1,0:T(8,128)(2,1)S(1)} async-done(((bf16[8,128,128]{2,1,0:T(8,128)(2,1)}), bf16[8,128,128]{2,1,0:T(8,128)(2,1)S(1)}, u32[]{:S(2)}, u32[]{:S(2)}) %all-to-all-start) | async-done | bytes 262176 | tf_op jit(solution)/shard_map/all_to_all | solution.py:361
  43.3 1.3 %shard_map.65 = f32[512,2,256]{2,1,0:T(2,128)} custom-call(bf16[8,128,128]{2,1,0:T(8,128)(2,1)S(1)} %all-to-all-done.lines_ref, bf16[256,512]{1,0:T(8,128)(2,1)S(1)} %get-tuple-element.43.taps_ref, f32[512,512]{1,0:T(8,128)S(1)} %get-tuple-element.44.sum_ref), custom_call_target="tpu_custom_call" | custom-call | flops 1000 | bytes 1000 | tf_op jit(solution)/shard_map/pallas_call | solution.py:369
  (10 shorter events, 0.0 us)
Async XLA Ops:
  0.0 1.2 %copy-start = (bf16[32,2,8192]{2,1,0:T(2,128)(2,1)S(1)}, bf16[32,2,8192]{2,1,0:T(2,128)(2,1)}, u32[]{:S(2)}) copy-start(bf16[32,2,8192]{2,1,0:T(2,128)(2,1)} %raw_ref.11) | copy-start | bytes 3145732
  1.2 1.5 %copy-start.1 = (bf16[32,2,8192]{2,1,0:T(2,128)(2,1)S(1)}, bf16[32,2,8192]{2,1,0:T(2,128)(2,1)}, u32[]{:S(2)}) copy-start(bf16[32,2,8192]{2,1,0:T(2,128)(2,1)} %raw_ref.11) | copy-start | bytes 3145732
  1.2 7.9 %collective-permute-start = (bf16[16,2,4096]{2,1,0:T(2,128)(2,1)S(1)}, bf16[16,2,4096]{2,1,0:T(2,128)(2,1)S(1)}, u32[]{:S(2)}, u32[]{:S(2)}) collective-permute-start(bf16[16,2,4096]{2,1,0:T(2,128)(2,1)S(1)} %get-tuple-element.28), channel_id=1, source_target_pairs={{1,3},{5,7},{9,11},{13,15},{17,19},{21,23},{25,27},{29,31}} | collective-permute-start | bytes 786440 | tf_op jit(solution)/shard_map/ppermute | solution.py:314
  2.7 5.9 %copy-start.2 = (bf16[8,2,512]{2,1,0:T(2,128)(2,1)S(1)}, bf16[8,2,512]{2,1,0:T(2,128)(2,1)}, u32[]{:S(2)}) copy-start(bf16[8,2,512]{2,1,0:T(2,128)(2,1)} %refs_ref.1) | copy-start | bytes 49156
  2.7 5.9 %copy-start.3 = (bf16[2,1024]{1,0:T(2,128)(2,1)S(1)}, bf16[2,1024]{1,0:T(2,128)(2,1)}, u32[]{:S(2)}) copy-start(bf16[2,1024]{1,0:T(2,128)(2,1)} %chirp_ref.1) | copy-start | bytes 12292
  2.9 5.7 %copy-start.4 = (s32[4,8]{1,0:T(4,128)S(1)}, s32[4,8]{1,0:T(4,128)}, u32[]{:S(2)}) copy-start(s32[4,8]{1,0:T(4,128)} %index_ref.1) | copy-start | bytes 388
  2.9 9.2 %collective-permute-start.1 = (bf16[41,32,128]{2,1,0:T(8,128)(2,1)S(1)}, bf16[41,32,128]{2,1,0:T(8,128)(2,1)S(1)}, u32[]{:S(2)}, u32[]{:S(2)}) collective-permute-start(bf16[41,32,128]{2,1,0:T(8,128)(2,1)S(1)} %get-tuple-element.33), channel_id=1, source_target_pairs={{0,1},{1,2},{2,3},{4,5},{5,6},{6,7},{8,9},{9,10},{10,11},{12,13},{... | collective-permute-start | bytes 1007624 | tf_op jit(solution)/shard_map/ppermute | solution.py:318
  9.6 10.2 %collective-permute-start.3 = (bf16[41,32,128]{2,1,0:T(8,128)(2,1)S(1)}, bf16[41,32,128]{2,1,0:T(8,128)(2,1)S(1)}, u32[]{:S(2)}, u32[]{:S(2)}) collective-permute-start(bf16[41,32,128]{2,1,0:T(8,128)(2,1)S(1)} %get-tuple-element.40), channel_id=1, source_target_pairs={{0,1},{1,2},{2,3},{4,5},{5,6},{6,7},{8,9},{9,10},{10,11},{12,13},{... | collective-permute-start | bytes 1007624 | tf_op jit(solution)/shard_map/ppermute | solution.py:318
  11.5 8.1 %collective-permute-start.2 = (bf16[16,2,4096]{2,1,0:T(2,128)(2,1)S(1)}, bf16[16,2,4096]{2,1,0:T(2,128)(2,1)S(1)}, u32[]{:S(2)}, u32[]{:S(2)}) collective-permute-start(bf16[16,2,4096]{2,1,0:T(2,128)(2,1)S(1)} %get-tuple-element.37), channel_id=1, source_target_pairs={{1,3},{5,7},{9,11},{13,15},{17,19},{21,23},{25,27},{29,31}} | collective-permute-start | bytes 786440 | tf_op jit(solution)/shard_map/ppermute | solution.py:314
  13.8 15.4 %all-to-all-start.1 = ((bf16[8,144,128]{2,1,0:T(8,128)(2,1)}), bf16[8,144,128]{2,1,0:T(8,128)(2,1)}, u32[]{:S(2)}, u32[]{:S(2)}) async-start(bf16[8,144,128]{2,1,0:T(8,128)(2,1)} %get-tuple-element.42), calls=%async_computation.1 | async-start | bytes 589824 | tf_op jit(solution)/shard_map/all_to_all | solution.py:361
  29.1 14.2 %all-to-all-start = ((bf16[8,128,128]{2,1,0:T(8,128)(2,1)}), bf16[8,128,128]{2,1,0:T(8,128)(2,1)S(1)}, u32[]{:S(2)}, u32[]{:S(2)}) async-start(bf16[8,128,128]{2,1,0:T(8,128)(2,1)} %get-tuple-element.41), calls=%async_computation | async-start | bytes 524288 | tf_op jit(solution)/shard_map/all_to_all | solution.py:361

commit v11 on v9

--- a/solution.py
+++ b/solution.py
@@ -27,27 +27,43 @@
         target[first + t] = source[:, :, t * LANES : (t + 1) * LANES].reshape(shape)
 
 
-def far_kernel(raw_ref, far_ref, turn_ref):
+def far_kernel(raw_ref, far_ref, turn_ref, sems):
     turn_ref[...] = jnp.zeros_like(turn_ref)
-    width = far_ref.shape[2]
+    pulses, _, width = far_ref.shape
+    pieces = sems.shape[0]
+    each = pulses // pieces
 
     @pl.when(lax.axis_index("sa") == 1)
     def _():
-        far_ref[...] = raw_ref[:, :, raw_ref.shape[2] - width :]
-
-
-def near_kernel(turn_in_ref, window_ref, raw_ref, near_ref, turn_ref):
+        copies = []
+        for at in range(pieces):
+            own = pl.ds(at * each, each)
+            source = raw_ref.at[own, :, pl.ds(raw_ref.shape[2] - width, width)]
+            copies.append(pltpu.make_async_copy(source, far_ref.at[own], sems.at[at]))
+            copies[-1].start()
+        for copy in copies:
+            copy.wait()
+
+
+def near_kernel(turn_in_ref, window_ref, raw_ref, near_ref, edge_ref, turn_ref):
     turn_ref[...] = turn_in_ref[...]
     span = near_ref.shape[0]
+    half = edge_ref.shape[0]
     tiles = raw_ref.shape[2] // LANES
     sub_index = lax.axis_index("sa")
-    offset = window_ref[0] // LANES
-    first = jnp.where(sub_index == 0, tiles - span, jnp.where(sub_index == 1, offset, 0))
-
-    @pl.when(sub_index < 3)
-    def _():
-        start = pl.multiple_of(first * LANES, LANES)
+
+    @pl.when(sub_index == 0)
+    def _():
+        retile(raw_ref.at[:, :, pl.ds((tiles - half) * LANES, half * LANES)], edge_ref, 0, half)
+
+    @pl.when(sub_index == 1)
+    def _():
+        start = pl.multiple_of(window_ref[0] // LANES * LANES, LANES)
         retile(raw_ref.at[:, :, pl.ds(start, span * LANES)], near_ref, 0, span)
+
+    @pl.when(sub_index == 2)
+    def _():
+        retile(raw_ref, edge_ref, 0, span - half + 16)
 
 
 def prep_kernel(turn_in_ref, window_ref, index_ref, chirp_ref, refs_ref, taps_ref, rows_ref, turn_ref):
@@ -86,64 +102,14 @@
     rows_ref[...] = jnp.stack(pieces, axis=1).astype(BF)
 
 
-def arrange_kernel(turn_in_ref, window_ref, raw_ref, far_ref, out_ref, ahead_ref):
-    span = out_ref.shape[0]
-    ahead = ahead_ref.shape[0]
-    tail = 16 + ahead
-    half = far_ref.shape[2] // LANES
-    offset = window_ref[0] // LANES
-    sub_index = lax.axis_index("sa")
-
-    start = pl.multiple_of(offset * LANES, LANES)
-
-    @pl.when(sub_index == 0)
-    def _():
-        retile(raw_ref.at[:, :, pl.ds(start, span * LANES)], out_ref, 0, span)
-
-    @pl.when(sub_index == 1)
-    def _():
-        retile(raw_ref, out_ref, 0, tail)
-
-    @pl.when(sub_index == 3)
-    def _():
-        retile(far_ref.at[:, :, pl.ds(start, ahead * LANES)], ahead_ref, 0, ahead)
-        retile(far_ref, out_ref, 0, half)
-
-
-def compress_kernel(window_ref, arranged_ref, near_ref, ahead_ref, taps_ref, rows_ref, out_ref, held):
-    half, rows, _ = near_ref.shape
-    targets, _, _ = out_ref.shape
-    span = arranged_ref.shape[0]
-    tail = held.shape[0] - half
+def compress(held, base, taps_ref, rows_ref, out_ref):
+    rows = held.shape[1]
+    targets = out_ref.shape[0]
+    tap_tiles = taps_ref.shape[0] // LANES
     group = 8
-    tap_tiles = taps_ref.shape[0] // LANES
-    per_target = half // targets
-    sub_index = lax.axis_index("sa")
-
-    @pl.when(sub_index == 0)
-    def _():
-        held[:span] = arranged_ref[...]
-
-    @pl.when(sub_index == 1)
-    def _():
-        held[:half] = near_ref[...]
-        held[half:] = arranged_ref[:tail]
-
-    @pl.when(sub_index == 2)
-    def _():
-        held[:half] = near_ref[...]
-        held[half:span] = ahead_ref[...]
-
-    @pl.when(sub_index == 3)
-    def _():
-        held[:half] = arranged_ref[:half]
-        held[half:] = near_ref[:tail]
-
-    base = jnp.where(lax.rem(sub_index, 2) == 1, window_ref[0] // LANES, 0)
+    per_target = max(1, (out_ref.shape[1] - rows_ref.shape[1]) // rows)
     even = lax.rem(lax.broadcasted_iota(jnp.int32, (1, 8, LANES), 1), 2) == 0
-    if out_ref.shape[1] > per_target * rows:
-        out_ref[:, per_target * rows :] = rows_ref[...]
-    for step in range(half // group):
+    for step in range(targets * per_target // group):
         blocks = [
             held[pl.ds(base + group * step + t, group)].reshape(group * rows, LANES) for t in range(tap_tiles)
         ]
@@ -155,6 +121,47 @@
         out_ref[pl.ds(step * count, count), : per_target * rows] = total.astype(BF).reshape(
             count, per_target * rows, LANES
         )
+    out_ref[:, per_target * rows :] = rows_ref[...]
+
+
+def early_kernel(turn_in_ref, window_ref, raw_ref, far_ref, edge_ref, taps_ref, rows_ref, out_ref, turn_ref, held):
+    turn_ref[...] = turn_in_ref[...]
+    half = edge_ref.shape[0]
+    tail = held.shape[0] - half
+    span = tail - 16 + half
+    sub_index = lax.axis_index("sa")
+    offset = window_ref[0] // LANES
+
+    @pl.when(sub_index == 0)
+    def _():
+        start = pl.multiple_of(offset * LANES, LANES)
+        retile(raw_ref.at[:, :, pl.ds(start, span * LANES)], held, 0, span)
+
+    @pl.when(sub_index == 1)
+    def _():
+        held[:half] = edge_ref[...]
+        retile(raw_ref, held, half, tail)
+
+    @pl.when(sub_index == 3)
+    def _():
+        retile(far_ref, held, 0, half)
+        held[half:] = edge_ref[:tail]
+
+    @pl.when(sub_index != 2)
+    def _():
+        compress(held, jnp.where(sub_index == 0, 0, offset), taps_ref, rows_ref, out_ref)
+
+
+def late_kernel(near_ref, taps_ref, rows_ref, early_ref, out_ref):
+    sub_index = lax.axis_index("sa")
+
+    @pl.when(sub_index != 2)
+    def _():
+        out_ref[...] = early_ref[...]
+
+    @pl.when(sub_index == 2)
+    def _():
+        compress(near_ref, 0, taps_ref, rows_ref, out_ref)
 
 
 def azimuth_kernel(lines_ref, out_ref, columns_held, taps, made, sems):
@@ -251,7 +258,7 @@
         in_specs=blocks[: -len(outs)],
         out_specs=tuple(blocks[-len(outs) :]),
         scratch_shapes=list(scratch),
-        compiler_params=pltpu.CompilerParams(vmem_limit_bytes=vmem * 2**20),
+        compiler_params=pltpu.CompilerParams(vmem_limit_bytes=int(vmem * 2**20)),
         cost_estimate=pl.CostEstimate(flops=flops, bytes_accessed=1000, transcendentals=0),
     )
 
@@ -273,33 +280,38 @@
     token = shape((8, LANES), F32)
     short = bin_count % LANES == 0 and total_pulses == L // 2
 
-    far, turn = call(far_kernel, (shape((pulses, 2, half * LANES), BF), token), "vvv")(raw_echo)
+    far, turn = call(
+        far_kernel,
+        (shape((pulses, 2, half * LANES), BF), token),
+        "avv",
+        [pltpu.SemaphoreType.DMA((8,))],
+        53,
+    )(raw_echo)
     far = lax.ppermute(far, "sa", [(1, 3)])
-    near, turn = call(near_kernel, (shape((half, rows, LANES), BF), token), "vsvvv")(turn, window_start, raw_echo)
-    near = lax.ppermute(near, "sa", [(0, 1), (1, 2), (2, 3)])
+    near, edge, turn = call(
+        near_kernel, (shape((span, rows, LANES), BF), shape((half, rows, LANES), BF), token), "vsvvvv"
+    )(turn, window_start, raw_echo)
+    near = lax.ppermute(near, "sa", [(1, 2)])
+    edge = lax.ppermute(edge, "sa", [(0, 1), (2, 3)])
+    targets = pulse_devices if short else half // 8
     taps, own_rows, turn = call(
         prep_kernel,
         (shape((tap_tiles * LANES, 2 * LANES), BF), shape((pulse_devices, 16, LANES), BF), token),
         "vsvvvvvv",
     )(turn, window_start, migration_index, chirp_replica, azimuth_refs)
-    arranged, ahead = call(
-        arrange_kernel,
-        (shape((span, rows, LANES), BF), shape((span - half, rows, LANES), BF)),
-        "vsvvvv",
+    extra = own_rows if short else jnp.zeros((targets, 16, LANES), BF)
+    made = shape((targets, half // targets * rows + 16, LANES), BF)
+    early, turn = call(
+        early_kernel,
+        (made, token),
+        "vsvvvvvvv",
+        [pltpu.VMEM((span + 16, rows, LANES), BF)],
         flops=10**10,
-    )(turn, window_start, raw_echo, far)
-    ahead = lax.ppermute(ahead, "sa", [(3, 2)])
-
-    targets, extra = (pulse_devices, 16) if short else (half // 8, 0)
-    (compressed,) = call(
-        compress_kernel,
-        (shape((targets, half // targets * rows + extra, LANES), BF),),
-        "svvvvvv",
-        [pltpu.VMEM((span + 16, rows, LANES), BF)],
-    )(window_start, arranged, near, ahead, taps, own_rows)
+    )(turn, window_start, raw_echo, far, edge, taps, extra)
+    (compressed,) = call(late_kernel, (made,), "vvvvv")(near, taps, extra, early)
 
     if not short:
-        kept = compressed.reshape(half, pulses, 2, LANES).transpose(0, 3, 2, 1)
+        kept = compressed[:, :-16].reshape(half, pulses, 2, LANES).transpose(0, 3, 2, 1)
         outgoing = kept.reshape(pulse_devices, bin_count, 2, pulses)
         turned = lax.all_to_all(outgoing, "pa", split_axis=0, concat_axis=3, tiled=True)
         rows_in = lax.all_to_all(own_rows, "pa", split_axis=0, concat_axis=0, tiled=True)

time: 39.1 us -> 37.9 us (0.969)
  blocking collectives: 18.6 us -> 17 us
  local copies, waits for them, and re-layouts: 1.25 us -> 0.02 us
  waiting for transfers between devices: 9.89 us -> 10.8 us
  Pallas kernels: 4.18 us -> 4.74 us
    all_to_all x1, blocking collectives: 18.6 us -> 17 us  [on_device(): lax.all_to_all(compressed, 'pa', split_axis=0, concat_axis=0, tiled=True)]
    unnamed x10 -> x8, local copies, waits for them, and re-layouts: 1.25 us -> 0.02 us
    ppermute x2, waiting for transfers between devices: 9.89 us -> 10.8 us  [the longest x1 10.8 us: on_device(): near = lax.ppermute(near, 'sa', [(1, 2)])]
    pallas_call x4, Pallas kernels: 1.9 us -> 2.46 us  [the longest x1 1.52 us: on_device(): compressed, = call(late_kernel, (made,), 'vvvvv')(near, taps, extra, early)]
  transfers between devices with their start and end apart: 3 -> 3, of which waited for: 1 -> 1; matrix products, arithmetic and copies ran while one was open for 0% -> 0% of each run, Pallas kernels for 2% -> 4%
where the time goes in v11:
time: 37.9 us; the launch traced here: 37.7 us
  blocking collectives  17 us (45%)
  waiting for transfers between devices  10.8 us (28%)
  Pallas kernels  4.74 us (13%)
  starting transfers between devices  4.27 us (11%)
  between operations  0.78 us (2%)
    all_to_all x1, blocking collectives, on_device(): lax.all_to_all(compressed, 'pa', split_axis=0, concat_axis=0, tiled=True)  17 us
    ppermute x1, waiting for transfers between devices, on_device(): near = lax.ppermute(near, 'sa', [(1, 2)])  10.8 us
    ppermute x1, starting transfers between devices, on_device(): edge = lax.ppermute(edge, 'sa', [(0, 1), (2, 3)])  2.15 us
    pallas_call x1, Pallas kernels, on_device(): call(azimuth_kernel, (shape((bin_count, 2, total_pulses), F32),), 'va', [...  1.76 us
    pallas_call x1, Pallas kernels, on_device(): compressed, = call(late_kernel, (made,), 'vvvvv')(near, taps, extra, early)  1.52 us
    ppermute x1, starting transfers between devices, on_device(): near = lax.ppermute(near, 'sa', [(1, 2)])  1.29 us
    ppermute x1, starting transfers between devices, on_device(): far = lax.ppermute(far, 'sa', [(1, 3)])  0.83 us
  transfers between devices with their start and end apart: 3, of which 1 were waited for; matrix products, arithmetic and copies ran while one was open for 0% of the time, Pallas kernels for 4%

profile of v11, /device:TPU:2, one launch (start us, length us, event | category | flops | bytes accessed | tf_op | source)
XLA Modules:
  0.0 37.7 jit_solution(275948872696949056)
XLA Ops:
  0.0 0.0 copy-start
  0.0 0.1 shard_map.55
  0.1 0.8 %collective-permute-start.1 = (bf16[32,2,4096]{2,1,0:T(2,128)(2,1)S(1)}, bf16[32,2,4096]{2,1,0:T(2,128)(2,1)S(1)}, u32[]{:S(2)}, u32[]{:S(2)}) collective-permute-start(bf16[32,2,4096]{2,1,0:T(2,128)(2,1)S(1)} %get-tuple-element.20), channel_id=1, source_target_pairs={{1,3},{5,7},{9,11},{13,15},{17,19},{21,23},{25,27},{29,31}} | collective-permute-start | bytes 1572872 | tf_op jit(solution)/shard_map/ppermute | solution.py:290
  1.6 0.0 copy-done
  1.6 0.0 copy-start.1
  1.6 0.0 copy-start.3
  1.6 0.2 shard_map.56
  1.8 0.0 copy-start.2
  1.9 2.2 %collective-permute-start.2 = (bf16[32,64,128]{2,1,0:T(8,128)(2,1)S(1)}, bf16[32,64,128]{2,1,0:T(8,128)(2,1)S(1)}, u32[]{:S(2)}, u32[]{:S(2)}) collective-permute-start(bf16[32,64,128]{2,1,0:T(8,128)(2,1)S(1)} %get-tuple-element.21), channel_id=1, source_target_pairs={{0,1},{2,3},{4,5},{6,7},{8,9},{10,11},{12,13},{14,15},{16,17},{18,... | collective-permute-start | bytes 1572872 | tf_op jit(solution)/shard_map/ppermute | solution.py:295
  4.0 1.3 %collective-permute-start = (bf16[41,64,128]{2,1,0:T(8,128)(2,1)S(1)}, bf16[41,64,128]{2,1,0:T(8,128)(2,1)S(1)}, u32[]{:S(2)}, u32[]{:S(2)}) collective-permute-start(bf16[41,64,128]{2,1,0:T(8,128)(2,1)S(1)} %get-tuple-element.15), channel_id=1, source_target_pairs={{1,2},{5,6},{9,10},{13,14},{17,18},{21,22},{25,26},{29,30}} | collective-permute-start | bytes 2015240 | tf_op jit(solution)/shard_map/ppermute | solution.py:294
  5.3 0.0 copy-done.1
  5.3 0.0 copy-done.3
  5.3 0.0 copy-done.2
  5.4 0.5 %shard_map.57 = (bf16[1280,256]{1,0:T(8,128)(2,1)S(1)}, bf16[8,16,128]{2,1,0:T(8,128)(2,1)S(1)}, f32[8,128]{1,0:T(8,128)S(1)}) custom-call(f32[8,128]{1,0:T(8,128)S(1)} %get-tuple-element.16.turn_in_ref, s32[1]{0:T(128)S(6)} %copy.6.window_ref, s32[4,8]{1,0:T(4,128)S(1)} %copy-done.3, bf16[2,1024]{1,0:T(2,128)(2,1)S(1)} %copy-done.2, ...), custom_call_target="tpu_custom_call" | custom-call | flops 1000 | bytes 1000 | tf_op jit(solution)/shard_map/pallas_call | solution.py:297
  5.9 0.0 collective-permute-done.1.far_ref
  5.9 0.0 collective-permute-done.2.edge_ref
  5.9 0.6 %shard_map.58 = (bf16[8,272,128]{2,1,0:T(8,128)(2,1)S(1)}, f32[8,128]{1,0:T(8,128)}) custom-call(f32[8,128]{1,0:T(8,128)S(1)} %get-tuple-element.19.turn_in_ref, s32[1]{0:T(128)S(6)} %copy.6.window_ref, bf16[32,2,8192]{2,1,0:T(2,128)(2,1)S(1)} %copy-done, bf16[32,2,4096]{2,1,0:T(2,128)(2,1)S(1)} %collective-permute-done.1.far_ref, ...), custom_call_target="tpu_custom_call" | custom-call | flops 10000000000 | bytes 1000 | tf_op jit(solution)/shard_map/pallas_call | solution.py:304
  6.5 10.8 %collective-permute-done.near_ref = bf16[41,64,128]{2,1,0:T(8,128)(2,1)S(1)} collective-permute-done((bf16[41,64,128]{2,1,0:T(8,128)(2,1)S(1)}, bf16[41,64,128]{2,1,0:T(8,128)(2,1)S(1)}, u32[]{:S(2)}, u32[]{:S(2)}) %collective-permute-start) | collective-permute-done | bytes 671776 | tf_op jit(solution)/shard_map/ppermute | solution.py:294
  17.4 1.5 %shard_map.59 = bf16[8,272,128]{2,1,0:T(8,128)(2,1)S(1)} custom-call(bf16[41,64,128]{2,1,0:T(8,128)(2,1)S(1)} %collective-permute-done.near_ref, bf16[1280,256]{1,0:T(8,128)(2,1)S(1)} %get-tuple-element.17.taps_ref, bf16[8,16,128]{2,1,0:T(8,128)(2,1)S(1)} %get-tuple-element.18.rows_ref, bf16[8,272,128]{2,1,0:T(8,128)(2,1)S(1)} %get-tuple-element.22.early_ref), custom_call_target="tpu_custom_call" | custom-call | flops 1000 | bytes 1000 | tf_op jit(solution)/shard_map/pallas_call | solution.py:311
  18.9 17.0 %all_to_all.5.lines_ref = bf16[8,272,128]{2,1,0:T(8,128)(2,1)S(1)} all-to-all(bf16[8,272,128]{2,1,0:T(8,128)(2,1)S(1)} %shard_map.59), channel_id=1, replica_groups=mesh['pa'=8,'sa'=4] {'pa'}, dimensions={0} | all-to-all | bytes 1114112 | tf_op jit(solution)/shard_map/all_to_all | solution.py:321
  35.9 1.8 %shard_map.60 = f32[512,2,256]{2,1,0:T(2,128)} custom-call(bf16[8,272,128]{2,1,0:T(8,128)(2,1)S(1)} %all_to_all.5.lines_ref), custom_call_target="tpu_custom_call" | custom-call | flops 1000 | bytes 1000 | tf_op jit(solution)/shard_map/pallas_call | solution.py:323
Async XLA Ops:
  0.0 1.6 %copy-start = (bf16[32,2,8192]{2,1,0:T(2,128)(2,1)S(1)}, bf16[32,2,8192]{2,1,0:T(2,128)(2,1)}, u32[]{:S(2)}) copy-start(bf16[32,2,8192]{2,1,0:T(2,128)(2,1)} %raw_ref.5) | copy-start | bytes 3145732
  0.1 5.8 %collective-permute-start.1 = (bf16[32,2,4096]{2,1,0:T(2,128)(2,1)S(1)}, bf16[32,2,4096]{2,1,0:T(2,128)(2,1)S(1)}, u32[]{:S(2)}, u32[]{:S(2)}) collective-permute-start(bf16[32,2,4096]{2,1,0:T(2,128)(2,1)S(1)} %get-tuple-element.20), channel_id=1, source_target_pairs={{1,3},{5,7},{9,11},{13,15},{17,19},{21,23},{25,27},{29,31}} | collective-permute-start | bytes 1572872 | tf_op jit(solution)/shard_map/ppermute | solution.py:290
  1.6 3.7 %copy-start.1 = (bf16[8,2,512]{2,1,0:T(2,128)(2,1)S(1)}, bf16[8,2,512]{2,1,0:T(2,128)(2,1)}, u32[]{:S(2)}) copy-start(bf16[8,2,512]{2,1,0:T(2,128)(2,1)} %refs_ref.1) | copy-start | bytes 49156
  1.6 3.7 %copy-start.3 = (s32[4,8]{1,0:T(4,128)S(1)}, s32[4,8]{1,0:T(4,128)}, u32[]{:S(2)}) copy-start(s32[4,8]{1,0:T(4,128)} %index_ref.1) | copy-start | bytes 388
  1.8 3.5 %copy-start.2 = (bf16[2,1024]{1,0:T(2,128)(2,1)S(1)}, bf16[2,1024]{1,0:T(2,128)(2,1)}, u32[]{:S(2)}) copy-start(bf16[2,1024]{1,0:T(2,128)(2,1)} %chirp_ref.1) | copy-start | bytes 12292
  1.9 4.0 %collective-permute-start.2 = (bf16[32,64,128]{2,1,0:T(8,128)(2,1)S(1)}, bf16[32,64,128]{2,1,0:T(8,128)(2,1)S(1)}, u32[]{:S(2)}, u32[]{:S(2)}) collective-permute-start(bf16[32,64,128]{2,1,0:T(8,128)(2,1)S(1)} %get-tuple-element.21), channel_id=1, source_target_pairs={{0,1},{2,3},{4,5},{6,7},{8,9},{10,11},{12,13},{14,15},{16,17},{18,... | collective-permute-start | bytes 1572872 | tf_op jit(solution)/shard_map/ppermute | solution.py:295
  4.0 13.3 %collective-permute-start = (bf16[41,64,128]{2,1,0:T(8,128)(2,1)S(1)}, bf16[41,64,128]{2,1,0:T(8,128)(2,1)S(1)}, u32[]{:S(2)}, u32[]{:S(2)}) collective-permute-start(bf16[41,64,128]{2,1,0:T(8,128)(2,1)S(1)} %get-tuple-element.15), channel_id=1, source_target_pairs={{1,2},{5,6},{9,10},{13,14},{17,18},{21,22},{25,26},{29,30}} | collective-permute-start | bytes 2015240 | tf_op jit(solution)/shard_map/ppermute | solution.py:294

commit v12 on v11

--- a/solution.py
+++ b/solution.py
@@ -27,11 +27,12 @@
         target[first + t] = source[:, :, t * LANES : (t + 1) * LANES].reshape(shape)
 
 
-def far_kernel(raw_ref, far_ref, turn_ref, sems):
+def far_kernel(raw_ref, far_ref, turn_ref, natural, sems):
     turn_ref[...] = jnp.zeros_like(turn_ref)
-    pulses, _, width = far_ref.shape
+    half, rows, _ = far_ref.shape
     pieces = sems.shape[0]
-    each = pulses // pieces
+    each = rows // 2 // pieces
+    width = half * LANES
 
     @pl.when(lax.axis_index("sa") == 1)
     def _():
@@ -39,15 +40,16 @@
         for at in range(pieces):
             own = pl.ds(at * each, each)
             source = raw_ref.at[own, :, pl.ds(raw_ref.shape[2] - width, width)]
-            copies.append(pltpu.make_async_copy(source, far_ref.at[own], sems.at[at]))
+            copies.append(pltpu.make_async_copy(source, natural.at[own], sems.at[at]))
             copies[-1].start()
-        for copy in copies:
+        for at, copy in enumerate(copies):
             copy.wait()
-
-
-def near_kernel(turn_in_ref, window_ref, raw_ref, near_ref, edge_ref, turn_ref):
+            own = pl.ds(at * each, each)
+            retile(natural.at[own], far_ref.at[:, pl.ds(at * each * 2, each * 2)], 0, half)
+
+
+def edge_kernel(turn_in_ref, raw_ref, edge_ref, turn_ref):
     turn_ref[...] = turn_in_ref[...]
-    span = near_ref.shape[0]
     half = edge_ref.shape[0]
     tiles = raw_ref.shape[2] // LANES
     sub_index = lax.axis_index("sa")
@@ -56,14 +58,9 @@
     def _():
         retile(raw_ref.at[:, :, pl.ds((tiles - half) * LANES, half * LANES)], edge_ref, 0, half)
 
-    @pl.when(sub_index == 1)
-    def _():
-        start = pl.multiple_of(window_ref[0] // LANES * LANES, LANES)
-        retile(raw_ref.at[:, :, pl.ds(start, span * LANES)], near_ref, 0, span)
-
     @pl.when(sub_index == 2)
     def _():
-        retile(raw_ref, edge_ref, 0, span - half + 16)
+        retile(raw_ref, edge_ref, 0, half)
 
 
 def prep_kernel(turn_in_ref, window_ref, index_ref, chirp_ref, refs_ref, taps_ref, rows_ref, turn_ref):
@@ -102,12 +99,12 @@
     rows_ref[...] = jnp.stack(pieces, axis=1).astype(BF)
 
 
-def compress(held, base, taps_ref, rows_ref, out_ref):
+def compress(held, base, taps_ref, out_ref):
     rows = held.shape[1]
     targets = out_ref.shape[0]
     tap_tiles = taps_ref.shape[0] // LANES
     group = 8
-    per_target = max(1, (out_ref.shape[1] - rows_ref.shape[1]) // rows)
+    per_target = out_ref.shape[1] // rows
     even = lax.rem(lax.broadcasted_iota(jnp.int32, (1, 8, LANES), 1), 2) == 0
     for step in range(targets * per_target // group):
         blocks = [
@@ -121,7 +118,17 @@
         out_ref[pl.ds(step * count, count), : per_target * rows] = total.astype(BF).reshape(
             count, per_target * rows, LANES
         )
-    out_ref[:, per_target * rows :] = rows_ref[...]
+
+
+def ahead_kernel(turn_in_ref, window_ref, raw_ref, taps_ref, out_ref, turn_ref, held):
+    turn_ref[...] = turn_in_ref[...]
+    span = held.shape[0]
+
+    @pl.when(lax.axis_index("sa") == 1)
+    def _():
+        start = pl.multiple_of(window_ref[0] // LANES * LANES, LANES)
+        retile(raw_ref.at[:, :, pl.ds(start, span * LANES)], held, 0, span)
+        compress(held, 0, taps_ref, out_ref)
 
 
 def early_kernel(turn_in_ref, window_ref, raw_ref, far_ref, edge_ref, taps_ref, rows_ref, out_ref, turn_ref, held):
@@ -144,15 +151,17 @@
 
     @pl.when(sub_index == 3)
     def _():
-        retile(far_ref, held, 0, half)
+        held[:half] = far_ref[...]
         held[half:] = edge_ref[:tail]
 
     @pl.when(sub_index != 2)
     def _():
-        compress(held, jnp.where(sub_index == 0, 0, offset), taps_ref, rows_ref, out_ref)
-
-
-def late_kernel(near_ref, taps_ref, rows_ref, early_ref, out_ref):
+        compress(held, jnp.where(sub_index == 0, 0, offset), taps_ref, out_ref)
+        out_ref[:, out_ref.shape[1] - rows_ref.shape[1] :] = rows_ref[...]
+
+
+def late_kernel(near_ref, rows_ref, early_ref, out_ref):
+    bins = near_ref.shape[1]
     sub_index = lax.axis_index("sa")
 
     @pl.when(sub_index != 2)
@@ -161,7 +170,8 @@
 
     @pl.when(sub_index == 2)
     def _():
-        compress(near_ref, 0, taps_ref, rows_ref, out_ref)
+        out_ref[:, :bins] = near_ref[...]
+        out_ref[:, bins:] = rows_ref[...]
 
 
 def azimuth_kernel(lines_ref, out_ref, columns_held, taps, made, sems):
@@ -280,27 +290,33 @@
     token = shape((8, LANES), F32)
     short = bin_count % LANES == 0 and total_pulses == L // 2
 
+    targets = pulse_devices if short else half // 8
+    slot = half // targets * rows
+
     far, turn = call(
         far_kernel,
-        (shape((pulses, 2, half * LANES), BF), token),
+        (shape((half, rows, LANES), BF), token),
         "avv",
-        [pltpu.SemaphoreType.DMA((8,))],
+        [pltpu.VMEM((pulses, 2, half * LANES), BF), pltpu.SemaphoreType.DMA((4,))],
         53,
     )(raw_echo)
     far = lax.ppermute(far, "sa", [(1, 3)])
-    near, edge, turn = call(
-        near_kernel, (shape((span, rows, LANES), BF), shape((half, rows, LANES), BF), token), "vsvvvv"
-    )(turn, window_start, raw_echo)
-    near = lax.ppermute(near, "sa", [(1, 2)])
+    edge, turn = call(edge_kernel, (shape((half, rows, LANES), BF), token), "vvvv")(turn, raw_echo)
     edge = lax.ppermute(edge, "sa", [(0, 1), (2, 3)])
-    targets = pulse_devices if short else half // 8
     taps, own_rows, turn = call(
         prep_kernel,
         (shape((tap_tiles * LANES, 2 * LANES), BF), shape((pulse_devices, 16, LANES), BF), token),
         "vsvvvvvv",
     )(turn, window_start, migration_index, chirp_replica, azimuth_refs)
+    near, turn = call(
+        ahead_kernel,
+        (shape((targets, slot, LANES), BF), token),
+        "vsvvvv",
+        [pltpu.VMEM((span, rows, LANES), BF)],
+    )(turn, window_start, raw_echo, taps)
+    near = lax.ppermute(near, "sa", [(1, 2)])
     extra = own_rows if short else jnp.zeros((targets, 16, LANES), BF)
-    made = shape((targets, half // targets * rows + 16, LANES), BF)
+    made = shape((targets, slot + 16, LANES), BF)
     early, turn = call(
         early_kernel,
         (made, token),
@@ -308,7 +324,7 @@
         [pltpu.VMEM((span + 16, rows, LANES), BF)],
         flops=10**10,
     )(turn, window_start, raw_echo, far, edge, taps, extra)
-    (compressed,) = call(late_kernel, (made,), "vvvvv")(near, taps, extra, early)
+    (compressed,) = call(late_kernel, (made,), "vvvv")(near, extra, early)
 
     if not short:
         kept = compressed[:, :-16].reshape(half, pulses, 2, LANES).transpose(0, 3, 2, 1)

time: 37.9 us -> 35.9 us (0.947)
  waiting for transfers between devices: 10.8 us -> 9.23 us
  Pallas kernels: 4.74 us -> 3.28 us
  blocking collectives: 17 us -> 18.2 us
    ppermute x1, waiting for transfers between devices: 10.8 us -> 9.23 us  [on_device(): near = lax.ppermute(near, 'sa', [(1, 2)])]
    pallas_call x3 -> x4, Pallas kernels: 1.83 us -> 0.37 us  [the longest x1 0.28 us: on_device(): call(edge_kernel, (shape((half, rows, LANES), BF), token), 'vvvv')]
    all_to_all x1, blocking collectives: 17 us -> 18.2 us  [on_device(): lax.all_to_all(compressed, 'pa', split_axis=0, concat_axis=0, tiled=True)]
where the time goes in v12:
time: 35.9 us; the launch traced here: 35.7 us
  blocking collectives  18.2 us (51%)
  waiting for transfers between devices  9.23 us (26%)
  starting transfers between devices  3.91 us (11%)
  Pallas kernels  3.28 us (9%)
  between operations  0.75 us (2%)
  local copies, waits for them, and re-layouts  0.36 us (1%)
    all_to_all x1, blocking collectives, on_device(): lax.all_to_all(compressed, 'pa', split_axis=0, concat_axis=0, tiled=True)  18.2 us
    ppermute x1, waiting for transfers between devices, on_device(): near = lax.ppermute(near, 'sa', [(1, 2)])  9.23 us
    ppermute x1, starting transfers between devices, on_device(): edge = lax.ppermute(edge, 'sa', [(0, 1), (2, 3)])  1.8 us
    pallas_call x1, Pallas kernels, on_device(): call(azimuth_kernel, (shape((bin_count, 2, total_pulses), F32),), 'va', [...  1.76 us
    ppermute x1, starting transfers between devices, on_device(): near = lax.ppermute(near, 'sa', [(1, 2)])  1.29 us
    ppermute x1, starting transfers between devices, on_device(): far = lax.ppermute(far, 'sa', [(1, 3)])  0.83 us
  transfers between devices with their start and end apart: 3, of which 1 were waited for; matrix products, arithmetic and copies ran while one was open for 0% of the time, Pallas kernels for 4%

profile of v12, /device:TPU:2, one launch (start us, length us, event | category | flops | bytes accessed | tf_op | source)
XLA Modules:
  0.0 35.7 jit_solution(6741197509935831395)
XLA Ops:
  0.0 0.0 copy-start
  0.0 0.8 %collective-permute-start.1 = (bf16[32,64,128]{2,1,0:T(8,128)(2,1)S(1)}, bf16[32,64,128]{2,1,0:T(8,128)(2,1)S(1)}, u32[]{:S(2)}, u32[]{:S(2)}) collective-permute-start(bf16[32,64,128]{2,1,0:T(8,128)(2,1)S(1)} %get-tuple-element.22), channel_id=1, source_target_pairs={{1,3},{5,7},{9,11},{13,15},{17,19},{21,23},{25,27},{29,31}} | collective-permute-start | bytes 1572872 | tf_op jit(solution)/shard_map/ppermute | solution.py:303
  0.9 0.3 copy-done
  1.2 0.0 copy-start.1
  1.2 0.0 copy-start.3
  1.2 0.3 shard_map.56
  1.5 0.0 copy-start.2
  1.5 1.8 %collective-permute-start.2 = (bf16[32,64,128]{2,1,0:T(8,128)(2,1)S(1)}, bf16[32,64,128]{2,1,0:T(8,128)(2,1)S(1)}, u32[]{:S(2)}, u32[]{:S(2)}) collective-permute-start(bf16[32,64,128]{2,1,0:T(8,128)(2,1)S(1)} %get-tuple-element.23), channel_id=1, source_target_pairs={{0,1},{2,3},{4,5},{6,7},{8,9},{10,11},{12,13},{14,15},{16,17},{18,... | collective-permute-start | bytes 1572872 | tf_op jit(solution)/shard_map/ppermute | solution.py:305
  4.0 0.0 copy-done.1
  4.0 0.0 copy-done.3
  4.0 0.0 copy-done.2
  4.0 0.5 %shard_map.57 = (bf16[1280,256]{1,0:T(8,128)(2,1)S(1)}, bf16[8,16,128]{2,1,0:T(8,128)(2,1)S(1)}, f32[8,128]{1,0:T(8,128)S(1)}) custom-call(f32[8,128]{1,0:T(8,128)S(1)} %get-tuple-element.16.turn_in_ref, s32[1]{0:T(128)S(6)} %copy.6.window_ref, s32[4,8]{1,0:T(4,128)S(1)} %copy-done.3, bf16[2,1024]{1,0:T(2,128)(2,1)S(1)} %copy-done.2, ...), custom_call_target="tpu_custom_call" | custom-call | flops 1000 | bytes 1000 | tf_op jit(solution)/shard_map/pallas_call | solution.py:306
  4.6 1.3 %collective-permute-start = (bf16[8,256,128]{2,1,0:T(8,128)(2,1)S(1)}, bf16[8,256,128]{2,1,0:T(8,128)(2,1)S(1)}, u32[]{:S(2)}, u32[]{:S(2)}) collective-permute-start(bf16[8,256,128]{2,1,0:T(8,128)(2,1)S(1)} %get-tuple-element.19), channel_id=1, source_target_pairs={{1,2},{5,6},{9,10},{13,14},{17,18},{21,22},{25,26},{29,30}} | collective-permute-start | bytes 1572872 | tf_op jit(solution)/shard_map/ppermute | solution.py:317
  5.9 0.0 collective-permute-done.1.far_ref
  5.9 0.0 collective-permute-done.2.edge_ref
  5.9 0.6 %shard_map.59 = (bf16[8,272,128]{2,1,0:T(8,128)(2,1)S(1)}, f32[8,128]{1,0:T(8,128)}) custom-call(f32[8,128]{1,0:T(8,128)S(1)} %get-tuple-element.21.turn_in_ref, s32[1]{0:T(128)S(6)} %copy.6.window_ref, bf16[32,2,8192]{2,1,0:T(2,128)(2,1)S(1)} %copy-done, bf16[32,64,128]{2,1,0:T(8,128)(2,1)S(1)} %collective-permute-done.1.far_ref, ...), custom_call_target="tpu_custom_call" | custom-call | flops 10000000000 | bytes 1000 | tf_op jit(solution)/shard_map/pallas_call | solution.py:320
  6.5 9.2 %collective-permute-done.near_ref = bf16[8,256,128]{2,1,0:T(8,128)(2,1)S(1)} collective-permute-done((bf16[8,256,128]{2,1,0:T(8,128)(2,1)S(1)}, bf16[8,256,128]{2,1,0:T(8,128)(2,1)S(1)}, u32[]{:S(2)}, u32[]{:S(2)}) %collective-permute-start) | collective-permute-done | bytes 524320 | tf_op jit(solution)/shard_map/ppermute | solution.py:317
  15.8 18.2 %all_to_all.5.lines_ref = bf16[8,272,128]{2,1,0:T(8,128)(2,1)S(1)} all-to-all(bf16[8,272,128]{2,1,0:T(8,128)(2,1)S(1)} %shard_map.60), channel_id=1, replica_groups=mesh['pa'=8,'sa'=4] {'pa'}, dimensions={0} | all-to-all | bytes 1114112 | tf_op jit(solution)/shard_map/all_to_all | solution.py:337
  33.9 1.8 %shard_map.61 = f32[512,2,256]{2,1,0:T(2,128)} custom-call(bf16[8,272,128]{2,1,0:T(8,128)(2,1)S(1)} %all_to_all.5.lines_ref), custom_call_target="tpu_custom_call" | custom-call | flops 1000 | bytes 1000 | tf_op jit(solution)/shard_map/pallas_call | solution.py:339
  (3 shorter events, 0.1 us)
Async XLA Ops:
  0.0 1.2 %copy-start = (bf16[32,2,8192]{2,1,0:T(2,128)(2,1)S(1)}, bf16[32,2,8192]{2,1,0:T(2,128)(2,1)}, u32[]{:S(2)}) copy-start(bf16[32,2,8192]{2,1,0:T(2,128)(2,1)} %raw_ref.7) | copy-start | bytes 3145732
  0.0 5.8 %collective-permute-start.1 = (bf16[32,64,128]{2,1,0:T(8,128)(2,1)S(1)}, bf16[32,64,128]{2,1,0:T(8,128)(2,1)S(1)}, u32[]{:S(2)}, u32[]{:S(2)}) collective-permute-start(bf16[32,64,128]{2,1,0:T(8,128)(2,1)S(1)} %get-tuple-element.22), channel_id=1, source_target_pairs={{1,3},{5,7},{9,11},{13,15},{17,19},{21,23},{25,27},{29,31}} | collective-permute-start | bytes 1572872 | tf_op jit(solution)/shard_map/ppermute | solution.py:303
  1.2 2.8 %copy-start.1 = (bf16[8,2,512]{2,1,0:T(2,128)(2,1)S(1)}, bf16[8,2,512]{2,1,0:T(2,128)(2,1)}, u32[]{:S(2)}) copy-start(bf16[8,2,512]{2,1,0:T(2,128)(2,1)} %refs_ref.1) | copy-start | bytes 49156
  1.2 2.8 %copy-start.3 = (s32[4,8]{1,0:T(4,128)S(1)}, s32[4,8]{1,0:T(4,128)}, u32[]{:S(2)}) copy-start(s32[4,8]{1,0:T(4,128)} %index_ref.1) | copy-start | bytes 388
  1.5 2.5 %copy-start.2 = (bf16[2,1024]{1,0:T(2,128)(2,1)S(1)}, bf16[2,1024]{1,0:T(2,128)(2,1)}, u32[]{:S(2)}) copy-start(bf16[2,1024]{1,0:T(2,128)(2,1)} %chirp_ref.1) | copy-start | bytes 12292
  1.5 4.3 %collective-permute-start.2 = (bf16[32,64,128]{2,1,0:T(8,128)(2,1)S(1)}, bf16[32,64,128]{2,1,0:T(8,128)(2,1)S(1)}, u32[]{:S(2)}, u32[]{:S(2)}) collective-permute-start(bf16[32,64,128]{2,1,0:T(8,128)(2,1)S(1)} %get-tuple-element.23), channel_id=1, source_target_pairs={{0,1},{2,3},{4,5},{6,7},{8,9},{10,11},{12,13},{14,15},{16,17},{18,... | collective-permute-start | bytes 1572872 | tf_op jit(solution)/shard_map/ppermute | solution.py:305
  4.6 11.2 %collective-permute-start = (bf16[8,256,128]{2,1,0:T(8,128)(2,1)S(1)}, bf16[8,256,128]{2,1,0:T(8,128)(2,1)S(1)}, u32[]{:S(2)}, u32[]{:S(2)}) collective-permute-start(bf16[8,256,128]{2,1,0:T(8,128)(2,1)S(1)} %get-tuple-element.19), channel_id=1, source_target_pairs={{1,2},{5,6},{9,10},{13,14},{17,18},{21,22},{25,26},{29,30}} | collective-permute-start | bytes 1572872 | tf_op jit(solution)/shard_map/ppermute | solution.py:317

commit v13 on v12

--- a/solution.py
+++ b/solution.py
@@ -131,8 +131,11 @@
         compress(held, 0, taps_ref, out_ref)
 
 
-def early_kernel(turn_in_ref, window_ref, raw_ref, far_ref, edge_ref, taps_ref, rows_ref, out_ref, turn_ref, held):
+def gate_kernel(turn_in_ref, _, turn_ref):
     turn_ref[...] = turn_in_ref[...]
+
+
+def early_kernel(turn_in_ref, window_ref, raw_ref, far_ref, edge_ref, taps_ref, out_ref, held):
     half = edge_ref.shape[0]
     tail = held.shape[0] - half
     span = tail - 16 + half
@@ -157,11 +160,10 @@
     @pl.when(sub_index != 2)
     def _():
         compress(held, jnp.where(sub_index == 0, 0, offset), taps_ref, out_ref)
-        out_ref[:, out_ref.shape[1] - rows_ref.shape[1] :] = rows_ref[...]
-
-
-def late_kernel(near_ref, rows_ref, early_ref, out_ref):
-    bins = near_ref.shape[1]
+
+
+def late_kernel(near_ref, early_ref, out_ref, turn_ref):
+    turn_ref[...] = jnp.zeros_like(turn_ref)
     sub_index = lax.axis_index("sa")
 
     @pl.when(sub_index != 2)
@@ -170,16 +172,12 @@
 
     @pl.when(sub_index == 2)
     def _():
-        out_ref[:, :bins] = near_ref[...]
-        out_ref[:, bins:] = rows_ref[...]
-
-
-def azimuth_kernel(lines_ref, out_ref, columns_held, taps, made, sems):
-    bins, _, pulses = out_ref.shape
-    tiles = bins // LANES
-    sources = lines_ref.shape[0]
-    rows = (lines_ref.shape[1] - 16) // tiles
-    picked = jnp.sum(lines_ref[:, tiles * rows :].astype(F32), axis=0)
+        out_ref[...] = near_ref[...]
+
+
+def azimuth_taps_kernel(turn_in_ref, rows_ref, taps_ref, columns_held):
+    pulses = taps_ref.shape[0] // 2
+    picked = rows_ref[0].astype(F32)
     pieces = L // LANES
     row = [
         jnp.concatenate([picked[part * pieces + t : part * pieces + t + 1] for t in range(pieces)], axis=1)
@@ -199,11 +197,18 @@
                     :, column * LANES : (column + 1) * LANES
                 ]
     for column in range(2 * columns):
-        taps[:, column * LANES : (column + 1) * LANES] = columns_held[column].astype(BF)
+        taps_ref[:, column * LANES : (column + 1) * LANES] = columns_held[column].astype(BF)
+
+
+def azimuth_kernel(lines_ref, taps_ref, out_ref, made, sems):
+    bins, _, pulses = out_ref.shape
+    tiles = bins // LANES
+    sources = lines_ref.shape[0]
+    rows = lines_ref.shape[1] // tiles
     copies = []
     for tile in range(tiles):
         lines = lines_ref[:, tile * rows : (tile + 1) * rows].reshape(sources * rows, LANES)
-        focused = lax.dot_general(lines, taps[...], (((0,), (0,)), ((), ())), preferred_element_type=F32)
+        focused = lax.dot_general(lines, taps_ref[...], (((0,), (0,)), ((), ())), preferred_element_type=F32)
         into = pl.ds(tile * LANES, LANES)
         made[into, 0, :] = focused[:, :pulses]
         made[into, 1, :] = focused[:, pulses:]
@@ -291,7 +296,7 @@
     short = bin_count % LANES == 0 and total_pulses == L // 2
 
     targets = pulse_devices if short else half // 8
-    slot = half // targets * rows
+    made = shape((targets, half // targets * rows, LANES), BF)
 
     far, turn = call(
         far_kernel,
@@ -308,45 +313,34 @@
         (shape((tap_tiles * LANES, 2 * LANES), BF), shape((pulse_devices, 16, LANES), BF), token),
         "vsvvvvvv",
     )(turn, window_start, migration_index, chirp_replica, azimuth_refs)
-    near, turn = call(
-        ahead_kernel,
-        (shape((targets, slot, LANES), BF), token),
-        "vsvvvv",
-        [pltpu.VMEM((span, rows, LANES), BF)],
-    )(turn, window_start, raw_echo, taps)
+    row_in = lax.psum_scatter(own_rows, "pa", scatter_dimension=0, tiled=True)
+    near, turn = call(ahead_kernel, (made, token), "vsvvvv", [pltpu.VMEM((span, rows, LANES), BF)])(
+        turn, window_start, raw_echo, taps
+    )
     near = lax.ppermute(near, "sa", [(1, 2)])
-    extra = own_rows if short else jnp.zeros((targets, 16, LANES), BF)
-    made = shape((targets, slot + 16, LANES), BF)
-    early, turn = call(
-        early_kernel,
-        (made, token),
-        "vsvvvvvvv",
-        [pltpu.VMEM((span + 16, rows, LANES), BF)],
-        flops=10**10,
-    )(turn, window_start, raw_echo, far, edge, taps, extra)
-    (compressed,) = call(late_kernel, (made,), "vvvv")(near, extra, early)
+    (turn,) = call(gate_kernel, (token,), "vav", flops=10**10)(turn, far)
+    (early,) = call(
+        early_kernel, (made,), "vsvvvvv", [pltpu.VMEM((span + 16, rows, LANES), BF)], flops=10**10
+    )(turn, window_start, raw_echo, far, edge, taps)
+    compressed, turn = call(late_kernel, (made, token), "vvvv")(near, early)
 
     if not short:
-        kept = compressed[:, :-16].reshape(half, pulses, 2, LANES).transpose(0, 3, 2, 1)
+        kept = compressed.reshape(half, pulses, 2, LANES).transpose(0, 3, 2, 1)
         outgoing = kept.reshape(pulse_devices, bin_count, 2, pulses)
         turned = lax.all_to_all(outgoing, "pa", split_axis=0, concat_axis=3, tiled=True)
-        rows_in = lax.all_to_all(own_rows, "pa", split_axis=0, concat_axis=0, tiled=True)
-        reference_row = jnp.sum(rows_in[:, :8].astype(F32), axis=0).astype(BF).reshape(2, L)
-        return focus_long(turned[0], reference_row)
+        return focus_long(turned[0], row_in[0, :8].reshape(2, L))
 
     lines = lax.all_to_all(compressed, "pa", split_axis=0, concat_axis=0, tiled=True)
     width = 2 * total_pulses
+    (azimuth_taps,) = call(
+        azimuth_taps_kernel, (shape((width, width), BF),), "vvv", [pltpu.VMEM((width // LANES, width, LANES), F32)]
+    )(turn, row_in)
     (focused,) = call(
         azimuth_kernel,
         (shape((bin_count, 2, total_pulses), F32),),
-        "va",
-        [
-            pltpu.VMEM((width // LANES, width, LANES), F32),
-            pltpu.VMEM((width, width), BF),
-            pltpu.VMEM((bin_count, 2, total_pulses), F32),
-            pltpu.SemaphoreType.DMA((bin_count // LANES,)),
-        ],
-    )(lines)
+        "vva",
+        [pltpu.VMEM((bin_count, 2, total_pulses), F32), pltpu.SemaphoreType.DMA((bin_count // LANES,))],
+    )(lines, azimuth_taps)
     return focused[None]
 
 

time: 35.9 us -> 99.5 us (2.77); the launches traced: 35.7 us -> 97.8 us
  waiting for transfers between devices: 9.23 us -> 68.7 us
  blocking collectives: 18.2 us -> 0 us
  between operations: 0.75 us -> 14.2 us
  starting transfers between devices: 3.91 us -> 9.77 us
    reduce_scatter x0 -> x1, waiting for transfers between devices: none -> 58.2 us  [on_device(): row_in = lax.psum_scatter(own_rows, 'pa', scatter_dimension=0, tiled=True)]
    all_to_all x1 -> x0, blocking collectives: 18.2 us -> none  [on_device(): lax.all_to_all(compressed, 'pa', split_axis=0, concat_axis=0, tiled=True)]
    all_to_all x0 -> x1, starting transfers between devices: none -> 5.83 us  [on_device(): lax.all_to_all(compressed, 'pa', split_axis=0, concat_axis=0, tiled=True)]
    pallas_call x4 -> x6, Pallas kernels: 2.43 us -> 2.71 us  [the longest x1 1.34 us: on_device(): call(azimuth_kernel, (shape((bin_count, 2, total_pulses), F32),), 'vva',...]
  transfers between devices with their start and end apart: 3 -> 5, of which waited for: 1 -> 2; matrix products, arithmetic and copies ran while one was open for 0% -> 0% of each run, Pallas kernels for 4% -> 2%
where the time goes in v13:
time: 99.5 us; the launch traced here: 97.8 us
  waiting for transfers between devices  68.7 us (69%)
  between operations  14.2 us (14%)
  starting transfers between devices  9.77 us (10%)
  Pallas kernels  4.08 us (4%)
  local copies, waits for them, and re-layouts  1.04 us (1%)
    reduce_scatter x1, waiting for transfers between devices, on_device(): row_in = lax.psum_scatter(own_rows, 'pa', scatter_dimension=0, tiled=True)  58.2 us
    ppermute x1, waiting for transfers between devices, on_device(): near = lax.ppermute(near, 'sa', [(1, 2)])  9.8 us
    all_to_all x1, starting transfers between devices, on_device(): lax.all_to_all(compressed, 'pa', split_axis=0, concat_axis=0, tiled=True)  5.83 us
  transfers between devices with their start and end apart: 5, of which 2 were waited for; matrix products, arithmetic and copies ran while one was open for 0% of the time, Pallas kernels for 2%

profile of v13, /device:TPU:2, one launch (start us, length us, event | category | flops | bytes accessed | tf_op | source)
XLA Modules:
  0.0 97.8 jit_solution(14926981452251379241)
XLA Ops:
  6.5 0.0 copy-start
  6.6 0.8 collective-permute-start.1
  7.4 0.3 copy-done
  7.8 0.0 copy-start.1
  7.8 0.3 shard_map.56
  8.0 0.0 copy-start.3
  8.1 1.8 %collective-permute-start.2 = (bf16[32,64,128]{2,1,0:T(8,128)(2,1)S(1)}, bf16[32,64,128]{2,1,0:T(8,128)(2,1)S(1)}, u32[]{:S(2)}, u32[]{:S(2)}) collective-permute-start(bf16[32,64,128]{2,1,0:T(8,128)(2,1)S(1)} %get-tuple-element.23), channel_id=1, source_target_pairs={{0,1},{2,3},{4,5},{6,7},{8,9},{10,11},{12,13},{14,15},{16,17},{18,... | collective-permute-start | bytes 1572872 | tf_op jit(solution)/shard_map/ppermute | solution.py:310
  10.5 0.0 copy-done.1
  10.5 0.0 copy-done.4
  10.5 0.0 copy-done.3
  10.5 1.0 %shard_map.57 = (bf16[1280,256]{1,0:T(8,128)(2,1)S(1)}, bf16[8,16,128]{2,1,0:T(8,128)(2,1)}, f32[8,128]{1,0:T(8,128)S(1)}) custom-call(f32[8,128]{1,0:T(8,128)S(1)} %get-tuple-element.17.turn_in_ref, s32[1]{0:T(128)S(6)} %copy.6.window_ref, s32[4,8]{1,0:T(4,128)S(1)} %copy-done.4, bf16[2,1024]{1,0:T(2,128)(2,1)S(1)} %copy-done.3, ...), custom_call_target="tpu_custom_call" | custom-call | flops 1000 | bytes 1000 | tf_op jit(solution)/shard_map/pallas_call | solution.py:311
  11.6 1.3 %collective-permute-start = (bf16[8,256,128]{2,1,0:T(8,128)(2,1)S(1)}, bf16[8,256,128]{2,1,0:T(8,128)(2,1)S(1)}, u32[]{:S(2)}, u32[]{:S(2)}) collective-permute-start(bf16[8,256,128]{2,1,0:T(8,128)(2,1)S(1)} %get-tuple-element.20), channel_id=1, source_target_pairs={{1,2},{5,6},{9,10},{13,14},{17,18},{21,22},{25,26},{29,30}} | collective-permute-start | bytes 1572872 | tf_op jit(solution)/shard_map/ppermute | solution.py:320
  12.9 0.0 collective-permute-done.1._.far_ref
  12.9 0.0 collective-permute-done.2.edge_ref
  13.0 9.8 %collective-permute-done.near_ref = bf16[8,256,128]{2,1,0:T(8,128)(2,1)S(1)} collective-permute-done((bf16[8,256,128]{2,1,0:T(8,128)(2,1)S(1)}, bf16[8,256,128]{2,1,0:T(8,128)(2,1)S(1)}, u32[]{:S(2)}, u32[]{:S(2)}) %collective-permute-start) | collective-permute-done | bytes 524320 | tf_op jit(solution)/shard_map/ppermute | solution.py:320
  22.8 0.8 shard_map.61
  23.6 5.8 %all-to-all-start = ((bf16[8,256,128]{2,1,0:T(8,128)(2,1)}), bf16[8,256,128]{2,1,0:T(8,128)(2,1)S(1)}, u32[]{:S(2)}, u32[]{:S(2)}) async-start(bf16[8,256,128]{2,1,0:T(8,128)(2,1)} %get-tuple-element.24), calls=%async_computation | async-start | bytes 1048576 | tf_op jit(solution)/shard_map/all_to_all | solution.py:333
  29.4 0.0 reduce-scatter.2.cloned.1.call-start
  29.5 0.7 reduce-scatter.2.cloned.1.call-update
  30.1 58.2 %reduce-scatter.2.cloned.1.call-done.rows_ref = bf16[1,16,128]{2,1,0:T(8,128)(2,1)} async-done(((bf16[8,16,128]{2,1,0:T(8,128)(2,1)}), bf16[1,16,128]{2,1,0:T(8,128)(2,1)}) %reduce-scatter.2.cloned.1.call-update) | async-done | bytes 4112 | tf_op jit(solution)/shard_map/reduce_scatter | solution.py:316
  88.3 0.7 copy-done.2
  89.0 0.5 shard_map.62.taps_ref
  89.5 0.0 all-to-all-done.lines_ref
  89.5 1.3 %shard_map.63 = f32[512,2,256]{2,1,0:T(2,128)} custom-call(bf16[8,256,128]{2,1,0:T(8,128)(2,1)S(1)} %all-to-all-done.lines_ref, bf16[512,512]{1,0:T(8,128)(2,1)S(1)} %shard_map.62.taps_ref), custom_call_target="tpu_custom_call" | custom-call | flops 1000 | bytes 1000 | tf_op jit(solution)/shard_map/pallas_call | solution.py:338
  (6 shorter events, 0.1 us)
Async XLA Ops:
  6.5 1.2 %copy-start = (bf16[32,2,8192]{2,1,0:T(2,128)(2,1)S(1)}, bf16[32,2,8192]{2,1,0:T(2,128)(2,1)}, u32[]{:S(2)}) copy-start(bf16[32,2,8192]{2,1,0:T(2,128)(2,1)} %raw_ref.7) | copy-start | bytes 3145732
  6.6 6.3 %collective-permute-start.1 = (bf16[32,64,128]{2,1,0:T(8,128)(2,1)S(1)}, bf16[32,64,128]{2,1,0:T(8,128)(2,1)S(1)}, u32[]{:S(2)}, u32[]{:S(2)}) collective-permute-start(bf16[32,64,128]{2,1,0:T(8,128)(2,1)S(1)} %get-tuple-element.22), channel_id=1, source_target_pairs={{1,3},{5,7},{9,11},{13,15},{17,19},{21,23},{25,27},{29,31}} | collective-permute-start | bytes 1572872 | tf_op jit(solution)/shard_map/ppermute | solution.py:308
  7.8 2.8 %copy-start.1 = (bf16[8,2,512]{2,1,0:T(2,128)(2,1)S(1)}, bf16[8,2,512]{2,1,0:T(2,128)(2,1)}, u32[]{:S(2)}) copy-start(bf16[8,2,512]{2,1,0:T(2,128)(2,1)} %refs_ref.1) | copy-start | bytes 49156
  7.8 2.8 %copy-start.4 = (s32[4,8]{1,0:T(4,128)S(1)}, s32[4,8]{1,0:T(4,128)}, u32[]{:S(2)}) copy-start(s32[4,8]{1,0:T(4,128)} %index_ref.1) | copy-start | bytes 388
  8.0 2.5 %copy-start.3 = (bf16[2,1024]{1,0:T(2,128)(2,1)S(1)}, bf16[2,1024]{1,0:T(2,128)(2,1)}, u32[]{:S(2)}) copy-start(bf16[2,1024]{1,0:T(2,128)(2,1)} %chirp_ref.1) | copy-start | bytes 12292
  8.1 4.8 %collective-permute-start.2 = (bf16[32,64,128]{2,1,0:T(8,128)(2,1)S(1)}, bf16[32,64,128]{2,1,0:T(8,128)(2,1)S(1)}, u32[]{:S(2)}, u32[]{:S(2)}) collective-permute-start(bf16[32,64,128]{2,1,0:T(8,128)(2,1)S(1)} %get-tuple-element.23), channel_id=1, source_target_pairs={{0,1},{2,3},{4,5},{6,7},{8,9},{10,11},{12,13},{14,15},{16,17},{18,... | collective-permute-start | bytes 1572872 | tf_op jit(solution)/shard_map/ppermute | solution.py:310
  11.6 11.2 %collective-permute-start = (bf16[8,256,128]{2,1,0:T(8,128)(2,1)S(1)}, bf16[8,256,128]{2,1,0:T(8,128)(2,1)S(1)}, u32[]{:S(2)}, u32[]{:S(2)}) collective-permute-start(bf16[8,256,128]{2,1,0:T(8,128)(2,1)S(1)} %get-tuple-element.20), channel_id=1, source_target_pairs={{1,2},{5,6},{9,10},{13,14},{17,18},{21,22},{25,26},{29,30}} | collective-permute-start | bytes 1572872 | tf_op jit(solution)/shard_map/ppermute | solution.py:320
  23.6 66.0 %all-to-all-start = ((bf16[8,256,128]{2,1,0:T(8,128)(2,1)}), bf16[8,256,128]{2,1,0:T(8,128)(2,1)S(1)}, u32[]{:S(2)}, u32[]{:S(2)}) async-start(bf16[8,256,128]{2,1,0:T(8,128)(2,1)} %get-tuple-element.24), calls=%async_computation | async-start | bytes 1048576 | tf_op jit(solution)/shard_map/all_to_all | solution.py:333
  29.4 58.9 %reduce-scatter.2.cloned.1.call-start = ((), (), s32[]{:S(2)}) async-start(), calls=%async_computation.2 | async-start | bytes 36864 | tf_op jit(solution)/shard_map/reduce_scatter | solution.py:316
  88.3 0.7 copy-start.2
Sparse Core Ops, SparseCore 0:
  33.4 54.9 reduce-scatter.1

commit v14 on v12

--- a/solution.py
+++ b/solution.py
@@ -131,8 +131,7 @@
         compress(held, 0, taps_ref, out_ref)
 
 
-def early_kernel(turn_in_ref, window_ref, raw_ref, far_ref, edge_ref, taps_ref, rows_ref, out_ref, turn_ref, held):
-    turn_ref[...] = turn_in_ref[...]
+def early_kernel(turn_in_ref, window_ref, raw_ref, far_ref, edge_ref, taps_ref, rows_ref, out_ref, held):
     half = edge_ref.shape[0]
     tail = held.shape[0] - half
     span = tail - 16 + half
@@ -175,8 +174,10 @@
 
 
 def azimuth_kernel(lines_ref, out_ref, columns_held, taps, made, sems):
-    bins, _, pulses = out_ref.shape
-    tiles = bins // LANES
+    pulses = taps.shape[0] // 2
+    columns = pulses // LANES
+    tiles = sems.shape[0]
+    each = out_ref.shape[0] // tiles
     sources = lines_ref.shape[0]
     rows = (lines_ref.shape[1] - 16) // tiles
     picked = jnp.sum(lines_ref[:, tiles * rows :].astype(F32), axis=0)
@@ -191,7 +192,6 @@
     for part in range(2):
         spread = jnp.broadcast_to(moved[part : part + 1], (pulses, L))
         parts.append(pltpu.roll(spread, 0, 1, stride=1, stride_axis=0)[:, :pulses])
-    columns = pulses // LANES
     for part, pair in enumerate(((parts[0], -parts[1]), (parts[1], parts[0]))):
         for target in range(2):
             for column in range(columns):
@@ -204,9 +204,13 @@
     for tile in range(tiles):
         lines = lines_ref[:, tile * rows : (tile + 1) * rows].reshape(sources * rows, LANES)
         focused = lax.dot_general(lines, taps[...], (((0,), (0,)), ((), ())), preferred_element_type=F32)
-        into = pl.ds(tile * LANES, LANES)
-        made[into, 0, :] = focused[:, :pulses]
-        made[into, 1, :] = focused[:, pulses:]
+        into = pl.ds(tile * each, each)
+        for part in range(2):
+            for column in range(columns):
+                lane = part * pulses + column * LANES
+                made[pl.ds(tile * each + 2 * column + part, LANES, stride=2 * columns), :] = focused[
+                    :, lane : lane + LANES
+                ]
         copies.append(pltpu.make_async_copy(made.at[into], out_ref.at[into], sems.at[tile]))
         copies[-1].start()
     for copy in copies:
@@ -317,10 +321,10 @@
     near = lax.ppermute(near, "sa", [(1, 2)])
     extra = own_rows if short else jnp.zeros((targets, 16, LANES), BF)
     made = shape((targets, slot + 16, LANES), BF)
-    early, turn = call(
+    (early,) = call(
         early_kernel,
-        (made, token),
-        "vsvvvvvvv",
+        (made,),
+        "vsvvvvvv",
         [pltpu.VMEM((span + 16, rows, LANES), BF)],
         flops=10**10,
     )(turn, window_start, raw_echo, far, edge, taps, extra)
@@ -338,16 +342,17 @@
     width = 2 * total_pulses
     (focused,) = call(
         azimuth_kernel,
-        (shape((bin_count, 2, total_pulses), F32),),
+        (shape((bin_count * width // LANES, LANES), F32),),
         "va",
         [
             pltpu.VMEM((width // LANES, width, LANES), F32),
             pltpu.VMEM((width, width), BF),
-            pltpu.VMEM((bin_count, 2, total_pulses), F32),
+            pltpu.VMEM((bin_count * width // LANES, LANES), F32),
             pltpu.SemaphoreType.DMA((bin_count // LANES,)),
         ],
     )(lines)
-    return focused[None]
+    focused = focused.reshape(1, bin_count, total_pulses // LANES, 2, LANES).swapaxes(2, 3)
+    return focused.reshape(1, bin_count, 2, total_pulses)
 
 
 def solution(mesh):

time: 35.9 us -> 35.3 us (0.983)
  Pallas kernels: 3.28 us -> 2.6 us
  blocking collectives: 18.2 us -> 17.6 us
  waiting for transfers between devices: 9.23 us -> 9.82 us
    pallas_call x2, Pallas kernels: 2.38 us -> 1.71 us  [the longest x1 1.67 us: on_device(): call(azimuth_kernel, (shape((bin_count * width // LANES, LANES), F32),),...]
    ppermute x1, waiting for transfers between devices: 9.23 us -> 9.81 us  [on_device(): near = lax.ppermute(near, 'sa', [(1, 2)])]
    all_to_all x1, blocking collectives: 18.2 us -> 17.6 us  [on_device(): lax.all_to_all(compressed, 'pa', split_axis=0, concat_axis=0, tiled=True)]
  transfers between devices with their start and end apart: 3 -> 3, of which waited for: 1 -> 1; matrix products, arithmetic and copies ran while one was open for 0% -> 0% of each run, Pallas kernels for 4% -> 2%
where the time goes in v14:
time: 35.3 us; the launch traced here: 35 us
  blocking collectives  17.6 us (50%)
  waiting for transfers between devices  9.82 us (28%)
  starting transfers between devices  3.91 us (11%)
  Pallas kernels  2.6 us (7%)
  between operations  0.76 us (2%)
  local copies, waits for them, and re-layouts  0.36 us (1%)
    all_to_all x1, blocking collectives, on_device(): lax.all_to_all(compressed, 'pa', split_axis=0, concat_axis=0, tiled=True)  17.6 us
    ppermute x1, waiting for transfers between devices, on_device(): near = lax.ppermute(near, 'sa', [(1, 2)])  9.81 us
    ppermute x1, starting transfers between devices, on_device(): edge = lax.ppermute(edge, 'sa', [(0, 1), (2, 3)])  1.8 us
    pallas_call x1, Pallas kernels, on_device(): call(azimuth_kernel, (shape((bin_count * width // LANES, LANES), F32),),...  1.67 us
    ppermute x1, starting transfers between devices, on_device(): near = lax.ppermute(near, 'sa', [(1, 2)])  1.29 us
    ppermute x1, starting transfers between devices, on_device(): far = lax.ppermute(far, 'sa', [(1, 3)])  0.83 us
  transfers between devices with their start and end apart: 3, of which 1 were waited for; matrix products, arithmetic and copies ran while one was open for 0% of the time, Pallas kernels for 2%

profile of v14, /device:TPU:2, one launch (start us, length us, event | category | flops | bytes accessed | tf_op | source)
XLA Modules:
  0.0 35.0 jit_solution(17854059344082469486)
XLA Ops:
  0.0 0.0 copy-start
  0.0 0.8 %collective-permute-start.1 = (bf16[32,64,128]{2,1,0:T(8,128)(2,1)S(1)}, bf16[32,64,128]{2,1,0:T(8,128)(2,1)S(1)}, u32[]{:S(2)}, u32[]{:S(2)}) collective-permute-start(bf16[32,64,128]{2,1,0:T(8,128)(2,1)S(1)} %get-tuple-element.21), channel_id=1, source_target_pairs={{1,3},{5,7},{9,11},{13,15},{17,19},{21,23},{25,27},{29,31}} | collective-permute-start | bytes 1572872 | tf_op jit(solution)/shard_map/ppermute | solution.py:307
  0.9 0.3 copy-done
  1.2 0.0 copy-start.1
  1.2 0.0 copy-start.3
  1.2 0.3 shard_map.56
  1.5 0.0 copy-start.2
  1.5 1.8 %collective-permute-start.2 = (bf16[32,64,128]{2,1,0:T(8,128)(2,1)S(1)}, bf16[32,64,128]{2,1,0:T(8,128)(2,1)S(1)}, u32[]{:S(2)}, u32[]{:S(2)}) collective-permute-start(bf16[32,64,128]{2,1,0:T(8,128)(2,1)S(1)} %get-tuple-element.22), channel_id=1, source_target_pairs={{0,1},{2,3},{4,5},{6,7},{8,9},{10,11},{12,13},{14,15},{16,17},{18,... | collective-permute-start | bytes 1572872 | tf_op jit(solution)/shard_map/ppermute | solution.py:309
  4.0 0.0 copy-done.1
  4.0 0.0 copy-done.3
  4.0 0.0 copy-done.2
  4.0 0.5 %shard_map.57 = (bf16[1280,256]{1,0:T(8,128)(2,1)S(1)}, bf16[8,16,128]{2,1,0:T(8,128)(2,1)S(1)}, f32[8,128]{1,0:T(8,128)S(1)}) custom-call(f32[8,128]{1,0:T(8,128)S(1)} %get-tuple-element.15.turn_in_ref, s32[1]{0:T(128)S(6)} %copy.7.window_ref, s32[4,8]{1,0:T(4,128)S(1)} %copy-done.3, bf16[2,1024]{1,0:T(2,128)(2,1)S(1)} %copy-done.2, ...), custom_call_target="tpu_custom_call" | custom-call | flops 1000 | bytes 1000 | tf_op jit(solution)/shard_map/pallas_call | solution.py:310
  4.6 1.3 %collective-permute-start = (bf16[8,256,128]{2,1,0:T(8,128)(2,1)S(1)}, bf16[8,256,128]{2,1,0:T(8,128)(2,1)S(1)}, u32[]{:S(2)}, u32[]{:S(2)}) collective-permute-start(bf16[8,256,128]{2,1,0:T(8,128)(2,1)S(1)} %get-tuple-element.18), channel_id=1, source_target_pairs={{1,2},{5,6},{9,10},{13,14},{17,18},{21,22},{25,26},{29,30}} | collective-permute-start | bytes 1572872 | tf_op jit(solution)/shard_map/ppermute | solution.py:321
  5.9 0.0 collective-permute-done.1.far_ref
  5.9 0.0 collective-permute-done.2.edge_ref
  5.9 9.8 %collective-permute-done.near_ref = bf16[8,256,128]{2,1,0:T(8,128)(2,1)S(1)} collective-permute-done((bf16[8,256,128]{2,1,0:T(8,128)(2,1)S(1)}, bf16[8,256,128]{2,1,0:T(8,128)(2,1)S(1)}, u32[]{:S(2)}, u32[]{:S(2)}) %collective-permute-start) | collective-permute-done | bytes 524320 | tf_op jit(solution)/shard_map/ppermute | solution.py:321
  15.8 17.6 %all_to_all.5.lines_ref = bf16[8,272,128]{2,1,0:T(8,128)(2,1)S(1)} all-to-all(bf16[8,272,128]{2,1,0:T(8,128)(2,1)S(1)} %shard_map.60), channel_id=1, replica_groups=mesh['pa'=8,'sa'=4] {'pa'}, dimensions={0} | all-to-all | bytes 1114112 | tf_op jit(solution)/shard_map/all_to_all | solution.py:341
  33.4 1.7 %shard_map.61 = f32[2048,128]{1,0:T(8,128)} custom-call(bf16[8,272,128]{2,1,0:T(8,128)(2,1)S(1)} %all_to_all.5.lines_ref), custom_call_target="tpu_custom_call" | custom-call | flops 1000 | bytes 1000 | tf_op jit(solution)/shard_map/pallas_call | solution.py:343
  (4 shorter events, 0.1 us)
Async XLA Ops:
  0.0 1.2 %copy-start = (bf16[32,2,8192]{2,1,0:T(2,128)(2,1)S(1)}, bf16[32,2,8192]{2,1,0:T(2,128)(2,1)}, u32[]{:S(2)}) copy-start(bf16[32,2,8192]{2,1,0:T(2,128)(2,1)} %raw_ref.7) | copy-start | bytes 3145732
  0.0 5.8 %collective-permute-start.1 = (bf16[32,64,128]{2,1,0:T(8,128)(2,1)S(1)}, bf16[32,64,128]{2,1,0:T(8,128)(2,1)S(1)}, u32[]{:S(2)}, u32[]{:S(2)}) collective-permute-start(bf16[32,64,128]{2,1,0:T(8,128)(2,1)S(1)} %get-tuple-element.21), channel_id=1, source_target_pairs={{1,3},{5,7},{9,11},{13,15},{17,19},{21,23},{25,27},{29,31}} | collective-permute-start | bytes 1572872 | tf_op jit(solution)/shard_map/ppermute | solution.py:307
  1.2 2.8 %copy-start.1 = (bf16[8,2,512]{2,1,0:T(2,128)(2,1)S(1)}, bf16[8,2,512]{2,1,0:T(2,128)(2,1)}, u32[]{:S(2)}) copy-start(bf16[8,2,512]{2,1,0:T(2,128)(2,1)} %refs_ref.1) | copy-start | bytes 49156
  1.2 2.8 %copy-start.3 = (s32[4,8]{1,0:T(4,128)S(1)}, s32[4,8]{1,0:T(4,128)}, u32[]{:S(2)}) copy-start(s32[4,8]{1,0:T(4,128)} %index_ref.1) | copy-start | bytes 388
  1.5 2.5 %copy-start.2 = (bf16[2,1024]{1,0:T(2,128)(2,1)S(1)}, bf16[2,1024]{1,0:T(2,128)(2,1)}, u32[]{:S(2)}) copy-start(bf16[2,1024]{1,0:T(2,128)(2,1)} %chirp_ref.1) | copy-start | bytes 12292
  1.5 4.3 %collective-permute-start.2 = (bf16[32,64,128]{2,1,0:T(8,128)(2,1)S(1)}, bf16[32,64,128]{2,1,0:T(8,128)(2,1)S(1)}, u32[]{:S(2)}, u32[]{:S(2)}) collective-permute-start(bf16[32,64,128]{2,1,0:T(8,128)(2,1)S(1)} %get-tuple-element.22), channel_id=1, source_target_pairs={{0,1},{2,3},{4,5},{6,7},{8,9},{10,11},{12,13},{14,15},{16,17},{18,... | collective-permute-start | bytes 1572872 | tf_op jit(solution)/shard_map/ppermute | solution.py:309
  4.6 11.2 %collective-permute-start = (bf16[8,256,128]{2,1,0:T(8,128)(2,1)S(1)}, bf16[8,256,128]{2,1,0:T(8,128)(2,1)S(1)}, u32[]{:S(2)}, u32[]{:S(2)}) collective-permute-start(bf16[8,256,128]{2,1,0:T(8,128)(2,1)S(1)} %get-tuple-element.18), channel_id=1, source_target_pairs={{1,2},{5,6},{9,10},{13,14},{17,18},{21,22},{25,26},{29,30}} | collective-permute-start | bytes 1572872 | tf_op jit(solution)/shard_map/ppermute | solution.py:321

commit v15 on v14

--- a/solution.py
+++ b/solution.py
@@ -8,6 +8,7 @@
 R = 16384
 L = 512
 LANES = 128
+EXTRA = 8
 BF = jnp.bfloat16
 F32 = jnp.float32
 
@@ -27,14 +28,14 @@
         target[first + t] = source[:, :, t * LANES : (t + 1) * LANES].reshape(shape)
 
 
-def far_kernel(raw_ref, far_ref, turn_ref, natural, sems):
+def tail_kernel(raw_ref, tail_ref, turn_ref, natural, sems):
     turn_ref[...] = jnp.zeros_like(turn_ref)
-    half, rows, _ = far_ref.shape
+    half, rows, _ = tail_ref.shape
     pieces = sems.shape[0]
     each = rows // 2 // pieces
     width = half * LANES
 
-    @pl.when(lax.axis_index("sa") == 1)
+    @pl.when(lax.axis_index("sa") < 2)
     def _():
         copies = []
         for at in range(pieces):
@@ -45,22 +46,15 @@
         for at, copy in enumerate(copies):
             copy.wait()
             own = pl.ds(at * each, each)
-            retile(natural.at[own], far_ref.at[:, pl.ds(at * each * 2, each * 2)], 0, half)
-
-
-def edge_kernel(turn_in_ref, raw_ref, edge_ref, turn_ref):
+            retile(natural.at[own], tail_ref.at[:, pl.ds(at * each * 2, each * 2)], 0, half)
+
+
+def head_kernel(turn_in_ref, raw_ref, head_ref, turn_ref):
     turn_ref[...] = turn_in_ref[...]
-    half = edge_ref.shape[0]
-    tiles = raw_ref.shape[2] // LANES
-    sub_index = lax.axis_index("sa")
-
-    @pl.when(sub_index == 0)
-    def _():
-        retile(raw_ref.at[:, :, pl.ds((tiles - half) * LANES, half * LANES)], edge_ref, 0, half)
-
-    @pl.when(sub_index == 2)
-    def _():
-        retile(raw_ref, edge_ref, 0, half)
+
+    @pl.when(lax.axis_index("sa") == 2)
+    def _():
+        retile(raw_ref, head_ref, 0, head_ref.shape[0])
 
 
 def prep_kernel(turn_in_ref, window_ref, index_ref, chirp_ref, refs_ref, taps_ref, rows_ref, turn_ref):
@@ -131,10 +125,10 @@
         compress(held, 0, taps_ref, out_ref)
 
 
-def early_kernel(turn_in_ref, window_ref, raw_ref, far_ref, edge_ref, taps_ref, rows_ref, out_ref, held):
-    half = edge_ref.shape[0]
-    tail = held.shape[0] - half
-    span = tail - 16 + half
+def early_kernel(turn_in_ref, window_ref, raw_ref, tail_ref, head_ref, taps_ref, rows_ref, out_ref, held):
+    half = tail_ref.shape[0]
+    more = head_ref.shape[0]
+    span = half + more - 16
     sub_index = lax.axis_index("sa")
     offset = window_ref[0] // LANES
 
@@ -145,13 +139,13 @@
 
     @pl.when(sub_index == 1)
     def _():
-        held[:half] = edge_ref[...]
-        retile(raw_ref, held, half, tail)
+        held[:half] = tail_ref[...]
+        retile(raw_ref, held, half, more)
 
     @pl.when(sub_index == 3)
     def _():
-        held[:half] = far_ref[...]
-        held[half:] = edge_ref[:tail]
+        held[:half] = tail_ref[...]
+        held[half:] = head_ref[...]
 
     @pl.when(sub_index != 2)
     def _():
@@ -179,7 +173,7 @@
     tiles = sems.shape[0]
     each = out_ref.shape[0] // tiles
     sources = lines_ref.shape[0]
-    rows = (lines_ref.shape[1] - 16) // tiles
+    rows = (lines_ref.shape[1] - EXTRA) // tiles
     picked = jnp.sum(lines_ref[:, tiles * rows :].astype(F32), axis=0)
     pieces = L // LANES
     row = [
@@ -297,19 +291,19 @@
     targets = pulse_devices if short else half // 8
     slot = half // targets * rows
 
-    far, turn = call(
-        far_kernel,
+    tail, turn = call(
+        tail_kernel,
         (shape((half, rows, LANES), BF), token),
         "avv",
         [pltpu.VMEM((pulses, 2, half * LANES), BF), pltpu.SemaphoreType.DMA((4,))],
         53,
     )(raw_echo)
-    far = lax.ppermute(far, "sa", [(1, 3)])
-    edge, turn = call(edge_kernel, (shape((half, rows, LANES), BF), token), "vvvv")(turn, raw_echo)
-    edge = lax.ppermute(edge, "sa", [(0, 1), (2, 3)])
+    tail = lax.ppermute(tail, "sa", [(0, 1), (1, 3)])
+    head, turn = call(head_kernel, (shape((span - half + 16, rows, LANES), BF), token), "vvvv")(turn, raw_echo)
+    head = lax.ppermute(head, "sa", [(2, 3)])
     taps, own_rows, turn = call(
         prep_kernel,
-        (shape((tap_tiles * LANES, 2 * LANES), BF), shape((pulse_devices, 16, LANES), BF), token),
+        (shape((tap_tiles * LANES, 2 * LANES), BF), shape((pulse_devices, EXTRA, LANES), BF), token),
         "vsvvvvvv",
     )(turn, window_start, migration_index, chirp_replica, azimuth_refs)
     near, turn = call(
@@ -319,19 +313,19 @@
         [pltpu.VMEM((span, rows, LANES), BF)],
     )(turn, window_start, raw_echo, taps)
     near = lax.ppermute(near, "sa", [(1, 2)])
-    extra = own_rows if short else jnp.zeros((targets, 16, LANES), BF)
-    made = shape((targets, slot + 16, LANES), BF)
+    extra = own_rows if short else jnp.zeros((targets, EXTRA, LANES), BF)
+    made = shape((targets, slot + EXTRA, LANES), BF)
     (early,) = call(
         early_kernel,
         (made,),
         "vsvvvvvv",
         [pltpu.VMEM((span + 16, rows, LANES), BF)],
         flops=10**10,
-    )(turn, window_start, raw_echo, far, edge, taps, extra)
+    )(turn, window_start, raw_echo, tail, head, taps, extra)
     (compressed,) = call(late_kernel, (made,), "vvvv")(near, extra, early)
 
     if not short:
-        kept = compressed[:, :-16].reshape(half, pulses, 2, LANES).transpose(0, 3, 2, 1)
+        kept = compressed[:, :-EXTRA].reshape(half, pulses, 2, LANES).transpose(0, 3, 2, 1)
         outgoing = kept.reshape(pulse_devices, bin_count, 2, pulses)
         turned = lax.all_to_all(outgoing, "pa", split_axis=0, concat_axis=3, tiled=True)
         rows_in = lax.all_to_all(own_rows, "pa", split_axis=0, concat_axis=0, tiled=True)

time: 35.3 us -> 35 us (level)
  no operation moved by 1% of the time
where the time goes in v15:
time: 35 us; the launch traced here: 34.8 us
  blocking collectives  17.3 us (49%)
  waiting for transfers between devices  9.83 us (28%)
  starting transfers between devices  3.96 us (11%)
  Pallas kernels  2.55 us (7%)
  between operations  0.76 us (2%)
  local copies, waits for them, and re-layouts  0.36 us (1%)
    all_to_all x1, blocking collectives, on_device(): lax.all_to_all(compressed, 'pa', split_axis=0, concat_axis=0, tiled=True)  17.3 us
    ppermute x1, waiting for transfers between devices, on_device(): near = lax.ppermute(near, 'sa', [(1, 2)])  9.82 us
    ppermute x1, starting transfers between devices, on_device(): head = lax.ppermute(head, 'sa', [(2, 3)])  1.84 us
    pallas_call x1, Pallas kernels, on_device(): call(azimuth_kernel, (shape((bin_count * width // LANES, LANES), F32),),...  1.68 us
    ppermute x1, starting transfers between devices, on_device(): near = lax.ppermute(near, 'sa', [(1, 2)])  1.29 us
    ppermute x1, starting transfers between devices, on_device(): tail = lax.ppermute(tail, 'sa', [(0, 1), (1, 3)])  0.83 us
  transfers between devices with their start and end apart: 3, of which 1 were waited for; matrix products, arithmetic and copies ran while one was open for 0% of the time, Pallas kernels for 2%

profile of v15, /device:TPU:2, one launch (start us, length us, event | category | flops | bytes accessed | tf_op | source)
XLA Modules:
  0.0 34.8 jit_solution(16689153531779420597)
XLA Ops:
  0.0 0.0 copy-start
  0.0 0.8 %collective-permute-start.1 = (bf16[32,64,128]{2,1,0:T(8,128)(2,1)S(1)}, bf16[32,64,128]{2,1,0:T(8,128)(2,1)S(1)}, u32[]{:S(2)}, u32[]{:S(2)}) collective-permute-start(bf16[32,64,128]{2,1,0:T(8,128)(2,1)S(1)} %get-tuple-element.21), channel_id=1, source_target_pairs={{0,1},{1,3},{4,5},{5,7},{8,9},{9,11},{12,13},{13,15},{16,17},{17,1... | collective-permute-start | bytes 1572872 | tf_op jit(solution)/shard_map/ppermute | solution.py:301
  0.9 0.3 copy-done
  1.2 0.0 copy-start.1
  1.2 0.0 copy-start.3
  1.2 0.2 shard_map.56
  1.5 0.0 copy-start.2
  1.5 1.8 %collective-permute-start.2 = (bf16[25,64,128]{2,1,0:T(8,128)(2,1)S(1)}, bf16[25,64,128]{2,1,0:T(8,128)(2,1)S(1)}, u32[]{:S(2)}, u32[]{:S(2)}) collective-permute-start(bf16[25,64,128]{2,1,0:T(8,128)(2,1)S(1)} %get-tuple-element.22), channel_id=1, source_target_pairs={{2,3},{6,7},{10,11},{14,15},{18,19},{22,23},{26,27},{30,31}} | collective-permute-start | bytes 1228808 | tf_op jit(solution)/shard_map/ppermute | solution.py:303
  4.0 0.0 copy-done.1
  4.0 0.0 copy-done.3
  4.0 0.0 copy-done.2
  4.0 0.5 %shard_map.57 = (bf16[1280,256]{1,0:T(8,128)(2,1)S(1)}, bf16[8,8,128]{2,1,0:T(8,128)(2,1)S(1)}, f32[8,128]{1,0:T(8,128)S(1)}) custom-call(f32[8,128]{1,0:T(8,128)S(1)} %get-tuple-element.15.turn_in_ref, s32[1]{0:T(128)S(6)} %copy.7.window_ref, s32[4,8]{1,0:T(4,128)S(1)} %copy-done.3, bf16[2,1024]{1,0:T(2,128)(2,1)S(1)} %copy-done.2, ...), custom_call_target="tpu_custom_call" | custom-call | flops 1000 | bytes 1000 | tf_op jit(solution)/shard_map/pallas_call | solution.py:304
  4.6 1.3 %collective-permute-start = (bf16[8,256,128]{2,1,0:T(8,128)(2,1)S(1)}, bf16[8,256,128]{2,1,0:T(8,128)(2,1)S(1)}, u32[]{:S(2)}, u32[]{:S(2)}) collective-permute-start(bf16[8,256,128]{2,1,0:T(8,128)(2,1)S(1)} %get-tuple-element.18), channel_id=1, source_target_pairs={{1,2},{5,6},{9,10},{13,14},{17,18},{21,22},{25,26},{29,30}} | collective-permute-start | bytes 1572872 | tf_op jit(solution)/shard_map/ppermute | solution.py:315
  5.9 0.0 collective-permute-done.2.head_ref
  5.9 0.0 collective-permute-done.1.tail_ref
  5.9 9.8 %collective-permute-done.near_ref = bf16[8,256,128]{2,1,0:T(8,128)(2,1)S(1)} collective-permute-done((bf16[8,256,128]{2,1,0:T(8,128)(2,1)S(1)}, bf16[8,256,128]{2,1,0:T(8,128)(2,1)S(1)}, u32[]{:S(2)}, u32[]{:S(2)}) %collective-permute-start) | collective-permute-done | bytes 524320 | tf_op jit(solution)/shard_map/ppermute | solution.py:315
  15.8 17.3 %all_to_all.5.lines_ref = bf16[8,264,128]{2,1,0:T(8,128)(2,1)S(1)} all-to-all(bf16[8,264,128]{2,1,0:T(8,128)(2,1)S(1)} %shard_map.60), channel_id=1, replica_groups=mesh['pa'=8,'sa'=4] {'pa'}, dimensions={0} | all-to-all | bytes 1081344 | tf_op jit(solution)/shard_map/all_to_all | solution.py:335
  33.1 1.7 %shard_map.61 = f32[2048,128]{1,0:T(8,128)} custom-call(bf16[8,264,128]{2,1,0:T(8,128)(2,1)S(1)} %all_to_all.5.lines_ref), custom_call_target="tpu_custom_call" | custom-call | flops 1000 | bytes 1000 | tf_op jit(solution)/shard_map/pallas_call | solution.py:337
  (4 shorter events, 0.1 us)
Async XLA Ops:
  0.0 1.2 %copy-start = (bf16[32,2,8192]{2,1,0:T(2,128)(2,1)S(1)}, bf16[32,2,8192]{2,1,0:T(2,128)(2,1)}, u32[]{:S(2)}) copy-start(bf16[32,2,8192]{2,1,0:T(2,128)(2,1)} %raw_ref.7) | copy-start | bytes 3145732
  0.0 5.8 %collective-permute-start.1 = (bf16[32,64,128]{2,1,0:T(8,128)(2,1)S(1)}, bf16[32,64,128]{2,1,0:T(8,128)(2,1)S(1)}, u32[]{:S(2)}, u32[]{:S(2)}) collective-permute-start(bf16[32,64,128]{2,1,0:T(8,128)(2,1)S(1)} %get-tuple-element.21), channel_id=1, source_target_pairs={{0,1},{1,3},{4,5},{5,7},{8,9},{9,11},{12,13},{13,15},{16,17},{17,1... | collective-permute-start | bytes 1572872 | tf_op jit(solution)/shard_map/ppermute | solution.py:301
  1.2 2.7 %copy-start.1 = (bf16[8,2,512]{2,1,0:T(2,128)(2,1)S(1)}, bf16[8,2,512]{2,1,0:T(2,128)(2,1)}, u32[]{:S(2)}) copy-start(bf16[8,2,512]{2,1,0:T(2,128)(2,1)} %refs_ref.1) | copy-start | bytes 49156
  1.2 2.8 %copy-start.3 = (s32[4,8]{1,0:T(4,128)S(1)}, s32[4,8]{1,0:T(4,128)}, u32[]{:S(2)}) copy-start(s32[4,8]{1,0:T(4,128)} %index_ref.1) | copy-start | bytes 388
  1.5 2.5 %copy-start.2 = (bf16[2,1024]{1,0:T(2,128)(2,1)S(1)}, bf16[2,1024]{1,0:T(2,128)(2,1)}, u32[]{:S(2)}) copy-start(bf16[2,1024]{1,0:T(2,128)(2,1)} %chirp_ref.1) | copy-start | bytes 12292
  1.5 4.4 %collective-permute-start.2 = (bf16[25,64,128]{2,1,0:T(8,128)(2,1)S(1)}, bf16[25,64,128]{2,1,0:T(8,128)(2,1)S(1)}, u32[]{:S(2)}, u32[]{:S(2)}) collective-permute-start(bf16[25,64,128]{2,1,0:T(8,128)(2,1)S(1)} %get-tuple-element.22), channel_id=1, source_target_pairs={{2,3},{6,7},{10,11},{14,15},{18,19},{22,23},{26,27},{30,31}} | collective-permute-start | bytes 1228808 | tf_op jit(solution)/shard_map/ppermute | solution.py:303
  4.6 11.2 %collective-permute-start = (bf16[8,256,128]{2,1,0:T(8,128)(2,1)S(1)}, bf16[8,256,128]{2,1,0:T(8,128)(2,1)S(1)}, u32[]{:S(2)}, u32[]{:S(2)}) collective-permute-start(bf16[8,256,128]{2,1,0:T(8,128)(2,1)S(1)} %get-tuple-element.18), channel_id=1, source_target_pairs={{1,2},{5,6},{9,10},{13,14},{17,18},{21,22},{25,26},{29,30}} | collective-permute-start | bytes 1572872 | tf_op jit(solution)/shard_map/ppermute | solution.py:315

commit v16 on v15

--- a/solution.py
+++ b/solution.py
@@ -170,8 +170,9 @@
 def azimuth_kernel(lines_ref, out_ref, columns_held, taps, made, sems):
     pulses = taps.shape[0] // 2
     columns = pulses // LANES
-    tiles = sems.shape[0]
-    each = out_ref.shape[0] // tiles
+    pieces_out = sems.shape[0]
+    each = out_ref.shape[0] // pieces_out
+    tiles = out_ref.shape[0] // (2 * columns * LANES)
     sources = lines_ref.shape[0]
     rows = (lines_ref.shape[1] - EXTRA) // tiles
     picked = jnp.sum(lines_ref[:, tiles * rows :].astype(F32), axis=0)
@@ -194,18 +195,23 @@
                 ]
     for column in range(2 * columns):
         taps[:, column * LANES : (column + 1) * LANES] = columns_held[column].astype(BF)
+    lines = [
+        lines_ref[:, tile * rows : (tile + 1) * rows].reshape(sources * rows, LANES) for tile in range(tiles)
+    ]
+    focused = lax.dot_general(
+        jnp.concatenate(lines, axis=1), taps[...], (((0,), (0,)), ((), ())), preferred_element_type=F32
+    )
     copies = []
-    for tile in range(tiles):
-        lines = lines_ref[:, tile * rows : (tile + 1) * rows].reshape(sources * rows, LANES)
-        focused = lax.dot_general(lines, taps[...], (((0,), (0,)), ((), ())), preferred_element_type=F32)
-        into = pl.ds(tile * each, each)
+    bins = each // (2 * columns)
+    for piece in range(pieces_out):
+        into = pl.ds(piece * each, each)
         for part in range(2):
             for column in range(columns):
                 lane = part * pulses + column * LANES
-                made[pl.ds(tile * each + 2 * column + part, LANES, stride=2 * columns), :] = focused[
-                    :, lane : lane + LANES
+                made[pl.ds(piece * each + 2 * column + part, bins, stride=2 * columns), :] = focused[
+                    piece * bins : (piece + 1) * bins, lane : lane + LANES
                 ]
-        copies.append(pltpu.make_async_copy(made.at[into], out_ref.at[into], sems.at[tile]))
+        copies.append(pltpu.make_async_copy(made.at[into], out_ref.at[into], sems.at[piece]))
         copies[-1].start()
     for copy in copies:
         copy.wait()
@@ -342,7 +348,7 @@
             pltpu.VMEM((width // LANES, width, LANES), F32),
             pltpu.VMEM((width, width), BF),
             pltpu.VMEM((bin_count * width // LANES, LANES), F32),
-            pltpu.SemaphoreType.DMA((bin_count // LANES,)),
+            pltpu.SemaphoreType.DMA((2 * bin_count // LANES,)),
         ],
     )(lines)
     focused = focused.reshape(1, bin_count, total_pulses // LANES, 2, LANES).swapaxes(2, 3)

time: 35 us -> 35.1 us (level)
  no operation moved by 1% of the time
where the time goes in v16:
time: 35.1 us; the launch traced here: 34.9 us
  blocking collectives  17.3 us (49%)
  waiting for transfers between devices  9.83 us (28%)
  starting transfers between devices  3.96 us (11%)
  Pallas kernels  2.66 us (8%)
  between operations  0.76 us (2%)
  local copies, waits for them, and re-layouts  0.36 us (1%)
    all_to_all x1, blocking collectives, on_device(): lax.all_to_all(compressed, 'pa', split_axis=0, concat_axis=0, tiled=True)  17.3 us
    ppermute x1, waiting for transfers between devices, on_device(): near = lax.ppermute(near, 'sa', [(1, 2)])  9.82 us
    ppermute x1, starting transfers between devices, on_device(): head = lax.ppermute(head, 'sa', [(2, 3)])  1.84 us
    pallas_call x1, Pallas kernels, on_device(): call(azimuth_kernel, (shape((bin_count * width // LANES, LANES), F32),),...  1.79 us
    ppermute x1, starting transfers between devices, on_device(): near = lax.ppermute(near, 'sa', [(1, 2)])  1.29 us
    ppermute x1, starting transfers between devices, on_device(): tail = lax.ppermute(tail, 'sa', [(0, 1), (1, 3)])  0.83 us
  transfers between devices with their start and end apart: 3, of which 1 were waited for; matrix products, arithmetic and copies ran while one was open for 0% of the time, Pallas kernels for 2%

profile of v16, /device:TPU:2, one launch (start us, length us, event | category | flops | bytes accessed | tf_op | source)
XLA Modules:
  0.0 34.9 jit_solution(17494302764593192375)
XLA Ops:
  0.0 0.0 copy-start
  0.0 0.8 %collective-permute-start.1 = (bf16[32,64,128]{2,1,0:T(8,128)(2,1)S(1)}, bf16[32,64,128]{2,1,0:T(8,128)(2,1)S(1)}, u32[]{:S(2)}, u32[]{:S(2)}) collective-permute-start(bf16[32,64,128]{2,1,0:T(8,128)(2,1)S(1)} %get-tuple-element.21), channel_id=1, source_target_pairs={{0,1},{1,3},{4,5},{5,7},{8,9},{9,11},{12,13},{13,15},{16,17},{17,1... | collective-permute-start | bytes 1572872 | tf_op jit(solution)/shard_map/ppermute | solution.py:307
  0.9 0.3 copy-done
  1.2 0.0 copy-start.1
  1.2 0.0 copy-start.3
  1.2 0.2 shard_map.56
  1.5 0.0 copy-start.2
  1.5 1.8 %collective-permute-start.2 = (bf16[25,64,128]{2,1,0:T(8,128)(2,1)S(1)}, bf16[25,64,128]{2,1,0:T(8,128)(2,1)S(1)}, u32[]{:S(2)}, u32[]{:S(2)}) collective-permute-start(bf16[25,64,128]{2,1,0:T(8,128)(2,1)S(1)} %get-tuple-element.22), channel_id=1, source_target_pairs={{2,3},{6,7},{10,11},{14,15},{18,19},{22,23},{26,27},{30,31}} | collective-permute-start | bytes 1228808 | tf_op jit(solution)/shard_map/ppermute | solution.py:309
  4.0 0.0 copy-done.1
  4.0 0.0 copy-done.3
  4.0 0.0 copy-done.2
  4.0 0.5 %shard_map.57 = (bf16[1280,256]{1,0:T(8,128)(2,1)S(1)}, bf16[8,8,128]{2,1,0:T(8,128)(2,1)S(1)}, f32[8,128]{1,0:T(8,128)S(1)}) custom-call(f32[8,128]{1,0:T(8,128)S(1)} %get-tuple-element.15.turn_in_ref, s32[1]{0:T(128)S(6)} %copy.7.window_ref, s32[4,8]{1,0:T(4,128)S(1)} %copy-done.3, bf16[2,1024]{1,0:T(2,128)(2,1)S(1)} %copy-done.2, ...), custom_call_target="tpu_custom_call" | custom-call | flops 1000 | bytes 1000 | tf_op jit(solution)/shard_map/pallas_call | solution.py:310
  4.6 1.3 %collective-permute-start = (bf16[8,256,128]{2,1,0:T(8,128)(2,1)S(1)}, bf16[8,256,128]{2,1,0:T(8,128)(2,1)S(1)}, u32[]{:S(2)}, u32[]{:S(2)}) collective-permute-start(bf16[8,256,128]{2,1,0:T(8,128)(2,1)S(1)} %get-tuple-element.18), channel_id=1, source_target_pairs={{1,2},{5,6},{9,10},{13,14},{17,18},{21,22},{25,26},{29,30}} | collective-permute-start | bytes 1572872 | tf_op jit(solution)/shard_map/ppermute | solution.py:321
  5.9 0.0 collective-permute-done.2.head_ref
  5.9 0.0 collective-permute-done.1.tail_ref
  5.9 9.8 %collective-permute-done.near_ref = bf16[8,256,128]{2,1,0:T(8,128)(2,1)S(1)} collective-permute-done((bf16[8,256,128]{2,1,0:T(8,128)(2,1)S(1)}, bf16[8,256,128]{2,1,0:T(8,128)(2,1)S(1)}, u32[]{:S(2)}, u32[]{:S(2)}) %collective-permute-start) | collective-permute-done | bytes 524320 | tf_op jit(solution)/shard_map/ppermute | solution.py:321
  15.8 17.3 %all_to_all.5.lines_ref = bf16[8,264,128]{2,1,0:T(8,128)(2,1)S(1)} all-to-all(bf16[8,264,128]{2,1,0:T(8,128)(2,1)S(1)} %shard_map.60), channel_id=1, replica_groups=mesh['pa'=8,'sa'=4] {'pa'}, dimensions={0} | all-to-all | bytes 1081344 | tf_op jit(solution)/shard_map/all_to_all | solution.py:341
  33.1 1.8 %shard_map.61 = f32[2048,128]{1,0:T(8,128)} custom-call(bf16[8,264,128]{2,1,0:T(8,128)(2,1)S(1)} %all_to_all.5.lines_ref), custom_call_target="tpu_custom_call" | custom-call | flops 1000 | bytes 1000 | tf_op jit(solution)/shard_map/pallas_call | solution.py:343
  (4 shorter events, 0.1 us)
Async XLA Ops:
  0.0 1.2 %copy-start = (bf16[32,2,8192]{2,1,0:T(2,128)(2,1)S(1)}, bf16[32,2,8192]{2,1,0:T(2,128)(2,1)}, u32[]{:S(2)}) copy-start(bf16[32,2,8192]{2,1,0:T(2,128)(2,1)} %raw_ref.7) | copy-start | bytes 3145732
  0.0 5.8 %collective-permute-start.1 = (bf16[32,64,128]{2,1,0:T(8,128)(2,1)S(1)}, bf16[32,64,128]{2,1,0:T(8,128)(2,1)S(1)}, u32[]{:S(2)}, u32[]{:S(2)}) collective-permute-start(bf16[32,64,128]{2,1,0:T(8,128)(2,1)S(1)} %get-tuple-element.21), channel_id=1, source_target_pairs={{0,1},{1,3},{4,5},{5,7},{8,9},{9,11},{12,13},{13,15},{16,17},{17,1... | collective-permute-start | bytes 1572872 | tf_op jit(solution)/shard_map/ppermute | solution.py:307
  1.2 2.7 %copy-start.1 = (bf16[8,2,512]{2,1,0:T(2,128)(2,1)S(1)}, bf16[8,2,512]{2,1,0:T(2,128)(2,1)}, u32[]{:S(2)}) copy-start(bf16[8,2,512]{2,1,0:T(2,128)(2,1)} %refs_ref.1) | copy-start | bytes 49156
  1.2 2.8 %copy-start.3 = (s32[4,8]{1,0:T(4,128)S(1)}, s32[4,8]{1,0:T(4,128)}, u32[]{:S(2)}) copy-start(s32[4,8]{1,0:T(4,128)} %index_ref.1) | copy-start | bytes 388
  1.5 2.5 %copy-start.2 = (bf16[2,1024]{1,0:T(2,128)(2,1)S(1)}, bf16[2,1024]{1,0:T(2,128)(2,1)}, u32[]{:S(2)}) copy-start(bf16[2,1024]{1,0:T(2,128)(2,1)} %chirp_ref.1) | copy-start | bytes 12292
  1.5 4.4 %collective-permute-start.2 = (bf16[25,64,128]{2,1,0:T(8,128)(2,1)S(1)}, bf16[25,64,128]{2,1,0:T(8,128)(2,1)S(1)}, u32[]{:S(2)}, u32[]{:S(2)}) collective-permute-start(bf16[25,64,128]{2,1,0:T(8,128)(2,1)S(1)} %get-tuple-element.22), channel_id=1, source_target_pairs={{2,3},{6,7},{10,11},{14,15},{18,19},{22,23},{26,27},{30,31}} | collective-permute-start | bytes 1228808 | tf_op jit(solution)/shard_map/ppermute | solution.py:309
  4.6 11.2 %collective-permute-start = (bf16[8,256,128]{2,1,0:T(8,128)(2,1)S(1)}, bf16[8,256,128]{2,1,0:T(8,128)(2,1)S(1)}, u32[]{:S(2)}, u32[]{:S(2)}) collective-permute-start(bf16[8,256,128]{2,1,0:T(8,128)(2,1)S(1)} %get-tuple-element.18), channel_id=1, source_target_pairs={{1,2},{5,6},{9,10},{13,14},{17,18},{21,22},{25,26},{29,30}} | collective-permute-start | bytes 1572872 | tf_op jit(solution)/shard_map/ppermute | solution.py:321

commit v17 on v15

--- a/solution.py
+++ b/solution.py
@@ -88,6 +88,7 @@
         picked = lax.dot_general(
             picks, refs_ref[:, part, :].astype(F32), (((0,), (0,)), ((), ())), preferred_element_type=F32
         )
+        picked = reversed_lanes(picked.astype(BF))
         pieces += [picked[:, t * LANES : (t + 1) * LANES] for t in range(L // LANES)]
     pieces += [jnp.zeros((targets, LANES), F32)] * (rows_ref.shape[1] - len(pieces))
     rows_ref[...] = jnp.stack(pieces, axis=1).astype(BF)
@@ -176,24 +177,31 @@
     rows = (lines_ref.shape[1] - EXTRA) // tiles
     picked = jnp.sum(lines_ref[:, tiles * rows :].astype(F32), axis=0)
     pieces = L // LANES
-    row = [
-        jnp.concatenate([picked[part * pieces + t : part * pieces + t + 1] for t in range(pieces)], axis=1)
+    row = jnp.concatenate(
+        [
+            jnp.concatenate([picked[part * pieces + t : part * pieces + t + 1] for t in range(pieces)], axis=1)
+            for part in range(2)
+        ],
+        axis=0,
+    )
+    moved = pltpu.roll(jnp.concatenate([row] * 4, axis=0), L - (pulses - 1), 1)
+    skewed = [
+        pltpu.roll(jnp.broadcast_to(moved[part : part + 1], (LANES, L)), 0, 1, stride=1, stride_axis=0)
         for part in range(2)
     ]
-    row = jnp.concatenate(row + [jnp.zeros((14, L), F32)], axis=0).astype(BF)
-    moved = pltpu.roll(reversed_lanes(row), L - (pulses - 1), 1)
-    parts = []
-    for part in range(2):
-        spread = jnp.broadcast_to(moved[part : part + 1], (pulses, L))
-        parts.append(pltpu.roll(spread, 0, 1, stride=1, stride_axis=0)[:, :pulses])
-    for part, pair in enumerate(((parts[0], -parts[1]), (parts[1], parts[0]))):
-        for target in range(2):
+    for apart in range(1 - columns, columns):
+        at = apart % pieces * LANES
+        straight, crossed = (skewed[part][:, at : at + LANES] for part in range(2))
+        for target, pair in enumerate(((straight, crossed), (-crossed, straight))):
+            slot = (apart + columns - 1) * 2 + target
+            for part in range(2):
+                columns_held[slot, pl.ds(part, LANES, stride=2), :] = pair[part]
+            block = columns_held[slot].astype(BF)
             for column in range(columns):
-                columns_held[target * columns + column, pl.ds(part, pulses, stride=2), :] = pair[target][
-                    :, column * LANES : (column + 1) * LANES
-                ]
-    for column in range(2 * columns):
-        taps[:, column * LANES : (column + 1) * LANES] = columns_held[column].astype(BF)
+                line = column - apart
+                if 0 <= line < columns:
+                    lane = target * pulses + column * LANES
+                    taps[2 * line * LANES : 2 * (line + 1) * LANES, lane : lane + LANES] = block
     copies = []
     for tile in range(tiles):
         lines = lines_ref[:, tile * rows : (tile + 1) * rows].reshape(sources * rows, LANES)
@@ -330,7 +338,7 @@
         turned = lax.all_to_all(outgoing, "pa", split_axis=0, concat_axis=3, tiled=True)
         rows_in = lax.all_to_all(own_rows, "pa", split_axis=0, concat_axis=0, tiled=True)
         reference_row = jnp.sum(rows_in[:, :8].astype(F32), axis=0).astype(BF).reshape(2, L)
-        return focus_long(turned[0], reference_row)
+        return focus_long(turned[0], reference_row[:, ::-1])
 
     lines = lax.all_to_all(compressed, "pa", split_axis=0, concat_axis=0, tiled=True)
     width = 2 * total_pulses
@@ -339,7 +347,7 @@
         (shape((bin_count * width // LANES, LANES), F32),),
         "va",
         [
-            pltpu.VMEM((width // LANES, width, LANES), F32),
+            pltpu.VMEM((width // LANES * 2 - 2, 2 * LANES, LANES), F32),
             pltpu.VMEM((width, width), BF),
             pltpu.VMEM((bin_count * width // LANES, LANES), F32),
             pltpu.SemaphoreType.DMA((bin_count // LANES,)),

time: 35 us -> 34.9 us (level)
  no operation moved by 1% of the time
where the time goes in v17:
time: 34.9 us; the launch traced here: 34.6 us
  blocking collectives  17.3 us (50%)
  waiting for transfers between devices  9.84 us (28%)
  starting transfers between devices  3.96 us (11%)
  Pallas kernels  2.39 us (7%)
  between operations  0.76 us (2%)
  local copies, waits for them, and re-layouts  0.36 us (1%)
    all_to_all x1, blocking collectives, on_device(): lax.all_to_all(compressed, 'pa', split_axis=0, concat_axis=0, tiled=True)  17.3 us
    ppermute x1, waiting for transfers between devices, on_device(): near = lax.ppermute(near, 'sa', [(1, 2)])  9.84 us
    ppermute x1, starting transfers between devices, on_device(): head = lax.ppermute(head, 'sa', [(2, 3)])  1.84 us
    pallas_call x1, Pallas kernels, on_device(): call(azimuth_kernel, (shape((bin_count * width // LANES, LANES), F32),),...  1.54 us
    ppermute x1, starting transfers between devices, on_device(): near = lax.ppermute(near, 'sa', [(1, 2)])  1.29 us
    ppermute x1, starting transfers between devices, on_device(): tail = lax.ppermute(tail, 'sa', [(0, 1), (1, 3)])  0.83 us
  transfers between devices with their start and end apart: 3, of which 1 were waited for; matrix products, arithmetic and copies ran while one was open for 0% of the time, Pallas kernels for 2%

profile of v17, /device:TPU:2, one launch (start us, length us, event | category | flops | bytes accessed | tf_op | source)
XLA Modules:
  0.0 34.6 jit_solution(12591313162920922236)
XLA Ops:
  0.0 0.0 copy-start
  0.0 0.8 %collective-permute-start.1 = (bf16[32,64,128]{2,1,0:T(8,128)(2,1)S(1)}, bf16[32,64,128]{2,1,0:T(8,128)(2,1)S(1)}, u32[]{:S(2)}, u32[]{:S(2)}) collective-permute-start(bf16[32,64,128]{2,1,0:T(8,128)(2,1)S(1)} %get-tuple-element.21), channel_id=1, source_target_pairs={{0,1},{1,3},{4,5},{5,7},{8,9},{9,11},{12,13},{13,15},{16,17},{17,1... | collective-permute-start | bytes 1572872 | tf_op jit(solution)/shard_map/ppermute | solution.py:309
  0.9 0.3 copy-done
  1.2 0.0 copy-start.1
  1.2 0.0 copy-start.3
  1.2 0.2 shard_map.56
  1.5 0.0 copy-start.2
  1.5 1.8 %collective-permute-start.2 = (bf16[25,64,128]{2,1,0:T(8,128)(2,1)S(1)}, bf16[25,64,128]{2,1,0:T(8,128)(2,1)S(1)}, u32[]{:S(2)}, u32[]{:S(2)}) collective-permute-start(bf16[25,64,128]{2,1,0:T(8,128)(2,1)S(1)} %get-tuple-element.22), channel_id=1, source_target_pairs={{2,3},{6,7},{10,11},{14,15},{18,19},{22,23},{26,27},{30,31}} | collective-permute-start | bytes 1228808 | tf_op jit(solution)/shard_map/ppermute | solution.py:311
  4.0 0.0 copy-done.1
  4.0 0.0 copy-done.3
  4.0 0.0 copy-done.2
  4.0 0.5 %shard_map.57 = (bf16[1280,256]{1,0:T(8,128)(2,1)S(1)}, bf16[8,8,128]{2,1,0:T(8,128)(2,1)S(1)}, f32[8,128]{1,0:T(8,128)S(1)}) custom-call(f32[8,128]{1,0:T(8,128)S(1)} %get-tuple-element.15.turn_in_ref, s32[1]{0:T(128)S(6)} %copy.7.window_ref, s32[4,8]{1,0:T(4,128)S(1)} %copy-done.3, bf16[2,1024]{1,0:T(2,128)(2,1)S(1)} %copy-done.2, ...), custom_call_target="tpu_custom_call" | custom-call | flops 1000 | bytes 1000 | tf_op jit(solution)/shard_map/pallas_call | solution.py:312
  4.5 1.3 %collective-permute-start = (bf16[8,256,128]{2,1,0:T(8,128)(2,1)S(1)}, bf16[8,256,128]{2,1,0:T(8,128)(2,1)S(1)}, u32[]{:S(2)}, u32[]{:S(2)}) collective-permute-start(bf16[8,256,128]{2,1,0:T(8,128)(2,1)S(1)} %get-tuple-element.18), channel_id=1, source_target_pairs={{1,2},{5,6},{9,10},{13,14},{17,18},{21,22},{25,26},{29,30}} | collective-permute-start | bytes 1572872 | tf_op jit(solution)/shard_map/ppermute | solution.py:323
  5.8 0.0 collective-permute-done.2.head_ref
  5.8 0.0 collective-permute-done.1.tail_ref
  5.9 9.8 %collective-permute-done.near_ref = bf16[8,256,128]{2,1,0:T(8,128)(2,1)S(1)} collective-permute-done((bf16[8,256,128]{2,1,0:T(8,128)(2,1)S(1)}, bf16[8,256,128]{2,1,0:T(8,128)(2,1)S(1)}, u32[]{:S(2)}, u32[]{:S(2)}) %collective-permute-start) | collective-permute-done | bytes 524320 | tf_op jit(solution)/shard_map/ppermute | solution.py:323
  15.8 17.3 %all_to_all.5.lines_ref = bf16[8,264,128]{2,1,0:T(8,128)(2,1)S(1)} all-to-all(bf16[8,264,128]{2,1,0:T(8,128)(2,1)S(1)} %shard_map.60), channel_id=1, replica_groups=mesh['pa'=8,'sa'=4] {'pa'}, dimensions={0} | all-to-all | bytes 1081344 | tf_op jit(solution)/shard_map/all_to_all | solution.py:343
  33.1 1.5 %shard_map.61 = f32[2048,128]{1,0:T(8,128)} custom-call(bf16[8,264,128]{2,1,0:T(8,128)(2,1)S(1)} %all_to_all.5.lines_ref), custom_call_target="tpu_custom_call" | custom-call | flops 1000 | bytes 1000 | tf_op jit(solution)/shard_map/pallas_call | solution.py:345
  (4 shorter events, 0.1 us)
Async XLA Ops:
  0.0 1.2 %copy-start = (bf16[32,2,8192]{2,1,0:T(2,128)(2,1)S(1)}, bf16[32,2,8192]{2,1,0:T(2,128)(2,1)}, u32[]{:S(2)}) copy-start(bf16[32,2,8192]{2,1,0:T(2,128)(2,1)} %raw_ref.7) | copy-start | bytes 3145732
  0.0 5.8 %collective-permute-start.1 = (bf16[32,64,128]{2,1,0:T(8,128)(2,1)S(1)}, bf16[32,64,128]{2,1,0:T(8,128)(2,1)S(1)}, u32[]{:S(2)}, u32[]{:S(2)}) collective-permute-start(bf16[32,64,128]{2,1,0:T(8,128)(2,1)S(1)} %get-tuple-element.21), channel_id=1, source_target_pairs={{0,1},{1,3},{4,5},{5,7},{8,9},{9,11},{12,13},{13,15},{16,17},{17,1... | collective-permute-start | bytes 1572872 | tf_op jit(solution)/shard_map/ppermute | solution.py:309
  1.2 2.7 %copy-start.1 = (bf16[8,2,512]{2,1,0:T(2,128)(2,1)S(1)}, bf16[8,2,512]{2,1,0:T(2,128)(2,1)}, u32[]{:S(2)}) copy-start(bf16[8,2,512]{2,1,0:T(2,128)(2,1)} %refs_ref.1) | copy-start | bytes 49156
  1.2 2.8 %copy-start.3 = (s32[4,8]{1,0:T(4,128)S(1)}, s32[4,8]{1,0:T(4,128)}, u32[]{:S(2)}) copy-start(s32[4,8]{1,0:T(4,128)} %index_ref.1) | copy-start | bytes 388
  1.5 2.5 %copy-start.2 = (bf16[2,1024]{1,0:T(2,128)(2,1)S(1)}, bf16[2,1024]{1,0:T(2,128)(2,1)}, u32[]{:S(2)}) copy-start(bf16[2,1024]{1,0:T(2,128)(2,1)} %chirp_ref.1) | copy-start | bytes 12292
  1.5 4.4 %collective-permute-start.2 = (bf16[25,64,128]{2,1,0:T(8,128)(2,1)S(1)}, bf16[25,64,128]{2,1,0:T(8,128)(2,1)S(1)}, u32[]{:S(2)}, u32[]{:S(2)}) collective-permute-start(bf16[25,64,128]{2,1,0:T(8,128)(2,1)S(1)} %get-tuple-element.22), channel_id=1, source_target_pairs={{2,3},{6,7},{10,11},{14,15},{18,19},{22,23},{26,27},{30,31}} | collective-permute-start | bytes 1228808 | tf_op jit(solution)/shard_map/ppermute | solution.py:311
  4.5 11.2 %collective-permute-start = (bf16[8,256,128]{2,1,0:T(8,128)(2,1)S(1)}, bf16[8,256,128]{2,1,0:T(8,128)(2,1)S(1)}, u32[]{:S(2)}, u32[]{:S(2)}) collective-permute-start(bf16[8,256,128]{2,1,0:T(8,128)(2,1)S(1)} %get-tuple-element.18), channel_id=1, source_target_pairs={{1,2},{5,6},{9,10},{13,14},{17,18},{21,22},{25,26},{29,30}} | collective-permute-start | bytes 1572872 | tf_op jit(solution)/shard_map/ppermute | solution.py:323

commit v18 on v17

--- a/solution.py
+++ b/solution.py
@@ -28,7 +28,7 @@
         target[first + t] = source[:, :, t * LANES : (t + 1) * LANES].reshape(shape)
 
 
-def tail_kernel(raw_ref, tail_ref, turn_ref, natural, sems):
+def tail_first_kernel(raw_ref, tail_ref, turn_ref, natural, sems):
     turn_ref[...] = jnp.zeros_like(turn_ref)
     half, rows, _ = tail_ref.shape
     pieces = sems.shape[0]
@@ -49,10 +49,19 @@
             retile(natural.at[own], tail_ref.at[:, pl.ds(at * each * 2, each * 2)], 0, half)
 
 
-def head_kernel(turn_in_ref, raw_ref, head_ref, turn_ref):
+def tail_second_kernel(turn_in_ref, raw_ref, tail_ref, head_ref, turn_ref):
     turn_ref[...] = turn_in_ref[...]
-
-    @pl.when(lax.axis_index("sa") == 2)
+    half, rows, _ = tail_ref.shape
+    pulses = rows // 2
+    sub_index = lax.axis_index("sa")
+
+    @pl.when(sub_index < 2)
+    def _():
+        own = pl.ds(raw_ref.shape[0] - pulses, pulses)
+        width = half * LANES
+        retile(raw_ref.at[own, :, pl.ds(raw_ref.shape[2] - width, width)], tail_ref, 0, half)
+
+    @pl.when(sub_index == 2)
     def _():
         retile(raw_ref, head_ref, 0, head_ref.shape[0])
 
@@ -94,14 +103,13 @@
     rows_ref[...] = jnp.stack(pieces, axis=1).astype(BF)
 
 
-def compress(held, base, taps_ref, out_ref):
+def compress(held, base, taps_ref, out_ref, first_row, tile_rows):
     rows = held.shape[1]
-    targets = out_ref.shape[0]
     tap_tiles = taps_ref.shape[0] // LANES
-    group = 8
-    per_target = out_ref.shape[1] // rows
+    group = 8 if rows > 32 else 512 // rows
+    per_target = out_ref.shape[1] // tile_rows
     even = lax.rem(lax.broadcasted_iota(jnp.int32, (1, 8, LANES), 1), 2) == 0
-    for step in range(targets * per_target // group):
+    for step in range(out_ref.shape[0] * per_target // group):
         blocks = [
             held[pl.ds(base + group * step + t, group)].reshape(group * rows, LANES) for t in range(tap_tiles)
         ]
@@ -110,9 +118,10 @@
         crossed = product[:, LANES:].reshape(-1, 8, LANES)
         total = straight + jnp.where(even, pltpu.roll(crossed, 7, 1), -pltpu.roll(crossed, 1, 1))
         count = group // per_target
-        out_ref[pl.ds(step * count, count), : per_target * rows] = total.astype(BF).reshape(
-            count, per_target * rows, LANES
-        )
+        total = total.astype(BF).reshape(count, per_target, rows, LANES)
+        for tile in range(per_target):
+            at = tile * tile_rows + first_row
+            out_ref[pl.ds(step * count, count), at : at + rows] = total[:, tile]
 
 
 def ahead_kernel(turn_in_ref, window_ref, raw_ref, taps_ref, out_ref, turn_ref, held):
@@ -123,35 +132,58 @@
     def _():
         start = pl.multiple_of(window_ref[0] // LANES * LANES, LANES)
         retile(raw_ref.at[:, :, pl.ds(start, span * LANES)], held, 0, span)
-        compress(held, 0, taps_ref, out_ref)
-
-
-def early_kernel(turn_in_ref, window_ref, raw_ref, tail_ref, head_ref, taps_ref, rows_ref, out_ref, held):
-    half = tail_ref.shape[0]
+        compress(held, 0, taps_ref, out_ref, 0, held.shape[1])
+
+
+def gate_kernel(turn_in_ref, _, turn_ref):
+    turn_ref[...] = turn_in_ref[...]
+
+
+def fill_window(first_pulse, offset, raw_ref, tail_ref, head_ref, held):
+    half, rows, _ = tail_ref.shape
     more = head_ref.shape[0]
     span = half + more - 16
     sub_index = lax.axis_index("sa")
-    offset = window_ref[0] // LANES
+    pulses = pl.ds(first_pulse, rows // 2)
 
     @pl.when(sub_index == 0)
     def _():
         start = pl.multiple_of(offset * LANES, LANES)
-        retile(raw_ref.at[:, :, pl.ds(start, span * LANES)], held, 0, span)
+        retile(raw_ref.at[pulses, :, pl.ds(start, span * LANES)], held, 0, span)
 
     @pl.when(sub_index == 1)
     def _():
         held[:half] = tail_ref[...]
-        retile(raw_ref, held, half, more)
+        retile(raw_ref.at[pulses], held, half, more)
 
     @pl.when(sub_index == 3)
     def _():
         held[:half] = tail_ref[...]
-        held[half:] = head_ref[...]
-
-    @pl.when(sub_index != 2)
-    def _():
-        compress(held, jnp.where(sub_index == 0, 0, offset), taps_ref, out_ref)
-        out_ref[:, out_ref.shape[1] - rows_ref.shape[1] :] = rows_ref[...]
+        held[half:] = head_ref[:, 2 * first_pulse : 2 * first_pulse + rows]
+
+    return jnp.where(sub_index == 0, 0, offset)
+
+
+def first_kernel(turn_in_ref, window_ref, raw_ref, tail_ref, head_ref, taps_ref, out_ref, held):
+    @pl.when(lax.axis_index("sa") != 2)
+    def _():
+        base = fill_window(0, window_ref[0] // LANES, raw_ref, tail_ref, head_ref, held)
+        compress(held, base, taps_ref, out_ref, 0, held.shape[1])
+
+
+def second_kernel(window_ref, raw_ref, tail_ref, head_ref, taps_ref, rows_ref, first_ref, out_ref, held):
+    rows = held.shape[1]
+    tile_rows = head_ref.shape[1]
+    before = tile_rows - rows
+    bins = out_ref.shape[1] - rows_ref.shape[1]
+
+    @pl.when(lax.axis_index("sa") != 2)
+    def _():
+        base = fill_window(before // 2, window_ref[0] // LANES, raw_ref, tail_ref, head_ref, held)
+        for tile in range(bins // tile_rows):
+            out_ref[:, tile * tile_rows : tile * tile_rows + before] = first_ref[:, tile * before : (tile + 1) * before]
+        out_ref[:, bins:] = rows_ref[...]
+        compress(held, base, taps_ref, out_ref.at[:, pl.ds(0, bins)], before, tile_rows)
 
 
 def late_kernel(near_ref, rows_ref, early_ref, out_ref):
@@ -299,15 +331,22 @@
     targets = pulse_devices if short else half // 8
     slot = half // targets * rows
 
+    to_next = [(0, 1), (1, 3)]
+    first_rows = rows // 4 * 3
     tail, turn = call(
-        tail_kernel,
-        (shape((half, rows, LANES), BF), token),
+        tail_first_kernel,
+        (shape((half, first_rows, LANES), BF), token),
         "avv",
-        [pltpu.VMEM((pulses, 2, half * LANES), BF), pltpu.SemaphoreType.DMA((4,))],
+        [pltpu.VMEM((first_rows // 2, 2, half * LANES), BF), pltpu.SemaphoreType.DMA((3,))],
         53,
     )(raw_echo)
-    tail = lax.ppermute(tail, "sa", [(0, 1), (1, 3)])
-    head, turn = call(head_kernel, (shape((span - half + 16, rows, LANES), BF), token), "vvvv")(turn, raw_echo)
+    tail_first = lax.ppermute(tail, "sa", to_next)
+    tail, head, turn = call(
+        tail_second_kernel,
+        (shape((half, rows - first_rows, LANES), BF), shape((span - half + 16, rows, LANES), BF), token),
+        "vvvvv",
+    )(turn, raw_echo)
+    tail_second = lax.ppermute(tail, "sa", to_next)
     head = lax.ppermute(head, "sa", [(2, 3)])
     taps, own_rows, turn = call(
         prep_kernel,
@@ -323,13 +362,21 @@
     near = lax.ppermute(near, "sa", [(1, 2)])
     extra = own_rows if short else jnp.zeros((targets, EXTRA, LANES), BF)
     made = shape((targets, slot + EXTRA, LANES), BF)
+    (turn,) = call(gate_kernel, (token,), "vav", flops=10**10)(turn, tail_first)
+    (first,) = call(
+        first_kernel,
+        (shape((targets, slot // rows * first_rows, LANES), BF),),
+        "vsvvvvv",
+        [pltpu.VMEM((span + 16, first_rows, LANES), BF)],
+        flops=10**10,
+    )(turn, window_start, raw_echo, tail_first, head, taps)
     (early,) = call(
-        early_kernel,
+        second_kernel,
         (made,),
-        "vsvvvvvv",
-        [pltpu.VMEM((span + 16, rows, LANES), BF)],
+        "svvvvvvv",
+        [pltpu.VMEM((span + 16, rows - first_rows, LANES), BF)],
         flops=10**10,
-    )(turn, window_start, raw_echo, tail, head, taps, extra)
+    )(window_start, raw_echo, tail_second, head, taps, extra, first)
     (compressed,) = call(late_kernel, (made,), "vvvv")(near, extra, early)
 
     if not short:

time: 34.9 us -> 35.8 us (1.026)
  starting transfers between devices: 3.96 us -> 5.23 us
  blocking collectives: 17.3 us -> 16.9 us
    ppermute x1 -> x2, starting transfers between devices: 0.83 us -> 1.49 us  [the longest x1 0.82 us: on_device(): tail_first = lax.ppermute(tail, 'sa', to_next)]
    ppermute x1, starting transfers between devices: 1.84 us -> 2.45 us  [on_device(): head = lax.ppermute(head, 'sa', [(2, 3)])]
    all_to_all x1, blocking collectives: 17.3 us -> 16.9 us  [on_device(): lax.all_to_all(compressed, 'pa', split_axis=0, concat_axis=0, tiled=True)]
  transfers between devices with their start and end apart: 3 -> 4, of which waited for: 1 -> 1; matrix products, arithmetic and copies ran while one was open for 0% -> 0% of each run, Pallas kernels for 2% -> 2%
where the time goes in v18:
time: 35.8 us; the launch traced here: 35.6 us
  blocking collectives  16.9 us (47%)
  waiting for transfers between devices  9.83 us (27%)
  starting transfers between devices  5.23 us (15%)
  Pallas kernels  2.38 us (7%)
  between operations  0.8 us (2%)
  local copies, waits for them, and re-layouts  0.38 us (1%)
    all_to_all x1, blocking collectives, on_device(): lax.all_to_all(compressed, 'pa', split_axis=0, concat_axis=0, tiled=True)  16.9 us
    ppermute x1, waiting for transfers between devices, on_device(): near = lax.ppermute(near, 'sa', [(1, 2)])  9.83 us
    ppermute x1, starting transfers between devices, on_device(): head = lax.ppermute(head, 'sa', [(2, 3)])  2.45 us
    pallas_call x1, Pallas kernels, on_device(): call(azimuth_kernel, (shape((bin_count * width // LANES, LANES), F32),),...  1.54 us
    ppermute x1, starting transfers between devices, on_device(): near = lax.ppermute(near, 'sa', [(1, 2)])  1.29 us
    ppermute x1, starting transfers between devices, on_device(): tail_first = lax.ppermute(tail, 'sa', to_next)  0.82 us
  transfers between devices with their start and end apart: 4, of which 1 were waited for; matrix products, arithmetic and copies ran while one was open for 0% of the time, Pallas kernels for 2%

profile of v18, /device:TPU:2, one launch (start us, length us, event | category | flops | bytes accessed | tf_op | source)
XLA Modules:
  0.0 35.6 jit_solution(17566511420067915693)
XLA Ops:
  0.0 0.0 copy-start
  0.0 0.8 %collective-permute-start.3 = (bf16[32,48,128]{2,1,0:T(8,128)(2,1)S(1)}, bf16[32,48,128]{2,1,0:T(8,128)(2,1)S(1)}, u32[]{:S(2)}, u32[]{:S(2)}) collective-permute-start(bf16[32,48,128]{2,1,0:T(8,128)(2,1)S(1)} %get-tuple-element.24), channel_id=1, source_target_pairs={{0,1},{1,3},{4,5},{5,7},{8,9},{9,11},{12,13},{13,15},{16,17},{17,1... | collective-permute-start | bytes 1179656 | tf_op jit(solution)/shard_map/ppermute | solution.py:343
  0.9 0.4 %copy-done = bf16[32,2,8192]{2,1,0:T(2,128)(2,1)S(1)} copy-done((bf16[32,2,8192]{2,1,0:T(2,128)(2,1)S(1)}, bf16[32,2,8192]{2,1,0:T(2,128)(2,1)}, u32[]{:S(2)}) %copy-start) | copy-done | bytes 1048600
  1.2 0.0 copy-start.1
  1.2 0.2 shard_map.56
  1.5 0.0 copy-start.2
  1.5 0.7 %collective-permute-start.1 = (bf16[32,16,128]{2,1,0:T(8,128)(2,1)S(1)}, bf16[32,16,128]{2,1,0:T(8,128)(2,1)S(1)}, u32[]{:S(2)}, u32[]{:S(2)}) collective-permute-start(bf16[32,16,128]{2,1,0:T(8,128)(2,1)S(1)} %get-tuple-element.21), channel_id=1, source_target_pairs={{0,1},{1,3},{4,5},{5,7},{8,9},{9,11},{12,13},{13,15},{16,17},{17,1... | collective-permute-start | bytes 393224 | tf_op jit(solution)/shard_map/ppermute | solution.py:349
  2.1 0.0 copy-start.3
  2.2 2.5 %collective-permute-start.2 = (bf16[25,64,128]{2,1,0:T(8,128)(2,1)S(1)}, bf16[25,64,128]{2,1,0:T(8,128)(2,1)S(1)}, u32[]{:S(2)}, u32[]{:S(2)}) collective-permute-start(bf16[25,64,128]{2,1,0:T(8,128)(2,1)S(1)} %get-tuple-element.22), channel_id=1, source_target_pairs={{2,3},{6,7},{10,11},{14,15},{18,19},{22,23},{26,27},{30,31}} | collective-permute-start | bytes 1228808 | tf_op jit(solution)/shard_map/ppermute | solution.py:350
  5.3 0.0 copy-done.1
  5.3 0.0 copy-done.2
  5.3 0.0 copy-done.3
  5.3 0.5 %shard_map.57 = (bf16[1280,256]{1,0:T(8,128)(2,1)S(1)}, bf16[8,8,128]{2,1,0:T(8,128)(2,1)S(1)}, f32[8,128]{1,0:T(8,128)S(1)}) custom-call(f32[8,128]{1,0:T(8,128)S(1)} %get-tuple-element.16.turn_in_ref, s32[1]{0:T(128)S(6)} %copy.7.window_ref, s32[4,8]{1,0:T(4,128)S(1)} %copy-done.3, bf16[2,1024]{1,0:T(2,128)(2,1)S(1)} %copy-done.2, ...), custom_call_target="tpu_custom_call" | custom-call | flops 1000 | bytes 1000 | tf_op jit(solution)/shard_map/pallas_call | solution.py:351
  5.8 1.3 %collective-permute-start = (bf16[8,256,128]{2,1,0:T(8,128)(2,1)S(1)}, bf16[8,256,128]{2,1,0:T(8,128)(2,1)S(1)}, u32[]{:S(2)}, u32[]{:S(2)}) collective-permute-start(bf16[8,256,128]{2,1,0:T(8,128)(2,1)S(1)} %get-tuple-element.19), channel_id=1, source_target_pairs={{1,2},{5,6},{9,10},{13,14},{17,18},{21,22},{25,26},{29,30}} | collective-permute-start | bytes 1572872 | tf_op jit(solution)/shard_map/ppermute | solution.py:362
  7.1 0.0 collective-permute-done.3._.tail_ref
  7.2 0.0 collective-permute-done.2.head_ref
  7.2 0.0 collective-permute-done.1.tail_ref
  7.2 9.8 %collective-permute-done.near_ref = bf16[8,256,128]{2,1,0:T(8,128)(2,1)S(1)} collective-permute-done((bf16[8,256,128]{2,1,0:T(8,128)(2,1)S(1)}, bf16[8,256,128]{2,1,0:T(8,128)(2,1)S(1)}, u32[]{:S(2)}, u32[]{:S(2)}) %collective-permute-start) | collective-permute-done | bytes 524320 | tf_op jit(solution)/shard_map/ppermute | solution.py:362
  17.1 16.9 %all_to_all.5.lines_ref = bf16[8,264,128]{2,1,0:T(8,128)(2,1)S(1)} all-to-all(bf16[8,264,128]{2,1,0:T(8,128)(2,1)S(1)} %shard_map.62), channel_id=1, replica_groups=mesh['pa'=8,'sa'=4] {'pa'}, dimensions={0} | all-to-all | bytes 1081344 | tf_op jit(solution)/shard_map/all_to_all | solution.py:390
  34.0 1.5 %shard_map.63 = f32[2048,128]{1,0:T(8,128)} custom-call(bf16[8,264,128]{2,1,0:T(8,128)(2,1)S(1)} %all_to_all.5.lines_ref), custom_call_target="tpu_custom_call" | custom-call | flops 1000 | bytes 1000 | tf_op jit(solution)/shard_map/pallas_call | solution.py:392
  (6 shorter events, 0.1 us)
Async XLA Ops:
  0.0 1.2 %copy-start = (bf16[32,2,8192]{2,1,0:T(2,128)(2,1)S(1)}, bf16[32,2,8192]{2,1,0:T(2,128)(2,1)}, u32[]{:S(2)}) copy-start(bf16[32,2,8192]{2,1,0:T(2,128)(2,1)} %raw_ref.9) | copy-start | bytes 3145732
  0.0 7.1 %collective-permute-start.3 = (bf16[32,48,128]{2,1,0:T(8,128)(2,1)S(1)}, bf16[32,48,128]{2,1,0:T(8,128)(2,1)S(1)}, u32[]{:S(2)}, u32[]{:S(2)}) collective-permute-start(bf16[32,48,128]{2,1,0:T(8,128)(2,1)S(1)} %get-tuple-element.24), channel_id=1, source_target_pairs={{0,1},{1,3},{4,5},{5,7},{8,9},{9,11},{12,13},{13,15},{16,17},{17,1... | collective-permute-start | bytes 1179656 | tf_op jit(solution)/shard_map/ppermute | solution.py:343
  1.2 4.0 %copy-start.1 = (bf16[8,2,512]{2,1,0:T(2,128)(2,1)S(1)}, bf16[8,2,512]{2,1,0:T(2,128)(2,1)}, u32[]{:S(2)}) copy-start(bf16[8,2,512]{2,1,0:T(2,128)(2,1)} %refs_ref.1) | copy-start | bytes 49156
  1.5 3.8 %copy-start.2 = (bf16[2,1024]{1,0:T(2,128)(2,1)S(1)}, bf16[2,1024]{1,0:T(2,128)(2,1)}, u32[]{:S(2)}) copy-start(bf16[2,1024]{1,0:T(2,128)(2,1)} %chirp_ref.1) | copy-start | bytes 12292
  1.5 5.7 %collective-permute-start.1 = (bf16[32,16,128]{2,1,0:T(8,128)(2,1)S(1)}, bf16[32,16,128]{2,1,0:T(8,128)(2,1)S(1)}, u32[]{:S(2)}, u32[]{:S(2)}) collective-permute-start(bf16[32,16,128]{2,1,0:T(8,128)(2,1)S(1)} %get-tuple-element.21), channel_id=1, source_target_pairs={{0,1},{1,3},{4,5},{5,7},{8,9},{9,11},{12,13},{13,15},{16,17},{17,1... | collective-permute-start | bytes 393224 | tf_op jit(solution)/shard_map/ppermute | solution.py:349
  2.1 3.1 %copy-start.3 = (s32[4,8]{1,0:T(4,128)S(1)}, s32[4,8]{1,0:T(4,128)}, u32[]{:S(2)}) copy-start(s32[4,8]{1,0:T(4,128)} %index_ref.1) | copy-start | bytes 388
  2.2 5.0 %collective-permute-start.2 = (bf16[25,64,128]{2,1,0:T(8,128)(2,1)S(1)}, bf16[25,64,128]{2,1,0:T(8,128)(2,1)S(1)}, u32[]{:S(2)}, u32[]{:S(2)}) collective-permute-start(bf16[25,64,128]{2,1,0:T(8,128)(2,1)S(1)} %get-tuple-element.22), channel_id=1, source_target_pairs={{2,3},{6,7},{10,11},{14,15},{18,19},{22,23},{26,27},{30,31}} | collective-permute-start | bytes 1228808 | tf_op jit(solution)/shard_map/ppermute | solution.py:350
  5.8 11.2 %collective-permute-start = (bf16[8,256,128]{2,1,0:T(8,128)(2,1)S(1)}, bf16[8,256,128]{2,1,0:T(8,128)(2,1)S(1)}, u32[]{:S(2)}, u32[]{:S(2)}) collective-permute-start(bf16[8,256,128]{2,1,0:T(8,128)(2,1)S(1)} %get-tuple-element.19), channel_id=1, source_target_pairs={{1,2},{5,6},{9,10},{13,14},{17,18},{21,22},{25,26},{29,30}} | collective-permute-start | bytes 1572872 | tf_op jit(solution)/shard_map/ppermute | solution.py:362

commit v19 on v18

--- a/solution.py
+++ b/solution.py
@@ -49,24 +49,19 @@
             retile(natural.at[own], tail_ref.at[:, pl.ds(at * each * 2, each * 2)], 0, half)
 
 
-def tail_second_kernel(turn_in_ref, raw_ref, tail_ref, head_ref, turn_ref):
+def tail_second_kernel(turn_in_ref, raw_ref, tail_ref, turn_ref):
     turn_ref[...] = turn_in_ref[...]
     half, rows, _ = tail_ref.shape
     pulses = rows // 2
-    sub_index = lax.axis_index("sa")
-
-    @pl.when(sub_index < 2)
+
+    @pl.when(lax.axis_index("sa") < 2)
     def _():
         own = pl.ds(raw_ref.shape[0] - pulses, pulses)
         width = half * LANES
         retile(raw_ref.at[own, :, pl.ds(raw_ref.shape[2] - width, width)], tail_ref, 0, half)
 
-    @pl.when(sub_index == 2)
-    def _():
-        retile(raw_ref, head_ref, 0, head_ref.shape[0])
-
-
-def prep_kernel(turn_in_ref, window_ref, index_ref, chirp_ref, refs_ref, taps_ref, rows_ref, turn_ref):
+
+def range_taps_kernel(turn_in_ref, window_ref, chirp_ref, taps_ref, turn_ref):
     turn_ref[...] = turn_in_ref[...]
     taps = chirp_ref.shape[1]
     blocks = taps_ref.shape[0] // LANES
@@ -85,6 +80,10 @@
             taps_ref[t * LANES : (t + 1) * LANES, part * LANES : (part + 1) * LANES] = skewed[
                 :, first : first + LANES
             ].astype(BF)
+
+
+def rows_kernel(turn_in_ref, index_ref, refs_ref, rows_ref, turn_ref):
+    turn_ref[...] = turn_in_ref[...]
     own = refs_ref.shape[0]
     groups, targets = index_ref.shape
     first_row = lax.axis_index("pa") * own
@@ -134,14 +133,22 @@
         retile(raw_ref.at[:, :, pl.ds(start, span * LANES)], held, 0, span)
         compress(held, 0, taps_ref, out_ref, 0, held.shape[1])
 
+    @pl.when(lax.axis_index("sa") == 2)
+    def _():
+        rows = held.shape[1]
+        per_target = out_ref.shape[1] // rows
+        for t in range(out_ref.shape[0] * per_target):
+            tile = raw_ref[:, :, t * LANES : (t + 1) * LANES].reshape(rows, LANES)
+            out_ref[t // per_target, t % per_target * rows : (t % per_target + 1) * rows] = tile
+
 
 def gate_kernel(turn_in_ref, _, turn_ref):
     turn_ref[...] = turn_in_ref[...]
 
 
-def fill_window(first_pulse, offset, raw_ref, tail_ref, head_ref, held):
+def fill_own(first_pulse, offset, raw_ref, tail_ref, held):
     half, rows, _ = tail_ref.shape
-    more = head_ref.shape[0]
+    more = held.shape[0] - half
     span = half + more - 16
     sub_index = lax.axis_index("sa")
     pulses = pl.ds(first_pulse, rows // 2)
@@ -156,48 +163,71 @@
         held[:half] = tail_ref[...]
         retile(raw_ref.at[pulses], held, half, more)
 
+
+def fill_far(first_pulse, tail_ref, near_ref, held):
+    half, rows, _ = tail_ref.shape
+    tile_rows = near_ref.shape[1] * near_ref.shape[0] // half
+    per_target = near_ref.shape[1] // tile_rows
+    held[:half] = tail_ref[...]
+    for t in range(held.shape[0] - half):
+        at = t % per_target * tile_rows + 2 * first_pulse
+        held[half + t] = near_ref[t // per_target, at : at + rows]
+
+
+def first_own_kernel(turn_in_ref, window_ref, raw_ref, tail_ref, taps_ref, out_ref, turn_ref, held):
+    turn_ref[...] = turn_in_ref[...]
+    sub_index = lax.axis_index("sa")
+    offset = window_ref[0] // LANES
+
+    @pl.when(sub_index < 2)
+    def _():
+        fill_own(0, offset, raw_ref, tail_ref, held)
+        compress(held, jnp.where(sub_index == 0, 0, offset), taps_ref, out_ref, 0, held.shape[1])
+
+
+def first_far_kernel(turn_in_ref, window_ref, tail_ref, near_ref, taps_ref, own_ref, out_ref, turn_ref, held):
+    turn_ref[...] = turn_in_ref[...]
+    sub_index = lax.axis_index("sa")
+
+    @pl.when(sub_index < 2)
+    def _():
+        out_ref[...] = own_ref[...]
+
     @pl.when(sub_index == 3)
     def _():
-        held[:half] = tail_ref[...]
-        held[half:] = head_ref[:, 2 * first_pulse : 2 * first_pulse + rows]
-
-    return jnp.where(sub_index == 0, 0, offset)
-
-
-def first_kernel(turn_in_ref, window_ref, raw_ref, tail_ref, head_ref, taps_ref, out_ref, held):
-    @pl.when(lax.axis_index("sa") != 2)
-    def _():
-        base = fill_window(0, window_ref[0] // LANES, raw_ref, tail_ref, head_ref, held)
-        compress(held, base, taps_ref, out_ref, 0, held.shape[1])
-
-
-def second_kernel(window_ref, raw_ref, tail_ref, head_ref, taps_ref, rows_ref, first_ref, out_ref, held):
+        fill_far(0, tail_ref, near_ref, held)
+        compress(held, window_ref[0] // LANES, taps_ref, out_ref, 0, held.shape[1])
+
+
+def second_kernel(
+    turn_in_ref, window_ref, raw_ref, tail_ref, near_ref, taps_ref, rows_ref, first_ref, out_ref, held
+):
     rows = held.shape[1]
-    tile_rows = head_ref.shape[1]
+    bins = near_ref.shape[1]
+    tile_rows = 2 * raw_ref.shape[0]
     before = tile_rows - rows
-    bins = out_ref.shape[1] - rows_ref.shape[1]
-
-    @pl.when(lax.axis_index("sa") != 2)
-    def _():
-        base = fill_window(before // 2, window_ref[0] // LANES, raw_ref, tail_ref, head_ref, held)
+    sub_index = lax.axis_index("sa")
+    offset = window_ref[0] // LANES
+    out_ref[:, bins:] = rows_ref[...]
+
+    @pl.when(sub_index == 2)
+    def _():
+        out_ref[:, :bins] = near_ref[...]
+
+    @pl.when(sub_index < 2)
+    def _():
+        fill_own(before // 2, offset, raw_ref, tail_ref, held)
+
+    @pl.when(sub_index == 3)
+    def _():
+        fill_far(before // 2, tail_ref, near_ref, held)
+
+    @pl.when(sub_index != 2)
+    def _():
         for tile in range(bins // tile_rows):
             out_ref[:, tile * tile_rows : tile * tile_rows + before] = first_ref[:, tile * before : (tile + 1) * before]
-        out_ref[:, bins:] = rows_ref[...]
+        base = jnp.where(sub_index == 0, 0, offset)
         compress(held, base, taps_ref, out_ref.at[:, pl.ds(0, bins)], before, tile_rows)
-
-
-def late_kernel(near_ref, rows_ref, early_ref, out_ref):
-    bins = near_ref.shape[1]
-    sub_index = lax.axis_index("sa")
-
-    @pl.when(sub_index != 2)
-    def _():
-        out_ref[...] = early_ref[...]
-
-    @pl.when(sub_index == 2)
-    def _():
-        out_ref[:, :bins] = near_ref[...]
-        out_ref[:, bins:] = rows_ref[...]
 
 
 def azimuth_kernel(lines_ref, out_ref, columns_held, taps, made, sems):
@@ -341,43 +371,38 @@
         53,
     )(raw_echo)
     tail_first = lax.ppermute(tail, "sa", to_next)
-    tail, head, turn = call(
-        tail_second_kernel,
-        (shape((half, rows - first_rows, LANES), BF), shape((span - half + 16, rows, LANES), BF), token),
-        "vvvvv",
+    tail, turn = call(
+        tail_second_kernel, (shape((half, rows - first_rows, LANES), BF), token), "vvvv"
     )(turn, raw_echo)
     tail_second = lax.ppermute(tail, "sa", to_next)
-    head = lax.ppermute(head, "sa", [(2, 3)])
-    taps, own_rows, turn = call(
-        prep_kernel,
-        (shape((tap_tiles * LANES, 2 * LANES), BF), shape((pulse_devices, EXTRA, LANES), BF), token),
-        "vsvvvvvv",
-    )(turn, window_start, migration_index, chirp_replica, azimuth_refs)
+    taps, turn = call(range_taps_kernel, (shape((tap_tiles * LANES, 2 * LANES), BF), token), "vsvvv")(
+        turn, window_start, chirp_replica
+    )
     near, turn = call(
-        ahead_kernel,
-        (shape((targets, slot, LANES), BF), token),
-        "vsvvvv",
-        [pltpu.VMEM((span, rows, LANES), BF)],
+        ahead_kernel, (shape((targets, slot, LANES), BF), token), "vsvvvv", [pltpu.VMEM((span, rows, LANES), BF)]
     )(turn, window_start, raw_echo, taps)
-    near = lax.ppermute(near, "sa", [(1, 2)])
+    near = lax.ppermute(near, "sa", [(1, 2), (2, 3)])
+    (turn,) = call(gate_kernel, (token,), "vav", flops=10**10)(turn, tail_first)
+    own_rows, turn = call(rows_kernel, (shape((pulse_devices, EXTRA, LANES), BF), token), "vvvvv")(
+        turn, migration_index, azimuth_refs
+    )
     extra = own_rows if short else jnp.zeros((targets, EXTRA, LANES), BF)
     made = shape((targets, slot + EXTRA, LANES), BF)
-    (turn,) = call(gate_kernel, (token,), "vav", flops=10**10)(turn, tail_first)
-    (first,) = call(
-        first_kernel,
-        (shape((targets, slot // rows * first_rows, LANES), BF),),
-        "vsvvvvv",
-        [pltpu.VMEM((span + 16, first_rows, LANES), BF)],
-        flops=10**10,
-    )(turn, window_start, raw_echo, tail_first, head, taps)
-    (early,) = call(
+    first_shape = shape((targets, slot // rows * first_rows, LANES), BF)
+    first_held = pltpu.VMEM((span + 16, first_rows, LANES), BF)
+    first, turn = call(first_own_kernel, (first_shape, token), "vsvvvvv", [first_held], flops=10**10)(
+        turn, window_start, raw_echo, tail_first, taps
+    )
+    first, turn = call(first_far_kernel, (first_shape, token), "vsvvvvvv", [first_held], flops=10**10)(
+        turn, window_start, tail_first, near, taps, first
+    )
+    (compressed,) = call(
         second_kernel,
         (made,),
-        "svvvvvvv",
+        "vsvvvvvvv",
         [pltpu.VMEM((span + 16, rows - first_rows, LANES), BF)],
         flops=10**10,
-    )(window_start, raw_echo, tail_second, head, taps, extra, first)
-    (compressed,) = call(late_kernel, (made,), "vvvv")(near, extra, early)
+    )(turn, window_start, raw_echo, tail_second, near, taps, extra, first)
 
     if not short:
         kept = compressed[:, :-EXTRA].reshape(half, pulses, 2, LANES).transpose(0, 3, 2, 1)

time: 35.8 us -> 35.9 us (level)
  the two profiles are of different devices: /device:TPU:2 before, /device:TPU:1 now
where the time goes in v19:
time: 35.9 us; the launch traced here: 35.6 us
  blocking collectives  16.9 us (47%)
  Pallas kernels  7.56 us (21%)
  starting transfers between devices  6.12 us (17%)
  waiting for transfers between devices  3.46 us (10%)
  between operations  0.8 us (2%)
  local copies, waits for them, and re-layouts  0.71 us (2%)
    all_to_all x1, blocking collectives, on_device(): lax.all_to_all(compressed, 'pa', split_axis=0, concat_axis=0, tiled=True)  16.9 us
    ppermute x1, waiting for transfers between devices, on_device(): near = lax.ppermute(near, 'sa', [(1, 2), (2, 3)])  3.46 us
    ppermute x1, starting transfers between devices, on_device(): tail_first = lax.ppermute(tail, 'sa', to_next)  2.87 us
    ppermute x1, starting transfers between devices, on_device(): tail_second = lax.ppermute(tail, 'sa', to_next)  1.92 us
    pallas_call x1, Pallas kernels, on_device(): call(ahead_kernel, (shape((targets, slot, LANES), BF), token), 'vsvvvv',...  1.67 us
    pallas_call x1, Pallas kernels, on_device(): call(azimuth_kernel, (shape((bin_count * width // LANES, LANES), F32),),...  1.54 us
    pallas_call x1, Pallas kernels, on_device(): call(first_own_kernel, (first_shape, token), 'vsvvvvv', [first_held], flo...  1.4 us
    ppermute x1, starting transfers between devices, on_device(): near = lax.ppermute(near, 'sa', [(1, 2), (2, 3)])  1.32 us
  transfers between devices with their start and end apart: 3, of which 1 were waited for; matrix products, arithmetic and copies ran while one was open for 0% of the time, Pallas kernels for 12%

profile of v19, /device:TPU:1, one launch (start us, length us, event | category | flops | bytes accessed | tf_op | source)
XLA Modules:
  0.0 35.6 jit_solution(10465719214250561924)
XLA Ops:
  0.0 0.0 copy-start
  0.0 1.2 %shard_map.55 = (bf16[32,48,128]{2,1,0:T(8,128)(2,1)S(1)}, f32[8,128]{1,0:T(8,128)S(1)}) custom-call(bf16[32,2,8192]{2,1,0:T(2,128)(2,1)} %raw_ref.9), custom_call_target="tpu_custom_call" | custom-call | flops 1000 | bytes 1000 | tf_op jit(solution)/shard_map/pallas_call | solution.py:366
  1.2 2.9 %collective-permute-start = (bf16[32,48,128]{2,1,0:T(8,128)(2,1)S(1)}, bf16[32,48,128]{2,1,0:T(8,128)(2,1)S(1)}, u32[]{:S(2)}, u32[]{:S(2)}) collective-permute-start(bf16[32,48,128]{2,1,0:T(8,128)(2,1)S(1)} %get-tuple-element.24), channel_id=1, source_target_pairs={{0,1},{1,3},{4,5},{5,7},{8,9},{9,11},{12,13},{13,15},{16,17},{17,1... | collective-permute-start | bytes 1179656 | tf_op jit(solution)/shard_map/ppermute | solution.py:373
  4.1 0.0 copy-done
  4.1 0.1 shard_map.56
  4.2 0.0 copy-start.2
  4.2 1.9 %collective-permute-start.2 = (bf16[32,16,128]{2,1,0:T(8,128)(2,1)S(1)}, bf16[32,16,128]{2,1,0:T(8,128)(2,1)S(1)}, u32[]{:S(2)}, u32[]{:S(2)}) collective-permute-start(bf16[32,16,128]{2,1,0:T(8,128)(2,1)S(1)} %get-tuple-element.30), channel_id=1, source_target_pairs={{0,1},{1,3},{4,5},{5,7},{8,9},{9,11},{12,13},{13,15},{16,17},{17,1... | collective-permute-start | bytes 393224 | tf_op jit(solution)/shard_map/ppermute | solution.py:377
  6.8 0.0 copy-done.2
  6.8 0.5 %shard_map.57 = (bf16[1280,256]{1,0:T(8,128)(2,1)S(1)}, f32[8,128]{1,0:T(8,128)S(1)}) custom-call(f32[8,128]{1,0:T(8,128)S(1)} %get-tuple-element.20.turn_in_ref, s32[1]{0:T(128)S(6)} %copy.7.window_ref, bf16[2,1024]{1,0:T(2,128)(2,1)S(1)} %copy-done.2), custom_call_target="tpu_custom_call" | custom-call | flops 1000 | bytes 1000 | tf_op jit(solution)/shard_map/pallas_call | solution.py:378
  7.3 1.7 %shard_map.58 = (bf16[8,256,128]{2,1,0:T(8,128)(2,1)S(1)}, f32[8,128]{1,0:T(8,128)S(1)}) custom-call(f32[8,128]{1,0:T(8,128)S(1)} %get-tuple-element.21.turn_in_ref, s32[1]{0:T(128)S(6)} %copy.7.window_ref, bf16[32,2,8192]{2,1,0:T(2,128)(2,1)S(1)} %copy-done, bf16[1280,256]{1,0:T(8,128)(2,1)S(1)} %get-tuple-element.22.taps_ref), custom_call_target="tpu_custom_call" | custom-call | flops 1000 | bytes 1000 | tf_op jit(solution)/shard_map/pallas_call | solution.py:381
  9.0 1.3 %collective-permute-start.1 = (bf16[8,256,128]{2,1,0:T(8,128)(2,1)S(1)}, bf16[8,256,128]{2,1,0:T(8,128)(2,1)S(1)}, u32[]{:S(2)}, u32[]{:S(2)}) collective-permute-start(bf16[8,256,128]{2,1,0:T(8,128)(2,1)S(1)} %get-tuple-element.27), channel_id=1, source_target_pairs={{1,2},{2,3},{5,6},{6,7},{9,10},{10,11},{13,14},{14,15},{17,18},{18... | collective-permute-start | bytes 1572872 | tf_op jit(solution)/shard_map/ppermute | solution.py:384
  10.3 0.0 collective-permute-done._.tail_ref
  10.4 0.0 copy-start.1
  10.4 0.0 copy-start.3
  10.4 0.7 %copy-done.1 = bf16[8,2,512]{2,1,0:T(2,128)(2,1)S(1)} copy-done((bf16[8,2,512]{2,1,0:T(2,128)(2,1)S(1)}, bf16[8,2,512]{2,1,0:T(2,128)(2,1)}, u32[]{:S(2)}) %copy-start.1) | copy-done | bytes 16408
  11.1 0.0 copy-done.3
  11.1 0.5 %shard_map.60 = (bf16[8,8,128]{2,1,0:T(8,128)(2,1)S(1)}, f32[8,128]{1,0:T(8,128)S(1)}) custom-call(f32[8,128]{1,0:T(8,128)S(1)} %shard_map.59.turn_in_ref, s32[4,8]{1,0:T(4,128)S(1)} %copy-done.3, bf16[8,2,512]{2,1,0:T(2,128)(2,1)S(1)} %copy-done.1), custom_call_target="tpu_custom_call" | custom-call | flops 1000 | bytes 1000 | tf_op jit(solution)/shard_map/pallas_call | solution.py:386
  11.6 1.4 %shard_map.61 = (bf16[8,192,128]{2,1,0:T(8,128)(2,1)S(1)}, f32[8,128]{1,0:T(8,128)S(1)}) custom-call(f32[8,128]{1,0:T(8,128)S(1)} %get-tuple-element.25.turn_in_ref, s32[1]{0:T(128)S(6)} %copy.7.window_ref, bf16[32,2,8192]{2,1,0:T(2,128)(2,1)S(1)} %copy-done, bf16[32,48,128]{2,1,0:T(8,128)(2,1)S(1)} %collective-permute-done._.tail_ref, ...), custom_call_target="tpu_custom_call" | custom-call | flops 10000000000 | bytes 1000 | tf_op jit(solution)/shard_map/pallas_call | solution.py:393
  13.0 3.5 %collective-permute-done.1.near_ref = bf16[8,256,128]{2,1,0:T(8,128)(2,1)S(1)} collective-permute-done((bf16[8,256,128]{2,1,0:T(8,128)(2,1)S(1)}, bf16[8,256,128]{2,1,0:T(8,128)(2,1)S(1)}, u32[]{:S(2)}, u32[]{:S(2)}) %collective-permute-start.1) | collective-permute-done | bytes 524320 | tf_op jit(solution)/shard_map/ppermute | solution.py:384
  16.5 0.0 collective-permute-done.2.tail_ref
  16.5 0.6 %shard_map.63 = bf16[8,264,128]{2,1,0:T(8,128)(2,1)S(1)} custom-call(f32[8,128]{1,0:T(8,128)S(1)} %get-tuple-element.29.turn_in_ref, s32[1]{0:T(128)S(6)} %copy.7.window_ref, bf16[32,2,8192]{2,1,0:T(2,128)(2,1)S(1)} %copy-done, bf16[32,16,128]{2,1,0:T(8,128)(2,1)S(1)} %collective-permute-done.2.tail_ref, ...), custom_call_target="tpu_custom_call" | custom-call | flops 10000000000 | bytes 1000 | tf_op jit(solution)/shard_map/pallas_call | solution.py:399
  17.1 16.9 %all_to_all.5.lines_ref = bf16[8,264,128]{2,1,0:T(8,128)(2,1)S(1)} all-to-all(bf16[8,264,128]{2,1,0:T(8,128)(2,1)S(1)} %shard_map.63), channel_id=1, replica_groups=mesh['pa'=8,'sa'=4] {'pa'}, dimensions={0} | all-to-all | bytes 1081344 | tf_op jit(solution)/shard_map/all_to_all | solution.py:415
  34.0 1.5 %shard_map.64 = f32[2048,128]{1,0:T(8,128)} custom-call(bf16[8,264,128]{2,1,0:T(8,128)(2,1)S(1)} %all_to_all.5.lines_ref), custom_call_target="tpu_custom_call" | custom-call | flops 1000 | bytes 1000 | tf_op jit(solution)/shard_map/pallas_call | solution.py:417
  (2 shorter events, 0.0 us)
Async XLA Ops:
  0.0 4.1 %copy-start = (bf16[32,2,8192]{2,1,0:T(2,128)(2,1)S(1)}, bf16[32,2,8192]{2,1,0:T(2,128)(2,1)}, u32[]{:S(2)}) copy-start(bf16[32,2,8192]{2,1,0:T(2,128)(2,1)} %raw_ref.9) | copy-start | bytes 3145732
  1.2 9.1 %collective-permute-start = (bf16[32,48,128]{2,1,0:T(8,128)(2,1)S(1)}, bf16[32,48,128]{2,1,0:T(8,128)(2,1)S(1)}, u32[]{:S(2)}, u32[]{:S(2)}) collective-permute-start(bf16[32,48,128]{2,1,0:T(8,128)(2,1)S(1)} %get-tuple-element.24), channel_id=1, source_target_pairs={{0,1},{1,3},{4,5},{5,7},{8,9},{9,11},{12,13},{13,15},{16,17},{17,1... | collective-permute-start | bytes 1179656 | tf_op jit(solution)/shard_map/ppermute | solution.py:373
  4.2 2.6 %copy-start.2 = (bf16[2,1024]{1,0:T(2,128)(2,1)S(1)}, bf16[2,1024]{1,0:T(2,128)(2,1)}, u32[]{:S(2)}) copy-start(bf16[2,1024]{1,0:T(2,128)(2,1)} %chirp_ref.1) | copy-start | bytes 12292
  4.2 12.2 %collective-permute-start.2 = (bf16[32,16,128]{2,1,0:T(8,128)(2,1)S(1)}, bf16[32,16,128]{2,1,0:T(8,128)(2,1)S(1)}, u32[]{:S(2)}, u32[]{:S(2)}) collective-permute-start(bf16[32,16,128]{2,1,0:T(8,128)(2,1)S(1)} %get-tuple-element.30), channel_id=1, source_target_pairs={{0,1},{1,3},{4,5},{5,7},{8,9},{9,11},{12,13},{13,15},{16,17},{17,1... | collective-permute-start | bytes 393224 | tf_op jit(solution)/shard_map/ppermute | solution.py:377
  9.0 7.4 %collective-permute-start.1 = (bf16[8,256,128]{2,1,0:T(8,128)(2,1)S(1)}, bf16[8,256,128]{2,1,0:T(8,128)(2,1)S(1)}, u32[]{:S(2)}, u32[]{:S(2)}) collective-permute-start(bf16[8,256,128]{2,1,0:T(8,128)(2,1)S(1)} %get-tuple-element.27), channel_id=1, source_target_pairs={{1,2},{2,3},{5,6},{6,7},{9,10},{10,11},{13,14},{14,15},{17,18},{18... | collective-permute-start | bytes 1572872 | tf_op jit(solution)/shard_map/ppermute | solution.py:384
  10.4 0.7 %copy-start.1 = (bf16[8,2,512]{2,1,0:T(2,128)(2,1)S(1)}, bf16[8,2,512]{2,1,0:T(2,128)(2,1)}, u32[]{:S(2)}) copy-start(bf16[8,2,512]{2,1,0:T(2,128)(2,1)} %refs_ref.1) | copy-start | bytes 49156
  10.4 0.7 %copy-start.3 = (s32[4,8]{1,0:T(4,128)S(1)}, s32[4,8]{1,0:T(4,128)}, u32[]{:S(2)}) copy-start(s32[4,8]{1,0:T(4,128)} %index_ref.1) | copy-start | bytes 388

commit v20 on v17

--- a/solution.py
+++ b/solution.py
@@ -28,14 +28,14 @@
         target[first + t] = source[:, :, t * LANES : (t + 1) * LANES].reshape(shape)
 
 
-def tail_kernel(raw_ref, tail_ref, turn_ref, natural, sems):
+def tail_first_kernel(raw_ref, tail_ref, turn_ref, natural, sems):
     turn_ref[...] = jnp.zeros_like(turn_ref)
     half, rows, _ = tail_ref.shape
     pieces = sems.shape[0]
     each = rows // 2 // pieces
     width = half * LANES
 
-    @pl.when(lax.axis_index("sa") < 2)
+    @pl.when(lax.axis_index("sa") == 1)
     def _():
         copies = []
         for at in range(pieces):
@@ -49,12 +49,16 @@
             retile(natural.at[own], tail_ref.at[:, pl.ds(at * each * 2, each * 2)], 0, half)
 
 
-def head_kernel(turn_in_ref, raw_ref, head_ref, turn_ref):
-    turn_ref[...] = turn_in_ref[...]
-
-    @pl.when(lax.axis_index("sa") == 2)
-    def _():
-        retile(raw_ref, head_ref, 0, head_ref.shape[0])
+def tail_second_kernel(turn_in_ref, raw_ref, tail_ref, turn_ref):
+    turn_ref[...] = turn_in_ref[...]
+    half, rows, _ = tail_ref.shape
+    pulses = rows // 2
+
+    @pl.when(lax.axis_index("sa") == 1)
+    def _():
+        own = pl.ds(raw_ref.shape[0] - pulses, pulses)
+        width = half * LANES
+        retile(raw_ref.at[own, :, pl.ds(raw_ref.shape[2] - width, width)], tail_ref, 0, half)
 
 
 def prep_kernel(turn_in_ref, window_ref, index_ref, chirp_ref, refs_ref, taps_ref, rows_ref, turn_ref):
@@ -94,14 +98,13 @@
     rows_ref[...] = jnp.stack(pieces, axis=1).astype(BF)
 
 
-def compress(held, base, taps_ref, out_ref):
+def compress(held, base, taps_ref, out_ref, first_row, tile_rows):
     rows = held.shape[1]
-    targets = out_ref.shape[0]
     tap_tiles = taps_ref.shape[0] // LANES
-    group = 8
-    per_target = out_ref.shape[1] // rows
+    group = 8 if rows > 32 else 512 // rows
+    per_target = out_ref.shape[1] // tile_rows
     even = lax.rem(lax.broadcasted_iota(jnp.int32, (1, 8, LANES), 1), 2) == 0
-    for step in range(targets * per_target // group):
+    for step in range(out_ref.shape[0] * per_target // group):
         blocks = [
             held[pl.ds(base + group * step + t, group)].reshape(group * rows, LANES) for t in range(tap_tiles)
         ]
@@ -110,62 +113,112 @@
         crossed = product[:, LANES:].reshape(-1, 8, LANES)
         total = straight + jnp.where(even, pltpu.roll(crossed, 7, 1), -pltpu.roll(crossed, 1, 1))
         count = group // per_target
-        out_ref[pl.ds(step * count, count), : per_target * rows] = total.astype(BF).reshape(
-            count, per_target * rows, LANES
-        )
-
-
-def ahead_kernel(turn_in_ref, window_ref, raw_ref, taps_ref, out_ref, turn_ref, held):
+        total = total.astype(BF).reshape(count, per_target, rows, LANES)
+        for tile in range(per_target):
+            at = tile * tile_rows + first_row
+            out_ref[pl.ds(step * count, count), at : at + rows] = total[:, tile]
+
+
+def own_kernel(turn_in_ref, window_ref, raw_ref, taps_ref, out_ref, turn_ref, held):
     turn_ref[...] = turn_in_ref[...]
     span = held.shape[0]
 
-    @pl.when(lax.axis_index("sa") == 1)
+    @pl.when(lax.axis_index("sa") == 0)
     def _():
         start = pl.multiple_of(window_ref[0] // LANES * LANES, LANES)
         retile(raw_ref.at[:, :, pl.ds(start, span * LANES)], held, 0, span)
-        compress(held, 0, taps_ref, out_ref)
-
-
-def early_kernel(turn_in_ref, window_ref, raw_ref, tail_ref, head_ref, taps_ref, rows_ref, out_ref, held):
+        compress(held, 0, taps_ref, out_ref, 0, held.shape[1])
+
+
+def hand_tiles(raw_ref, first, out_ref):
+    rows = 2 * raw_ref.shape[0]
+    per_target = out_ref.shape[1] // rows
+    for t in range(out_ref.shape[0] * per_target):
+        start = (first + t) * LANES
+        at = t % per_target * rows
+        out_ref[t // per_target, at : at + rows] = raw_ref[:, :, start : start + LANES].reshape(rows, LANES)
+
+
+def ahead_kernel(turn_in_ref, window_ref, raw_ref, taps_ref, out_ref, turn_ref, held):
+    turn_ref[...] = turn_in_ref[...]
+    span = held.shape[0]
+    tiles = raw_ref.shape[2] // LANES
+    count = out_ref.shape[0] * out_ref.shape[1] // held.shape[1]
+    sub_index = lax.axis_index("sa")
+
+    @pl.when(sub_index == 0)
+    def _():
+        hand_tiles(raw_ref, tiles - count, out_ref)
+
+    @pl.when(sub_index == 1)
+    def _():
+        start = pl.multiple_of(window_ref[0] // LANES * LANES, LANES)
+        retile(raw_ref.at[:, :, pl.ds(start, span * LANES)], held, 0, span)
+        compress(held, 0, taps_ref, out_ref, 0, held.shape[1])
+
+    @pl.when(sub_index == 2)
+    def _():
+        hand_tiles(raw_ref, 0, out_ref)
+
+
+def gate_kernel(turn_in_ref, _, turn_ref):
+    turn_ref[...] = turn_in_ref[...]
+
+
+def take_tiles(near_ref, tile_rows, first_row, held, into, count):
+    rows = held.shape[1]
+    per_target = near_ref.shape[1] // tile_rows
+    for t in range(count):
+        at = t % per_target * tile_rows + first_row
+        held[into + t] = near_ref[t // per_target, at : at + rows]
+
+
+def middle_kernel(
+    turn_in_ref, window_ref, raw_ref, tail_ref, near_ref, own_ref, taps_ref, rows_ref, out_ref, turn_ref, held, far_held
+):
+    turn_ref[...] = turn_in_ref[...]
     half = tail_ref.shape[0]
-    more = head_ref.shape[0]
-    span = half + more - 16
+    more = held.shape[0] - half
+    bins = near_ref.shape[1]
+    tile_rows = held.shape[1]
     sub_index = lax.axis_index("sa")
     offset = window_ref[0] // LANES
+    made = out_ref.at[:, pl.ds(0, bins)]
+    out_ref[:, bins:] = rows_ref[...]
 
     @pl.when(sub_index == 0)
     def _():
-        start = pl.multiple_of(offset * LANES, LANES)
-        retile(raw_ref.at[:, :, pl.ds(start, span * LANES)], held, 0, span)
+        made[...] = own_ref[...]
 
     @pl.when(sub_index == 1)
     def _():
+        take_tiles(near_ref, tile_rows, 0, held, 0, half)
+        retile(raw_ref, held, half, more)
+        compress(held, offset, taps_ref, made, 0, tile_rows)
+
+    @pl.when(sub_index == 2)
+    def _():
+        made[...] = near_ref[...]
+
+    @pl.when(sub_index == 3)
+    def _():
+        far_held[:half] = tail_ref[...]
+        take_tiles(near_ref, tile_rows, 0, far_held, half, more)
+        compress(far_held, offset, taps_ref, made, 0, tile_rows)
+
+
+def last_kernel(turn_in_ref, window_ref, tail_ref, near_ref, taps_ref, middle_ref, out_ref, held):
+    half, rows, _ = tail_ref.shape
+    bins = near_ref.shape[1]
+    tile_rows = bins * near_ref.shape[0] // half
+    out_ref[...] = middle_ref[...]
+
+    @pl.when(lax.axis_index("sa") == 3)
+    def _():
         held[:half] = tail_ref[...]
-        retile(raw_ref, held, half, more)
-
-    @pl.when(sub_index == 3)
-    def _():
-        held[:half] = tail_ref[...]
-        held[half:] = head_ref[...]
-
-    @pl.when(sub_index != 2)
-    def _():
-        compress(held, jnp.where(sub_index == 0, 0, offset), taps_ref, out_ref)
-        out_ref[:, out_ref.shape[1] - rows_ref.shape[1] :] = rows_ref[...]
-
-
-def late_kernel(near_ref, rows_ref, early_ref, out_ref):
-    bins = near_ref.shape[1]
-    sub_index = lax.axis_index("sa")
-
-    @pl.when(sub_index != 2)
-    def _():
-        out_ref[...] = early_ref[...]
-
-    @pl.when(sub_index == 2)
-    def _():
-        out_ref[:, :bins] = near_ref[...]
-        out_ref[:, bins:] = rows_ref[...]
+        take_tiles(near_ref, tile_rows, tile_rows - rows, held, half, held.shape[0] - half)
+        made = out_ref.at[:, pl.ds(0, bins)]
+        compress(held, window_ref[0] // LANES, taps_ref, made, tile_rows - rows, tile_rows)
 
 
 def azimuth_kernel(lines_ref, out_ref, columns_held, taps, made, sems):
@@ -299,38 +352,43 @@
     targets = pulse_devices if short else half // 8
     slot = half // targets * rows
 
+    first_rows = rows // 4 * 3
+    part = shape((targets, slot, LANES), BF)
     tail, turn = call(
-        tail_kernel,
-        (shape((half, rows, LANES), BF), token),
+        tail_first_kernel,
+        (shape((half, first_rows, LANES), BF), token),
         "avv",
-        [pltpu.VMEM((pulses, 2, half * LANES), BF), pltpu.SemaphoreType.DMA((4,))],
+        [pltpu.VMEM((first_rows // 2, 2, half * LANES), BF), pltpu.SemaphoreType.DMA((3,))],
         53,
     )(raw_echo)
-    tail = lax.ppermute(tail, "sa", [(0, 1), (1, 3)])
-    head, turn = call(head_kernel, (shape((span - half + 16, rows, LANES), BF), token), "vvvv")(turn, raw_echo)
-    head = lax.ppermute(head, "sa", [(2, 3)])
+    tail_first = lax.ppermute(tail, "sa", [(1, 3)])
     taps, own_rows, turn = call(
         prep_kernel,
         (shape((tap_tiles * LANES, 2 * LANES), BF), shape((pulse_devices, EXTRA, LANES), BF), token),
         "vsvvvvvv",
     )(turn, window_start, migration_index, chirp_replica, azimuth_refs)
-    near, turn = call(
-        ahead_kernel,
-        (shape((targets, slot, LANES), BF), token),
-        "vsvvvv",
-        [pltpu.VMEM((span, rows, LANES), BF)],
-    )(turn, window_start, raw_echo, taps)
-    near = lax.ppermute(near, "sa", [(1, 2)])
+    window_held = [pltpu.VMEM((span, rows, LANES), BF)]
+    own, turn = call(own_kernel, (part, token), "vsvvvv", window_held)(turn, window_start, raw_echo, taps)
+    near, turn = call(ahead_kernel, (part, token), "vsvvvv", window_held)(turn, window_start, raw_echo, taps)
+    near = lax.ppermute(near, "sa", [(0, 1), (1, 2), (2, 3)])
+    (turn,) = call(gate_kernel, (token,), "vav", flops=10**10)(turn, tail_first)
+    tail, turn = call(
+        tail_second_kernel, (shape((half, rows - first_rows, LANES), BF), token), "vvvv"
+    )(turn, raw_echo)
+    tail_second = lax.ppermute(tail, "sa", [(1, 3)])
     extra = own_rows if short else jnp.zeros((targets, EXTRA, LANES), BF)
     made = shape((targets, slot + EXTRA, LANES), BF)
-    (early,) = call(
-        early_kernel,
-        (made,),
-        "vsvvvvvv",
-        [pltpu.VMEM((span + 16, rows, LANES), BF)],
+    wide = span + 16
+    middle, turn = call(
+        middle_kernel,
+        (made, token),
+        "vsvvvvvvvv",
+        [pltpu.VMEM((wide, rows, LANES), BF), pltpu.VMEM((wide, first_rows, LANES), BF)],
         flops=10**10,
-    )(turn, window_start, raw_echo, tail, head, taps, extra)
-    (compressed,) = call(late_kernel, (made,), "vvvv")(near, extra, early)
+    )(turn, window_start, raw_echo, tail_first, near, own, taps, extra)
+    (compressed,) = call(
+        last_kernel, (made,), "vsvvvvv", [pltpu.VMEM((wide, rows - first_rows, LANES), BF)], flops=10**10
+    )(turn, window_start, tail_second, near, taps, middle)
 
     if not short:
         kept = compressed[:, :-EXTRA].reshape(half, pulses, 2, LANES).transpose(0, 3, 2, 1)

time: 34.9 us -> 41.1 us (1.18); the launches traced: 34.6 us -> 40.3 us
  blocking collectives: 17.3 us -> 22.3 us
  local copies, waits for them, and re-layouts: 0.36 us -> 1.4 us
    all_to_all x1, blocking collectives: 17.3 us -> 22.3 us  [on_device(): lax.all_to_all(compressed, 'pa', split_axis=0, concat_axis=0, tiled=True)]
    unnamed x8, local copies, waits for them, and re-layouts: 0.36 us -> 1.4 us
where the time goes in v20:
time: 41.1 us; the launch traced here: 40.3 us
  blocking collectives  22.3 us (54%)
  waiting for transfers between devices  9.79 us (24%)
  starting transfers between devices  3.56 us (9%)
  Pallas kernels  2.48 us (6%)
  local copies, waits for them, and re-layouts  1.4 us (3%)
  between operations  0.79 us (2%)
    all_to_all x1, blocking collectives, on_device(): lax.all_to_all(compressed, 'pa', split_axis=0, concat_axis=0, tiled=True)  22.3 us
    ppermute x1, waiting for transfers between devices, on_device(): near = lax.ppermute(near, 'sa', [(0, 1), (1, 2), (2, 3)])  9.78 us
    ppermute x1, starting transfers between devices, on_device(): near = lax.ppermute(near, 'sa', [(0, 1), (1, 2), (2, 3)])  2.07 us
    pallas_call x1, Pallas kernels, on_device(): call(azimuth_kernel, (shape((bin_count * width // LANES, LANES), F32),),...  1.54 us
    unnamed x8, local copies, waits for them, and re-layouts  1.4 us
  transfers between devices with their start and end apart: 3, of which 1 were waited for; matrix products, arithmetic and copies ran while one was open for 0% of the time, Pallas kernels for 2%

profile of v20, /device:TPU:2, one launch (start us, length us, event | category | flops | bytes accessed | tf_op | source)
XLA Modules:
  0.0 40.3 jit_solution(6994294892660260164)
XLA Ops:
  0.0 0.0 copy-start
  0.0 0.0 copy-start.2
  0.1 0.8 %collective-permute-start = (bf16[32,48,128]{2,1,0:T(8,128)(2,1)S(1)}, bf16[32,48,128]{2,1,0:T(8,128)(2,1)S(1)}, u32[]{:S(2)}, u32[]{:S(2)}) collective-permute-start(bf16[32,48,128]{2,1,0:T(8,128)(2,1)S(1)} %get-tuple-element.23), channel_id=1, source_target_pairs={{1,3},{5,7},{9,11},{13,15},{17,19},{21,23},{25,27},{29,31}} | collective-permute-start | bytes 1179656 | tf_op jit(solution)/shard_map/ppermute | solution.py:364
  1.5 0.0 copy-done.2
  1.5 0.0 copy-start.1
  1.5 0.7 %copy-done.1 = bf16[8,2,512]{2,1,0:T(2,128)(2,1)S(1)} copy-done((bf16[8,2,512]{2,1,0:T(2,128)(2,1)S(1)}, bf16[8,2,512]{2,1,0:T(2,128)(2,1)}, u32[]{:S(2)}) %copy-start.1) | copy-done | bytes 16408
  2.3 0.0 copy-start.3
  2.3 0.7 %copy-done.3 = s32[4,8]{1,0:T(4,128)S(1)} copy-done((s32[4,8]{1,0:T(4,128)S(1)}, s32[4,8]{1,0:T(4,128)}, u32[]{:S(2)}) %copy-start.3) | copy-done | bytes 152
  2.9 0.5 %shard_map.56 = (bf16[1280,256]{1,0:T(8,128)(2,1)S(1)}, bf16[8,8,128]{2,1,0:T(8,128)(2,1)S(1)}, f32[8,128]{1,0:T(8,128)S(1)}) custom-call(f32[8,128]{1,0:T(8,128)S(1)} %get-tuple-element.18.turn_in_ref, s32[1]{0:T(128)S(6)} %copy.7.window_ref, s32[4,8]{1,0:T(4,128)S(1)} %copy-done.3, bf16[2,1024]{1,0:T(2,128)(2,1)S(1)} %copy-done.2, ...), custom_call_target="tpu_custom_call" | custom-call | flops 1000 | bytes 1000 | tf_op jit(solution)/shard_map/pallas_call | solution.py:365
  3.5 0.0 copy-done
  3.5 0.3 shard_map.58
  3.8 2.1 %collective-permute-start.1 = (bf16[8,256,128]{2,1,0:T(8,128)(2,1)S(1)}, bf16[8,256,128]{2,1,0:T(8,128)(2,1)S(1)}, u32[]{:S(2)}, u32[]{:S(2)}) collective-permute-start(bf16[8,256,128]{2,1,0:T(8,128)(2,1)S(1)} %get-tuple-element.25), channel_id=1, source_target_pairs={{0,1},{1,2},{2,3},{4,5},{5,6},{6,7},{8,9},{9,10},{10,11},{12,13},{... | collective-permute-start | bytes 1572872 | tf_op jit(solution)/shard_map/ppermute | solution.py:373
  5.9 0.0 collective-permute-done._.tail_ref
  5.9 0.7 %collective-permute-start.2 = (bf16[32,16,128]{2,1,0:T(8,128)(2,1)S(1)}, bf16[32,16,128]{2,1,0:T(8,128)(2,1)S(1)}, u32[]{:S(2)}, u32[]{:S(2)}) collective-permute-start(bf16[32,16,128]{2,1,0:T(8,128)(2,1)S(1)} %get-tuple-element.29), channel_id=1, source_target_pairs={{1,3},{5,7},{9,11},{13,15},{17,19},{21,23},{25,27},{29,31}} | collective-permute-start | bytes 393224 | tf_op jit(solution)/shard_map/ppermute | solution.py:378
  6.6 9.8 %collective-permute-done.1.near_ref = bf16[8,256,128]{2,1,0:T(8,128)(2,1)S(1)} collective-permute-done((bf16[8,256,128]{2,1,0:T(8,128)(2,1)S(1)}, bf16[8,256,128]{2,1,0:T(8,128)(2,1)S(1)}, u32[]{:S(2)}, u32[]{:S(2)}) %collective-permute-start.1) | collective-permute-done | bytes 524320 | tf_op jit(solution)/shard_map/ppermute | solution.py:373
  16.4 0.0 collective-permute-done.2.tail_ref
  16.5 22.3 %all_to_all.5.lines_ref = bf16[8,264,128]{2,1,0:T(8,128)(2,1)S(1)} all-to-all(bf16[8,264,128]{2,1,0:T(8,128)(2,1)S(1)} %shard_map.62), channel_id=1, replica_groups=mesh['pa'=8,'sa'=4] {'pa'}, dimensions={0} | all-to-all | bytes 1081344 | tf_op jit(solution)/shard_map/all_to_all | solution.py:401
  38.8 1.5 %shard_map.63 = f32[2048,128]{1,0:T(8,128)} custom-call(bf16[8,264,128]{2,1,0:T(8,128)(2,1)S(1)} %all_to_all.5.lines_ref), custom_call_target="tpu_custom_call" | custom-call | flops 1000 | bytes 1000 | tf_op jit(solution)/shard_map/pallas_call | solution.py:403
  (6 shorter events, 0.1 us)
Async XLA Ops:
  0.0 3.5 %copy-start = (bf16[32,2,8192]{2,1,0:T(2,128)(2,1)S(1)}, bf16[32,2,8192]{2,1,0:T(2,128)(2,1)}, u32[]{:S(2)}) copy-start(bf16[32,2,8192]{2,1,0:T(2,128)(2,1)} %raw_ref.9) | copy-start | bytes 3145732
  0.0 1.5 %copy-start.2 = (bf16[2,1024]{1,0:T(2,128)(2,1)S(1)}, bf16[2,1024]{1,0:T(2,128)(2,1)}, u32[]{:S(2)}) copy-start(bf16[2,1024]{1,0:T(2,128)(2,1)} %chirp_ref.1) | copy-start | bytes 12292
  0.1 5.8 %collective-permute-start = (bf16[32,48,128]{2,1,0:T(8,128)(2,1)S(1)}, bf16[32,48,128]{2,1,0:T(8,128)(2,1)S(1)}, u32[]{:S(2)}, u32[]{:S(2)}) collective-permute-start(bf16[32,48,128]{2,1,0:T(8,128)(2,1)S(1)} %get-tuple-element.23), channel_id=1, source_target_pairs={{1,3},{5,7},{9,11},{13,15},{17,19},{21,23},{25,27},{29,31}} | collective-permute-start | bytes 1179656 | tf_op jit(solution)/shard_map/ppermute | solution.py:364
  1.5 0.7 %copy-start.1 = (bf16[8,2,512]{2,1,0:T(2,128)(2,1)S(1)}, bf16[8,2,512]{2,1,0:T(2,128)(2,1)}, u32[]{:S(2)}) copy-start(bf16[8,2,512]{2,1,0:T(2,128)(2,1)} %refs_ref.1) | copy-start | bytes 49156
  2.3 0.7 %copy-start.3 = (s32[4,8]{1,0:T(4,128)S(1)}, s32[4,8]{1,0:T(4,128)}, u32[]{:S(2)}) copy-start(s32[4,8]{1,0:T(4,128)} %index_ref.1) | copy-start | bytes 388
  3.8 12.6 %collective-permute-start.1 = (bf16[8,256,128]{2,1,0:T(8,128)(2,1)S(1)}, bf16[8,256,128]{2,1,0:T(8,128)(2,1)S(1)}, u32[]{:S(2)}, u32[]{:S(2)}) collective-permute-start(bf16[8,256,128]{2,1,0:T(8,128)(2,1)S(1)} %get-tuple-element.25), channel_id=1, source_target_pairs={{0,1},{1,2},{2,3},{4,5},{5,6},{6,7},{8,9},{9,10},{10,11},{12,13},{... | collective-permute-start | bytes 1572872 | tf_op jit(solution)/shard_map/ppermute | solution.py:373
  5.9 10.5 %collective-permute-start.2 = (bf16[32,16,128]{2,1,0:T(8,128)(2,1)S(1)}, bf16[32,16,128]{2,1,0:T(8,128)(2,1)S(1)}, u32[]{:S(2)}, u32[]{:S(2)}) collective-permute-start(bf16[32,16,128]{2,1,0:T(8,128)(2,1)S(1)} %get-tuple-element.29), channel_id=1, source_target_pairs={{1,3},{5,7},{9,11},{13,15},{17,19},{21,23},{25,27},{29,31}} | collective-permute-start | bytes 393224 | tf_op jit(solution)/shard_map/ppermute | solution.py:378

commit v21 on v17

--- a/solution.py
+++ b/solution.py
@@ -206,15 +206,16 @@
     for tile in range(tiles):
         lines = lines_ref[:, tile * rows : (tile + 1) * rows].reshape(sources * rows, LANES)
         focused = lax.dot_general(lines, taps[...], (((0,), (0,)), ((), ())), preferred_element_type=F32)
-        into = pl.ds(tile * each, each)
         for part in range(2):
             for column in range(columns):
                 lane = part * pulses + column * LANES
                 made[pl.ds(tile * each + 2 * column + part, LANES, stride=2 * columns), :] = focused[
                     :, lane : lane + LANES
                 ]
-        copies.append(pltpu.make_async_copy(made.at[into], out_ref.at[into], sems.at[tile]))
-        copies[-1].start()
+        for piece in range(2):
+            into = pl.ds(tile * each + piece * each // 2, each // 2)
+            copies.append(pltpu.make_async_copy(made.at[into], out_ref.at[into], sems.at[tile, piece]))
+            copies[-1].start(priority=piece)
     for copy in copies:
         copy.wait()
 
@@ -350,7 +351,7 @@
             pltpu.VMEM((width // LANES * 2 - 2, 2 * LANES, LANES), F32),
             pltpu.VMEM((width, width), BF),
             pltpu.VMEM((bin_count * width // LANES, LANES), F32),
-            pltpu.SemaphoreType.DMA((bin_count // LANES,)),
+            pltpu.SemaphoreType.DMA((bin_count // LANES, 2)),
         ],
     )(lines)
     focused = focused.reshape(1, bin_count, total_pulses // LANES, 2, LANES).swapaxes(2, 3)

time: 34.9 us -> 34.9 us (level)
  no operation moved by 1% of the time
where the time goes in v21:
time: 34.9 us; the launch traced here: 34.6 us
  blocking collectives  17.3 us (50%)
  waiting for transfers between devices  9.84 us (28%)
  starting transfers between devices  3.96 us (11%)
  Pallas kernels  2.42 us (7%)
  between operations  0.76 us (2%)
  local copies, waits for them, and re-layouts  0.36 us (1%)
    all_to_all x1, blocking collectives, on_device(): lax.all_to_all(compressed, 'pa', split_axis=0, concat_axis=0, tiled=True)  17.3 us
    ppermute x1, waiting for transfers between devices, on_device(): near = lax.ppermute(near, 'sa', [(1, 2)])  9.84 us
    ppermute x1, starting transfers between devices, on_device(): head = lax.ppermute(head, 'sa', [(2, 3)])  1.84 us
    pallas_call x1, Pallas kernels, on_device(): call(azimuth_kernel, (shape((bin_count * width // LANES, LANES), F32),),...  1.57 us
    ppermute x1, starting transfers between devices, on_device(): near = lax.ppermute(near, 'sa', [(1, 2)])  1.29 us
    ppermute x1, starting transfers between devices, on_device(): tail = lax.ppermute(tail, 'sa', [(0, 1), (1, 3)])  0.83 us
  transfers between devices with their start and end apart: 3, of which 1 were waited for; matrix products, arithmetic and copies ran while one was open for 0% of the time, Pallas kernels for 2%

profile of v21, /device:TPU:2, one launch (start us, length us, event | category | flops | bytes accessed | tf_op | source)
XLA Modules:
  0.0 34.6 jit_solution(597366376342352294)
XLA Ops:
  0.0 0.0 copy-start
  0.0 0.8 %collective-permute-start.1 = (bf16[32,64,128]{2,1,0:T(8,128)(2,1)S(1)}, bf16[32,64,128]{2,1,0:T(8,128)(2,1)S(1)}, u32[]{:S(2)}, u32[]{:S(2)}) collective-permute-start(bf16[32,64,128]{2,1,0:T(8,128)(2,1)S(1)} %get-tuple-element.21), channel_id=1, source_target_pairs={{0,1},{1,3},{4,5},{5,7},{8,9},{9,11},{12,13},{13,15},{16,17},{17,1... | collective-permute-start | bytes 1572872 | tf_op jit(solution)/shard_map/ppermute | solution.py:310
  0.9 0.3 copy-done
  1.2 0.0 copy-start.1
  1.2 0.0 copy-start.3
  1.2 0.2 shard_map.56
  1.5 0.0 copy-start.2
  1.5 1.8 %collective-permute-start.2 = (bf16[25,64,128]{2,1,0:T(8,128)(2,1)S(1)}, bf16[25,64,128]{2,1,0:T(8,128)(2,1)S(1)}, u32[]{:S(2)}, u32[]{:S(2)}) collective-permute-start(bf16[25,64,128]{2,1,0:T(8,128)(2,1)S(1)} %get-tuple-element.22), channel_id=1, source_target_pairs={{2,3},{6,7},{10,11},{14,15},{18,19},{22,23},{26,27},{30,31}} | collective-permute-start | bytes 1228808 | tf_op jit(solution)/shard_map/ppermute | solution.py:312
  4.0 0.0 copy-done.1
  4.0 0.0 copy-done.3
  4.0 0.0 copy-done.2
  4.0 0.5 %shard_map.57 = (bf16[1280,256]{1,0:T(8,128)(2,1)S(1)}, bf16[8,8,128]{2,1,0:T(8,128)(2,1)S(1)}, f32[8,128]{1,0:T(8,128)S(1)}) custom-call(f32[8,128]{1,0:T(8,128)S(1)} %get-tuple-element.15.turn_in_ref, s32[1]{0:T(128)S(6)} %copy.7.window_ref, s32[4,8]{1,0:T(4,128)S(1)} %copy-done.3, bf16[2,1024]{1,0:T(2,128)(2,1)S(1)} %copy-done.2, ...), custom_call_target="tpu_custom_call" | custom-call | flops 1000 | bytes 1000 | tf_op jit(solution)/shard_map/pallas_call | solution.py:313
  4.5 1.3 %collective-permute-start = (bf16[8,256,128]{2,1,0:T(8,128)(2,1)S(1)}, bf16[8,256,128]{2,1,0:T(8,128)(2,1)S(1)}, u32[]{:S(2)}, u32[]{:S(2)}) collective-permute-start(bf16[8,256,128]{2,1,0:T(8,128)(2,1)S(1)} %get-tuple-element.18), channel_id=1, source_target_pairs={{1,2},{5,6},{9,10},{13,14},{17,18},{21,22},{25,26},{29,30}} | collective-permute-start | bytes 1572872 | tf_op jit(solution)/shard_map/ppermute | solution.py:324
  5.8 0.0 collective-permute-done.2.head_ref
  5.8 0.0 collective-permute-done.1.tail_ref
  5.9 9.8 %collective-permute-done.near_ref = bf16[8,256,128]{2,1,0:T(8,128)(2,1)S(1)} collective-permute-done((bf16[8,256,128]{2,1,0:T(8,128)(2,1)S(1)}, bf16[8,256,128]{2,1,0:T(8,128)(2,1)S(1)}, u32[]{:S(2)}, u32[]{:S(2)}) %collective-permute-start) | collective-permute-done | bytes 524320 | tf_op jit(solution)/shard_map/ppermute | solution.py:324
  15.8 17.3 %all_to_all.5.lines_ref = bf16[8,264,128]{2,1,0:T(8,128)(2,1)S(1)} all-to-all(bf16[8,264,128]{2,1,0:T(8,128)(2,1)S(1)} %shard_map.60), channel_id=1, replica_groups=mesh['pa'=8,'sa'=4] {'pa'}, dimensions={0} | all-to-all | bytes 1081344 | tf_op jit(solution)/shard_map/all_to_all | solution.py:344
  33.1 1.6 %shard_map.61 = f32[2048,128]{1,0:T(8,128)} custom-call(bf16[8,264,128]{2,1,0:T(8,128)(2,1)S(1)} %all_to_all.5.lines_ref), custom_call_target="tpu_custom_call" | custom-call | flops 1000 | bytes 1000 | tf_op jit(solution)/shard_map/pallas_call | solution.py:346
  (4 shorter events, 0.1 us)
Async XLA Ops:
  0.0 1.2 %copy-start = (bf16[32,2,8192]{2,1,0:T(2,128)(2,1)S(1)}, bf16[32,2,8192]{2,1,0:T(2,128)(2,1)}, u32[]{:S(2)}) copy-start(bf16[32,2,8192]{2,1,0:T(2,128)(2,1)} %raw_ref.7) | copy-start | bytes 3145732
  0.0 5.8 %collective-permute-start.1 = (bf16[32,64,128]{2,1,0:T(8,128)(2,1)S(1)}, bf16[32,64,128]{2,1,0:T(8,128)(2,1)S(1)}, u32[]{:S(2)}, u32[]{:S(2)}) collective-permute-start(bf16[32,64,128]{2,1,0:T(8,128)(2,1)S(1)} %get-tuple-element.21), channel_id=1, source_target_pairs={{0,1},{1,3},{4,5},{5,7},{8,9},{9,11},{12,13},{13,15},{16,17},{17,1... | collective-permute-start | bytes 1572872 | tf_op jit(solution)/shard_map/ppermute | solution.py:310
  1.2 2.7 %copy-start.1 = (bf16[8,2,512]{2,1,0:T(2,128)(2,1)S(1)}, bf16[8,2,512]{2,1,0:T(2,128)(2,1)}, u32[]{:S(2)}) copy-start(bf16[8,2,512]{2,1,0:T(2,128)(2,1)} %refs_ref.1) | copy-start | bytes 49156
  1.2 2.8 %copy-start.3 = (s32[4,8]{1,0:T(4,128)S(1)}, s32[4,8]{1,0:T(4,128)}, u32[]{:S(2)}) copy-start(s32[4,8]{1,0:T(4,128)} %index_ref.1) | copy-start | bytes 388
  1.5 2.5 %copy-start.2 = (bf16[2,1024]{1,0:T(2,128)(2,1)S(1)}, bf16[2,1024]{1,0:T(2,128)(2,1)}, u32[]{:S(2)}) copy-start(bf16[2,1024]{1,0:T(2,128)(2,1)} %chirp_ref.1) | copy-start | bytes 12292
  1.5 4.4 %collective-permute-start.2 = (bf16[25,64,128]{2,1,0:T(8,128)(2,1)S(1)}, bf16[25,64,128]{2,1,0:T(8,128)(2,1)S(1)}, u32[]{:S(2)}, u32[]{:S(2)}) collective-permute-start(bf16[25,64,128]{2,1,0:T(8,128)(2,1)S(1)} %get-tuple-element.22), channel_id=1, source_target_pairs={{2,3},{6,7},{10,11},{14,15},{18,19},{22,23},{26,27},{30,31}} | collective-permute-start | bytes 1228808 | tf_op jit(solution)/shard_map/ppermute | solution.py:312
  4.5 11.2 %collective-permute-start = (bf16[8,256,128]{2,1,0:T(8,128)(2,1)S(1)}, bf16[8,256,128]{2,1,0:T(8,128)(2,1)S(1)}, u32[]{:S(2)}, u32[]{:S(2)}) collective-permute-start(bf16[8,256,128]{2,1,0:T(8,128)(2,1)S(1)} %get-tuple-element.18), channel_id=1, source_target_pairs={{1,2},{5,6},{9,10},{13,14},{17,18},{21,22},{25,26},{29,30}} | collective-permute-start | bytes 1572872 | tf_op jit(solution)/shard_map/ppermute | solution.py:324

commit v22 on v17

--- a/solution.py
+++ b/solution.py
@@ -98,7 +98,7 @@
     rows = held.shape[1]
     targets = out_ref.shape[0]
     tap_tiles = taps_ref.shape[0] // LANES
-    group = 8
+    group = 16
     per_target = out_ref.shape[1] // rows
     even = lax.rem(lax.broadcasted_iota(jnp.int32, (1, 8, LANES), 1), 2) == 0
     for step in range(targets * per_target // group):

time: 34.9 us -> 34.8 us (level)
  no operation moved by 1% of the time
where the time goes in v22:
time: 34.8 us; the launch traced here: 34.6 us
  blocking collectives  17.3 us (50%)
  waiting for transfers between devices  9.84 us (28%)
  starting transfers between devices  3.96 us (11%)
  Pallas kernels  2.4 us (7%)
  between operations  0.76 us (2%)
  local copies, waits for them, and re-layouts  0.36 us (1%)
    all_to_all x1, blocking collectives, on_device(): lax.all_to_all(compressed, 'pa', split_axis=0, concat_axis=0, tiled=True)  17.3 us
    ppermute x1, waiting for transfers between devices, on_device(): near = lax.ppermute(near, 'sa', [(1, 2)])  9.84 us
    ppermute x1, starting transfers between devices, on_device(): head = lax.ppermute(head, 'sa', [(2, 3)])  1.84 us
    pallas_call x1, Pallas kernels, on_device(): call(azimuth_kernel, (shape((bin_count * width // LANES, LANES), F32),),...  1.54 us
    ppermute x1, starting transfers between devices, on_device(): near = lax.ppermute(near, 'sa', [(1, 2)])  1.29 us
    ppermute x1, starting transfers between devices, on_device(): tail = lax.ppermute(tail, 'sa', [(0, 1), (1, 3)])  0.83 us
  transfers between devices with their start and end apart: 3, of which 1 were waited for; matrix products, arithmetic and copies ran while one was open for 0% of the time, Pallas kernels for 2%

profile of v22, /device:TPU:2, one launch (start us, length us, event | category | flops | bytes accessed | tf_op | source)
XLA Modules:
  0.0 34.6 jit_solution(1081032312935039523)
XLA Ops:
  0.0 0.0 copy-start
  0.0 0.8 %collective-permute-start.1 = (bf16[32,64,128]{2,1,0:T(8,128)(2,1)S(1)}, bf16[32,64,128]{2,1,0:T(8,128)(2,1)S(1)}, u32[]{:S(2)}, u32[]{:S(2)}) collective-permute-start(bf16[32,64,128]{2,1,0:T(8,128)(2,1)S(1)} %get-tuple-element.21), channel_id=1, source_target_pairs={{0,1},{1,3},{4,5},{5,7},{8,9},{9,11},{12,13},{13,15},{16,17},{17,1... | collective-permute-start | bytes 1572872 | tf_op jit(solution)/shard_map/ppermute | solution.py:309
  0.9 0.3 copy-done
  1.2 0.0 copy-start.1
  1.2 0.0 copy-start.3
  1.2 0.2 shard_map.56
  1.5 0.0 copy-start.2
  1.5 1.8 %collective-permute-start.2 = (bf16[25,64,128]{2,1,0:T(8,128)(2,1)S(1)}, bf16[25,64,128]{2,1,0:T(8,128)(2,1)S(1)}, u32[]{:S(2)}, u32[]{:S(2)}) collective-permute-start(bf16[25,64,128]{2,1,0:T(8,128)(2,1)S(1)} %get-tuple-element.22), channel_id=1, source_target_pairs={{2,3},{6,7},{10,11},{14,15},{18,19},{22,23},{26,27},{30,31}} | collective-permute-start | bytes 1228808 | tf_op jit(solution)/shard_map/ppermute | solution.py:311
  4.0 0.0 copy-done.1
  4.0 0.0 copy-done.3
  4.0 0.0 copy-done.2
  4.0 0.5 %shard_map.57 = (bf16[1280,256]{1,0:T(8,128)(2,1)S(1)}, bf16[8,8,128]{2,1,0:T(8,128)(2,1)S(1)}, f32[8,128]{1,0:T(8,128)S(1)}) custom-call(f32[8,128]{1,0:T(8,128)S(1)} %get-tuple-element.15.turn_in_ref, s32[1]{0:T(128)S(6)} %copy.7.window_ref, s32[4,8]{1,0:T(4,128)S(1)} %copy-done.3, bf16[2,1024]{1,0:T(2,128)(2,1)S(1)} %copy-done.2, ...), custom_call_target="tpu_custom_call" | custom-call | flops 1000 | bytes 1000 | tf_op jit(solution)/shard_map/pallas_call | solution.py:312
  4.5 1.3 %collective-permute-start = (bf16[8,256,128]{2,1,0:T(8,128)(2,1)S(1)}, bf16[8,256,128]{2,1,0:T(8,128)(2,1)S(1)}, u32[]{:S(2)}, u32[]{:S(2)}) collective-permute-start(bf16[8,256,128]{2,1,0:T(8,128)(2,1)S(1)} %get-tuple-element.18), channel_id=1, source_target_pairs={{1,2},{5,6},{9,10},{13,14},{17,18},{21,22},{25,26},{29,30}} | collective-permute-start | bytes 1572872 | tf_op jit(solution)/shard_map/ppermute | solution.py:323
  5.8 0.0 collective-permute-done.2.head_ref
  5.8 0.0 collective-permute-done.1.tail_ref
  5.9 9.8 %collective-permute-done.near_ref = bf16[8,256,128]{2,1,0:T(8,128)(2,1)S(1)} collective-permute-done((bf16[8,256,128]{2,1,0:T(8,128)(2,1)S(1)}, bf16[8,256,128]{2,1,0:T(8,128)(2,1)S(1)}, u32[]{:S(2)}, u32[]{:S(2)}) %collective-permute-start) | collective-permute-done | bytes 524320 | tf_op jit(solution)/shard_map/ppermute | solution.py:323
  15.8 17.3 %all_to_all.5.lines_ref = bf16[8,264,128]{2,1,0:T(8,128)(2,1)S(1)} all-to-all(bf16[8,264,128]{2,1,0:T(8,128)(2,1)S(1)} %shard_map.60), channel_id=1, replica_groups=mesh['pa'=8,'sa'=4] {'pa'}, dimensions={0} | all-to-all | bytes 1081344 | tf_op jit(solution)/shard_map/all_to_all | solution.py:343
  33.1 1.5 %shard_map.61 = f32[2048,128]{1,0:T(8,128)} custom-call(bf16[8,264,128]{2,1,0:T(8,128)(2,1)S(1)} %all_to_all.5.lines_ref), custom_call_target="tpu_custom_call" | custom-call | flops 1000 | bytes 1000 | tf_op jit(solution)/shard_map/pallas_call | solution.py:345
  (4 shorter events, 0.1 us)
Async XLA Ops:
  0.0 1.2 %copy-start = (bf16[32,2,8192]{2,1,0:T(2,128)(2,1)S(1)}, bf16[32,2,8192]{2,1,0:T(2,128)(2,1)}, u32[]{:S(2)}) copy-start(bf16[32,2,8192]{2,1,0:T(2,128)(2,1)} %raw_ref.7) | copy-start | bytes 3145732
  0.0 5.8 %collective-permute-start.1 = (bf16[32,64,128]{2,1,0:T(8,128)(2,1)S(1)}, bf16[32,64,128]{2,1,0:T(8,128)(2,1)S(1)}, u32[]{:S(2)}, u32[]{:S(2)}) collective-permute-start(bf16[32,64,128]{2,1,0:T(8,128)(2,1)S(1)} %get-tuple-element.21), channel_id=1, source_target_pairs={{0,1},{1,3},{4,5},{5,7},{8,9},{9,11},{12,13},{13,15},{16,17},{17,1... | collective-permute-start | bytes 1572872 | tf_op jit(solution)/shard_map/ppermute | solution.py:309
  1.2 2.7 %copy-start.1 = (bf16[8,2,512]{2,1,0:T(2,128)(2,1)S(1)}, bf16[8,2,512]{2,1,0:T(2,128)(2,1)}, u32[]{:S(2)}) copy-start(bf16[8,2,512]{2,1,0:T(2,128)(2,1)} %refs_ref.1) | copy-start | bytes 49156
  1.2 2.8 %copy-start.3 = (s32[4,8]{1,0:T(4,128)S(1)}, s32[4,8]{1,0:T(4,128)}, u32[]{:S(2)}) copy-start(s32[4,8]{1,0:T(4,128)} %index_ref.1) | copy-start | bytes 388
  1.5 2.5 %copy-start.2 = (bf16[2,1024]{1,0:T(2,128)(2,1)S(1)}, bf16[2,1024]{1,0:T(2,128)(2,1)}, u32[]{:S(2)}) copy-start(bf16[2,1024]{1,0:T(2,128)(2,1)} %chirp_ref.1) | copy-start | bytes 12292
  1.5 4.4 %collective-permute-start.2 = (bf16[25,64,128]{2,1,0:T(8,128)(2,1)S(1)}, bf16[25,64,128]{2,1,0:T(8,128)(2,1)S(1)}, u32[]{:S(2)}, u32[]{:S(2)}) collective-permute-start(bf16[25,64,128]{2,1,0:T(8,128)(2,1)S(1)} %get-tuple-element.22), channel_id=1, source_target_pairs={{2,3},{6,7},{10,11},{14,15},{18,19},{22,23},{26,27},{30,31}} | collective-permute-start | bytes 1228808 | tf_op jit(solution)/shard_map/ppermute | solution.py:311
  4.5 11.2 %collective-permute-start = (bf16[8,256,128]{2,1,0:T(8,128)(2,1)S(1)}, bf16[8,256,128]{2,1,0:T(8,128)(2,1)S(1)}, u32[]{:S(2)}, u32[]{:S(2)}) collective-permute-start(bf16[8,256,128]{2,1,0:T(8,128)(2,1)S(1)} %get-tuple-element.18), channel_id=1, source_target_pairs={{1,2},{5,6},{9,10},{13,14},{17,18},{21,22},{25,26},{29,30}} | collective-permute-start | bytes 1572872 | tf_op jit(solution)/shard_map/ppermute | solution.py:323

commit v23 on v17

--- a/solution.py
+++ b/solution.py
@@ -89,6 +89,7 @@
             picks, refs_ref[:, part, :].astype(F32), (((0,), (0,)), ((), ())), preferred_element_type=F32
         )
         picked = reversed_lanes(picked.astype(BF))
+        picked = pltpu.roll(picked, L // 2 + 1, 1)
         pieces += [picked[:, t * LANES : (t + 1) * LANES] for t in range(L // LANES)]
     pieces += [jnp.zeros((targets, LANES), F32)] * (rows_ref.shape[1] - len(pieces))
     rows_ref[...] = jnp.stack(pieces, axis=1).astype(BF)
@@ -177,18 +178,10 @@
     rows = (lines_ref.shape[1] - EXTRA) // tiles
     picked = jnp.sum(lines_ref[:, tiles * rows :].astype(F32), axis=0)
     pieces = L // LANES
-    row = jnp.concatenate(
-        [
-            jnp.concatenate([picked[part * pieces + t : part * pieces + t + 1] for t in range(pieces)], axis=1)
-            for part in range(2)
-        ],
-        axis=0,
-    )
-    moved = pltpu.roll(jnp.concatenate([row] * 4, axis=0), L - (pulses - 1), 1)
-    skewed = [
-        pltpu.roll(jnp.broadcast_to(moved[part : part + 1], (LANES, L)), 0, 1, stride=1, stride_axis=0)
-        for part in range(2)
-    ]
+    skewed = []
+    for part in range(2):
+        spread = [jnp.broadcast_to(picked[part * pieces + t][None], (LANES, LANES)) for t in range(pieces)]
+        skewed.append(pltpu.roll(jnp.concatenate(spread, axis=1), 0, 1, stride=1, stride_axis=0))
     for apart in range(1 - columns, columns):
         at = apart % pieces * LANES
         straight, crossed = (skewed[part][:, at : at + LANES] for part in range(2))
@@ -338,7 +331,8 @@
         turned = lax.all_to_all(outgoing, "pa", split_axis=0, concat_axis=3, tiled=True)
         rows_in = lax.all_to_all(own_rows, "pa", split_axis=0, concat_axis=0, tiled=True)
         reference_row = jnp.sum(rows_in[:, :8].astype(F32), axis=0).astype(BF).reshape(2, L)
-        return focus_long(turned[0], reference_row[:, ::-1])
+        reference_row = jnp.roll(reference_row, -(L // 2 + 1), axis=1)[:, ::-1]
+        return focus_long(turned[0], reference_row)
 
     lines = lax.all_to_all(compressed, "pa", split_axis=0, concat_axis=0, tiled=True)
     width = 2 * total_pulses

time: 34.9 us -> 34.8 us (level)
  no operation moved by 1% of the time
where the time goes in v23:
time: 34.8 us; the launch traced here: 34.5 us
  blocking collectives  17.3 us (50%)
  waiting for transfers between devices  9.8 us (28%)
  starting transfers between devices  3.96 us (11%)
  Pallas kernels  2.37 us (7%)
  between operations  0.76 us (2%)
  local copies, waits for them, and re-layouts  0.36 us (1%)
    all_to_all x1, blocking collectives, on_device(): lax.all_to_all(compressed, 'pa', split_axis=0, concat_axis=0, tiled=True)  17.3 us
    ppermute x1, waiting for transfers between devices, on_device(): near = lax.ppermute(near, 'sa', [(1, 2)])  9.79 us
    ppermute x1, starting transfers between devices, on_device(): head = lax.ppermute(head, 'sa', [(2, 3)])  1.84 us
    pallas_call x1, Pallas kernels, on_device(): call(azimuth_kernel, (shape((bin_count * width // LANES, LANES), F32),),...  1.47 us
    ppermute x1, starting transfers between devices, on_device(): near = lax.ppermute(near, 'sa', [(1, 2)])  1.29 us
    ppermute x1, starting transfers between devices, on_device(): tail = lax.ppermute(tail, 'sa', [(0, 1), (1, 3)])  0.83 us
  transfers between devices with their start and end apart: 3, of which 1 were waited for; matrix products, arithmetic and copies ran while one was open for 0% of the time, Pallas kernels for 2%

profile of v23, /device:TPU:2, one launch (start us, length us, event | category | flops | bytes accessed | tf_op | source)
XLA Modules:
  0.0 34.5 jit_solution(13162225416839576807)
XLA Ops:
  0.0 0.0 copy-start
  0.0 0.8 %collective-permute-start.1 = (bf16[32,64,128]{2,1,0:T(8,128)(2,1)S(1)}, bf16[32,64,128]{2,1,0:T(8,128)(2,1)S(1)}, u32[]{:S(2)}, u32[]{:S(2)}) collective-permute-start(bf16[32,64,128]{2,1,0:T(8,128)(2,1)S(1)} %get-tuple-element.21), channel_id=1, source_target_pairs={{0,1},{1,3},{4,5},{5,7},{8,9},{9,11},{12,13},{13,15},{16,17},{17,1... | collective-permute-start | bytes 1572872 | tf_op jit(solution)/shard_map/ppermute | solution.py:302
  0.9 0.3 copy-done
  1.2 0.0 copy-start.1
  1.2 0.0 copy-start.3
  1.2 0.2 shard_map.56
  1.5 0.0 copy-start.2
  1.5 1.8 %collective-permute-start.2 = (bf16[25,64,128]{2,1,0:T(8,128)(2,1)S(1)}, bf16[25,64,128]{2,1,0:T(8,128)(2,1)S(1)}, u32[]{:S(2)}, u32[]{:S(2)}) collective-permute-start(bf16[25,64,128]{2,1,0:T(8,128)(2,1)S(1)} %get-tuple-element.22), channel_id=1, source_target_pairs={{2,3},{6,7},{10,11},{14,15},{18,19},{22,23},{26,27},{30,31}} | collective-permute-start | bytes 1228808 | tf_op jit(solution)/shard_map/ppermute | solution.py:304
  4.0 0.0 copy-done.1
  4.0 0.0 copy-done.3
  4.0 0.0 copy-done.2
  4.0 0.6 %shard_map.57 = (bf16[1280,256]{1,0:T(8,128)(2,1)S(1)}, bf16[8,8,128]{2,1,0:T(8,128)(2,1)S(1)}, f32[8,128]{1,0:T(8,128)S(1)}) custom-call(f32[8,128]{1,0:T(8,128)S(1)} %get-tuple-element.15.turn_in_ref, s32[1]{0:T(128)S(6)} %copy.7.window_ref, s32[4,8]{1,0:T(4,128)S(1)} %copy-done.3, bf16[2,1024]{1,0:T(2,128)(2,1)S(1)} %copy-done.2, ...), custom_call_target="tpu_custom_call" | custom-call | flops 1000 | bytes 1000 | tf_op jit(solution)/shard_map/pallas_call | solution.py:305
  4.6 1.3 %collective-permute-start = (bf16[8,256,128]{2,1,0:T(8,128)(2,1)S(1)}, bf16[8,256,128]{2,1,0:T(8,128)(2,1)S(1)}, u32[]{:S(2)}, u32[]{:S(2)}) collective-permute-start(bf16[8,256,128]{2,1,0:T(8,128)(2,1)S(1)} %get-tuple-element.18), channel_id=1, source_target_pairs={{1,2},{5,6},{9,10},{13,14},{17,18},{21,22},{25,26},{29,30}} | collective-permute-start | bytes 1572872 | tf_op jit(solution)/shard_map/ppermute | solution.py:316
  5.9 0.0 collective-permute-done.2.head_ref
  5.9 0.0 collective-permute-done.1.tail_ref
  5.9 9.8 %collective-permute-done.near_ref = bf16[8,256,128]{2,1,0:T(8,128)(2,1)S(1)} collective-permute-done((bf16[8,256,128]{2,1,0:T(8,128)(2,1)S(1)}, bf16[8,256,128]{2,1,0:T(8,128)(2,1)S(1)}, u32[]{:S(2)}, u32[]{:S(2)}) %collective-permute-start) | collective-permute-done | bytes 524320 | tf_op jit(solution)/shard_map/ppermute | solution.py:316
  15.8 17.3 %all_to_all.5.lines_ref = bf16[8,264,128]{2,1,0:T(8,128)(2,1)S(1)} all-to-all(bf16[8,264,128]{2,1,0:T(8,128)(2,1)S(1)} %shard_map.60), channel_id=1, replica_groups=mesh['pa'=8,'sa'=4] {'pa'}, dimensions={0} | all-to-all | bytes 1081344 | tf_op jit(solution)/shard_map/all_to_all | solution.py:337
  33.1 1.5 %shard_map.61 = f32[2048,128]{1,0:T(8,128)} custom-call(bf16[8,264,128]{2,1,0:T(8,128)(2,1)S(1)} %all_to_all.5.lines_ref), custom_call_target="tpu_custom_call" | custom-call | flops 1000 | bytes 1000 | tf_op jit(solution)/shard_map/pallas_call | solution.py:339
  (4 shorter events, 0.1 us)
Async XLA Ops:
  0.0 1.2 %copy-start = (bf16[32,2,8192]{2,1,0:T(2,128)(2,1)S(1)}, bf16[32,2,8192]{2,1,0:T(2,128)(2,1)}, u32[]{:S(2)}) copy-start(bf16[32,2,8192]{2,1,0:T(2,128)(2,1)} %raw_ref.7) | copy-start | bytes 3145732
  0.0 5.8 %collective-permute-start.1 = (bf16[32,64,128]{2,1,0:T(8,128)(2,1)S(1)}, bf16[32,64,128]{2,1,0:T(8,128)(2,1)S(1)}, u32[]{:S(2)}, u32[]{:S(2)}) collective-permute-start(bf16[32,64,128]{2,1,0:T(8,128)(2,1)S(1)} %get-tuple-element.21), channel_id=1, source_target_pairs={{0,1},{1,3},{4,5},{5,7},{8,9},{9,11},{12,13},{13,15},{16,17},{17,1... | collective-permute-start | bytes 1572872 | tf_op jit(solution)/shard_map/ppermute | solution.py:302
  1.2 2.7 %copy-start.1 = (bf16[8,2,512]{2,1,0:T(2,128)(2,1)S(1)}, bf16[8,2,512]{2,1,0:T(2,128)(2,1)}, u32[]{:S(2)}) copy-start(bf16[8,2,512]{2,1,0:T(2,128)(2,1)} %refs_ref.1) | copy-start | bytes 49156
  1.2 2.8 %copy-start.3 = (s32[4,8]{1,0:T(4,128)S(1)}, s32[4,8]{1,0:T(4,128)}, u32[]{:S(2)}) copy-start(s32[4,8]{1,0:T(4,128)} %index_ref.1) | copy-start | bytes 388
  1.5 2.5 %copy-start.2 = (bf16[2,1024]{1,0:T(2,128)(2,1)S(1)}, bf16[2,1024]{1,0:T(2,128)(2,1)}, u32[]{:S(2)}) copy-start(bf16[2,1024]{1,0:T(2,128)(2,1)} %chirp_ref.1) | copy-start | bytes 12292
  1.5 4.4 %collective-permute-start.2 = (bf16[25,64,128]{2,1,0:T(8,128)(2,1)S(1)}, bf16[25,64,128]{2,1,0:T(8,128)(2,1)S(1)}, u32[]{:S(2)}, u32[]{:S(2)}) collective-permute-start(bf16[25,64,128]{2,1,0:T(8,128)(2,1)S(1)} %get-tuple-element.22), channel_id=1, source_target_pairs={{2,3},{6,7},{10,11},{14,15},{18,19},{22,23},{26,27},{30,31}} | collective-permute-start | bytes 1228808 | tf_op jit(solution)/shard_map/ppermute | solution.py:304
  4.6 11.2 %collective-permute-start = (bf16[8,256,128]{2,1,0:T(8,128)(2,1)S(1)}, bf16[8,256,128]{2,1,0:T(8,128)(2,1)S(1)}, u32[]{:S(2)}, u32[]{:S(2)}) collective-permute-start(bf16[8,256,128]{2,1,0:T(8,128)(2,1)S(1)} %get-tuple-element.18), channel_id=1, source_target_pairs={{1,2},{5,6},{9,10},{13,14},{17,18},{21,22},{25,26},{29,30}} | collective-permute-start | bytes 1572872 | tf_op jit(solution)/shard_map/ppermute | solution.py:316

commit v24 on v23

--- a/solution.py
+++ b/solution.py
@@ -8,7 +8,7 @@
 R = 16384
 L = 512
 LANES = 128
-EXTRA = 8
+EXTRA = 16
 BF = jnp.bfloat16
 F32 = jnp.float32
 
@@ -41,7 +41,7 @@
         for at in range(pieces):
             own = pl.ds(at * each, each)
             source = raw_ref.at[own, :, pl.ds(raw_ref.shape[2] - width, width)]
-            copies.append(pltpu.make_async_copy(source, natural.at[own], sems.at[at]))
+            copies.append(pltpu.make_async_copy(source, natural.at[own, :, pl.ds(0, width)], sems.at[at]))
             copies[-1].start()
         for at, copy in enumerate(copies):
             copy.wait()
@@ -296,7 +296,7 @@
         tail_kernel,
         (shape((half, rows, LANES), BF), token),
         "avv",
-        [pltpu.VMEM((pulses, 2, half * LANES), BF), pltpu.SemaphoreType.DMA((4,))],
+        [pltpu.VMEM((pulses, 2, (half + 8) * LANES), BF), pltpu.SemaphoreType.DMA((4,))],
         53,
     )(raw_echo)
     tail = lax.ppermute(tail, "sa", [(0, 1), (1, 3)])
@@ -341,9 +341,9 @@
         (shape((bin_count * width // LANES, LANES), F32),),
         "va",
         [
-            pltpu.VMEM((width // LANES * 2 - 2, 2 * LANES, LANES), F32),
+            pltpu.VMEM((width // LANES * 2 - 1, 2 * LANES, LANES), F32),
             pltpu.VMEM((width, width), BF),
-            pltpu.VMEM((bin_count * width // LANES, LANES), F32),
+            pltpu.VMEM((bin_count * width // LANES + 8, LANES), F32),
             pltpu.SemaphoreType.DMA((bin_count // LANES,)),
         ],
     )(lines)

time: 34.8 us -> 35.1 us (level)
  no operation moved by 1% of the time
where the time goes in v24:
time: 35.1 us; the launch traced here: 34.8 us
  blocking collectives  17.6 us (50%)
  waiting for transfers between devices  9.8 us (28%)
  starting transfers between devices  3.96 us (11%)
  Pallas kernels  2.38 us (7%)
  between operations  0.76 us (2%)
  local copies, waits for them, and re-layouts  0.36 us (1%)
    all_to_all x1, blocking collectives, on_device(): lax.all_to_all(compressed, 'pa', split_axis=0, concat_axis=0, tiled=True)  17.6 us
    ppermute x1, waiting for transfers between devices, on_device(): near = lax.ppermute(near, 'sa', [(1, 2)])  9.79 us
    ppermute x1, starting transfers between devices, on_device(): head = lax.ppermute(head, 'sa', [(2, 3)])  1.84 us
    pallas_call x1, Pallas kernels, on_device(): call(azimuth_kernel, (shape((bin_count * width // LANES, LANES), F32),),...  1.48 us
    ppermute x1, starting transfers between devices, on_device(): near = lax.ppermute(near, 'sa', [(1, 2)])  1.29 us
    ppermute x1, starting transfers between devices, on_device(): tail = lax.ppermute(tail, 'sa', [(0, 1), (1, 3)])  0.83 us
  transfers between devices with their start and end apart: 3, of which 1 were waited for; matrix products, arithmetic and copies ran while one was open for 0% of the time, Pallas kernels for 2%

profile of v24, /device:TPU:2, one launch (start us, length us, event | category | flops | bytes accessed | tf_op | source)
XLA Modules:
  0.0 34.8 jit_solution(14453671622388796138)
XLA Ops:
  0.0 0.0 copy-start
  0.0 0.8 %collective-permute-start.1 = (bf16[32,64,128]{2,1,0:T(8,128)(2,1)S(1)}, bf16[32,64,128]{2,1,0:T(8,128)(2,1)S(1)}, u32[]{:S(2)}, u32[]{:S(2)}) collective-permute-start(bf16[32,64,128]{2,1,0:T(8,128)(2,1)S(1)} %get-tuple-element.21), channel_id=1, source_target_pairs={{0,1},{1,3},{4,5},{5,7},{8,9},{9,11},{12,13},{13,15},{16,17},{17,1... | collective-permute-start | bytes 1572872 | tf_op jit(solution)/shard_map/ppermute | solution.py:302
  0.9 0.3 copy-done
  1.2 0.0 copy-start.1
  1.2 0.0 copy-start.3
  1.2 0.2 shard_map.56
  1.5 0.0 copy-start.2
  1.5 1.8 %collective-permute-start.2 = (bf16[25,64,128]{2,1,0:T(8,128)(2,1)S(1)}, bf16[25,64,128]{2,1,0:T(8,128)(2,1)S(1)}, u32[]{:S(2)}, u32[]{:S(2)}) collective-permute-start(bf16[25,64,128]{2,1,0:T(8,128)(2,1)S(1)} %get-tuple-element.22), channel_id=1, source_target_pairs={{2,3},{6,7},{10,11},{14,15},{18,19},{22,23},{26,27},{30,31}} | collective-permute-start | bytes 1228808 | tf_op jit(solution)/shard_map/ppermute | solution.py:304
  4.0 0.0 copy-done.1
  4.0 0.0 copy-done.3
  4.0 0.0 copy-done.2
  4.0 0.6 %shard_map.57 = (bf16[1280,256]{1,0:T(8,128)(2,1)S(1)}, bf16[8,16,128]{2,1,0:T(8,128)(2,1)S(1)}, f32[8,128]{1,0:T(8,128)S(1)}) custom-call(f32[8,128]{1,0:T(8,128)S(1)} %get-tuple-element.15.turn_in_ref, s32[1]{0:T(128)S(6)} %copy.7.window_ref, s32[4,8]{1,0:T(4,128)S(1)} %copy-done.3, bf16[2,1024]{1,0:T(2,128)(2,1)S(1)} %copy-done.2, ...), custom_call_target="tpu_custom_call" | custom-call | flops 1000 | bytes 1000 | tf_op jit(solution)/shard_map/pallas_call | solution.py:305
  4.6 1.3 %collective-permute-start = (bf16[8,256,128]{2,1,0:T(8,128)(2,1)S(1)}, bf16[8,256,128]{2,1,0:T(8,128)(2,1)S(1)}, u32[]{:S(2)}, u32[]{:S(2)}) collective-permute-start(bf16[8,256,128]{2,1,0:T(8,128)(2,1)S(1)} %get-tuple-element.18), channel_id=1, source_target_pairs={{1,2},{5,6},{9,10},{13,14},{17,18},{21,22},{25,26},{29,30}} | collective-permute-start | bytes 1572872 | tf_op jit(solution)/shard_map/ppermute | solution.py:316
  5.9 0.0 collective-permute-done.2.head_ref
  5.9 0.0 collective-permute-done.1.tail_ref
  5.9 9.8 %collective-permute-done.near_ref = bf16[8,256,128]{2,1,0:T(8,128)(2,1)S(1)} collective-permute-done((bf16[8,256,128]{2,1,0:T(8,128)(2,1)S(1)}, bf16[8,256,128]{2,1,0:T(8,128)(2,1)S(1)}, u32[]{:S(2)}, u32[]{:S(2)}) %collective-permute-start) | collective-permute-done | bytes 524320 | tf_op jit(solution)/shard_map/ppermute | solution.py:316
  15.8 17.6 %all_to_all.5.lines_ref = bf16[8,272,128]{2,1,0:T(8,128)(2,1)S(1)} all-to-all(bf16[8,272,128]{2,1,0:T(8,128)(2,1)S(1)} %shard_map.60), channel_id=1, replica_groups=mesh['pa'=8,'sa'=4] {'pa'}, dimensions={0} | all-to-all | bytes 1114112 | tf_op jit(solution)/shard_map/all_to_all | solution.py:337
  33.4 1.5 %shard_map.61 = f32[2048,128]{1,0:T(8,128)} custom-call(bf16[8,272,128]{2,1,0:T(8,128)(2,1)S(1)} %all_to_all.5.lines_ref), custom_call_target="tpu_custom_call" | custom-call | flops 1000 | bytes 1000 | tf_op jit(solution)/shard_map/pallas_call | solution.py:339
  (4 shorter events, 0.1 us)
Async XLA Ops:
  0.0 1.2 %copy-start = (bf16[32,2,8192]{2,1,0:T(2,128)(2,1)S(1)}, bf16[32,2,8192]{2,1,0:T(2,128)(2,1)}, u32[]{:S(2)}) copy-start(bf16[32,2,8192]{2,1,0:T(2,128)(2,1)} %raw_ref.7) | copy-start | bytes 3145732
  0.0 5.8 %collective-permute-start.1 = (bf16[32,64,128]{2,1,0:T(8,128)(2,1)S(1)}, bf16[32,64,128]{2,1,0:T(8,128)(2,1)S(1)}, u32[]{:S(2)}, u32[]{:S(2)}) collective-permute-start(bf16[32,64,128]{2,1,0:T(8,128)(2,1)S(1)} %get-tuple-element.21), channel_id=1, source_target_pairs={{0,1},{1,3},{4,5},{5,7},{8,9},{9,11},{12,13},{13,15},{16,17},{17,1... | collective-permute-start | bytes 1572872 | tf_op jit(solution)/shard_map/ppermute | solution.py:302
  1.2 2.7 %copy-start.1 = (bf16[8,2,512]{2,1,0:T(2,128)(2,1)S(1)}, bf16[8,2,512]{2,1,0:T(2,128)(2,1)}, u32[]{:S(2)}) copy-start(bf16[8,2,512]{2,1,0:T(2,128)(2,1)} %refs_ref.1) | copy-start | bytes 49156
  1.2 2.8 %copy-start.3 = (s32[4,8]{1,0:T(4,128)S(1)}, s32[4,8]{1,0:T(4,128)}, u32[]{:S(2)}) copy-start(s32[4,8]{1,0:T(4,128)} %index_ref.1) | copy-start | bytes 388
  1.5 2.5 %copy-start.2 = (bf16[2,1024]{1,0:T(2,128)(2,1)S(1)}, bf16[2,1024]{1,0:T(2,128)(2,1)}, u32[]{:S(2)}) copy-start(bf16[2,1024]{1,0:T(2,128)(2,1)} %chirp_ref.1) | copy-start | bytes 12292
  1.5 4.4 %collective-permute-start.2 = (bf16[25,64,128]{2,1,0:T(8,128)(2,1)S(1)}, bf16[25,64,128]{2,1,0:T(8,128)(2,1)S(1)}, u32[]{:S(2)}, u32[]{:S(2)}) collective-permute-start(bf16[25,64,128]{2,1,0:T(8,128)(2,1)S(1)} %get-tuple-element.22), channel_id=1, source_target_pairs={{2,3},{6,7},{10,11},{14,15},{18,19},{22,23},{26,27},{30,31}} | collective-permute-start | bytes 1228808 | tf_op jit(solution)/shard_map/ppermute | solution.py:304
  4.6 11.2 %collective-permute-start = (bf16[8,256,128]{2,1,0:T(8,128)(2,1)S(1)}, bf16[8,256,128]{2,1,0:T(8,128)(2,1)S(1)}, u32[]{:S(2)}, u32[]{:S(2)}) collective-permute-start(bf16[8,256,128]{2,1,0:T(8,128)(2,1)S(1)} %get-tuple-element.18), channel_id=1, source_target_pairs={{1,2},{5,6},{9,10},{13,14},{17,18},{21,22},{25,26},{29,30}} | collective-permute-start | bytes 1572872 | tf_op jit(solution)/shard_map/ppermute | solution.py:316

commit v25 on v24

--- a/solution.py
+++ b/solution.py
@@ -95,7 +95,7 @@
     rows_ref[...] = jnp.stack(pieces, axis=1).astype(BF)
 
 
-def compress(held, base, taps_ref, out_ref):
+def compress(held, base, taps_ref, out_ref, opening=None):
     rows = held.shape[1]
     targets = out_ref.shape[0]
     tap_tiles = taps_ref.shape[0] // LANES
@@ -103,8 +103,9 @@
     per_target = out_ref.shape[1] // rows
     even = lax.rem(lax.broadcasted_iota(jnp.int32, (1, 8, LANES), 1), 2) == 0
     for step in range(targets * per_target // group):
+        source = held if step or opening is None else opening
         blocks = [
-            held[pl.ds(base + group * step + t, group)].reshape(group * rows, LANES) for t in range(tap_tiles)
+            source[pl.ds(base + group * step + t, group)].reshape(group * rows, LANES) for t in range(tap_tiles)
         ]
         product = jnp.dot(jnp.concatenate(blocks, axis=1), taps_ref[...], preferred_element_type=F32)
         straight = product[:, :LANES].reshape(-1, 8, LANES)
@@ -144,14 +145,18 @@
         held[:half] = tail_ref[...]
         retile(raw_ref, held, half, more)
 
+    @pl.when(sub_index < 2)
+    def _():
+        compress(held, jnp.where(sub_index == 0, 0, offset), taps_ref, out_ref)
+
     @pl.when(sub_index == 3)
     def _():
         held[:half] = tail_ref[...]
         held[half:] = head_ref[...]
+        compress(held, offset, taps_ref, out_ref, tail_ref)
 
     @pl.when(sub_index != 2)
     def _():
-        compress(held, jnp.where(sub_index == 0, 0, offset), taps_ref, out_ref)
         out_ref[:, out_ref.shape[1] - rows_ref.shape[1] :] = rows_ref[...]
 
 

time: 35.1 us -> 35.1 us (level)
  no operation moved by 1% of the time
where the time goes in v25:
time: 35.1 us; the launch traced here: 34.8 us
  blocking collectives  17.6 us (50%)
  waiting for transfers between devices  9.79 us (28%)
  starting transfers between devices  3.96 us (11%)
  Pallas kernels  2.39 us (7%)
  between operations  0.76 us (2%)
  local copies, waits for them, and re-layouts  0.36 us (1%)
    all_to_all x1, blocking collectives, on_device(): lax.all_to_all(compressed, 'pa', split_axis=0, concat_axis=0, tiled=True)  17.6 us
    ppermute x1, waiting for transfers between devices, on_device(): near = lax.ppermute(near, 'sa', [(1, 2)])  9.79 us
    ppermute x1, starting transfers between devices, on_device(): head = lax.ppermute(head, 'sa', [(2, 3)])  1.84 us
    pallas_call x1, Pallas kernels, on_device(): call(azimuth_kernel, (shape((bin_count * width // LANES, LANES), F32),),...  1.48 us
    ppermute x1, starting transfers between devices, on_device(): near = lax.ppermute(near, 'sa', [(1, 2)])  1.29 us
    ppermute x1, starting transfers between devices, on_device(): tail = lax.ppermute(tail, 'sa', [(0, 1), (1, 3)])  0.83 us
  transfers between devices with their start and end apart: 3, of which 1 were waited for; matrix products, arithmetic and copies ran while one was open for 0% of the time, Pallas kernels for 2%

profile of v25, /device:TPU:2, one launch (start us, length us, event | category | flops | bytes accessed | tf_op | source)
XLA Modules:
  0.0 34.8 jit_solution(12833631966202298036)
XLA Ops:
  0.0 0.0 copy-start
  0.0 0.8 %collective-permute-start.1 = (bf16[32,64,128]{2,1,0:T(8,128)(2,1)S(1)}, bf16[32,64,128]{2,1,0:T(8,128)(2,1)S(1)}, u32[]{:S(2)}, u32[]{:S(2)}) collective-permute-start(bf16[32,64,128]{2,1,0:T(8,128)(2,1)S(1)} %get-tuple-element.21), channel_id=1, source_target_pairs={{0,1},{1,3},{4,5},{5,7},{8,9},{9,11},{12,13},{13,15},{16,17},{17,1... | collective-permute-start | bytes 1572872 | tf_op jit(solution)/shard_map/ppermute | solution.py:307
  0.9 0.3 copy-done
  1.2 0.0 copy-start.1
  1.2 0.0 copy-start.3
  1.2 0.2 shard_map.56
  1.5 0.0 copy-start.2
  1.5 1.8 %collective-permute-start.2 = (bf16[25,64,128]{2,1,0:T(8,128)(2,1)S(1)}, bf16[25,64,128]{2,1,0:T(8,128)(2,1)S(1)}, u32[]{:S(2)}, u32[]{:S(2)}) collective-permute-start(bf16[25,64,128]{2,1,0:T(8,128)(2,1)S(1)} %get-tuple-element.22), channel_id=1, source_target_pairs={{2,3},{6,7},{10,11},{14,15},{18,19},{22,23},{26,27},{30,31}} | collective-permute-start | bytes 1228808 | tf_op jit(solution)/shard_map/ppermute | solution.py:309
  4.0 0.0 copy-done.1
  4.0 0.0 copy-done.3
  4.0 0.0 copy-done.2
  4.0 0.6 %shard_map.57 = (bf16[1280,256]{1,0:T(8,128)(2,1)S(1)}, bf16[8,16,128]{2,1,0:T(8,128)(2,1)S(1)}, f32[8,128]{1,0:T(8,128)S(1)}) custom-call(f32[8,128]{1,0:T(8,128)S(1)} %get-tuple-element.15.turn_in_ref, s32[1]{0:T(128)S(6)} %copy.7.window_ref, s32[4,8]{1,0:T(4,128)S(1)} %copy-done.3, bf16[2,1024]{1,0:T(2,128)(2,1)S(1)} %copy-done.2, ...), custom_call_target="tpu_custom_call" | custom-call | flops 1000 | bytes 1000 | tf_op jit(solution)/shard_map/pallas_call | solution.py:310
  4.6 1.3 %collective-permute-start = (bf16[8,256,128]{2,1,0:T(8,128)(2,1)S(1)}, bf16[8,256,128]{2,1,0:T(8,128)(2,1)S(1)}, u32[]{:S(2)}, u32[]{:S(2)}) collective-permute-start(bf16[8,256,128]{2,1,0:T(8,128)(2,1)S(1)} %get-tuple-element.18), channel_id=1, source_target_pairs={{1,2},{5,6},{9,10},{13,14},{17,18},{21,22},{25,26},{29,30}} | collective-permute-start | bytes 1572872 | tf_op jit(solution)/shard_map/ppermute | solution.py:321
  5.9 0.0 collective-permute-done.2.head_ref
  5.9 0.0 collective-permute-done.1.tail_ref
  5.9 9.8 %collective-permute-done.near_ref = bf16[8,256,128]{2,1,0:T(8,128)(2,1)S(1)} collective-permute-done((bf16[8,256,128]{2,1,0:T(8,128)(2,1)S(1)}, bf16[8,256,128]{2,1,0:T(8,128)(2,1)S(1)}, u32[]{:S(2)}, u32[]{:S(2)}) %collective-permute-start) | collective-permute-done | bytes 524320 | tf_op jit(solution)/shard_map/ppermute | solution.py:321
  15.8 17.6 %all_to_all.5.lines_ref = bf16[8,272,128]{2,1,0:T(8,128)(2,1)S(1)} all-to-all(bf16[8,272,128]{2,1,0:T(8,128)(2,1)S(1)} %shard_map.60), channel_id=1, replica_groups=mesh['pa'=8,'sa'=4] {'pa'}, dimensions={0} | all-to-all | bytes 1114112 | tf_op jit(solution)/shard_map/all_to_all | solution.py:342
  33.3 1.5 %shard_map.61 = f32[2048,128]{1,0:T(8,128)} custom-call(bf16[8,272,128]{2,1,0:T(8,128)(2,1)S(1)} %all_to_all.5.lines_ref), custom_call_target="tpu_custom_call" | custom-call | flops 1000 | bytes 1000 | tf_op jit(solution)/shard_map/pallas_call | solution.py:344
  (4 shorter events, 0.1 us)
Async XLA Ops:
  0.0 1.2 %copy-start = (bf16[32,2,8192]{2,1,0:T(2,128)(2,1)S(1)}, bf16[32,2,8192]{2,1,0:T(2,128)(2,1)}, u32[]{:S(2)}) copy-start(bf16[32,2,8192]{2,1,0:T(2,128)(2,1)} %raw_ref.7) | copy-start | bytes 3145732
  0.0 5.8 %collective-permute-start.1 = (bf16[32,64,128]{2,1,0:T(8,128)(2,1)S(1)}, bf16[32,64,128]{2,1,0:T(8,128)(2,1)S(1)}, u32[]{:S(2)}, u32[]{:S(2)}) collective-permute-start(bf16[32,64,128]{2,1,0:T(8,128)(2,1)S(1)} %get-tuple-element.21), channel_id=1, source_target_pairs={{0,1},{1,3},{4,5},{5,7},{8,9},{9,11},{12,13},{13,15},{16,17},{17,1... | collective-permute-start | bytes 1572872 | tf_op jit(solution)/shard_map/ppermute | solution.py:307
  1.2 2.7 %copy-start.1 = (bf16[8,2,512]{2,1,0:T(2,128)(2,1)S(1)}, bf16[8,2,512]{2,1,0:T(2,128)(2,1)}, u32[]{:S(2)}) copy-start(bf16[8,2,512]{2,1,0:T(2,128)(2,1)} %refs_ref.1) | copy-start | bytes 49156
  1.2 2.8 %copy-start.3 = (s32[4,8]{1,0:T(4,128)S(1)}, s32[4,8]{1,0:T(4,128)}, u32[]{:S(2)}) copy-start(s32[4,8]{1,0:T(4,128)} %index_ref.1) | copy-start | bytes 388
  1.5 2.5 %copy-start.2 = (bf16[2,1024]{1,0:T(2,128)(2,1)S(1)}, bf16[2,1024]{1,0:T(2,128)(2,1)}, u32[]{:S(2)}) copy-start(bf16[2,1024]{1,0:T(2,128)(2,1)} %chirp_ref.1) | copy-start | bytes 12292
  1.5 4.4 %collective-permute-start.2 = (bf16[25,64,128]{2,1,0:T(8,128)(2,1)S(1)}, bf16[25,64,128]{2,1,0:T(8,128)(2,1)S(1)}, u32[]{:S(2)}, u32[]{:S(2)}) collective-permute-start(bf16[25,64,128]{2,1,0:T(8,128)(2,1)S(1)} %get-tuple-element.22), channel_id=1, source_target_pairs={{2,3},{6,7},{10,11},{14,15},{18,19},{22,23},{26,27},{30,31}} | collective-permute-start | bytes 1228808 | tf_op jit(solution)/shard_map/ppermute | solution.py:309
  4.6 11.2 %collective-permute-start = (bf16[8,256,128]{2,1,0:T(8,128)(2,1)S(1)}, bf16[8,256,128]{2,1,0:T(8,128)(2,1)S(1)}, u32[]{:S(2)}, u32[]{:S(2)}) collective-permute-start(bf16[8,256,128]{2,1,0:T(8,128)(2,1)S(1)} %get-tuple-element.18), channel_id=1, source_target_pairs={{1,2},{5,6},{9,10},{13,14},{17,18},{21,22},{25,26},{29,30}} | collective-permute-start | bytes 1572872 | tf_op jit(solution)/shard_map/ppermute | solution.py:321

commit v26 on v20

--- a/solution.py
+++ b/solution.py
@@ -8,7 +8,7 @@
 R = 16384
 L = 512
 LANES = 128
-EXTRA = 8
+EXTRA = 16
 BF = jnp.bfloat16
 F32 = jnp.float32
 
@@ -35,13 +35,13 @@
     each = rows // 2 // pieces
     width = half * LANES
 
-    @pl.when(lax.axis_index("sa") == 1)
+    @pl.when(lax.axis_index("sa") < 2)
     def _():
         copies = []
         for at in range(pieces):
             own = pl.ds(at * each, each)
             source = raw_ref.at[own, :, pl.ds(raw_ref.shape[2] - width, width)]
-            copies.append(pltpu.make_async_copy(source, natural.at[own], sems.at[at]))
+            copies.append(pltpu.make_async_copy(source, natural.at[own, :, pl.ds(0, width)], sems.at[at]))
             copies[-1].start()
         for at, copy in enumerate(copies):
             copy.wait()
@@ -93,6 +93,7 @@
             picks, refs_ref[:, part, :].astype(F32), (((0,), (0,)), ((), ())), preferred_element_type=F32
         )
         picked = reversed_lanes(picked.astype(BF))
+        picked = pltpu.roll(picked, L // 2 + 1, 1)
         pieces += [picked[:, t * LANES : (t + 1) * LANES] for t in range(L // LANES)]
     pieces += [jnp.zeros((targets, LANES), F32)] * (rows_ref.shape[1] - len(pieces))
     rows_ref[...] = jnp.stack(pieces, axis=1).astype(BF)
@@ -173,14 +174,31 @@
         held[into + t] = near_ref[t // per_target, at : at + rows]
 
 
+def fill_next(half, raw_ref, first_pulse, held):
+    rows = held.shape[1]
+    pulses = pl.ds(first_pulse, rows // 2)
+    retile(raw_ref.at[pulses], held, half, held.shape[0] - half)
+
+
+def first_kernel(turn_in_ref, window_ref, raw_ref, tail_ref, taps_ref, out_ref, turn_ref, held):
+    turn_ref[...] = turn_in_ref[...]
+    half = tail_ref.shape[0]
+
+    @pl.when(lax.axis_index("sa") == 1)
+    def _():
+        held[:half] = tail_ref[...]
+        fill_next(half, raw_ref, 0, held)
+        compress(held, window_ref[0] // LANES, taps_ref, out_ref, 0, held.shape[1])
+
+
 def middle_kernel(
-    turn_in_ref, window_ref, raw_ref, tail_ref, near_ref, own_ref, taps_ref, rows_ref, out_ref, turn_ref, held, far_held
+    turn_in_ref, window_ref, raw_ref, tail_ref, near_ref, own_ref, first_ref, taps_ref, rows_ref, out_ref, turn_ref, held, far_held
 ):
     turn_ref[...] = turn_in_ref[...]
-    half = tail_ref.shape[0]
-    more = held.shape[0] - half
+    half, before, _ = tail_ref.shape
+    rows = held.shape[1]
+    tile_rows = before + rows
     bins = near_ref.shape[1]
-    tile_rows = held.shape[1]
     sub_index = lax.axis_index("sa")
     offset = window_ref[0] // LANES
     made = out_ref.at[:, pl.ds(0, bins)]
@@ -192,9 +210,11 @@
 
     @pl.when(sub_index == 1)
     def _():
-        take_tiles(near_ref, tile_rows, 0, held, 0, half)
-        retile(raw_ref, held, half, more)
-        compress(held, offset, taps_ref, made, 0, tile_rows)
+        for tile in range(bins // tile_rows):
+            out_ref[:, tile * tile_rows : tile * tile_rows + before] = first_ref[:, tile * before : (tile + 1) * before]
+        take_tiles(near_ref, tile_rows, before, held, 0, half)
+        fill_next(half, raw_ref, before // 2, held)
+        compress(held, offset, taps_ref, made, before, tile_rows)
 
     @pl.when(sub_index == 2)
     def _():
@@ -203,7 +223,7 @@
     @pl.when(sub_index == 3)
     def _():
         far_held[:half] = tail_ref[...]
-        take_tiles(near_ref, tile_rows, 0, far_held, half, more)
+        take_tiles(near_ref, tile_rows, 0, far_held, half, far_held.shape[0] - half)
         compress(far_held, offset, taps_ref, made, 0, tile_rows)
 
 
@@ -230,18 +250,10 @@
     rows = (lines_ref.shape[1] - EXTRA) // tiles
     picked = jnp.sum(lines_ref[:, tiles * rows :].astype(F32), axis=0)
     pieces = L // LANES
-    row = jnp.concatenate(
-        [
-            jnp.concatenate([picked[part * pieces + t : part * pieces + t + 1] for t in range(pieces)], axis=1)
-            for part in range(2)
-        ],
-        axis=0,
-    )
-    moved = pltpu.roll(jnp.concatenate([row] * 4, axis=0), L - (pulses - 1), 1)
-    skewed = [
-        pltpu.roll(jnp.broadcast_to(moved[part : part + 1], (LANES, L)), 0, 1, stride=1, stride_axis=0)
-        for part in range(2)
-    ]
+    skewed = []
+    for part in range(2):
+        spread = [jnp.broadcast_to(picked[part * pieces + t][None], (LANES, LANES)) for t in range(pieces)]
+        skewed.append(pltpu.roll(jnp.concatenate(spread, axis=1), 0, 1, stride=1, stride_axis=0))
     for apart in range(1 - columns, columns):
         at = apart % pieces * LANES
         straight, crossed = (skewed[part][:, at : at + LANES] for part in range(2))
@@ -358,10 +370,14 @@
         tail_first_kernel,
         (shape((half, first_rows, LANES), BF), token),
         "avv",
-        [pltpu.VMEM((first_rows // 2, 2, half * LANES), BF), pltpu.SemaphoreType.DMA((3,))],
+        [pltpu.VMEM((first_rows // 2, 2, (half + 8) * LANES), BF), pltpu.SemaphoreType.DMA((3,))],
         53,
     )(raw_echo)
-    tail_first = lax.ppermute(tail, "sa", [(1, 3)])
+    tail_first = lax.ppermute(tail, "sa", [(0, 1), (1, 3)])
+    tail, turn = call(
+        tail_second_kernel, (shape((half, rows - first_rows, LANES), BF), token), "vvvv"
+    )(turn, raw_echo)
+    tail_second = lax.ppermute(tail, "sa", [(1, 3)])
     taps, own_rows, turn = call(
         prep_kernel,
         (shape((tap_tiles * LANES, 2 * LANES), BF), shape((pulse_devices, EXTRA, LANES), BF), token),
@@ -371,24 +387,25 @@
     own, turn = call(own_kernel, (part, token), "vsvvvv", window_held)(turn, window_start, raw_echo, taps)
     near, turn = call(ahead_kernel, (part, token), "vsvvvv", window_held)(turn, window_start, raw_echo, taps)
     near = lax.ppermute(near, "sa", [(0, 1), (1, 2), (2, 3)])
-    (turn,) = call(gate_kernel, (token,), "vav", flops=10**10)(turn, tail_first)
-    tail, turn = call(
-        tail_second_kernel, (shape((half, rows - first_rows, LANES), BF), token), "vvvv"
-    )(turn, raw_echo)
-    tail_second = lax.ppermute(tail, "sa", [(1, 3)])
     extra = own_rows if short else jnp.zeros((targets, EXTRA, LANES), BF)
     made = shape((targets, slot + EXTRA, LANES), BF)
     wide = span + 16
+    (turn,) = call(gate_kernel, (token,), "vav", flops=10**10)(turn, tail_first)
+    first_held = pltpu.VMEM((wide, first_rows, LANES), BF)
+    last_held = pltpu.VMEM((wide, rows - first_rows, LANES), BF)
+    first, turn = call(
+        first_kernel,
+        (shape((targets, slot // rows * first_rows, LANES), BF), token),
+        "vsvvvvv",
+        [first_held],
+        flops=10**10,
+    )(turn, window_start, raw_echo, tail_first, taps)
     middle, turn = call(
-        middle_kernel,
-        (made, token),
-        "vsvvvvvvvv",
-        [pltpu.VMEM((wide, rows, LANES), BF), pltpu.VMEM((wide, first_rows, LANES), BF)],
-        flops=10**10,
-    )(turn, window_start, raw_echo, tail_first, near, own, taps, extra)
-    (compressed,) = call(
-        last_kernel, (made,), "vsvvvvv", [pltpu.VMEM((wide, rows - first_rows, LANES), BF)], flops=10**10
-    )(turn, window_start, tail_second, near, taps, middle)
+        middle_kernel, (made, token), "vsvvvvvvvvv", [last_held, first_held], flops=10**10
+    )(turn, window_start, raw_echo, tail_first, near, own, first, taps, extra)
+    (compressed,) = call(last_kernel, (made,), "vsvvvvv", [last_held], flops=10**10)(
+        turn, window_start, tail_second, near, taps, middle
+    )
 
     if not short:
         kept = compressed[:, :-EXTRA].reshape(half, pulses, 2, LANES).transpose(0, 3, 2, 1)
@@ -396,7 +413,8 @@
         turned = lax.all_to_all(outgoing, "pa", split_axis=0, concat_axis=3, tiled=True)
         rows_in = lax.all_to_all(own_rows, "pa", split_axis=0, concat_axis=0, tiled=True)
         reference_row = jnp.sum(rows_in[:, :8].astype(F32), axis=0).astype(BF).reshape(2, L)
-        return focus_long(turned[0], reference_row[:, ::-1])
+        reference_row = jnp.roll(reference_row, -(L // 2 + 1), axis=1)[:, ::-1]
+        return focus_long(turned[0], reference_row)
 
     lines = lax.all_to_all(compressed, "pa", split_axis=0, concat_axis=0, tiled=True)
     width = 2 * total_pulses
@@ -405,9 +423,9 @@
         (shape((bin_count * width // LANES, LANES), F32),),
         "va",
         [
-            pltpu.VMEM((width // LANES * 2 - 2, 2 * LANES, LANES), F32),
+            pltpu.VMEM((width // LANES * 2 - 1, 2 * LANES, LANES), F32),
             pltpu.VMEM((width, width), BF),
-            pltpu.VMEM((bin_count * width // LANES, LANES), F32),
+            pltpu.VMEM((bin_count * width // LANES + 8, LANES), F32),
             pltpu.SemaphoreType.DMA((bin_count // LANES,)),
         ],
     )(lines)

time: 41.1 us -> 36.6 us (0.89)
  the two profiles are of different devices: /device:TPU:2 before, /device:TPU:1 now
where the time goes in v26:
time: 36.6 us; the launch traced here: 36.4 us
  blocking collectives  17.7 us (48%)
  Pallas kernels  7.08 us (19%)
  starting transfers between devices  6.1 us (17%)
  waiting for transfers between devices  4.71 us (13%)
  between operations  0.82 us (2%)
    all_to_all x1, blocking collectives, on_device(): lax.all_to_all(compressed, 'pa', split_axis=0, concat_axis=0, tiled=True)  17.7 us
    ppermute x1, waiting for transfers between devices, on_device(): near = lax.ppermute(near, 'sa', [(0, 1), (1, 2), (2, 3)])  4.71 us
    ppermute x1, starting transfers between devices, on_device(): tail_first = lax.ppermute(tail, 'sa', [(0, 1), (1, 3)])  2.88 us
    ppermute x1, starting transfers between devices, on_device(): near = lax.ppermute(near, 'sa', [(0, 1), (1, 2), (2, 3)])  1.92 us
    pallas_call x1, Pallas kernels, on_device(): call(ahead_kernel, (part, token), 'vsvvvv', window_held)  1.69 us
    pallas_call x1, Pallas kernels, on_device(): call(azimuth_kernel, (shape((bin_count * width // LANES, LANES), F32),),...  1.49 us
    pallas_call x1, Pallas kernels, on_device(): call(first_kernel, (shape((targets, slot // rows * first_rows, LANES), BF...  1.37 us
    ppermute x1, starting transfers between devices, on_device(): tail_second = lax.ppermute(tail, 'sa', [(1, 3)])  1.3 us
  transfers between devices with their start and end apart: 3, of which 1 were waited for; matrix products, arithmetic and copies ran while one was open for 0% of the time, Pallas kernels for 12%

profile of v26, /device:TPU:1, one launch (start us, length us, event | category | flops | bytes accessed | tf_op | source)
XLA Modules:
  0.0 36.4 jit_solution(10340383968385941104)
XLA Ops:
  0.0 0.0 copy-start
  0.0 1.2 %shard_map.55 = (bf16[32,48,128]{2,1,0:T(8,128)(2,1)S(1)}, f32[8,128]{1,0:T(8,128)S(1)}) custom-call(bf16[32,2,8192]{2,1,0:T(2,128)(2,1)} %raw_ref.11), custom_call_target="tpu_custom_call" | custom-call | flops 1000 | bytes 1000 | tf_op jit(solution)/shard_map/pallas_call | solution.py:369
  1.2 2.9 %collective-permute-start = (bf16[32,48,128]{2,1,0:T(8,128)(2,1)S(1)}, bf16[32,48,128]{2,1,0:T(8,128)(2,1)S(1)}, u32[]{:S(2)}, u32[]{:S(2)}) collective-permute-start(bf16[32,48,128]{2,1,0:T(8,128)(2,1)S(1)} %get-tuple-element.26), channel_id=1, source_target_pairs={{0,1},{1,3},{4,5},{5,7},{8,9},{9,11},{12,13},{13,15},{16,17},{17,1... | collective-permute-start | bytes 1179656 | tf_op jit(solution)/shard_map/ppermute | solution.py:376
  4.1 0.0 copy-done
  4.1 0.0 copy-start.1
  4.1 0.0 copy-start.3
  4.2 0.1 shard_map.56
  4.2 0.0 copy-start.2
  4.3 1.3 %collective-permute-start.2 = (bf16[32,16,128]{2,1,0:T(8,128)(2,1)S(1)}, bf16[32,16,128]{2,1,0:T(8,128)(2,1)S(1)}, u32[]{:S(2)}, u32[]{:S(2)}) collective-permute-start(bf16[32,16,128]{2,1,0:T(8,128)(2,1)S(1)} %get-tuple-element.33), channel_id=1, source_target_pairs={{1,3},{5,7},{9,11},{13,15},{17,19},{21,23},{25,27},{29,31}} | collective-permute-start | bytes 393224 | tf_op jit(solution)/shard_map/ppermute | solution.py:380
  6.2 0.0 copy-done.1
  6.2 0.0 copy-done.3
  6.2 0.0 copy-done.2
  6.2 0.6 %shard_map.57 = (bf16[1280,256]{1,0:T(8,128)(2,1)S(1)}, bf16[8,16,128]{2,1,0:T(8,128)(2,1)S(1)}, f32[8,128]{1,0:T(8,128)S(1)}) custom-call(f32[8,128]{1,0:T(8,128)S(1)} %get-tuple-element.21.turn_in_ref, s32[1]{0:T(128)S(6)} %copy.7.window_ref, s32[4,8]{1,0:T(4,128)S(1)} %copy-done.3, bf16[2,1024]{1,0:T(2,128)(2,1)S(1)} %copy-done.2, ...), custom_call_target="tpu_custom_call" | custom-call | flops 1000 | bytes 1000 | tf_op jit(solution)/shard_map/pallas_call | solution.py:381
  6.8 1.7 %shard_map.59 = (bf16[8,256,128]{2,1,0:T(8,128)(2,1)S(1)}, f32[8,128]{1,0:T(8,128)S(1)}) custom-call(f32[8,128]{1,0:T(8,128)S(1)} %get-tuple-element.24.turn_in_ref, s32[1]{0:T(128)S(6)} %copy.7.window_ref, bf16[32,2,8192]{2,1,0:T(2,128)(2,1)S(1)} %copy-done, bf16[1280,256]{1,0:T(8,128)(2,1)S(1)} %get-tuple-element.23.taps_ref), custom_call_target="tpu_custom_call" | custom-call | flops 1000 | bytes 1000 | tf_op jit(solution)/shard_map/pallas_call | solution.py:388
  8.5 1.9 %collective-permute-start.1 = (bf16[8,256,128]{2,1,0:T(8,128)(2,1)S(1)}, bf16[8,256,128]{2,1,0:T(8,128)(2,1)S(1)}, u32[]{:S(2)}, u32[]{:S(2)}) collective-permute-start(bf16[8,256,128]{2,1,0:T(8,128)(2,1)S(1)} %get-tuple-element.28), channel_id=1, source_target_pairs={{0,1},{1,2},{2,3},{4,5},{5,6},{6,7},{8,9},{9,10},{10,11},{12,13},{... | collective-permute-start | bytes 1572872 | tf_op jit(solution)/shard_map/ppermute | solution.py:389
  10.5 0.0 collective-permute-done._.tail_ref
  10.5 1.4 %shard_map.61 = (bf16[8,192,128]{2,1,0:T(8,128)(2,1)S(1)}, f32[8,128]{1,0:T(8,128)S(1)}) custom-call(f32[8,128]{1,0:T(8,128)S(1)} %shard_map.60.turn_in_ref, s32[1]{0:T(128)S(6)} %copy.7.window_ref, bf16[32,2,8192]{2,1,0:T(2,128)(2,1)S(1)} %copy-done, bf16[32,48,128]{2,1,0:T(8,128)(2,1)S(1)} %collective-permute-done._.tail_ref, ...), custom_call_target="tpu_custom_call" | custom-call | flops 10000000000 | bytes 1000 | tf_op jit(solution)/shard_map/pallas_call | solution.py:396
  11.9 4.7 %collective-permute-done.1.near_ref = bf16[8,256,128]{2,1,0:T(8,128)(2,1)S(1)} collective-permute-done((bf16[8,256,128]{2,1,0:T(8,128)(2,1)S(1)}, bf16[8,256,128]{2,1,0:T(8,128)(2,1)S(1)}, u32[]{:S(2)}, u32[]{:S(2)}) %collective-permute-start.1) | collective-permute-done | bytes 524320 | tf_op jit(solution)/shard_map/ppermute | solution.py:389
  16.6 0.6 %shard_map.62 = (bf16[8,272,128]{2,1,0:T(8,128)(2,1)S(1)}, f32[8,128]{1,0:T(8,128)S(1)}) custom-call(f32[8,128]{1,0:T(8,128)S(1)} %get-tuple-element.27.turn_in_ref, s32[1]{0:T(128)S(6)} %copy.7.window_ref, bf16[32,2,8192]{2,1,0:T(2,128)(2,1)S(1)} %copy-done, bf16[32,48,128]{2,1,0:T(8,128)(2,1)S(1)} %collective-permute-done._.tail_ref, ...), custom_call_target="tpu_custom_call" | custom-call | flops 10000000000 | bytes 1000 | tf_op jit(solution)/shard_map/pallas_call | solution.py:403
  17.2 0.0 collective-permute-done.2.tail_ref
  17.2 17.7 %all_to_all.5.lines_ref = bf16[8,272,128]{2,1,0:T(8,128)(2,1)S(1)} all-to-all(bf16[8,272,128]{2,1,0:T(8,128)(2,1)S(1)} %shard_map.63), channel_id=1, replica_groups=mesh['pa'=8,'sa'=4] {'pa'}, dimensions={0} | all-to-all | bytes 1114112 | tf_op jit(solution)/shard_map/all_to_all | solution.py:419
  34.9 1.5 %shard_map.64 = f32[2048,128]{1,0:T(8,128)} custom-call(bf16[8,272,128]{2,1,0:T(8,128)(2,1)S(1)} %all_to_all.5.lines_ref), custom_call_target="tpu_custom_call" | custom-call | flops 1000 | bytes 1000 | tf_op jit(solution)/shard_map/pallas_call | solution.py:421
  (3 shorter events, 0.1 us)
Async XLA Ops:
  0.0 4.1 %copy-start = (bf16[32,2,8192]{2,1,0:T(2,128)(2,1)S(1)}, bf16[32,2,8192]{2,1,0:T(2,128)(2,1)}, u32[]{:S(2)}) copy-start(bf16[32,2,8192]{2,1,0:T(2,128)(2,1)} %raw_ref.11) | copy-start | bytes 3145732
  1.2 9.2 %collective-permute-start = (bf16[32,48,128]{2,1,0:T(8,128)(2,1)S(1)}, bf16[32,48,128]{2,1,0:T(8,128)(2,1)S(1)}, u32[]{:S(2)}, u32[]{:S(2)}) collective-permute-start(bf16[32,48,128]{2,1,0:T(8,128)(2,1)S(1)} %get-tuple-element.26), channel_id=1, source_target_pairs={{0,1},{1,3},{4,5},{5,7},{8,9},{9,11},{12,13},{13,15},{16,17},{17,1... | collective-permute-start | bytes 1179656 | tf_op jit(solution)/shard_map/ppermute | solution.py:376
  4.1 2.1 %copy-start.1 = (bf16[8,2,512]{2,1,0:T(2,128)(2,1)S(1)}, bf16[8,2,512]{2,1,0:T(2,128)(2,1)}, u32[]{:S(2)}) copy-start(bf16[8,2,512]{2,1,0:T(2,128)(2,1)} %refs_ref.1) | copy-start | bytes 49156
  4.1 2.1 %copy-start.3 = (s32[4,8]{1,0:T(4,128)S(1)}, s32[4,8]{1,0:T(4,128)}, u32[]{:S(2)}) copy-start(s32[4,8]{1,0:T(4,128)} %index_ref.1) | copy-start | bytes 388
  4.2 2.0 %copy-start.2 = (bf16[2,1024]{1,0:T(2,128)(2,1)S(1)}, bf16[2,1024]{1,0:T(2,128)(2,1)}, u32[]{:S(2)}) copy-start(bf16[2,1024]{1,0:T(2,128)(2,1)} %chirp_ref.1) | copy-start | bytes 12292
  4.3 12.9 %collective-permute-start.2 = (bf16[32,16,128]{2,1,0:T(8,128)(2,1)S(1)}, bf16[32,16,128]{2,1,0:T(8,128)(2,1)S(1)}, u32[]{:S(2)}, u32[]{:S(2)}) collective-permute-start(bf16[32,16,128]{2,1,0:T(8,128)(2,1)S(1)} %get-tuple-element.33), channel_id=1, source_target_pairs={{1,3},{5,7},{9,11},{13,15},{17,19},{21,23},{25,27},{29,31}} | collective-permute-start | bytes 393224 | tf_op jit(solution)/shard_map/ppermute | solution.py:380
  8.5 8.0 %collective-permute-start.1 = (bf16[8,256,128]{2,1,0:T(8,128)(2,1)S(1)}, bf16[8,256,128]{2,1,0:T(8,128)(2,1)S(1)}, u32[]{:S(2)}, u32[]{:S(2)}) collective-permute-start(bf16[8,256,128]{2,1,0:T(8,128)(2,1)S(1)} %get-tuple-element.28), channel_id=1, source_target_pairs={{0,1},{1,2},{2,3},{4,5},{5,6},{6,7},{8,9},{9,10},{10,11},{12,13},{... | collective-permute-start | bytes 1572872 | tf_op jit(solution)/shard_map/ppermute | solution.py:389

commit v27 on v25

--- a/solution.py
+++ b/solution.py
@@ -8,7 +8,7 @@
 R = 16384
 L = 512
 LANES = 128
-EXTRA = 16
+EXTRA = 8
 BF = jnp.bfloat16
 F32 = jnp.float32
 
@@ -134,6 +134,7 @@
     span = half + more - 16
     sub_index = lax.axis_index("sa")
     offset = window_ref[0] // LANES
+    made = out_ref.at[:, pl.ds(EXTRA, out_ref.shape[1] - EXTRA)]
 
     @pl.when(sub_index == 0)
     def _():
@@ -147,21 +148,20 @@
 
     @pl.when(sub_index < 2)
     def _():
-        compress(held, jnp.where(sub_index == 0, 0, offset), taps_ref, out_ref)
+        compress(held, jnp.where(sub_index == 0, 0, offset), taps_ref, made)
 
     @pl.when(sub_index == 3)
     def _():
         held[:half] = tail_ref[...]
         held[half:] = head_ref[...]
-        compress(held, offset, taps_ref, out_ref, tail_ref)
+        compress(held, offset, taps_ref, made, tail_ref)
 
     @pl.when(sub_index != 2)
     def _():
-        out_ref[:, out_ref.shape[1] - rows_ref.shape[1] :] = rows_ref[...]
+        out_ref[:, :EXTRA] = rows_ref[...][:, :EXTRA]
 
 
 def late_kernel(near_ref, rows_ref, early_ref, out_ref):
-    bins = near_ref.shape[1]
     sub_index = lax.axis_index("sa")
 
     @pl.when(sub_index != 2)
@@ -170,8 +170,8 @@
 
     @pl.when(sub_index == 2)
     def _():
-        out_ref[:, :bins] = near_ref[...]
-        out_ref[:, bins:] = rows_ref[...]
+        out_ref[:, EXTRA:] = near_ref[...]
+        out_ref[:, :EXTRA] = rows_ref[...][:, :EXTRA]
 
 
 def azimuth_kernel(lines_ref, out_ref, columns_held, taps, made, sems):
@@ -181,7 +181,7 @@
     each = out_ref.shape[0] // tiles
     sources = lines_ref.shape[0]
     rows = (lines_ref.shape[1] - EXTRA) // tiles
-    picked = jnp.sum(lines_ref[:, tiles * rows :].astype(F32), axis=0)
+    picked = jnp.sum(lines_ref[:, :EXTRA].astype(F32), axis=0)
     pieces = L // LANES
     skewed = []
     for part in range(2):
@@ -202,7 +202,7 @@
                     taps[2 * line * LANES : 2 * (line + 1) * LANES, lane : lane + LANES] = block
     copies = []
     for tile in range(tiles):
-        lines = lines_ref[:, tile * rows : (tile + 1) * rows].reshape(sources * rows, LANES)
+        lines = lines_ref[:, EXTRA + tile * rows : EXTRA + (tile + 1) * rows].reshape(sources * rows, LANES)
         focused = lax.dot_general(lines, taps[...], (((0,), (0,)), ((), ())), preferred_element_type=F32)
         into = pl.ds(tile * each, each)
         for part in range(2):
@@ -309,7 +309,7 @@
     head = lax.ppermute(head, "sa", [(2, 3)])
     taps, own_rows, turn = call(
         prep_kernel,
-        (shape((tap_tiles * LANES, 2 * LANES), BF), shape((pulse_devices, EXTRA, LANES), BF), token),
+        (shape((tap_tiles * LANES, 2 * LANES), BF), shape((pulse_devices, 2 * EXTRA, LANES), BF), token),
         "vsvvvvvv",
     )(turn, window_start, migration_index, chirp_replica, azimuth_refs)
     near, turn = call(
@@ -319,7 +319,7 @@
         [pltpu.VMEM((span, rows, LANES), BF)],
     )(turn, window_start, raw_echo, taps)
     near = lax.ppermute(near, "sa", [(1, 2)])
-    extra = own_rows if short else jnp.zeros((targets, EXTRA, LANES), BF)
+    extra = own_rows if short else jnp.zeros((targets, 2 * EXTRA, LANES), BF)
     made = shape((targets, slot + EXTRA, LANES), BF)
     (early,) = call(
         early_kernel,
@@ -331,7 +331,7 @@
     (compressed,) = call(late_kernel, (made,), "vvvv")(near, extra, early)
 
     if not short:
-        kept = compressed[:, :-EXTRA].reshape(half, pulses, 2, LANES).transpose(0, 3, 2, 1)
+        kept = compressed[:, EXTRA:].reshape(half, pulses, 2, LANES).transpose(0, 3, 2, 1)
         outgoing = kept.reshape(pulse_devices, bin_count, 2, pulses)
         turned = lax.all_to_all(outgoing, "pa", split_axis=0, concat_axis=3, tiled=True)
         rows_in = lax.all_to_all(own_rows, "pa", split_axis=0, concat_axis=0, tiled=True)

time: 35.1 us -> 34.8 us (level)
  no operation moved by 1% of the time
where the time goes in v27:
time: 34.8 us; the launch traced here: 34.5 us
  blocking collectives  17.3 us (50%)
  waiting for transfers between devices  9.79 us (28%)
  starting transfers between devices  3.96 us (11%)
  Pallas kernels  2.38 us (7%)
  between operations  0.76 us (2%)
  local copies, waits for them, and re-layouts  0.36 us (1%)
    all_to_all x1, blocking collectives, on_device(): lax.all_to_all(compressed, 'pa', split_axis=0, concat_axis=0, tiled=True)  17.3 us
    ppermute x1, waiting for transfers between devices, on_device(): near = lax.ppermute(near, 'sa', [(1, 2)])  9.79 us
    ppermute x1, starting transfers between devices, on_device(): head = lax.ppermute(head, 'sa', [(2, 3)])  1.84 us
    pallas_call x1, Pallas kernels, on_device(): call(azimuth_kernel, (shape((bin_count * width // LANES, LANES), F32),),...  1.48 us
    ppermute x1, starting transfers between devices, on_device(): near = lax.ppermute(near, 'sa', [(1, 2)])  1.29 us
    ppermute x1, starting transfers between devices, on_device(): tail = lax.ppermute(tail, 'sa', [(0, 1), (1, 3)])  0.83 us
  transfers between devices with their start and end apart: 3, of which 1 were waited for; matrix products, arithmetic and copies ran while one was open for 0% of the time, Pallas kernels for 2%

profile of v27, /device:TPU:2, one launch (start us, length us, event | category | flops | bytes accessed | tf_op | source)
XLA Modules:
  0.0 34.5 jit_solution(17619081103003998074)
XLA Ops:
  0.0 0.0 copy-start
  0.0 0.8 %collective-permute-start.1 = (bf16[32,64,128]{2,1,0:T(8,128)(2,1)S(1)}, bf16[32,64,128]{2,1,0:T(8,128)(2,1)S(1)}, u32[]{:S(2)}, u32[]{:S(2)}) collective-permute-start(bf16[32,64,128]{2,1,0:T(8,128)(2,1)S(1)} %get-tuple-element.21), channel_id=1, source_target_pairs={{0,1},{1,3},{4,5},{5,7},{8,9},{9,11},{12,13},{13,15},{16,17},{17,1... | collective-permute-start | bytes 1572872 | tf_op jit(solution)/shard_map/ppermute | solution.py:307
  0.9 0.3 copy-done
  1.2 0.0 copy-start.1
  1.2 0.0 copy-start.3
  1.2 0.2 shard_map.56
  1.5 0.0 copy-start.2
  1.5 1.8 %collective-permute-start.2 = (bf16[25,64,128]{2,1,0:T(8,128)(2,1)S(1)}, bf16[25,64,128]{2,1,0:T(8,128)(2,1)S(1)}, u32[]{:S(2)}, u32[]{:S(2)}) collective-permute-start(bf16[25,64,128]{2,1,0:T(8,128)(2,1)S(1)} %get-tuple-element.22), channel_id=1, source_target_pairs={{2,3},{6,7},{10,11},{14,15},{18,19},{22,23},{26,27},{30,31}} | collective-permute-start | bytes 1228808 | tf_op jit(solution)/shard_map/ppermute | solution.py:309
  4.0 0.0 copy-done.1
  4.0 0.0 copy-done.3
  4.0 0.0 copy-done.2
  4.0 0.6 %shard_map.57 = (bf16[1280,256]{1,0:T(8,128)(2,1)S(1)}, bf16[8,16,128]{2,1,0:T(8,128)(2,1)S(1)}, f32[8,128]{1,0:T(8,128)S(1)}) custom-call(f32[8,128]{1,0:T(8,128)S(1)} %get-tuple-element.15.turn_in_ref, s32[1]{0:T(128)S(6)} %copy.7.window_ref, s32[4,8]{1,0:T(4,128)S(1)} %copy-done.3, bf16[2,1024]{1,0:T(2,128)(2,1)S(1)} %copy-done.2, ...), custom_call_target="tpu_custom_call" | custom-call | flops 1000 | bytes 1000 | tf_op jit(solution)/shard_map/pallas_call | solution.py:310
  4.6 1.3 %collective-permute-start = (bf16[8,256,128]{2,1,0:T(8,128)(2,1)S(1)}, bf16[8,256,128]{2,1,0:T(8,128)(2,1)S(1)}, u32[]{:S(2)}, u32[]{:S(2)}) collective-permute-start(bf16[8,256,128]{2,1,0:T(8,128)(2,1)S(1)} %get-tuple-element.18), channel_id=1, source_target_pairs={{1,2},{5,6},{9,10},{13,14},{17,18},{21,22},{25,26},{29,30}} | collective-permute-start | bytes 1572872 | tf_op jit(solution)/shard_map/ppermute | solution.py:321
  5.9 0.0 collective-permute-done.2.head_ref
  5.9 0.0 collective-permute-done.1.tail_ref
  5.9 9.8 %collective-permute-done.near_ref = bf16[8,256,128]{2,1,0:T(8,128)(2,1)S(1)} collective-permute-done((bf16[8,256,128]{2,1,0:T(8,128)(2,1)S(1)}, bf16[8,256,128]{2,1,0:T(8,128)(2,1)S(1)}, u32[]{:S(2)}, u32[]{:S(2)}) %collective-permute-start) | collective-permute-done | bytes 524320 | tf_op jit(solution)/shard_map/ppermute | solution.py:321
  15.8 17.3 %all_to_all.5.lines_ref = bf16[8,264,128]{2,1,0:T(8,128)(2,1)S(1)} all-to-all(bf16[8,264,128]{2,1,0:T(8,128)(2,1)S(1)} %shard_map.60), channel_id=1, replica_groups=mesh['pa'=8,'sa'=4] {'pa'}, dimensions={0} | all-to-all | bytes 1081344 | tf_op jit(solution)/shard_map/all_to_all | solution.py:342
  33.1 1.5 %shard_map.61 = f32[2048,128]{1,0:T(8,128)} custom-call(bf16[8,264,128]{2,1,0:T(8,128)(2,1)S(1)} %all_to_all.5.lines_ref), custom_call_target="tpu_custom_call" | custom-call | flops 1000 | bytes 1000 | tf_op jit(solution)/shard_map/pallas_call | solution.py:344
  (4 shorter events, 0.1 us)
Async XLA Ops:
  0.0 1.2 %copy-start = (bf16[32,2,8192]{2,1,0:T(2,128)(2,1)S(1)}, bf16[32,2,8192]{2,1,0:T(2,128)(2,1)}, u32[]{:S(2)}) copy-start(bf16[32,2,8192]{2,1,0:T(2,128)(2,1)} %raw_ref.7) | copy-start | bytes 3145732
  0.0 5.8 %collective-permute-start.1 = (bf16[32,64,128]{2,1,0:T(8,128)(2,1)S(1)}, bf16[32,64,128]{2,1,0:T(8,128)(2,1)S(1)}, u32[]{:S(2)}, u32[]{:S(2)}) collective-permute-start(bf16[32,64,128]{2,1,0:T(8,128)(2,1)S(1)} %get-tuple-element.21), channel_id=1, source_target_pairs={{0,1},{1,3},{4,5},{5,7},{8,9},{9,11},{12,13},{13,15},{16,17},{17,1... | collective-permute-start | bytes 1572872 | tf_op jit(solution)/shard_map/ppermute | solution.py:307
  1.2 2.7 %copy-start.1 = (bf16[8,2,512]{2,1,0:T(2,128)(2,1)S(1)}, bf16[8,2,512]{2,1,0:T(2,128)(2,1)}, u32[]{:S(2)}) copy-start(bf16[8,2,512]{2,1,0:T(2,128)(2,1)} %refs_ref.1) | copy-start | bytes 49156
  1.2 2.8 %copy-start.3 = (s32[4,8]{1,0:T(4,128)S(1)}, s32[4,8]{1,0:T(4,128)}, u32[]{:S(2)}) copy-start(s32[4,8]{1,0:T(4,128)} %index_ref.1) | copy-start | bytes 388
  1.5 2.5 %copy-start.2 = (bf16[2,1024]{1,0:T(2,128)(2,1)S(1)}, bf16[2,1024]{1,0:T(2,128)(2,1)}, u32[]{:S(2)}) copy-start(bf16[2,1024]{1,0:T(2,128)(2,1)} %chirp_ref.1) | copy-start | bytes 12292
  1.5 4.4 %collective-permute-start.2 = (bf16[25,64,128]{2,1,0:T(8,128)(2,1)S(1)}, bf16[25,64,128]{2,1,0:T(8,128)(2,1)S(1)}, u32[]{:S(2)}, u32[]{:S(2)}) collective-permute-start(bf16[25,64,128]{2,1,0:T(8,128)(2,1)S(1)} %get-tuple-element.22), channel_id=1, source_target_pairs={{2,3},{6,7},{10,11},{14,15},{18,19},{22,23},{26,27},{30,31}} | collective-permute-start | bytes 1228808 | tf_op jit(solution)/shard_map/ppermute | solution.py:309
  4.6 11.2 %collective-permute-start = (bf16[8,256,128]{2,1,0:T(8,128)(2,1)S(1)}, bf16[8,256,128]{2,1,0:T(8,128)(2,1)S(1)}, u32[]{:S(2)}, u32[]{:S(2)}) collective-permute-start(bf16[8,256,128]{2,1,0:T(8,128)(2,1)S(1)} %get-tuple-element.18), channel_id=1, source_target_pairs={{1,2},{5,6},{9,10},{13,14},{17,18},{21,22},{25,26},{29,30}} | collective-permute-start | bytes 1572872 | tf_op jit(solution)/shard_map/ppermute | solution.py:321

commit v28 on v27

--- a/solution.py
+++ b/solution.py
@@ -181,6 +181,10 @@
     each = out_ref.shape[0] // tiles
     sources = lines_ref.shape[0]
     rows = (lines_ref.shape[1] - EXTRA) // tiles
+    turned = [
+        lines_ref[:, EXTRA + tile * rows : EXTRA + (tile + 1) * rows].reshape(sources * rows, LANES).T
+        for tile in range(tiles)
+    ]
     picked = jnp.sum(lines_ref[:, :EXTRA].astype(F32), axis=0)
     pieces = L // LANES
     skewed = []
@@ -202,8 +206,7 @@
                     taps[2 * line * LANES : 2 * (line + 1) * LANES, lane : lane + LANES] = block
     copies = []
     for tile in range(tiles):
-        lines = lines_ref[:, EXTRA + tile * rows : EXTRA + (tile + 1) * rows].reshape(sources * rows, LANES)
-        focused = lax.dot_general(lines, taps[...], (((0,), (0,)), ((), ())), preferred_element_type=F32)
+        focused = jnp.dot(turned[tile], taps[...], preferred_element_type=F32)
         into = pl.ds(tile * each, each)
         for part in range(2):
             for column in range(columns):

time: 34.8 us -> 34.8 us (level)
  no operation moved by 1% of the time
where the time goes in v28:
time: 34.8 us; the launch traced here: 34.5 us
  blocking collectives  17.3 us (50%)
  waiting for transfers between devices  9.79 us (28%)
  starting transfers between devices  3.96 us (11%)
  Pallas kernels  2.39 us (7%)
  between operations  0.76 us (2%)
  local copies, waits for them, and re-layouts  0.36 us (1%)
    all_to_all x1, blocking collectives, on_device(): lax.all_to_all(compressed, 'pa', split_axis=0, concat_axis=0, tiled=True)  17.3 us
    ppermute x1, waiting for transfers between devices, on_device(): near = lax.ppermute(near, 'sa', [(1, 2)])  9.79 us
    ppermute x1, starting transfers between devices, on_device(): head = lax.ppermute(head, 'sa', [(2, 3)])  1.84 us
    pallas_call x1, Pallas kernels, on_device(): call(azimuth_kernel, (shape((bin_count * width // LANES, LANES), F32),),...  1.48 us
    ppermute x1, starting transfers between devices, on_device(): near = lax.ppermute(near, 'sa', [(1, 2)])  1.29 us
    ppermute x1, starting transfers between devices, on_device(): tail = lax.ppermute(tail, 'sa', [(0, 1), (1, 3)])  0.83 us
  transfers between devices with their start and end apart: 3, of which 1 were waited for; matrix products, arithmetic and copies ran while one was open for 0% of the time, Pallas kernels for 2%

profile of v28, /device:TPU:2, one launch (start us, length us, event | category | flops | bytes accessed | tf_op | source)
XLA Modules:
  0.0 34.5 jit_solution(13488880230303978762)
XLA Ops:
  0.0 0.0 copy-start
  0.0 0.8 %collective-permute-start.1 = (bf16[32,64,128]{2,1,0:T(8,128)(2,1)S(1)}, bf16[32,64,128]{2,1,0:T(8,128)(2,1)S(1)}, u32[]{:S(2)}, u32[]{:S(2)}) collective-permute-start(bf16[32,64,128]{2,1,0:T(8,128)(2,1)S(1)} %get-tuple-element.21), channel_id=1, source_target_pairs={{0,1},{1,3},{4,5},{5,7},{8,9},{9,11},{12,13},{13,15},{16,17},{17,1... | collective-permute-start | bytes 1572872 | tf_op jit(solution)/shard_map/ppermute | solution.py:310
  0.9 0.3 copy-done
  1.2 0.0 copy-start.1
  1.2 0.0 copy-start.3
  1.2 0.2 shard_map.56
  1.5 0.0 copy-start.2
  1.5 1.8 %collective-permute-start.2 = (bf16[25,64,128]{2,1,0:T(8,128)(2,1)S(1)}, bf16[25,64,128]{2,1,0:T(8,128)(2,1)S(1)}, u32[]{:S(2)}, u32[]{:S(2)}) collective-permute-start(bf16[25,64,128]{2,1,0:T(8,128)(2,1)S(1)} %get-tuple-element.22), channel_id=1, source_target_pairs={{2,3},{6,7},{10,11},{14,15},{18,19},{22,23},{26,27},{30,31}} | collective-permute-start | bytes 1228808 | tf_op jit(solution)/shard_map/ppermute | solution.py:312
  4.0 0.0 copy-done.1
  4.0 0.0 copy-done.3
  4.0 0.0 copy-done.2
  4.0 0.6 %shard_map.57 = (bf16[1280,256]{1,0:T(8,128)(2,1)S(1)}, bf16[8,16,128]{2,1,0:T(8,128)(2,1)S(1)}, f32[8,128]{1,0:T(8,128)S(1)}) custom-call(f32[8,128]{1,0:T(8,128)S(1)} %get-tuple-element.15.turn_in_ref, s32[1]{0:T(128)S(6)} %copy.7.window_ref, s32[4,8]{1,0:T(4,128)S(1)} %copy-done.3, bf16[2,1024]{1,0:T(2,128)(2,1)S(1)} %copy-done.2, ...), custom_call_target="tpu_custom_call" | custom-call | flops 1000 | bytes 1000 | tf_op jit(solution)/shard_map/pallas_call | solution.py:313
  4.6 1.3 %collective-permute-start = (bf16[8,256,128]{2,1,0:T(8,128)(2,1)S(1)}, bf16[8,256,128]{2,1,0:T(8,128)(2,1)S(1)}, u32[]{:S(2)}, u32[]{:S(2)}) collective-permute-start(bf16[8,256,128]{2,1,0:T(8,128)(2,1)S(1)} %get-tuple-element.18), channel_id=1, source_target_pairs={{1,2},{5,6},{9,10},{13,14},{17,18},{21,22},{25,26},{29,30}} | collective-permute-start | bytes 1572872 | tf_op jit(solution)/shard_map/ppermute | solution.py:324
  5.9 0.0 collective-permute-done.2.head_ref
  5.9 0.0 collective-permute-done.1.tail_ref
  5.9 9.8 %collective-permute-done.near_ref = bf16[8,256,128]{2,1,0:T(8,128)(2,1)S(1)} collective-permute-done((bf16[8,256,128]{2,1,0:T(8,128)(2,1)S(1)}, bf16[8,256,128]{2,1,0:T(8,128)(2,1)S(1)}, u32[]{:S(2)}, u32[]{:S(2)}) %collective-permute-start) | collective-permute-done | bytes 524320 | tf_op jit(solution)/shard_map/ppermute | solution.py:324
  15.8 17.3 %all_to_all.5.lines_ref = bf16[8,264,128]{2,1,0:T(8,128)(2,1)S(1)} all-to-all(bf16[8,264,128]{2,1,0:T(8,128)(2,1)S(1)} %shard_map.60), channel_id=1, replica_groups=mesh['pa'=8,'sa'=4] {'pa'}, dimensions={0} | all-to-all | bytes 1081344 | tf_op jit(solution)/shard_map/all_to_all | solution.py:345
  33.1 1.5 %shard_map.61 = f32[2048,128]{1,0:T(8,128)} custom-call(bf16[8,264,128]{2,1,0:T(8,128)(2,1)S(1)} %all_to_all.5.lines_ref), custom_call_target="tpu_custom_call" | custom-call | flops 1000 | bytes 1000 | tf_op jit(solution)/shard_map/pallas_call | solution.py:347
  (4 shorter events, 0.1 us)
Async XLA Ops:
  0.0 1.2 %copy-start = (bf16[32,2,8192]{2,1,0:T(2,128)(2,1)S(1)}, bf16[32,2,8192]{2,1,0:T(2,128)(2,1)}, u32[]{:S(2)}) copy-start(bf16[32,2,8192]{2,1,0:T(2,128)(2,1)} %raw_ref.7) | copy-start | bytes 3145732
  0.0 5.8 %collective-permute-start.1 = (bf16[32,64,128]{2,1,0:T(8,128)(2,1)S(1)}, bf16[32,64,128]{2,1,0:T(8,128)(2,1)S(1)}, u32[]{:S(2)}, u32[]{:S(2)}) collective-permute-start(bf16[32,64,128]{2,1,0:T(8,128)(2,1)S(1)} %get-tuple-element.21), channel_id=1, source_target_pairs={{0,1},{1,3},{4,5},{5,7},{8,9},{9,11},{12,13},{13,15},{16,17},{17,1... | collective-permute-start | bytes 1572872 | tf_op jit(solution)/shard_map/ppermute | solution.py:310
  1.2 2.7 %copy-start.1 = (bf16[8,2,512]{2,1,0:T(2,128)(2,1)S(1)}, bf16[8,2,512]{2,1,0:T(2,128)(2,1)}, u32[]{:S(2)}) copy-start(bf16[8,2,512]{2,1,0:T(2,128)(2,1)} %refs_ref.1) | copy-start | bytes 49156
  1.2 2.8 %copy-start.3 = (s32[4,8]{1,0:T(4,128)S(1)}, s32[4,8]{1,0:T(4,128)}, u32[]{:S(2)}) copy-start(s32[4,8]{1,0:T(4,128)} %index_ref.1) | copy-start | bytes 388
  1.5 2.5 %copy-start.2 = (bf16[2,1024]{1,0:T(2,128)(2,1)S(1)}, bf16[2,1024]{1,0:T(2,128)(2,1)}, u32[]{:S(2)}) copy-start(bf16[2,1024]{1,0:T(2,128)(2,1)} %chirp_ref.1) | copy-start | bytes 12292
  1.5 4.4 %collective-permute-start.2 = (bf16[25,64,128]{2,1,0:T(8,128)(2,1)S(1)}, bf16[25,64,128]{2,1,0:T(8,128)(2,1)S(1)}, u32[]{:S(2)}, u32[]{:S(2)}) collective-permute-start(bf16[25,64,128]{2,1,0:T(8,128)(2,1)S(1)} %get-tuple-element.22), channel_id=1, source_target_pairs={{2,3},{6,7},{10,11},{14,15},{18,19},{22,23},{26,27},{30,31}} | collective-permute-start | bytes 1228808 | tf_op jit(solution)/shard_map/ppermute | solution.py:312
  4.6 11.2 %collective-permute-start = (bf16[8,256,128]{2,1,0:T(8,128)(2,1)S(1)}, bf16[8,256,128]{2,1,0:T(8,128)(2,1)S(1)}, u32[]{:S(2)}, u32[]{:S(2)}) collective-permute-start(bf16[8,256,128]{2,1,0:T(8,128)(2,1)S(1)} %get-tuple-element.18), channel_id=1, source_target_pairs={{1,2},{5,6},{9,10},{13,14},{17,18},{21,22},{25,26},{29,30}} | collective-permute-start | bytes 1572872 | tf_op jit(solution)/shard_map/ppermute | solution.py:324

commit v29 on v28

--- a/solution.py
+++ b/solution.py
@@ -177,8 +177,7 @@
 def azimuth_kernel(lines_ref, out_ref, columns_held, taps, made, sems):
     pulses = taps.shape[0] // 2
     columns = pulses // LANES
-    tiles = sems.shape[0]
-    each = out_ref.shape[0] // tiles
+    tiles = out_ref.shape[0] // (2 * columns * LANES)
     sources = lines_ref.shape[0]
     rows = (lines_ref.shape[1] - EXTRA) // tiles
     turned = [
@@ -205,16 +204,17 @@
                     lane = target * pulses + column * LANES
                     taps[2 * line * LANES : 2 * (line + 1) * LANES, lane : lane + LANES] = block
     copies = []
-    for tile in range(tiles):
-        focused = jnp.dot(turned[tile], taps[...], preferred_element_type=F32)
-        into = pl.ds(tile * each, each)
+    spans = [(0, LANES // 2), (LANES // 2, LANES // 2)] + [(tile * LANES, LANES) for tile in range(1, tiles)]
+    for at, (first, bins) in enumerate(spans):
+        block = turned[first // LANES][first % LANES : first % LANES + bins]
+        focused = jnp.dot(block, taps[...], preferred_element_type=F32)
+        start = first * 2 * columns
         for part in range(2):
             for column in range(columns):
                 lane = part * pulses + column * LANES
-                made[pl.ds(tile * each + 2 * column + part, LANES, stride=2 * columns), :] = focused[
-                    :, lane : lane + LANES
-                ]
-        copies.append(pltpu.make_async_copy(made.at[into], out_ref.at[into], sems.at[tile]))
+                made[pl.ds(start + 2 * column + part, bins, stride=2 * columns), :] = focused[:, lane : lane + LANES]
+        into = pl.ds(start, bins * 2 * columns)
+        copies.append(pltpu.make_async_copy(made.at[into], out_ref.at[into], sems.at[at]))
         copies[-1].start()
     for copy in copies:
         copy.wait()
@@ -352,7 +352,7 @@
             pltpu.VMEM((width // LANES * 2 - 1, 2 * LANES, LANES), F32),
             pltpu.VMEM((width, width), BF),
             pltpu.VMEM((bin_count * width // LANES + 8, LANES), F32),
-            pltpu.SemaphoreType.DMA((bin_count // LANES,)),
+            pltpu.SemaphoreType.DMA((bin_count // LANES + 1,)),
         ],
     )(lines)
     focused = focused.reshape(1, bin_count, total_pulses // LANES, 2, LANES).swapaxes(2, 3)

time: 34.8 us -> 34.9 us (level)
  no operation moved by 1% of the time
where the time goes in v29:
time: 34.9 us; the launch traced here: 34.6 us
  blocking collectives  17.3 us (50%)
  waiting for transfers between devices  9.79 us (28%)
  starting transfers between devices  3.96 us (11%)
  Pallas kernels  2.49 us (7%)
  between operations  0.76 us (2%)
  local copies, waits for them, and re-layouts  0.36 us (1%)
    all_to_all x1, blocking collectives, on_device(): lax.all_to_all(compressed, 'pa', split_axis=0, concat_axis=0, tiled=True)  17.3 us
    ppermute x1, waiting for transfers between devices, on_device(): near = lax.ppermute(near, 'sa', [(1, 2)])  9.79 us
    ppermute x1, starting transfers between devices, on_device(): head = lax.ppermute(head, 'sa', [(2, 3)])  1.84 us
    pallas_call x1, Pallas kernels, on_device(): call(azimuth_kernel, (shape((bin_count * width // LANES, LANES), F32),),...  1.58 us
    ppermute x1, starting transfers between devices, on_device(): near = lax.ppermute(near, 'sa', [(1, 2)])  1.29 us
    ppermute x1, starting transfers between devices, on_device(): tail = lax.ppermute(tail, 'sa', [(0, 1), (1, 3)])  0.83 us
  transfers between devices with their start and end apart: 3, of which 1 were waited for; matrix products, arithmetic and copies ran while one was open for 0% of the time, Pallas kernels for 2%

profile of v29, /device:TPU:2, one launch (start us, length us, event | category | flops | bytes accessed | tf_op | source)
XLA Modules:
  0.0 34.6 jit_solution(12940121534964119540)
XLA Ops:
  0.0 0.0 copy-start
  0.0 0.8 %collective-permute-start.1 = (bf16[32,64,128]{2,1,0:T(8,128)(2,1)S(1)}, bf16[32,64,128]{2,1,0:T(8,128)(2,1)S(1)}, u32[]{:S(2)}, u32[]{:S(2)}) collective-permute-start(bf16[32,64,128]{2,1,0:T(8,128)(2,1)S(1)} %get-tuple-element.21), channel_id=1, source_target_pairs={{0,1},{1,3},{4,5},{5,7},{8,9},{9,11},{12,13},{13,15},{16,17},{17,1... | collective-permute-start | bytes 1572872 | tf_op jit(solution)/shard_map/ppermute | solution.py:310
  0.9 0.3 copy-done
  1.2 0.0 copy-start.1
  1.2 0.0 copy-start.3
  1.2 0.2 shard_map.56
  1.5 0.0 copy-start.2
  1.5 1.8 %collective-permute-start.2 = (bf16[25,64,128]{2,1,0:T(8,128)(2,1)S(1)}, bf16[25,64,128]{2,1,0:T(8,128)(2,1)S(1)}, u32[]{:S(2)}, u32[]{:S(2)}) collective-permute-start(bf16[25,64,128]{2,1,0:T(8,128)(2,1)S(1)} %get-tuple-element.22), channel_id=1, source_target_pairs={{2,3},{6,7},{10,11},{14,15},{18,19},{22,23},{26,27},{30,31}} | collective-permute-start | bytes 1228808 | tf_op jit(solution)/shard_map/ppermute | solution.py:312
  4.0 0.0 copy-done.1
  4.0 0.0 copy-done.3
  4.0 0.0 copy-done.2
  4.0 0.6 %shard_map.57 = (bf16[1280,256]{1,0:T(8,128)(2,1)S(1)}, bf16[8,16,128]{2,1,0:T(8,128)(2,1)S(1)}, f32[8,128]{1,0:T(8,128)S(1)}) custom-call(f32[8,128]{1,0:T(8,128)S(1)} %get-tuple-element.15.turn_in_ref, s32[1]{0:T(128)S(6)} %copy.7.window_ref, s32[4,8]{1,0:T(4,128)S(1)} %copy-done.3, bf16[2,1024]{1,0:T(2,128)(2,1)S(1)} %copy-done.2, ...), custom_call_target="tpu_custom_call" | custom-call | flops 1000 | bytes 1000 | tf_op jit(solution)/shard_map/pallas_call | solution.py:313
  4.6 1.3 %collective-permute-start = (bf16[8,256,128]{2,1,0:T(8,128)(2,1)S(1)}, bf16[8,256,128]{2,1,0:T(8,128)(2,1)S(1)}, u32[]{:S(2)}, u32[]{:S(2)}) collective-permute-start(bf16[8,256,128]{2,1,0:T(8,128)(2,1)S(1)} %get-tuple-element.18), channel_id=1, source_target_pairs={{1,2},{5,6},{9,10},{13,14},{17,18},{21,22},{25,26},{29,30}} | collective-permute-start | bytes 1572872 | tf_op jit(solution)/shard_map/ppermute | solution.py:324
  5.9 0.0 collective-permute-done.2.head_ref
  5.9 0.0 collective-permute-done.1.tail_ref
  5.9 9.8 %collective-permute-done.near_ref = bf16[8,256,128]{2,1,0:T(8,128)(2,1)S(1)} collective-permute-done((bf16[8,256,128]{2,1,0:T(8,128)(2,1)S(1)}, bf16[8,256,128]{2,1,0:T(8,128)(2,1)S(1)}, u32[]{:S(2)}, u32[]{:S(2)}) %collective-permute-start) | collective-permute-done | bytes 524320 | tf_op jit(solution)/shard_map/ppermute | solution.py:324
  15.8 17.3 %all_to_all.5.lines_ref = bf16[8,264,128]{2,1,0:T(8,128)(2,1)S(1)} all-to-all(bf16[8,264,128]{2,1,0:T(8,128)(2,1)S(1)} %shard_map.60), channel_id=1, replica_groups=mesh['pa'=8,'sa'=4] {'pa'}, dimensions={0} | all-to-all | bytes 1081344 | tf_op jit(solution)/shard_map/all_to_all | solution.py:345
  33.1 1.6 %shard_map.61 = f32[2048,128]{1,0:T(8,128)} custom-call(bf16[8,264,128]{2,1,0:T(8,128)(2,1)S(1)} %all_to_all.5.lines_ref), custom_call_target="tpu_custom_call" | custom-call | flops 1000 | bytes 1000 | tf_op jit(solution)/shard_map/pallas_call | solution.py:347
  (4 shorter events, 0.1 us)
Async XLA Ops:
  0.0 1.2 %copy-start = (bf16[32,2,8192]{2,1,0:T(2,128)(2,1)S(1)}, bf16[32,2,8192]{2,1,0:T(2,128)(2,1)}, u32[]{:S(2)}) copy-start(bf16[32,2,8192]{2,1,0:T(2,128)(2,1)} %raw_ref.7) | copy-start | bytes 3145732
  0.0 5.8 %collective-permute-start.1 = (bf16[32,64,128]{2,1,0:T(8,128)(2,1)S(1)}, bf16[32,64,128]{2,1,0:T(8,128)(2,1)S(1)}, u32[]{:S(2)}, u32[]{:S(2)}) collective-permute-start(bf16[32,64,128]{2,1,0:T(8,128)(2,1)S(1)} %get-tuple-element.21), channel_id=1, source_target_pairs={{0,1},{1,3},{4,5},{5,7},{8,9},{9,11},{12,13},{13,15},{16,17},{17,1... | collective-permute-start | bytes 1572872 | tf_op jit(solution)/shard_map/ppermute | solution.py:310
  1.2 2.7 %copy-start.1 = (bf16[8,2,512]{2,1,0:T(2,128)(2,1)S(1)}, bf16[8,2,512]{2,1,0:T(2,128)(2,1)}, u32[]{:S(2)}) copy-start(bf16[8,2,512]{2,1,0:T(2,128)(2,1)} %refs_ref.1) | copy-start | bytes 49156
  1.2 2.8 %copy-start.3 = (s32[4,8]{1,0:T(4,128)S(1)}, s32[4,8]{1,0:T(4,128)}, u32[]{:S(2)}) copy-start(s32[4,8]{1,0:T(4,128)} %index_ref.1) | copy-start | bytes 388
  1.5 2.5 %copy-start.2 = (bf16[2,1024]{1,0:T(2,128)(2,1)S(1)}, bf16[2,1024]{1,0:T(2,128)(2,1)}, u32[]{:S(2)}) copy-start(bf16[2,1024]{1,0:T(2,128)(2,1)} %chirp_ref.1) | copy-start | bytes 12292
  1.5 4.4 %collective-permute-start.2 = (bf16[25,64,128]{2,1,0:T(8,128)(2,1)S(1)}, bf16[25,64,128]{2,1,0:T(8,128)(2,1)S(1)}, u32[]{:S(2)}, u32[]{:S(2)}) collective-permute-start(bf16[25,64,128]{2,1,0:T(8,128)(2,1)S(1)} %get-tuple-element.22), channel_id=1, source_target_pairs={{2,3},{6,7},{10,11},{14,15},{18,19},{22,23},{26,27},{30,31}} | collective-permute-start | bytes 1228808 | tf_op jit(solution)/shard_map/ppermute | solution.py:312
  4.6 11.2 %collective-permute-start = (bf16[8,256,128]{2,1,0:T(8,128)(2,1)S(1)}, bf16[8,256,128]{2,1,0:T(8,128)(2,1)S(1)}, u32[]{:S(2)}, u32[]{:S(2)}) collective-permute-start(bf16[8,256,128]{2,1,0:T(8,128)(2,1)S(1)} %get-tuple-element.18), channel_id=1, source_target_pairs={{1,2},{5,6},{9,10},{13,14},{17,18},{21,22},{25,26},{29,30}} | collective-permute-start | bytes 1572872 | tf_op jit(solution)/shard_map/ppermute | solution.py:324
